TPU v7x, 32 devices: a whole 2x2x4 slice. The times are simulated.
32 devices in a mesh: track: 2 (over y), pix: 16 (over z, x, core).
Axes of the slice: x: 2, y: 2, z: 4, core: 2. Of those that a mesh axis runs over, the one named last changes fastest.
Arguments:
- phases: bfloat16 [2, 256, 131072], P('track', 'pix'), may hold values from -15 to 15
- coherent: int32 [2, 256, 1024], P('track', 'pix'), may hold values 0 or 1
- pairs: int32 [2, 256, 2], P('track'), may hold values from 0 to 199, as said below
- res_index: int32 [2, 4, 131072], P('track', None, 'pix'), may hold values from -128 to 128, as said below
- res_weight: float32 [2, 4, 131072], P('track', None, 'pix'), may hold values from 0.05 to 1
- coverage: int32 [2, 128, 8], P('track', 'pix'), may hold values 0 or 1
- los: float32 [2, 3], replicated
- north: float32 [128, 1024], P('pix'), may hold values from -6 to 6
Outputs:
- east_up: float32 [2, 128, 1024], P(None, 'pix', 'track')
- strain: float32 [3, 128, 1024], P(None, 'pix', 'track')
Inputs may be any that keep to these rules, and one draw needn't show every extreme that they name: `pairs`: each row holds an earlier epoch and a strictly later one. `res_index`: cell index plus offset lies within 0 to 131071.
All inputs are finite; a program needn't handle non-finite values. No bound on the sum of `coherent` or of `coverage` on one device may be relied on, other than what follows from the above.
Results may differ from a plain program's by a relative error of at most 0.0031.
Values may be sent and summed in bfloat16 or wider, within the bound.
No kernel may reach another device: no remote copies, remote signals or barrier semaphores. Data moves between devices by JAX's collectives and lax.ppermute only.
A program may use at most 128 MiB of HBM per device.

v0:
```python
import jax
import jax.numpy as jnp
from jax import lax
from jax.sharding import PartitionSpec as P

IFGS = 256
EPOCHS = 200
GRD = 8
GCOLS = 1024
HALO = 128
CTILE = 128


prior_var = 0.1
ridge_term = 0.5


def with_halo(shard, sides, width):
    for axis, dim in sides:
        size, length = (lax.axis_size(axis), shard.shape[dim])
        up = [(i, (i + 1) % size) for i in range(size - 1)]
        down = [(j, i) for i, j in up]
        last = lax.slice_in_dim(shard, length - width, length, axis=dim)
        initial = lax.slice_in_dim(shard, 0, width, axis=dim)
        before = lax.ppermute(last, axis, up)
        after = lax.ppermute(initial, axis, down)
        shard = jnp.concatenate([before, shard, after], axis=dim)
    return shard


def setup_track(pair_rows):
    epochs = jnp.arange(EPOCHS, dtype=jnp.int32)
    design = (epochs[None, :] == pair_rows[:, 1:2]).astype(jnp.float32) - (
        epochs[None, :] == pair_rows[:, 0:1]
    ).astype(jnp.float32)
    normal = jnp.dot(
        design.T, design, precision=lax.Precision.HIGHEST, preferred_element_type=jnp.float32
    ) + jnp.eye(EPOCHS, dtype=jnp.float32)
    factor = jnp.linalg.cholesky(normal)
    pseudo = jax.scipy.linalg.cho_solve((factor, True), design.T)
    centred = jnp.arange(EPOCHS).astype(jnp.float32) - (EPOCHS - 1) / 2.0
    slope = centred * (EPOCHS - 1) / jnp.sum(centred * centred)
    return (design.astype(jnp.bfloat16), pseudo.astype(jnp.bfloat16), slope)


def invert_block(stack, design_bf, pseudo_bf, slope):
    series = jnp.dot(pseudo_bf, stack, preferred_element_type=jnp.float32)
    velocity = jnp.dot(
        slope, series, precision=lax.Precision.HIGHEST, preferred_element_type=jnp.float32
    )
    fitted = jnp.dot(design_bf, series.astype(jnp.bfloat16), preferred_element_type=jnp.float32)
    misfit = stack.astype(jnp.float32) - fitted
    variance = jnp.sum(misfit * misfit, axis=0) / IFGS
    return jnp.stack([velocity, variance])


def solve_cells(vals, cover, north_part, los):
    east_c = los[:, 0][:, None, None]
    north_c = los[:, 1][:, None, None]
    up_c = los[:, 2][:, None, None]
    weight = cover / (vals[1] + prior_var)
    target = vals[0] - north_c * north_part[None]
    a11 = jnp.sum(weight * east_c * east_c, axis=0) + ridge_term
    a12 = jnp.sum(weight * east_c * up_c, axis=0)
    a22 = jnp.sum(weight * up_c * up_c, axis=0) + ridge_term
    b1 = jnp.sum(weight * east_c * target, axis=0)
    b2 = jnp.sum(weight * up_c * target, axis=0)
    determ = a11 * a22 - a12 * a12
    return ((a22 * b1 - a12 * b2) / determ, (a11 * b2 - a12 * b1) / determ)


def stencil(padded):
    east_p = padded[0]
    north_p = padded[1]
    exx = (east_p[1:-1, 2:] - east_p[1:-1, :-2]) / 2.0
    eyy = (north_p[2:, 1:-1] - north_p[:-2, 1:-1]) / 2.0
    exy = (east_p[2:, 1:-1] - east_p[:-2, 1:-1] + north_p[1:-1, 2:] - north_p[1:-1, :-2]) / 4.0
    return jnp.stack([exx, eyy, exy])


def widen_cover(cover):
    count, rows_here, tiles = cover.shape
    return jnp.broadcast_to(cover[:, :, :, None], (count, rows_here, tiles, CTILE)).reshape(
        count, rows_here, tiles * CTILE
    )


def per_device(phases, coherent, pairs, res_index, res_weight, coverage, los, north):
    design_bf, pseudo_bf, slope = setup_track(pairs[0])
    local_ifgs = phases.shape[1]
    cells = phases.shape[2]
    parts = lax.axis_size("pix")
    width = cells // parts
    blocks = coherent.shape[2]
    blocked = phases[0].reshape(local_ifgs, blocks, cells // blocks)
    masked = jnp.where(coherent[0][:, :, None] == 1, blocked, jnp.zeros((), jnp.bfloat16))
    masked = masked.reshape(local_ifgs, parts, width)
    fields = invert_block(
        lax.all_to_all(masked, "pix", split_axis=1, concat_axis=0, tiled=True)[:, 0, :],
        design_bf,
        pseudo_bf,
        slope,
    )
    extended = with_halo(fields, (("pix", 1),), HALO)
    position = jnp.arange(width, dtype=jnp.int32)
    local = position[None, :] + res_index[0] + HALO
    picked = jnp.take(extended, local, axis=1)
    weight = res_weight[0]
    grid = jnp.sum(picked * weight[None], axis=1) / jnp.sum(weight, axis=0)
    grid_four = grid.reshape(2, 1, GRD, GCOLS)
    cover_four = coverage.astype(jnp.float32).reshape(1, 1, GRD, coverage.shape[2])
    column_block = lax.axis_index("track")
    span = GCOLS // lax.axis_size("track")
    vals, cover = (
        lax.all_gather(grid_four, "track", axis=1, tiled=True),
        lax.all_gather(cover_four, "track", axis=1, tiled=True),
    )
    cover_cells = widen_cover(cover[0])
    east, up = solve_cells(vals, cover_cells, north, los)
    padded = with_halo(jnp.stack([east, north]), (("pix", 1),), 1)
    padded = jnp.pad(padded, ((0, 0), (0, 0), (1, 1)))
    strain = lax.dynamic_slice_in_dim(stencil(padded), column_block * span, span, 2)
    east_up = lax.dynamic_slice_in_dim(jnp.stack([east, up]), column_block * span, span, 2)
    return (east_up, strain)


def solution(mesh):
    in_specs = (
        P("track", "pix", None),
        P("track", "pix", None),
        P("track", None, None),
        P("track", None, "pix"),
        P("track", None, "pix"),
        P("track", "pix", None),
        P(),
        P("pix", None),
    )
    out_specs = (P(None, "pix", "track"), P(None, "pix", "track"))
    return jax.shard_map(
        per_device, mesh=mesh, in_specs=in_specs, out_specs=out_specs, check_vma=False
    )
```

profile of v0, /device:TPU:16, one launch (start us, length us, event | category | flops | bytes accessed | tf_op | source)
XLA Modules:
  0.0 285.9 jit_solution(6983933264739946609)
XLA Ops:
  0.6 0.9 compare_bitcast_fusion
  1.5 4.6 %broadcast_in_dim.46 = pred[16,1024,128]{2,1,0:T(8,128)(4,1)} broadcast(pred[16,1024]{1,0:T(8,128)(4,1)S(1)} %compare_bitcast_fusion), dimensions={0,1} | broadcast | bytes 2113536 | tf_op jit(solution)/shard_map/jit(_where)/broadcast_in_dim | solution.py:96
  6.1 5.3 %broadcast_in_dim.47 = pred[16,16,8192]{2,1,0:T(8,128)(4,1)S(1)} reshape(pred[16,1024,128]{2,1,0:T(8,128)(4,1)} %broadcast_in_dim.46) | data formatting | bytes 4194304 | tf_op jit(solution)/shard_map/jit(_where)/broadcast_in_dim | solution.py:96
  11.3 4.5 %copy.23 = bf16[2,8,16,8192]{3,2,1,0:T(8,128)(2,1)S(1)} copy(bf16[2,8,16,8192]{3,1,2,0:T(8,128)(2,1)} %bitcast.92) | data formatting | bytes 8388608
  15.9 0.7 bitcast_select_fusion
  16.5 4.3 %copy.20 = bf16[16,16,8192]{2,0,1:T(8,128)(2,1)} copy(bf16[16,16,8192]{2,1,0:T(8,128)(2,1)S(1)} %bitcast_select_fusion) | data formatting | bytes 8388608 | tf_op jit(solution)/shard_map/jit(_where)/select_n | solution.py:96
  20.8 0.0 copy-start.1
  20.8 6.3 %all-to-all-start = ((bf16[16,16,8192]{2,0,1:T(8,128)(2,1)}), bf16[16,16,8192]{2,0,1:T(8,128)(2,1)}, u32[]{:S(2)}, u32[]{:S(2)}) async-start(bf16[16,16,8192]{2,0,1:T(8,128)(2,1)} %copy.20), calls=%async_computation | async-start | bytes 8388608 | tf_op jit(solution)/shard_map/all_to_all | solution.py:99
  27.1 0.0 copy-done.5
  27.1 0.7 fusion.6
  27.9 0.1 copy.19
  28.0 0.1 fusion.8
  28.1 11.7 %cholesky.51 = f32[128,128]{1,0:T(8,128)S(1)} custom-call(f32[128,128]{1,0:T(8,128)S(1)} %cholesky.124), custom_call_target="Cholesky" | custom-call | tf_op jit(solution)/shard_map/jit(cholesky)/cholesky | solution.py:39
  39.8 9.8 %custom-call.18 = f32[1,128,128]{1,2,0:T(8,128)S(1)} custom-call(f32[1,128,128]{2,1,0:T(8,128)S(1)} %get-tuple-element.42), custom_call_target="InvertDiagBlocksLowerTriangular" | custom-call | tf_op jit(solution)/shard_map/jit(cholesky)/cholesky | solution.py:39
  49.7 0.2 constant_dynamic-update-slice_fusion
  49.9 0.2 convolution_subtract_fusion.3
  50.1 6.6 %cholesky.110 = f32[72,72]{1,0:T(8,128)S(1)} custom-call(f32[72,72]{1,0:T(8,128)S(1)} %convolution_subtract_fusion.3), custom_call_target="Cholesky" | custom-call | tf_op jit(solution)/shard_map/jit(cholesky)/cholesky | solution.py:39
  56.7 0.6 compare_reduce_fusion
  57.4 0.6 compare_reduce_fusion.1
  59.4 0.1 fusion.23
  59.5 19.7 %custom-call.19 = f32[2,128,128]{1,2,0:T(8,128)S(1)} custom-call(f32[2,128,128]{2,1,0:T(8,128)S(1)} %pad_maximum_fusion), custom_call_target="InvertDiagBlocksLowerTriangular" | custom-call | tf_op jit(solution)/shard_map/jit(_cho_solve)/triangular_solve | solution.py:40
  79.2 0.0 copy-done.1
  79.2 0.1 fusion.11
  79.3 0.0 copy-done
  79.3 0.1 reduce_sum.87
  79.4 0.8 multiply_reduce_fusion.6
  80.2 0.7 multiply_divide_fusion
  80.8 0.0 copy-done.3
  80.8 0.2 slice_reduce_fusion
  81.1 0.3 fusion.12
  81.4 0.2 convolution_subtract_fusion.2
  81.6 0.3 fusion.30
  81.9 0.2 fusion.43
  82.1 0.3 convolution_subtract_fusion.1
  82.4 0.3 convolution_convert_fusion
  82.7 0.1 compare_and_fusion
  82.9 37.0 %all-to-all-done = bf16[16,16,8192]{2,0,1:T(8,128)(2,1)} async-done(((bf16[16,16,8192]{2,0,1:T(8,128)(2,1)}), bf16[16,16,8192]{2,0,1:T(8,128)(2,1)}, u32[]{:S(2)}, u32[]{:S(2)}) %all-to-all-start) | async-done | bytes 4194336 | tf_op jit(solution)/shard_map/all_to_all | solution.py:99
  119.8 3.2 %fusion.18 = f32[200,8192]{1,0:T(8,128)S(1)} fusion(bf16[256,8192]{1,0:T(8,128)(2,1)} %bitcast.15, bf16[72,256]{1,0:T(8,128)(2,1)S(1)} %get-tuple-element.49, bf16[128,256]{1,0:T(8,128)(2,1)S(1)} %convolution_convert_fusion), kind=kOutput, calls=%fused_computation.45 | convolution fusion | flops 839065600 | bytes 10850304 | tf_op jit(solution)/shard_map/dot_general | solution.py:47
  123.0 4.0 %fusion.2 = f32[8192]{0:T(1024)S(1)} fusion(f32[200,8192]{1,0:T(8,128)S(1)} %fusion.18, bf16[256,8192]{1,0:T(8,128)(2,1)} %bitcast.15, s32[256]{0:T(256)S(1)} %bitcast.104, s32[256]{0:T(256)S(1)} %bitcast.101), kind=kOutput, calls=%fused_computation.6 | convolution fusion | flops 849186816 | bytes 10782720 | tf_op jit(solution)/shard_map/dot_general | solution.py:51
  127.0 0.0 copy-start.4
  127.0 3.2 %fusion.44 = f32[1,8192]{1,0:T(1,128)S(1)} fusion(f32[200,1]{0,1:T(1,128)S(1)} %bitcast.106, f32[200,8192]{1,0:T(8,128)S(1)} %fusion.18), kind=kOutput, calls=%fused_computation.126 | convolution fusion | flops 19660800 | bytes 6587168 | tf_op jit(solution)/shard_map/dot_general | solution.py:48
  130.3 1.9 collective-permute-start
  132.2 4.5 %collective-permute-start.1 = (f32[2,128]{1,0:T(2,128)S(1)}, f32[2,128]{1,0:T(2,128)S(1)}, u32[]{:S(2)}, u32[]{:S(2)}) collective-permute-start(f32[2,128]{1,0:T(2,128)S(1)} %get-tuple-element.40), channel_id=1, source_target_pairs={{1,0},{2,1},{3,2},{4,3},{5,4},{6,5},{7,6},{8,7},{9,8},{10,9},{11,1... | collective-permute-start | bytes 3080 | tf_op jit(solution)/shard_map/ppermute | solution.py:26
  136.7 0.0 copy-done.4
  136.8 4.3 %all-gather = f32[2,8,8]{2,1,0:T(8,128)S(1)} all-gather(f32[1,8,8]{2,1,0:T(8,128)S(1)} %convert_element_type.38), channel_id=2, replica_groups=mesh['track'=2,'pix'=16] {'track'}, dimensions={0}, use_global_device_ids=true | all-gather | bytes 768 | tf_op jit(solution)/shard_map/all_gather | solution.py:116
  141.1 0.1 broadcast_in_dim.43
  141.2 0.0 collective-permute-done
  141.2 0.0 collective-permute-done.1
  141.2 0.1 pad_maximum_fusion.1
  141.3 2.7 copy.21
  144.0 110.4 %gather_fusion = f32[32768,2]{1,0:T(8,128)} fusion(f32[2,8448]{0,1:T(8,128)} %copy.21, s32[32768]{0:T(1024)S(1)} %broadcast_clamp_fusion), kind=kCustom, calls=%fused_computation | custom fusion | bytes 655360 | tf_op jit(solution)/shard_map/jit(_take)/gather | solution.py:107
  254.4 14.8 %multiply_reduce_fusion = f32[8192,2]{1,0:T(8,128)} fusion(f32[4,8192,2]{2,1,0:T(8,128)} %bitcast.90, f32[4,8192]{1,0:T(4,128)S(1)} %bitcast.93, pred[4,8192]{1,0:T(4,128)(4,1)S(1)} %compare_and_fusion), kind=kLoop, calls=%fused_computation.1 | loop fusion | flops 180224 | bytes 491520 | tf_op jit(solution)/shard_map/reduce_sum | solution.py:109
  269.2 2.8 copy.22
  272.1 4.9 %all_gather.7 = f32[2,2,8,1024]{3,2,1,0:T(8,128)S(1)} all-gather(f32[2,1,8,1024]{3,2,1,0:T(8,128)S(1)} %broadcast_divide_fusion), channel_id=1, replica_groups=mesh['track'=2,'pix'=16] {'track'}, dimensions={1}, use_global_device_ids=true | all-gather | bytes 196608 | tf_op jit(solution)/shard_map/all_gather | solution.py:115
  277.0 0.0 copy-done.2
  277.0 0.1 multiply_reduce_fusion.2
  277.2 1.9 collective-permute-start.2
  279.1 4.5 %collective-permute-start.3 = (f32[2,1,1024]{2,1,0:T(1,128)S(1)}, f32[2,1,1024]{2,1,0:T(1,128)S(1)}, u32[]{:S(2)}, u32[]{:S(2)}) collective-permute-start(f32[2,1,1024]{2,1,0:T(1,128)S(1)} %get-tuple-element.38), channel_id=1, source_target_pairs={{1,0},{2,1},{3,2},{4,3},{5,4},{6,5},{7,6},{8,7},{9,8},{10,9},{11,1... | collective-permute-start | bytes 24584 | tf_op jit(solution)/shard_map/ppermute | solution.py:26
  283.6 0.6 fusion.33
  284.3 0.0 collective-permute-done.2
  284.3 0.7 collective-permute-done.3
  285.0 0.1 select_maximum_fusion
  285.2 0.1 fusion.35
  285.3 0.6 fusion.27
  (26 shorter events, 0.4 us)
Async XLA Ops:
  20.8 6.3 %copy-start.5 = (s32[1,256,2]{1,2,0:T(2,128)S(1)}, s32[1,256,2]{1,2,0:T(2,128)}, u32[]{:S(2)}) copy-start(s32[1,256,2]{1,2,0:T(2,128)} %param.10) | copy-start | bytes 6148
  20.8 58.4 %copy-start.1 = (s32[1,4,8192]{2,1,0:T(4,128)S(1)}, s32[1,4,8192]{2,1,0:T(4,128)}, u32[]{:S(2)}) copy-start(s32[1,4,8192]{2,1,0:T(4,128)} %param.11) | copy-start | bytes 393220
  20.8 58.4 %copy-start = (f32[1,4,8192]{2,1,0:T(4,128)S(1)}, f32[1,4,8192]{2,1,0:T(4,128)}, u32[]{:S(2)}) copy-start(f32[1,4,8192]{2,1,0:T(4,128)} %param.12) | copy-start | bytes 393220
  20.8 60.0 %copy-start.3 = (f32[2,3]{1,0:T(2,128)S(1)}, f32[2,3]{1,0:T(2,128)}, u32[]{:S(2)}) copy-start(f32[2,3]{1,0:T(2,128)} %param.14) | copy-start | bytes 76
  20.8 99.0 %all-to-all-start = ((bf16[16,16,8192]{2,0,1:T(8,128)(2,1)}), bf16[16,16,8192]{2,0,1:T(8,128)(2,1)}, u32[]{:S(2)}, u32[]{:S(2)}) async-start(bf16[16,16,8192]{2,0,1:T(8,128)(2,1)} %copy.20), calls=%async_computation | async-start | bytes 8388608 | tf_op jit(solution)/shard_map/all_to_all | solution.py:99
  127.0 9.7 %copy-start.4 = (s32[1,8,8]{2,1,0:T(8,128)S(1)}, s32[1,8,8]{2,1,0:T(8,128)}, u32[]{:S(2)}) copy-start(s32[1,8,8]{2,1,0:T(8,128)} %param.13) | copy-start | bytes 772
  130.3 11.0 %collective-permute-start = (f32[2,128]{1,0:T(2,128)S(1)}, f32[2,128]{1,0:T(2,128)S(1)}, u32[]{:S(2)}, u32[]{:S(2)}) collective-permute-start(f32[2,128]{1,0:T(2,128)S(1)} %get-tuple-element.39), channel_id=1, source_target_pairs={{0,1},{1,2},{2,3},{3,4},{4,5},{5,6},{6,7},{7,8},{8,9},{9,10},{10,1... | collective-permute-start | bytes 3080 | tf_op jit(solution)/shard_map/ppermute | solution.py:25
  132.2 9.1 %collective-permute-start.1 = (f32[2,128]{1,0:T(2,128)S(1)}, f32[2,128]{1,0:T(2,128)S(1)}, u32[]{:S(2)}, u32[]{:S(2)}) collective-permute-start(f32[2,128]{1,0:T(2,128)S(1)} %get-tuple-element.40), channel_id=1, source_target_pairs={{1,0},{2,1},{3,2},{4,3},{5,4},{6,5},{7,6},{8,7},{9,8},{10,9},{11,1... | collective-permute-start | bytes 3080 | tf_op jit(solution)/shard_map/ppermute | solution.py:26
  269.2 7.8 %copy-start.2 = (f32[8,1024]{1,0:T(8,128)S(1)}, f32[8,1024]{1,0:T(8,128)}, u32[]{:S(2)}) copy-start(f32[8,1024]{1,0:T(8,128)} %param.15) | copy-start | bytes 98308
  277.2 7.1 %collective-permute-start.2 = (f32[2,1,1024]{2,1,0:T(1,128)S(1)}, f32[2,1,1024]{2,1,0:T(1,128)S(1)}, u32[]{:S(2)}, u32[]{:S(2)}) collective-permute-start(f32[2,1,1024]{2,1,0:T(1,128)S(1)} %get-tuple-element.37), channel_id=1, source_target_pairs={{0,1},{1,2},{2,3},{3,4},{4,5},{5,6},{6,7},{7,8},{8,9},{9,10},{10,1... | collective-permute-start | bytes 24584 | tf_op jit(solution)/shard_map/ppermute | solution.py:25
  279.1 5.9 %collective-permute-start.3 = (f32[2,1,1024]{2,1,0:T(1,128)S(1)}, f32[2,1,1024]{2,1,0:T(1,128)S(1)}, u32[]{:S(2)}, u32[]{:S(2)}) collective-permute-start(f32[2,1,1024]{2,1,0:T(1,128)S(1)} %get-tuple-element.38), channel_id=1, source_target_pairs={{1,0},{2,1},{3,2},{4,3},{5,4},{6,5},{7,6},{8,7},{9,8},{10,9},{11,1... | collective-permute-start | bytes 24584 | tf_op jit(solution)/shard_map/ppermute | solution.py:26
where the time goes:
time: 288 us; the launch traced here: 286 us
  local copies, waits for them, and re-layouts  135 us (47%)
  other arithmetic  69.1 us (24%)
  waiting for transfers between devices  37.7 us (13%)
  starting transfers between devices  19.2 us (7%)
  matrix products  13.1 us (5%)
  blocking collectives  9.28 us (3%)
    gather x1, local copies, waits for them, and re-layouts, per_device(): picked = jnp.take(extended, local, axis=1)  110 us
    all_to_all x1, waiting for transfers between devices, per_device(): lax.all_to_all(masked, 'pix', split_axis=1, concat_axis=0, tiled=True)  37 us
    another operation x7, other arithmetic, setup_track(): factor = jnp.linalg.cholesky(normal)  29.4 us
    another operation x6, other arithmetic, setup_track(): pseudo = jax.scipy.linalg.cho_solve((factor, True), design.T)  19.8 us
    reduce_sum x2, other arithmetic, per_device(): grid = jnp.sum(picked * weight[None], axis=1) / jnp.sum(weight, axis=0)  14.8 us
    broadcast_in_dim x2, local copies, waits for them, and re-layouts, per_device(): jnp.where(coherent[0][:, :, None] == 1, blocked, jnp.zeros((), jnp.bfloat...  9.86 us
    ppermute x2, starting transfers between devices, with_halo(): after = lax.ppermute(initial, axis, down)  9.08 us
    all_to_all x1, starting transfers between devices, per_device(): lax.all_to_all(masked, 'pix', split_axis=1, concat_axis=0, tiled=True)  6.3 us
  transfers between devices with their start and end apart: 5, of which 2 were waited for; matrix products, arithmetic and copies ran while one was open for 19% of the time, Pallas kernels for 0%

commit v1 on v0

v1 whole, which is shorter than its diff:
```python
import functools

import jax
import jax.numpy as jnp
from jax import lax
from jax.experimental import pallas as pl
from jax.experimental.pallas import tpu as pltpu
from jax.sharding import PartitionSpec as P

EPOCHS = 200
ROWS = 208
HALO = 128
CTILE = 128
MBLK = 128
LANES = 128


prior_var = 0.1
ridge_term = 0.5


def pack_kernel(span, flags_ref, before_ref, x_ref, after_ref, out_ref):
    step = pl.program_id(0)
    steps = pl.num_programs(0)
    each = span // MBLK

    def flags_at(block):
        start = pl.multiple_of(block * LANES, LANES)
        return (flags_ref[:, pl.ds(start, LANES)] == 1).astype(jnp.float32)

    def masked(values, flags, j):
        spread = jnp.broadcast_to(flags[:, j : j + 1], values.shape).astype(jnp.bfloat16)
        return values * spread

    flags = flags_at(step)
    parts = out_ref.shape[0]
    for j in range(parts * each):
        part, inner = divmod(j, each)
        block = masked(x_ref[:, j * MBLK : (j + 1) * MBLK], flags, j)
        out_ref[part, :, HALO + inner * MBLK : HALO + (inner + 1) * MBLK] = block
        if inner == 0 and part > 0:
            out_ref[part - 1, :, HALO + span :] = block
        if inner == each - 1 and part < parts - 1:
            out_ref[part + 1, :, :HALO] = block
    earlier = flags_at(jnp.maximum(step - 1, 0))
    later = flags_at(jnp.minimum(step + 1, steps - 1))
    out_ref[0, :, :HALO] = masked(before_ref[...], earlier, LANES - 1)
    out_ref[parts - 1, :, HALO + span :] = masked(after_ref[...], later, 0)


def pack(phases, flags, parts):
    ifgs, cells = phases.shape
    blocks = flags.shape[1]
    span = cells // parts
    steps = blocks // LANES
    each = parts // steps
    return pl.pallas_call(
        functools.partial(pack_kernel, span),
        grid=(steps,),
        in_specs=[
            pl.BlockSpec((ifgs, blocks), lambda i: (0, 0)),
            pl.BlockSpec((ifgs, MBLK), lambda i: (0, jnp.maximum(i * LANES - 1, 0))),
            pl.BlockSpec((ifgs, each * span), lambda i: (0, i)),
            pl.BlockSpec((ifgs, MBLK), lambda i: (0, jnp.minimum((i + 1) * LANES, blocks - 1))),
        ],
        out_specs=pl.BlockSpec((each, ifgs, span + 2 * HALO), lambda i: (i, 0, 0)),
        out_shape=jax.ShapeDtypeStruct((parts, ifgs, span + 2 * HALO), jnp.bfloat16),
        compiler_params=pltpu.CompilerParams(vmem_limit_bytes=32 * 1024 * 1024),
        name="mask_pack",
    )(flags, phases, phases, phases)


def extend_kernel(pseudo_ref, slope_ref, out_ref):
    pseudo = pseudo_ref[...].astype(jnp.bfloat16)
    row = jnp.sum(pseudo.astype(jnp.float32) * slope_ref[...], axis=0, keepdims=True)
    high = row.astype(jnp.bfloat16).astype(jnp.float32)
    rest = row - high
    middle = rest.astype(jnp.bfloat16).astype(jnp.float32)
    low = rest - middle
    place = lax.broadcasted_iota(jnp.int32, (ROWS - EPOCHS, row.shape[1]), 0)
    terms = jnp.where(place == 0, high, jnp.where(place == 1, middle, jnp.where(place == 2, low, 0.0)))
    whole = jnp.concatenate([pseudo.astype(jnp.float32), terms], axis=0)
    out_ref[...] = whole.astype(jnp.bfloat16)


def setup_track(pair_rows):
    epochs = jnp.arange(ROWS, dtype=jnp.int32)
    wide = (epochs[None, :] == pair_rows[:, 1:2]).astype(jnp.float32) - (
        epochs[None, :] == pair_rows[:, 0:1]
    ).astype(jnp.float32)
    design = wide[:, :EPOCHS]
    normal = jnp.dot(
        design.T, design, precision=lax.Precision.HIGHEST, preferred_element_type=jnp.float32
    ) + jnp.eye(EPOCHS, dtype=jnp.float32)
    factor = jnp.linalg.cholesky(normal)
    pseudo = jax.scipy.linalg.cho_solve((factor, True), design.T)
    centred = jnp.arange(EPOCHS).astype(jnp.float32) - (EPOCHS - 1) / 2.0
    slope = centred * (EPOCHS - 1) / jnp.sum(centred * centred)
    extended = pl.pallas_call(
        extend_kernel,
        out_shape=jax.ShapeDtypeStruct((ROWS, pair_rows.shape[0]), jnp.bfloat16),
        name="extend_pseudo",
    )(pseudo, slope[:, None])
    return wide.astype(jnp.bfloat16), extended


def pick(source, lane):
    return jnp.take_along_axis(source, lane, axis=1, mode="promise_in_bounds")


def invert_kernel(
    tile, stack_ref, pseudo_ref, design_ref, index_ref, weight_ref, cover_ref, north_ref, los_ref, out_ref, fields_ref
):
    step = pl.program_id(0)
    ifgs, width = stack_ref.shape
    chunk_rows = width // LANES
    base = step * chunk_rows
    for first in range(0, width, tile):
        stack = stack_ref[:, first : first + tile]
        series = jnp.dot(pseudo_ref[...], stack, preferred_element_type=jnp.float32)
        velocity = jnp.sum(series[EPOCHS:], axis=0, keepdims=True)
        fitted = jnp.dot(design_ref[...], series.astype(jnp.bfloat16), preferred_element_type=jnp.float32)
        misfit = stack.astype(jnp.float32) - fitted
        variance = jnp.sum(misfit * misfit, axis=0, keepdims=True) / ifgs
        for k in range(tile // LANES):
            row = pl.ds(base + first // LANES + k, 1)
            fields_ref[0, row, :] = velocity[:, k * LANES : (k + 1) * LANES]
            fields_ref[1, row, :] = variance[:, k * LANES : (k + 1) * LANES]

    @pl.when(step == pl.num_programs(0) - 1)
    def _():
        taps, rows, _ = index_ref.shape
        lanes = lax.broadcasted_iota(jnp.int32, (8, LANES), 1)
        for r in range(0, rows, 8):
            here = slice(r, r + 8)
            near = [[fields_ref[f, r + k : r + k + 8, :] for k in range(3)] for f in range(2)]
            sums = [jnp.zeros((8, LANES), jnp.float32)] * 2
            total = jnp.zeros((8, LANES), jnp.float32)
            for b in range(taps):
                weight = weight_ref[b, here, :]
                place = lanes + index_ref[b, here, :] + HALO
                lane = place & (LANES - 1)
                which = place >> 7
                total = total + weight
                for f in range(2):
                    low, mid, high = (pick(near[f][k], lane) for k in range(3))
                    taken = jnp.where(which == 0, low, jnp.where(which == 1, mid, high))
                    sums[f] = sums[f] + taken * weight
            velocity = sums[0] / total
            variance = sums[1] / total
            out_ref[0, here, :] = cover_ref[here, :] / (variance + prior_var)
            out_ref[1, here, :] = velocity - los_ref[1] * north_ref[here, :]


def invert(stack, pseudo, design, index, weight, cover, north, los):
    ifgs, width = stack.shape
    rows = index.shape[1]
    blocks = width // LANES
    chunk_blocks = max(n for n in range(2, blocks + 1, 2) if blocks % n == 0 and n <= 24)
    chunk = chunk_blocks * LANES
    tile = 2 * LANES

    def whole(a):
        return pl.BlockSpec(a.shape, lambda i: (0,) * a.ndim)

    return pl.pallas_call(
        functools.partial(invert_kernel, tile),
        grid=(width // chunk,),
        in_specs=[
            pl.BlockSpec((ifgs, chunk), lambda i: (0, i)),
            whole(pseudo),
            whole(design),
            whole(index),
            whole(weight),
            whole(cover),
            whole(north),
            pl.BlockSpec(memory_space=pltpu.SMEM),
        ],
        out_specs=pl.BlockSpec((2, rows, LANES), lambda i: (0, 0, 0)),
        out_shape=jax.ShapeDtypeStruct((2, rows, LANES), jnp.float32),
        scratch_shapes=[pltpu.VMEM((2, -(-blocks // 8) * 8, LANES), jnp.float32)],
        compiler_params=pltpu.CompilerParams(vmem_limit_bytes=40 * 1024 * 1024),
        name="invert_resample",
    )(stack, pseudo, design, index, weight, cover, north, los)


def solve_kernel(tiles, vals_ref, north_ref, los_ref, east_ref, up_ref, first_ref, last_ref):
    tracks, _, rows, _ = vals_ref.shape
    a11 = a12 = a22 = b1 = b2 = 0.0
    for t in range(tracks):
        weight, target = vals_ref[t, 0], vals_ref[t, 1]
        east_c, up_c = los_ref[t, 0], los_ref[t, 2]
        by_east, by_up = weight * east_c, weight * up_c
        a11 = a11 + by_east * east_c
        a12 = a12 + by_east * up_c
        a22 = a22 + by_up * up_c
        b1 = b1 + by_east * target
        b2 = b2 + by_up * target
    a11 = a11 + ridge_term
    a22 = a22 + ridge_term
    determ = a11 * a22 - a12 * a12
    east = (a22 * b1 - a12 * b2) / determ
    up = (a11 * b2 - a12 * b1) / determ
    east_ref[...] = east
    up_ref[...] = up
    first_ref[0] = east[:tiles]
    first_ref[1] = north_ref[:tiles, :]
    last_ref[0] = east[rows - tiles :]
    last_ref[1] = north_ref[rows - tiles :, :]


def solve(vals, north, los, tiles):
    rows = vals.shape[2]
    field = jax.ShapeDtypeStruct((rows, LANES), jnp.float32)
    edge = jax.ShapeDtypeStruct((2, tiles, LANES), jnp.float32)
    vmem = pl.BlockSpec(memory_space=pltpu.VMEM)
    return pl.pallas_call(
        functools.partial(solve_kernel, tiles),
        in_specs=[vmem, vmem, pl.BlockSpec(memory_space=pltpu.SMEM)],
        out_specs=[vmem] * 4,
        out_shape=[field, field, edge, edge],
        name="solve_cells",
    )(vals, north, los)


def strain_kernel(tiles, own, block_ref, east_ref, up_ref, north_ref, before_ref, after_ref, east_up_ref, strain_ref, work_ref):
    rows = east_ref.shape[0]
    lane = lax.broadcasted_iota(jnp.int32, (rows, LANES), 1)
    tile = lax.broadcasted_iota(jnp.int32, (rows, LANES), 0) % tiles

    def across(field):
        right = jnp.where(tile == tiles - 1, 0.0, pltpu.roll(field, rows - 1, 0))
        left = jnp.where(tile == 0, 0.0, pltpu.roll(field, 1, 0))
        following = jnp.where(lane == LANES - 1, pltpu.roll(right, LANES - 1, 1), pltpu.roll(field, LANES - 1, 1))
        previous = jnp.where(lane == 0, pltpu.roll(left, 1, 1), pltpu.roll(field, 1, 1))
        return following - previous

    def down(field, which):
        below = jnp.concatenate([field[tiles:], after_ref[which]], axis=0)
        above = jnp.concatenate([before_ref[which], field[: rows - tiles]], axis=0)
        return below - above

    east = east_ref[...]
    north = north_ref[...]
    work_ref[0] = east
    work_ref[1] = up_ref[...]
    work_ref[2] = across(east) / 2.0
    work_ref[3] = down(north, 1) / 2.0
    work_ref[4] = (down(east, 0) + across(north)) / 4.0
    start = block_ref[0] * own
    for field in range(5):
        target, at = (east_up_ref, field) if field < 2 else (strain_ref, field - 2)
        for i in range(rows // tiles):
            for j in range(own):
                target[at, i : i + 1, j * LANES : (j + 1) * LANES] = work_ref[field, pl.ds(i * tiles + start + j, 1), :]


def strain(block, east, up, north, before, after, tiles, own):
    rows = east.shape[0]
    shape = (rows // tiles, own * LANES)
    vmem = pl.BlockSpec(memory_space=pltpu.VMEM)
    return pl.pallas_call(
        functools.partial(strain_kernel, tiles, own),
        in_specs=[pl.BlockSpec(memory_space=pltpu.SMEM)] + [vmem] * 5,
        out_specs=[vmem] * 2,
        out_shape=[jax.ShapeDtypeStruct((2, *shape), jnp.float32), jax.ShapeDtypeStruct((3, *shape), jnp.float32)],
        scratch_shapes=[pltpu.VMEM((5, rows, LANES), jnp.float32)],
        name="strain_rates",
    )(block, east, up, north, before, after)


def per_device(phases, coherent, pairs, res_index, res_weight, coverage, los, north):
    parts = lax.axis_size("pix")
    tracks = lax.axis_size("track")
    here = lax.axis_index("track")
    grid_rows, columns = north.shape
    tiles = columns // CTILE
    rows = grid_rows * tiles
    packed = pack(phases[0], coherent[0], parts)
    stack = lax.all_to_all(packed, "pix", split_axis=0, concat_axis=0, tiled=True)
    design, pseudo = setup_track(pairs[0])
    cells = north.reshape(rows, LANES)
    vals = invert(
        stack.reshape(-1, stack.shape[2]),
        pseudo,
        design,
        res_index.reshape(-1, rows, LANES),
        res_weight.reshape(-1, rows, LANES),
        coverage.astype(jnp.float32).reshape(rows, 1),
        cells,
        lax.dynamic_index_in_dim(los, here, 0, keepdims=False),
    )
    vals = lax.all_gather(vals, "track", axis=0)
    east, up, first, last = solve(vals, cells, los, tiles)
    onward = [(i, i + 1) for i in range(parts - 1)]
    back = [(j, i) for i, j in onward]
    before = lax.ppermute(last, "pix", onward)
    after = lax.ppermute(first, "pix", back)
    return tuple(strain(here.astype(jnp.int32)[None], east, up, cells, before, after, tiles, tiles // tracks))


def solution(mesh):
    in_specs = (
        P("track", "pix", None),
        P("track", "pix", None),
        P("track", None, None),
        P("track", None, "pix"),
        P("track", None, "pix"),
        P("track", "pix", None),
        P(),
        P("pix", None),
    )
    out_specs = (P(None, "pix", "track"), P(None, "pix", "track"))
    return jax.shard_map(
        per_device, mesh=mesh, in_specs=in_specs, out_specs=out_specs, check_vma=False
    )
```

time: 288 us -> 137 us (0.48)
  local copies, waits for them, and re-layouts: 135 us -> 6.98 us
  other arithmetic: 69.1 us -> 52.2 us
  Pallas kernels: 0 us -> 14 us
  matrix products: 13.1 us -> 2.78 us
  starting transfers between devices: 19.2 us -> 12.7 us
  blocking collectives: 9.28 us -> 5.05 us
    gather x1 -> x0, local copies, waits for them, and re-layouts: 110 us -> none  [per_device(): picked = jnp.take(extended, local, axis=1)]
    reduce_sum x3 -> x0, other arithmetic: 14.9 us -> none  [the longest x2 14.8 us: per_device(): grid = jnp.sum(picked * weight[None], axis=1) / jnp.sum(weight, axis=0)]
    pallas_call x0 -> x5, Pallas kernels: none -> 14 us  [the longest x1 6.09 us: invert(): pl.pallas_call(functools.partial(invert_kernel, tile), grid=(width // chu...]
    dot_general x3 -> x0, matrix products: 10.4 us -> none  [the longest x1 3.97 us: invert_block(): jnp.dot(design_bf, series.astype(jnp.bfloat16), preferred_element_type=jn...]
    broadcast_in_dim x4 -> x0, local copies, waits for them, and re-layouts: 9.96 us -> none  [the longest x2 9.86 us: per_device(): jnp.where(coherent[0][:, :, None] == 1, blocked, jnp.zeros((), jnp.bfloat...]
    ppermute x4 -> x2, starting transfers between devices: 12.9 us -> 6.45 us  [the longest x1 4.54 us: per_device(): after = lax.ppermute(first, 'pix', back)]
    select_n x1 -> x0, local copies, waits for them, and re-layouts: 4.27 us -> none  [per_device(): jnp.where(coherent[0][:, :, None] == 1, blocked, jnp.zeros((), jnp.bfloat...]
    all_gather x2 -> x1, blocking collectives: 9.28 us -> 5.05 us  [per_device(): vals = lax.all_gather(vals, 'track', axis=0)]
  transfers between devices with their start and end apart: 5 -> 3, of which waited for: 2 -> 2; matrix products, arithmetic and copies ran while one was open for 19% -> 41% of each run, Pallas kernels for 0% -> 1%
where the time goes in v1:
time: 137 us; the launch traced here: 134 us
  other arithmetic  52.2 us (38%)
  waiting for transfers between devices  38.3 us (28%)
  Pallas kernels  14 us (10%)
  starting transfers between devices  12.7 us (9%)
  local copies, waits for them, and re-layouts  6.98 us (5%)
  blocking collectives  5.05 us (4%)
  matrix products  2.78 us (2%)
  between operations  2.3 us (2%)
    all_to_all x1, waiting for transfers between devices, per_device(): lax.all_to_all(packed, 'pix', split_axis=0, concat_axis=0, tiled=True)  36.7 us
    another operation x7, other arithmetic, setup_track(): factor = jnp.linalg.cholesky(normal)  29.4 us
    another operation x7, other arithmetic, setup_track(): pseudo = jax.scipy.linalg.cho_solve((factor, True), design.T)  20.5 us
    unnamed x28, local copies, waits for them, and re-layouts  6.61 us
    all_to_all x1, starting transfers between devices, per_device(): lax.all_to_all(packed, 'pix', split_axis=0, concat_axis=0, tiled=True)  6.29 us
    pallas_call x1, Pallas kernels, invert(): pl.pallas_call(functools.partial(invert_kernel, tile), grid=(width // chu...  6.09 us
    all_gather x1, blocking collectives, per_device(): vals = lax.all_gather(vals, 'track', axis=0)  5.05 us
    ppermute x1, starting transfers between devices, per_device(): after = lax.ppermute(first, 'pix', back)  4.54 us
  transfers between devices with their start and end apart: 3, of which 2 were waited for; matrix products, arithmetic and copies ran while one was open for 41% of the time, Pallas kernels for 1%

profile of v1, /device:TPU:16, one launch (start us, length us, event | category | flops | bytes accessed | tf_op | source)
XLA Modules:
  0.0 134.3 jit_solution(894426224181580168)
XLA Ops:
  0.6 0.0 copy-start
  0.6 2.2 %copy-done = bf16[1,16,131072]{2,1,0:T(8,128)(2,1)S(1)} copy-done((bf16[1,16,131072]{2,1,0:T(8,128)(2,1)S(1)}, bf16[1,16,131072]{2,1,0:T(8,128)(2,1)}, u32[]{:S(2)}) %copy-start) | copy-done | bytes 4194328
  2.8 0.0 copy-start.4
  2.8 0.8 copy-done.4
  3.7 2.9 %mask_pack.1 = bf16[16,16,8448]{2,1,0:T(8,128)(2,1)S(1)} custom-call(s32[16,1024]{1,0:T(8,128)S(1)} %bitcast.59, bf16[16,131072]{1,0:T(8,128)(2,1)S(1)} %bitcast.54, bf16[16,131072]{1,0:T(8,128)(2,1)S(1)} %bitcast.55, bf16[16,131072]{1,0:T(8,128)(2,1)S(1)} %bitcast.56), custom_call_target="tpu_custom_call" | custom-call | tf_op jit(solution)/shard_map/mask_pack/pallas_call | solution.py:57
  6.6 0.0 copy-start.1
  6.6 2.0 %copy-done.1 = bf16[16,16,8448]{2,1,0:T(8,128)(2,1)} copy-done((bf16[16,16,8448]{2,1,0:T(8,128)(2,1)}, bf16[16,16,8448]{2,1,0:T(8,128)(2,1)S(1)}, u32[]{:S(2)}) %copy-start.1) | copy-done | bytes 4325400
  8.6 0.0 copy-start.11
  8.6 0.0 copy-start.5
  8.6 6.3 %all-to-all-start = ((bf16[16,16,8448]{2,1,0:T(8,128)(2,1)}), bf16[16,16,8448]{2,1,0:T(8,128)(2,1)}, u32[]{:S(2)}, u32[]{:S(2)}) async-start(bf16[16,16,8448]{2,1,0:T(8,128)(2,1)} %copy-done.1), calls=%async_computation | async-start | bytes 8650752 | tf_op jit(solution)/shard_map/all_to_all | solution.py:280
  14.9 0.0 copy-start.6
  14.9 0.0 copy-start.10
  14.9 0.0 copy-start.7
  14.9 0.0 copy-start.12
  15.0 0.0 copy-done.11
  15.0 0.1 fusion.6
  15.1 0.6 fusion
  15.7 0.1 copy.14
  15.9 11.7 %cholesky.51 = f32[128,128]{1,0:T(8,128)S(1)} custom-call(f32[128,128]{1,0:T(8,128)S(1)} %cholesky.124), custom_call_target="Cholesky" | custom-call | tf_op jit(solution)/shard_map/jit(cholesky)/cholesky | solution.py:95
  27.7 9.8 %custom-call.18 = f32[1,128,128]{1,2,0:T(8,128)S(1)} custom-call(f32[1,128,128]{2,1,0:T(8,128)S(1)} %get-tuple-element.31), custom_call_target="InvertDiagBlocksLowerTriangular" | custom-call | tf_op jit(solution)/shard_map/jit(cholesky)/cholesky | solution.py:95
  37.5 0.2 constant_dynamic-update-slice_fusion.1
  37.7 0.2 convolution_subtract_fusion.2
  37.9 6.6 %cholesky.110 = f32[72,72]{1,0:T(8,128)S(1)} custom-call(f32[72,72]{1,0:T(8,128)S(1)} %convolution_subtract_fusion.2), custom_call_target="Cholesky" | custom-call | tf_op jit(solution)/shard_map/jit(cholesky)/cholesky | solution.py:95
  44.5 0.6 compare_reduce_fusion.1
  45.2 0.6 compare_reduce_fusion
  47.2 0.1 fusion.7
  47.3 19.7 %custom-call.19 = f32[2,128,128]{1,2,0:T(8,128)S(1)} custom-call(f32[2,128,128]{2,1,0:T(8,128)S(1)} %pad_maximum_fusion.1), custom_call_target="InvertDiagBlocksLowerTriangular" | custom-call | tf_op jit(solution)/shard_map/jit(_cho_solve)/triangular_solve | solution.py:96
  67.0 0.1 copy.18
  67.1 0.0 copy-done.5
  67.1 0.0 copy-done.6
  67.2 0.0 copy-done.10
  67.2 0.1 reshape.102.cover_ref
  67.3 0.0 copy-done.7
  67.3 0.0 copy-start.2
  67.3 0.8 multiply_reduce_fusion
  68.1 0.3 fusion.4
  68.4 0.4 convolution_subtract_fusion
  68.8 0.3 fusion.13
  69.1 0.2 fusion.12
  69.3 0.3 convolution_subtract_fusion.1
  69.6 0.3 fusion.10
  69.9 0.7 pad_maximum_fusion.pseudo_ref
  70.6 1.3 broadcast_divide_fusion.slope_ref
  71.9 1.8 %extend_pseudo.1.pseudo_ref = bf16[208,256]{1,0:T(8,128)(2,1)} custom-call(f32[200,256]{1,0:T(8,128)} %pad_maximum_fusion.pseudo_ref, f32[200,1]{1,0:T(8,128)} %broadcast_divide_fusion.slope_ref), custom_call_target="tpu_custom_call" | custom-call | tf_op jit(solution)/shard_map/extend_pseudo/pallas_call | solution.py:99
  73.7 0.0 copy-done.12
  73.7 36.7 %all-to-all-done = bf16[16,16,8448]{2,1,0:T(8,128)(2,1)} async-done(((bf16[16,16,8448]{2,1,0:T(8,128)(2,1)}), bf16[16,16,8448]{2,1,0:T(8,128)(2,1)}, u32[]{:S(2)}, u32[]{:S(2)}) %all-to-all-start) | async-done | bytes 4325408 | tf_op jit(solution)/shard_map/all_to_all | solution.py:280
  110.4 0.0 copy-start.3
  110.4 0.9 copy-done.3
  111.3 6.1 %invert_resample.1 = f32[2,64,128]{2,1,0:T(8,128)S(1)} custom-call(bf16[256,8448]{1,0:T(8,128)(2,1)} %bitcast.3.stack_ref, bf16[208,256]{1,0:T(8,128)(2,1)S(1)} %copy-done.3, bf16[256,208]{1,0:T(8,128)(2,1)S(1)} %get-tuple-element.34.design_ref, s32[4,64,128]{2,1,0:T(8,128)S(1)} %bitcast.57, f32[4,64,128]{2,1,0:T(8,128)S(1)} %bitcast.58, ...), custom_call_target="tpu_custom_call" | custom-call | tf_op jit(solution)/shard_map/invert_resample/pallas_call | solution.py:166
  117.4 5.0 %all-gather = f32[4,64,128]{2,1,0:T(8,128)} all-gather(f32[2,64,128]{2,1,0:T(8,128)S(1)} %invert_resample.1), channel_id=2, replica_groups=mesh['track'=2,'pix'=16] {'track'}, dimensions={0}, use_global_device_ids=true | all-gather | bytes 196608 | tf_op jit(solution)/shard_map/all_gather | solution.py:293
  122.5 0.0 copy-done.2
  122.5 1.6 %solve_cells.1 = (f32[64,128]{1,0:T(8,128)}, f32[64,128]{1,0:T(8,128)}, f32[2,8,128]{2,1,0:T(8,128)}, f32[2,8,128]{2,1,0:T(8,128)}) custom-call(f32[2,2,64,128]{3,2,1,0:T(8,128)} %bitcast.60, f32[64,128]{1,0:T(8,128)} %copy-done.2, f32[2,3]{1,0:T(2,128)} %los_ref.1), custom_call_target="tpu_custom_call" | custom-call | tf_op jit(solution)/shard_map/solve_cells/pallas_call | solution.py:217
  124.1 1.9 %collective-permute-start = (f32[2,8,128]{2,1,0:T(8,128)}, f32[2,8,128]{2,1,0:T(8,128)S(1)}, u32[]{:S(2)}, u32[]{:S(2)}) collective-permute-start(f32[2,8,128]{2,1,0:T(8,128)} %get-tuple-element.8), channel_id=1, source_target_pairs={{0,1},{1,2},{2,3},{3,4},{4,5},{5,6},{6,7},{7,8},{8,9},{9,10},{10,1... | collective-permute-start | bytes 24584 | tf_op jit(solution)/shard_map/ppermute | solution.py:297
  126.0 4.5 %collective-permute-start.1 = (f32[2,8,128]{2,1,0:T(8,128)}, f32[2,8,128]{2,1,0:T(8,128)S(1)}, u32[]{:S(2)}, u32[]{:S(2)}) collective-permute-start(f32[2,8,128]{2,1,0:T(8,128)} %get-tuple-element.9), channel_id=1, source_target_pairs={{1,0},{2,1},{3,2},{4,3},{5,4},{6,5},{7,6},{8,7},{9,8},{10,9},{11,1... | collective-permute-start | bytes 24584 | tf_op jit(solution)/shard_map/ppermute | solution.py:298
  130.5 0.0 collective-permute-done.before_ref
  130.5 0.0 copy-start.8
  130.5 1.5 %collective-permute-done.1.after_ref = f32[2,8,128]{2,1,0:T(8,128)S(1)} collective-permute-done((f32[2,8,128]{2,1,0:T(8,128)}, f32[2,8,128]{2,1,0:T(8,128)S(1)}, u32[]{:S(2)}, u32[]{:S(2)}) %collective-permute-start.1) | collective-permute-done | bytes 8224 | tf_op jit(solution)/shard_map/ppermute | solution.py:298
  132.1 0.0 copy-start.9
  132.1 0.0 copy-done.8
  132.1 0.6 copy-done.9
  132.7 1.6 %strain_rates.1 = (f32[2,8,512]{2,1,0:T(8,128)}, f32[3,8,512]{2,1,0:T(8,128)}) custom-call(s32[1]{0:T(128)} %bitcast.block_ref, f32[64,128]{1,0:T(8,128)} %get-tuple-element.6.east_ref, f32[64,128]{1,0:T(8,128)} %get-tuple-element.7.up_ref, f32[64,128]{1,0:T(8,128)} %copy-done.2, f32[2,8,128]{2,1,0:T(8,128)} %copy-done.8, f32[2,8,128]{2,1,0:T(8,128)} %copy-done.9), custom_call_target="tpu_custom_call" | custom-call | tf_op jit(solution)/shard_map/strain_rates/pallas_call | solution.py:262
  (18 shorter events, 0.3 us)
Async XLA Ops:
  0.6 2.2 %copy-start = (bf16[1,16,131072]{2,1,0:T(8,128)(2,1)S(1)}, bf16[1,16,131072]{2,1,0:T(8,128)(2,1)}, u32[]{:S(2)}) copy-start(bf16[1,16,131072]{2,1,0:T(8,128)(2,1)} %param.8) | copy-start | bytes 12582916
  2.8 0.8 copy-start.4
  6.6 2.0 %copy-start.1 = (bf16[16,16,8448]{2,1,0:T(8,128)(2,1)}, bf16[16,16,8448]{2,1,0:T(8,128)(2,1)S(1)}, u32[]{:S(2)}) copy-start(bf16[16,16,8448]{2,1,0:T(8,128)(2,1)S(1)} %mask_pack.1) | copy-start | bytes 12976132
  8.6 6.3 %copy-start.11 = (s32[1,256,2]{1,2,0:T(2,128)S(1)}, s32[1,256,2]{1,2,0:T(2,128)}, u32[]{:S(2)}) copy-start(s32[1,256,2]{1,2,0:T(2,128)} %param.10) | copy-start | bytes 6148
  8.6 58.5 %copy-start.5 = (s32[1,4,8192]{2,1,0:T(4,128)S(1)}, s32[1,4,8192]{2,1,0:T(4,128)}, u32[]{:S(2)}) copy-start(s32[1,4,8192]{2,1,0:T(4,128)} %param.11) | copy-start | bytes 393220
  8.6 101.8 %all-to-all-start = ((bf16[16,16,8448]{2,1,0:T(8,128)(2,1)}), bf16[16,16,8448]{2,1,0:T(8,128)(2,1)}, u32[]{:S(2)}, u32[]{:S(2)}) async-start(bf16[16,16,8448]{2,1,0:T(8,128)(2,1)} %copy-done.1), calls=%async_computation | async-start | bytes 8650752 | tf_op jit(solution)/shard_map/all_to_all | solution.py:280
  14.9 52.2 %copy-start.6 = (f32[1,4,8192]{2,1,0:T(4,128)S(1)}, f32[1,4,8192]{2,1,0:T(4,128)}, u32[]{:S(2)}) copy-start(f32[1,4,8192]{2,1,0:T(4,128)} %param.12) | copy-start | bytes 393220
  14.9 52.3 %copy-start.10 = (s32[1,8,8]{2,1,0:T(8,128)S(1)}, s32[1,8,8]{2,1,0:T(8,128)}, u32[]{:S(2)}) copy-start(s32[1,8,8]{2,1,0:T(8,128)} %param.13) | copy-start | bytes 772
  14.9 52.3 %copy-start.7 = (f32[8,1024]{1,0:T(8,128)S(1)}, f32[8,1024]{1,0:T(8,128)}, u32[]{:S(2)}) copy-start(f32[8,1024]{1,0:T(8,128)} %param.15) | copy-start | bytes 98308
  14.9 58.7 %copy-start.12 = (f32[2,3]{1,0:T(2,128)S(1)}, f32[2,3]{1,0:T(2,128)}, u32[]{:S(2)}) copy-start(f32[2,3]{1,0:T(2,128)} %los_ref.1) | copy-start | bytes 76
  67.3 55.2 %copy-start.2 = (f32[64,128]{1,0:T(8,128)}, f32[64,128]{1,0:T(8,128)S(1)}, u32[]{:S(2)}) copy-start(f32[64,128]{1,0:T(8,128)S(1)} %reshape.71.north_ref) | copy-start | bytes 98308
  110.4 0.9 copy-start.3
  124.1 6.5 %collective-permute-start = (f32[2,8,128]{2,1,0:T(8,128)}, f32[2,8,128]{2,1,0:T(8,128)S(1)}, u32[]{:S(2)}, u32[]{:S(2)}) collective-permute-start(f32[2,8,128]{2,1,0:T(8,128)} %get-tuple-element.8), channel_id=1, source_target_pairs={{0,1},{1,2},{2,3},{3,4},{4,5},{5,6},{6,7},{7,8},{8,9},{9,10},{10,1... | collective-permute-start | bytes 24584 | tf_op jit(solution)/shard_map/ppermute | solution.py:297
  126.0 6.1 %collective-permute-start.1 = (f32[2,8,128]{2,1,0:T(8,128)}, f32[2,8,128]{2,1,0:T(8,128)S(1)}, u32[]{:S(2)}, u32[]{:S(2)}) collective-permute-start(f32[2,8,128]{2,1,0:T(8,128)} %get-tuple-element.9), channel_id=1, source_target_pairs={{1,0},{2,1},{3,2},{4,3},{5,4},{6,5},{7,6},{8,7},{9,8},{10,9},{11,1... | collective-permute-start | bytes 24584 | tf_op jit(solution)/shard_map/ppermute | solution.py:298
  130.5 1.5 %copy-start.8 = (f32[2,8,128]{2,1,0:T(8,128)}, f32[2,8,128]{2,1,0:T(8,128)S(1)}, u32[]{:S(2)}) copy-start(f32[2,8,128]{2,1,0:T(8,128)S(1)} %collective-permute-done.before_ref) | copy-start | bytes 24580
  132.1 0.6 copy-start.9

commit v2 on v1

v2 whole, which is shorter than its diff:
```python
import functools

import jax
import jax.numpy as jnp
from jax import lax
from jax.experimental import pallas as pl
from jax.experimental.pallas import tpu as pltpu
from jax.sharding import PartitionSpec as P

EPOCHS = 200
ROWS = 208
HALO = 128
CTILE = 128
MBLK = 128
LANES = 128
TILE = 256


prior_var = 0.1
ridge_term = 0.5
big = 56 * 1024 * 1024


def masked(values, flags, j):
    spread = jnp.broadcast_to(flags[:, j : j + 1], values.shape).astype(jnp.bfloat16)
    return values * spread


def flags_of(flags_ref, block):
    first = block // LANES * LANES
    return (flags_ref[:, first : first + LANES] == 1).astype(jnp.float32), block - first


def pack_edges_kernel(tiles, flags_ref, phases_ref, out_ref, near_ref, sem):
    parts = out_ref.shape[0]
    blocks = flags_ref.shape[1]
    span = blocks // parts
    reach = tiles + 1
    copies = []
    for b in range(parts + 1):
        low, high = max(span * b - reach, 0), min(span * b + reach, blocks)
        at = low - (span * b - reach)
        copies.append(
            pltpu.make_async_copy(
                phases_ref.at[:, pl.ds(low * MBLK, (high - low) * MBLK)],
                near_ref.at[b, :, pl.ds(at * MBLK, (high - low) * MBLK)],
                sem.at[b],
            )
        )
    for copy in copies:
        copy.start()
    empty = jnp.zeros((out_ref.shape[1], MBLK), jnp.bfloat16)
    out_ref[0, :, :MBLK] = empty
    out_ref[parts - 1, :, (2 * reach + 1) * MBLK :] = empty
    for b in range(parts + 1):
        copies[b].wait()
        for k in range(2 * reach):
            block = span * b - reach + k
            if not 0 <= block < blocks:
                continue
            flags, j = flags_of(flags_ref, block)
            value = masked(near_ref[b, :, k * MBLK : (k + 1) * MBLK], flags, j)
            if b > 0 and k <= reach:
                out_ref[b - 1, :, (reach + 1 + k) * MBLK : (reach + 2 + k) * MBLK] = value
            if b < parts and k >= reach - 1:
                out_ref[b, :, (k - reach + 1) * MBLK : (k - reach + 2) * MBLK] = value


def pack_edges(phases, flags, parts, tiles):
    ifgs = phases.shape[0]
    vmem = pl.BlockSpec(memory_space=pltpu.VMEM)
    return pl.pallas_call(
        functools.partial(pack_edges_kernel, tiles),
        in_specs=[vmem, pl.BlockSpec(memory_space=pltpu.HBM)],
        out_specs=vmem,
        out_shape=jax.ShapeDtypeStruct((parts, ifgs, 2 * (tiles + 2) * MBLK), jnp.bfloat16),
        scratch_shapes=[
            pltpu.VMEM((parts + 1, ifgs, 2 * (tiles + 1) * MBLK), jnp.bfloat16),
            pltpu.SemaphoreType.DMA((parts + 1,)),
        ],
        compiler_params=pltpu.CompilerParams(vmem_limit_bytes=big),
        name="pack_edges",
    )(flags, phases)


def pack_inner_kernel(reach, flags_ref, x_ref, out_ref):
    parts = out_ref.shape[0]
    each = LANES // parts
    start = pl.multiple_of(pl.program_id(0) * LANES, LANES)
    flags = (flags_ref[:, pl.ds(start, LANES)] == 1).astype(jnp.float32)
    for part in range(parts):
        for k in range(reach, each - reach):
            j = part * each + k
            value = masked(x_ref[:, j * MBLK : (j + 1) * MBLK], flags, j)
            out_ref[part, :, (k - reach) * MBLK : (k - reach + 1) * MBLK] = value


def pack_inner(phases, flags, parts, tiles):
    ifgs, cells = phases.shape
    blocks = flags.shape[1]
    steps = blocks // LANES
    each = parts // steps
    reach = tiles + 1
    width = (blocks // parts - 2 * reach) * MBLK
    return pl.pallas_call(
        functools.partial(pack_inner_kernel, reach),
        grid=(steps,),
        in_specs=[
            pl.BlockSpec((ifgs, blocks), lambda i: (0, 0)),
            pl.BlockSpec((ifgs, LANES * MBLK), lambda i: (0, i)),
        ],
        out_specs=pl.BlockSpec((each, ifgs, width), lambda i: (i, 0, 0)),
        out_shape=jax.ShapeDtypeStruct((parts, ifgs, width), jnp.bfloat16),
        compiler_params=pltpu.CompilerParams(vmem_limit_bytes=big),
        name="pack_inner",
    )(flags, phases)


def extend_kernel(pseudo_ref, slope_ref, out_ref):
    pseudo = pseudo_ref[...].astype(jnp.bfloat16)
    row = jnp.sum(pseudo.astype(jnp.float32) * slope_ref[...], axis=0, keepdims=True)
    high = row.astype(jnp.bfloat16).astype(jnp.float32)
    rest = row - high
    middle = rest.astype(jnp.bfloat16).astype(jnp.float32)
    low = rest - middle
    place = lax.broadcasted_iota(jnp.int32, (ROWS - EPOCHS, row.shape[1]), 0)
    terms = jnp.where(place == 0, high, jnp.where(place == 1, middle, jnp.where(place == 2, low, 0.0)))
    whole = jnp.concatenate([pseudo.astype(jnp.float32), terms], axis=0)
    out_ref[...] = whole.astype(jnp.bfloat16)


def setup_track(pair_rows):
    epochs = jnp.arange(ROWS, dtype=jnp.int32)
    wide = (epochs[None, :] == pair_rows[:, 1:2]).astype(jnp.float32) - (
        epochs[None, :] == pair_rows[:, 0:1]
    ).astype(jnp.float32)
    design = wide[:, :EPOCHS]
    normal = jnp.dot(
        design.T, design, precision=lax.Precision.HIGHEST, preferred_element_type=jnp.float32
    ) + jnp.eye(EPOCHS, dtype=jnp.float32)
    factor = jnp.linalg.cholesky(normal)
    pseudo = jax.scipy.linalg.cho_solve((factor, True), design.T)
    centred = jnp.arange(EPOCHS).astype(jnp.float32) - (EPOCHS - 1) / 2.0
    slope = centred * (EPOCHS - 1) / jnp.sum(centred * centred)
    extended = pl.pallas_call(
        extend_kernel,
        out_shape=jax.ShapeDtypeStruct((ROWS, pair_rows.shape[0]), jnp.bfloat16),
        name="extend_pseudo",
    )(pseudo, slope[:, None])
    return wide.astype(jnp.bfloat16), extended


def invert_tile(stack, pseudo_ref, design_ref, fields_ref, base):
    series = jnp.dot(pseudo_ref[...], stack, preferred_element_type=jnp.float32)
    velocity = jnp.sum(series[EPOCHS:], axis=0, keepdims=True)
    fitted = jnp.dot(design_ref[...], series.astype(jnp.bfloat16), preferred_element_type=jnp.float32)
    misfit = stack.astype(jnp.float32) - fitted
    variance = jnp.sum(misfit * misfit, axis=0, keepdims=True) / stack.shape[0]
    for k in range(stack.shape[1] // LANES):
        row = pl.ds(base + k, 1)
        fields_ref[0, row, :] = velocity[:, k * LANES : (k + 1) * LANES]
        fields_ref[1, row, :] = variance[:, k * LANES : (k + 1) * LANES]


def pick(source, lane):
    return jnp.take_along_axis(source, lane, axis=1, mode="promise_in_bounds")


def resample(fields_ref, base, first, count, index_ref, weight_ref, cover_ref, north_ref, los_ref, out_ref):
    lanes = lax.broadcasted_iota(jnp.int32, (8, LANES), 1)
    for r in range(0, count, 8):
        here = slice(first + r, first + r + 8)
        near = [[fields_ref[f, base + r + k : base + r + k + 8, :] for k in range(3)] for f in range(2)]
        sums = [jnp.zeros((8, LANES), jnp.float32)] * 2
        total = jnp.zeros((8, LANES), jnp.float32)
        for b in range(index_ref.shape[0]):
            weight = weight_ref[b, here, :]
            place = lanes + index_ref[b, here, :] + HALO
            lane = place & (LANES - 1)
            which = place >> 7
            total = total + weight
            for f in range(2):
                low, mid, high = (pick(near[f][k], lane) for k in range(3))
                taken = jnp.where(which == 0, low, jnp.where(which == 1, mid, high))
                sums[f] = sums[f] + taken * weight
        out_ref[0, here, :] = cover_ref[here, :] / (sums[1] / total + prior_var)
        out_ref[1, here, :] = sums[0] / total - los_ref[1] * north_ref[here, :]


def edges_kernel(
    tiles, stack_ref, pseudo_ref, design_ref, index_ref, weight_ref, cover_ref, north_ref, los_ref, out_ref, seam_ref, fields_ref
):
    for first in range(0, stack_ref.shape[1], TILE):
        invert_tile(stack_ref[:, first : first + TILE], pseudo_ref, design_ref, fields_ref, first // LANES)
    seam_ref[...] = fields_ref[:, tiles : tiles + 4, :]
    for half in range(2):
        resample(
            fields_ref, half * (tiles + 2), half * tiles, tiles,
            index_ref, weight_ref, cover_ref, north_ref, los_ref, out_ref,
        )


def edges(stack, pseudo, design, index, weight, cover, north, los, tiles):
    rows = 2 * (tiles + 2)
    vmem = pl.BlockSpec(memory_space=pltpu.VMEM)
    return pl.pallas_call(
        functools.partial(edges_kernel, tiles),
        in_specs=[vmem] * 7 + [pl.BlockSpec(memory_space=pltpu.SMEM)],
        out_specs=[vmem] * 2,
        out_shape=[
            jax.ShapeDtypeStruct((2, 2 * tiles, LANES), jnp.float32),
            jax.ShapeDtypeStruct((2, 4, LANES), jnp.float32),
        ],
        scratch_shapes=[pltpu.VMEM((2, -(-rows // 8) * 8, LANES), jnp.float32)],
        compiler_params=pltpu.CompilerParams(vmem_limit_bytes=big),
        name="edge_rows",
    )(stack, pseudo, design, index, weight, cover, north, los)


def inner_kernel(
    stack_ref, seam_ref, pseudo_ref, design_ref, index_ref, weight_ref, cover_ref, north_ref, los_ref, out_ref, fields_ref,
    held_ref, sem,
):
    ifgs, width = stack_ref.shape
    tiles = width // TILE
    cuts = [tiles * k // held_ref.shape[0] for k in range(held_ref.shape[0] + 1)]
    copies = []
    for k in range(held_ref.shape[0]):
        size = (cuts[k + 1] - cuts[k]) * TILE
        copies.append(
            pltpu.make_async_copy(
                stack_ref.at[:, pl.ds(cuts[k] * TILE, size)], held_ref.at[k, :, pl.ds(0, size)], sem.at[k]
            )
        )
        copies[k].start()
    pixel_rows = width // LANES
    fields_ref[:, 0:2, :] = seam_ref[:, 0:2, :]
    fields_ref[:, pixel_rows + 2 : pixel_rows + 4, :] = seam_ref[:, 2:4, :]
    for k in range(held_ref.shape[0]):
        copies[k].wait()
        for t in range(cuts[k + 1] - cuts[k]):
            invert_tile(
                held_ref[k, :, t * TILE : (t + 1) * TILE], pseudo_ref, design_ref, fields_ref,
                2 + (cuts[k] + t) * (TILE // LANES),
            )
    resample(
        fields_ref, 0, 0, index_ref.shape[1], index_ref, weight_ref, cover_ref, north_ref, los_ref, out_ref
    )


def inner(stack, seam, pseudo, design, index, weight, cover, north, los):
    ifgs, width = stack.shape
    rows = index.shape[1]
    pieces = 4
    largest = -(-(width // TILE) // pieces) * TILE
    vmem = pl.BlockSpec(memory_space=pltpu.VMEM)
    return pl.pallas_call(
        inner_kernel,
        in_specs=[pl.BlockSpec(memory_space=pltpu.HBM)] + [vmem] * 7 + [pl.BlockSpec(memory_space=pltpu.SMEM)],
        out_specs=vmem,
        out_shape=jax.ShapeDtypeStruct((2, rows, LANES), jnp.float32),
        scratch_shapes=[
            pltpu.VMEM((2, -(-(rows + 2) // 8) * 8, LANES), jnp.float32),
            pltpu.VMEM((pieces, ifgs, largest), jnp.bfloat16),
            pltpu.SemaphoreType.DMA((pieces,)),
        ],
        compiler_params=pltpu.CompilerParams(vmem_limit_bytes=big),
        name="inner_rows",
    )(stack, seam, pseudo, design, index, weight, cover, north, los)


def solve_cells(vals_ref, los_ref):
    a11 = a12 = a22 = b1 = b2 = 0.0
    for t in range(vals_ref.shape[0]):
        weight, target = vals_ref[t, 0], vals_ref[t, 1]
        east_c, up_c = los_ref[t, 0], los_ref[t, 2]
        by_east, by_up = weight * east_c, weight * up_c
        a11 = a11 + by_east * east_c
        a12 = a12 + by_east * up_c
        a22 = a22 + by_up * up_c
        b1 = b1 + by_east * target
        b2 = b2 + by_up * target
    a11 = a11 + ridge_term
    a22 = a22 + ridge_term
    determ = a11 * a22 - a12 * a12
    return (a22 * b1 - a12 * b2) / determ, (a11 * b2 - a12 * b1) / determ


def solve_kernel(tiles, vals_ref, north_ref, los_ref, solved_ref, first_ref, last_ref):
    east, up = solve_cells(vals_ref, los_ref)
    solved_ref[0] = east
    solved_ref[1] = up
    first_ref[0] = east[:tiles]
    first_ref[1] = north_ref[:tiles, :]
    last_ref[0] = east[tiles:]
    last_ref[1] = north_ref[tiles:, :]


def solve_edges(vals, north, los, tiles):
    edge = jax.ShapeDtypeStruct((2, tiles, LANES), jnp.float32)
    vmem = pl.BlockSpec(memory_space=pltpu.VMEM)
    return pl.pallas_call(
        functools.partial(solve_kernel, tiles),
        in_specs=[vmem, vmem, pl.BlockSpec(memory_space=pltpu.SMEM)],
        out_specs=[vmem] * 3,
        out_shape=[jax.ShapeDtypeStruct((2, 2 * tiles, LANES), jnp.float32), edge, edge],
        name="solve_edges",
    )(vals, north, los)


def final_kernel(
    tiles, own, block_ref, los_ref, vals_ref, solved_ref, north_ref, before_ref, after_ref, east_up_ref, strain_ref, work_ref
):
    rows = north_ref.shape[0]
    lane = lax.broadcasted_iota(jnp.int32, (rows, LANES), 1)
    tile = lax.broadcasted_iota(jnp.int32, (rows, LANES), 0) % tiles

    def across(field):
        right = jnp.where(tile == tiles - 1, 0.0, pltpu.roll(field, rows - 1, 0))
        left = jnp.where(tile == 0, 0.0, pltpu.roll(field, 1, 0))
        following = jnp.where(lane == LANES - 1, pltpu.roll(right, LANES - 1, 1), pltpu.roll(field, LANES - 1, 1))
        previous = jnp.where(lane == 0, pltpu.roll(left, 1, 1), pltpu.roll(field, 1, 1))
        return following - previous

    def down(field, which):
        below = jnp.concatenate([field[tiles:], after_ref[which]], axis=0)
        above = jnp.concatenate([before_ref[which], field[: rows - tiles]], axis=0)
        return below - above

    east, up = (
        jnp.concatenate([solved_ref[k, :tiles], middle, solved_ref[k, tiles:]], axis=0)
        for k, middle in enumerate(solve_cells(vals_ref, los_ref))
    )
    north = north_ref[...]
    work_ref[0] = east
    work_ref[1] = up
    work_ref[2] = across(east) / 2.0
    work_ref[3] = down(north, 1) / 2.0
    work_ref[4] = (down(east, 0) + across(north)) / 4.0
    start = block_ref[0] * own
    for field in range(5):
        target, at = (east_up_ref, field) if field < 2 else (strain_ref, field - 2)
        for i in range(rows // tiles):
            for j in range(own):
                target[at, i : i + 1, j * LANES : (j + 1) * LANES] = work_ref[field, pl.ds(i * tiles + start + j, 1), :]


def final(block, los, vals, solved, north, before, after, tiles, own):
    rows = north.shape[0]
    shape = (rows // tiles, own * LANES)
    vmem = pl.BlockSpec(memory_space=pltpu.VMEM)
    return pl.pallas_call(
        functools.partial(final_kernel, tiles, own),
        in_specs=[pl.BlockSpec(memory_space=pltpu.SMEM)] * 2 + [vmem] * 5,
        out_specs=[vmem] * 2,
        out_shape=[jax.ShapeDtypeStruct((2, *shape), jnp.float32), jax.ShapeDtypeStruct((3, *shape), jnp.float32)],
        scratch_shapes=[pltpu.VMEM((5, rows, LANES), jnp.float32)],
        name="solve_and_strain",
    )(block, los, vals, solved, north, before, after)


def per_device(phases, coherent, pairs, res_index, res_weight, coverage, los, north):
    parts = lax.axis_size("pix")
    tracks = lax.axis_size("track")
    here = lax.axis_index("track")
    grid_rows, columns = north.shape
    tiles = columns // CTILE
    rows = grid_rows * tiles
    edge_stack = lax.all_to_all(
        pack_edges(phases[0], coherent[0], parts, tiles), "pix", split_axis=0, concat_axis=0, tiled=True
    )
    inner_stack = lax.all_to_all(
        pack_inner(phases[0], coherent[0], parts, tiles), "pix", split_axis=0, concat_axis=0, tiled=True
    )
    design, pseudo = setup_track(pairs[0])
    cells = north.reshape(rows, LANES)
    own_los = lax.dynamic_index_in_dim(los, here, 0, keepdims=False)
    per_cell = (
        res_index.reshape(-1, rows, LANES),
        res_weight.reshape(-1, rows, LANES),
        coverage.astype(jnp.float32).reshape(rows, 1),
        cells,
    )
    at_edges = [jnp.concatenate([a[..., :tiles, :], a[..., rows - tiles :, :]], axis=-2) for a in per_cell]
    at_inner = [a[..., tiles : rows - tiles, :] for a in per_cell]

    def flat(stack):
        return stack.reshape(-1, stack.shape[2])

    edge_vals, seam = edges(flat(edge_stack), pseudo, design, *at_edges, own_los, tiles)
    edge_vals = lax.all_gather(edge_vals, "track", axis=0)
    solved, first, last = solve_edges(edge_vals, at_edges[3], los, tiles)
    onward = [(i, i + 1) for i in range(parts - 1)]
    back = [(j, i) for i, j in onward]
    before = lax.ppermute(last, "pix", onward)
    after = lax.ppermute(first, "pix", back)
    inner_vals = inner(flat(inner_stack), seam, pseudo, design, *at_inner, own_los)
    inner_vals = lax.all_gather(inner_vals, "track", axis=0)
    return tuple(
        final(
            here.astype(jnp.int32)[None], los, inner_vals, solved, cells, before, after, tiles, tiles // tracks
        )
    )


def solution(mesh):
    in_specs = (
        P("track", "pix", None),
        P("track", "pix", None),
        P("track", None, None),
        P("track", None, "pix"),
        P("track", None, "pix"),
        P("track", "pix", None),
        P(),
        P("pix", None),
    )
    out_specs = (P(None, "pix", "track"), P(None, "pix", "track"))
    return jax.shard_map(
        per_device, mesh=mesh, in_specs=in_specs, out_specs=out_specs, check_vma=False
    )
```

time: 137 us -> 166 us (1.21)
  waiting for transfers between devices: 38.3 us -> 22.9 us
  Pallas kernels: 14 us -> 26.7 us
  other arithmetic: 52.2 us -> 60.4 us
  local copies, waits for them, and re-layouts: 6.98 us -> 14.7 us
  matrix products: 2.78 us -> 9.06 us
  blocking collectives: 5.05 us -> 10.7 us
  starting transfers between devices: 12.7 us -> 17.3 us
    all_to_all x1 -> x2, waiting for transfers between devices: 36.7 us -> 22.9 us  [the longest x1 22.9 us: per_device(): lax.all_to_all(pack_edges(phases[0], coherent[0], parts, tiles), 'pix', s...]
    pallas_call x4 -> x6, Pallas kernels: 12.2 us -> 25 us  [the longest x1 7.1 us: pack_inner(): pl.pallas_call(functools.partial(pack_inner_kernel, reach), grid=(steps,)...]
    all_gather x1 -> x2, blocking collectives: 5.05 us -> 10.7 us  [the longest x1 5.51 us: per_device(): edge_vals = lax.all_gather(edge_vals, 'track', axis=0)]
    slice x0 -> x10, local copies, waits for them, and re-layouts: none -> 4.84 us  [the longest x6 4 us: per_device(): at_inner = [a[..., tiles:rows - tiles, :] for a in per_cell]]
    another operation x6, matrix products: 1.78 us -> 6.53 us  [setup_track(): pseudo = jax.scipy.linalg.cho_solve((factor, True), design.T)]
    all_to_all x1 -> x2, starting transfers between devices: 6.29 us -> 10.8 us  [the longest x1 6.17 us: per_device(): lax.all_to_all(pack_edges(phases[0], coherent[0], parts, tiles), 'pix', s...]
    another operation x7, other arithmetic: 29.4 us -> 32.1 us  [setup_track(): factor = jnp.linalg.cholesky(normal)]
    concatenate x0 -> x4, other arithmetic: none -> 1.92 us  [per_device(): jnp.concatenate([a[..., :tiles, :], a[..., rows - tiles:, :]], axis=-2)]
  transfers between devices with their start and end apart: 3 -> 4, of which waited for: 2 -> 1; matrix products, arithmetic and copies ran while one was open for 41% -> 49% of each run, Pallas kernels for 1% -> 12%
where the time goes in v2:
time: 166 us; the launch traced here: 164 us
  other arithmetic  60.4 us (36%)
  Pallas kernels  26.7 us (16%)
  waiting for transfers between devices  22.9 us (14%)
  starting transfers between devices  17.3 us (10%)
  local copies, waits for them, and re-layouts  14.7 us (9%)
  blocking collectives  10.7 us (6%)
  matrix products  9.06 us (5%)
  between operations  2.24 us (1%)
    another operation x7, other arithmetic, setup_track(): factor = jnp.linalg.cholesky(normal)  32.1 us
    all_to_all x1, waiting for transfers between devices, per_device(): lax.all_to_all(pack_edges(phases[0], coherent[0], parts, tiles), 'pix', s...  22.9 us
    another operation x7, other arithmetic, setup_track(): pseudo = jax.scipy.linalg.cho_solve((factor, True), design.T)  21.1 us
    pallas_call x1, Pallas kernels, pack_inner(): pl.pallas_call(functools.partial(pack_inner_kernel, reach), grid=(steps,)...  7.1 us
    pallas_call x1, Pallas kernels, inner(): pl.pallas_call(inner_kernel, in_specs=[pl.BlockSpec(memory_space=pltpu.HB...  6.68 us
    another operation x6, matrix products, setup_track(): pseudo = jax.scipy.linalg.cho_solve((factor, True), design.T)  6.53 us
    unnamed x20, local copies, waits for them, and re-layouts  6.39 us
    all_to_all x1, starting transfers between devices, per_device(): lax.all_to_all(pack_edges(phases[0], coherent[0], parts, tiles), 'pix', s...  6.17 us
  transfers between devices with their start and end apart: 4, of which 1 were waited for; matrix products, arithmetic and copies ran while one was open for 49% of the time, Pallas kernels for 12%

profile of v2, /device:TPU:16, one launch (start us, length us, event | category | flops | bytes accessed | tf_op | source)
XLA Modules:
  0.0 163.9 jit_solution(6307492791265856059)
XLA Ops:
  0.6 4.6 %pack_edges.1 = bf16[16,16,2560]{2,1,0:T(8,128)(2,1)} custom-call(s32[16,1024]{1,0:T(8,128)} %bitcast.71, bf16[16,131072]{1,0:T(8,128)(2,1)} %bitcast.62), custom_call_target="tpu_custom_call" | custom-call | tf_op jit(solution)/shard_map/pack_edges/pallas_call | solution.py:72
  5.2 6.2 %all-to-all-start.1 = ((bf16[16,16,2560]{2,1,0:T(8,128)(2,1)}), bf16[16,16,2560]{2,1,0:T(8,128)(2,1)S(1)}, u32[]{:S(2)}, u32[]{:S(2)}) async-start(bf16[16,16,2560]{2,1,0:T(8,128)(2,1)} %pack_edges.1), calls=%async_computation.1 | async-start | bytes 2621440 | tf_op jit(solution)/shard_map/all_to_all | solution.py:369
  11.4 7.1 %pack_inner.1 = bf16[16,16,5888]{2,1,0:T(8,128)(2,1)} custom-call(s32[16,1024]{1,0:T(8,128)} %bitcast.72, bf16[16,131072]{1,0:T(8,128)(2,1)} %bitcast.63), custom_call_target="tpu_custom_call" | custom-call | tf_op jit(solution)/shard_map/pack_inner/pallas_call | solution.py:105
  18.5 0.8 fusion.6
  19.3 22.9 %all-to-all-done.1 = bf16[16,16,2560]{2,1,0:T(8,128)(2,1)S(1)} async-done(((bf16[16,16,2560]{2,1,0:T(8,128)(2,1)}), bf16[16,16,2560]{2,1,0:T(8,128)(2,1)S(1)}, u32[]{:S(2)}, u32[]{:S(2)}) %all-to-all-start.1) | async-done | bytes 1310752 | tf_op jit(solution)/shard_map/all_to_all | solution.py:369
  42.2 1.1 copy-done.1
  43.3 4.6 %all-to-all-start = ((bf16[16,16,5888]{2,1,0:T(8,128)(2,1)}), bf16[16,16,5888]{2,1,0:T(8,128)(2,1)S(1)}, u32[]{:S(2)}, u32[]{:S(2)}) async-start(bf16[16,16,5888]{2,1,0:T(8,128)(2,1)} %pack_inner.1), calls=%async_computation | async-start | bytes 6029312 | tf_op jit(solution)/shard_map/all_to_all | solution.py:372
  47.9 0.6 fusion
  48.5 0.6 slice.150
  49.1 0.6 reshape.78.north_ref
  49.7 0.8 copy.17
  50.5 1.0 fusion.3
  51.5 0.7 copy-done.3
  52.2 11.7 %cholesky.51 = f32[128,128]{1,0:T(8,128)S(1)} custom-call(f32[128,128]{1,0:T(8,128)S(1)} %cholesky.124), custom_call_target="Cholesky" | custom-call | tf_op jit(solution)/shard_map/jit(cholesky)/cholesky | solution.py:141
  63.9 1.1 select_reduce_fusion
  65.1 10.6 %custom-call.18 = f32[1,128,128]{1,2,0:T(8,128)S(1)} custom-call(f32[1,128,128]{2,1,0:T(8,128)} %get-tuple-element.37), custom_call_target="InvertDiagBlocksLowerTriangular" | custom-call | tf_op jit(solution)/shard_map/jit(cholesky)/cholesky | solution.py:141
  75.7 1.0 constant_dynamic-update-slice_fusion.1
  76.7 1.0 convolution_subtract_fusion.2
  77.7 6.6 %cholesky.110 = f32[72,72]{1,0:T(8,128)S(1)} custom-call(f32[72,72]{1,0:T(8,128)S(1)} %convolution_subtract_fusion.2), custom_call_target="Cholesky" | custom-call | tf_op jit(solution)/shard_map/jit(cholesky)/cholesky | solution.py:141
  84.3 0.0 copy-start.7
  84.3 1.4 compare_reduce_fusion.1
  85.7 0.6 compare_reduce_fusion
  87.8 0.6 copy-done.2
  88.4 0.1 fusion.7
  88.5 20.3 %custom-call.19 = f32[2,128,128]{1,2,0:T(8,128)} custom-call(f32[2,128,128]{2,1,0:T(8,128)S(1)} %pad_maximum_fusion.1), custom_call_target="InvertDiagBlocksLowerTriangular" | custom-call | tf_op jit(solution)/shard_map/jit(_cho_solve)/triangular_solve | solution.py:142
  108.8 0.8 copy.21
  109.6 0.9 copy.30
  110.5 0.9 copy.29
  111.4 0.7 convert_element_type.37
  112.1 0.1 pad_maximum_fusion.4
  112.2 0.7 copy.22.cover_ref
  112.8 0.6 slice.178.index_ref
  113.5 0.7 slice.179.weight_ref
  114.2 0.7 slice.169.cover_ref
  114.8 1.4 slice.151.north_ref
  116.2 0.6 multiply_reduce_fusion
  116.8 1.2 fusion.4
  118.0 1.2 convolution_subtract_fusion
  119.2 1.1 fusion.13
  120.2 1.0 fusion.12
  121.2 1.1 convolution_subtract_fusion.1
  122.3 1.1 fusion.10
  123.4 0.7 pad_maximum_fusion.pseudo_ref
  124.1 2.2 %broadcast_divide_fusion.slope_ref = f32[200,1]{1,0:T(8,128)} fusion(f32[200,1]{1,0:T(8,128)} %copy.21, f32[]{:T(128)} %multiply_reduce_fusion), kind=kLoop, calls=%fused_computation.36 | loop fusion | flops 200 | bytes 1604 | tf_op jit(solution)/shard_map/div | solution.py:144
  126.3 1.8 %extend_pseudo.1.pseudo_ref = bf16[208,256]{1,0:T(8,128)(2,1)} custom-call(f32[200,256]{1,0:T(8,128)} %pad_maximum_fusion.pseudo_ref, f32[200,1]{1,0:T(8,128)} %broadcast_divide_fusion.slope_ref), custom_call_target="tpu_custom_call" | custom-call | tf_op jit(solution)/shard_map/extend_pseudo/pallas_call | solution.py:145
  128.1 0.5 dynamic-slice_bitcast_fusion.los_ref
  128.6 0.8 fusion.18
  129.4 0.6 pad_maximum_fusion.3.north_ref
  130.0 0.6 pad_add_fusion.index_ref
  130.7 0.6 pad_maximum_fusion.2.weight_ref
  131.3 3.3 %edge_rows.1 = (f32[2,16,128]{2,1,0:T(8,128)}, f32[2,4,128]{2,1,0:T(4,128)}) custom-call(bf16[256,2560]{1,0:T(8,128)(2,1)} %bitcast.65, bf16[208,256]{1,0:T(8,128)(2,1)} %extend_pseudo.1.pseudo_ref, bf16[256,208]{1,0:T(8,128)(2,1)} %get-tuple-element.44.design_ref, s32[4,16,128]{2,1,0:T(8,128)} %pad_add_fusion.index_ref, ...), custom_call_target="tpu_custom_call" | custom-call | tf_op jit(solution)/shard_map/edge_rows/pallas_call | solution.py:206
  134.6 5.5 %all-gather.1 = f32[4,16,128]{2,1,0:T(8,128)} all-gather(f32[2,16,128]{2,1,0:T(8,128)} %get-tuple-element.8), channel_id=3, replica_groups=mesh['track'=2,'pix'=16] {'track'}, dimensions={0}, use_global_device_ids=true | all-gather | bytes 49152 | tf_op jit(solution)/shard_map/all_gather | solution.py:391
  140.1 1.4 solve_edges.1
  141.6 1.9 %collective-permute-start = (f32[2,8,128]{2,1,0:T(8,128)}, f32[2,8,128]{2,1,0:T(8,128)S(1)}, u32[]{:S(2)}, u32[]{:S(2)}) collective-permute-start(f32[2,8,128]{2,1,0:T(8,128)} %get-tuple-element.10), channel_id=1, source_target_pairs={{0,1},{1,2},{2,3},{3,4},{4,5},{5,6},{6,7},{7,8},{8,9},{9,10},{10,1... | collective-permute-start | bytes 24584 | tf_op jit(solution)/shard_map/ppermute | solution.py:395
  143.5 4.5 %collective-permute-start.1 = (f32[2,8,128]{2,1,0:T(8,128)}, f32[2,8,128]{2,1,0:T(8,128)S(1)}, u32[]{:S(2)}, u32[]{:S(2)}) collective-permute-start(f32[2,8,128]{2,1,0:T(8,128)} %get-tuple-element.11), channel_id=1, source_target_pairs={{1,0},{2,1},{3,2},{4,3},{5,4},{6,5},{7,6},{8,7},{9,8},{10,9},{11,1... | collective-permute-start | bytes 24584 | tf_op jit(solution)/shard_map/ppermute | solution.py:396
  148.0 0.0 all-to-all-done
  148.1 1.6 copy-done
  149.7 6.7 %inner_rows.1 = f32[2,48,128]{2,1,0:T(8,128)} custom-call(bf16[256,5888]{1,0:T(8,128)(2,1)} %bitcast.64, f32[2,4,128]{2,1,0:T(4,128)} %get-tuple-element.7.seam_ref, bf16[208,256]{1,0:T(8,128)(2,1)} %extend_pseudo.1.pseudo_ref, bf16[256,208]{1,0:T(8,128)(2,1)} %get-tuple-element.44.design_ref, s32[4,48,128]{2,1,0:T(8,128)} %slice.178.index_ref, ...), custom_call_target="tpu_custom_call" | custom-call | tf_op jit(solution)/shard_map/inner_rows/pallas_call | solution.py:257
  156.3 5.2 %all-gather = f32[4,48,128]{2,1,0:T(8,128)} all-gather(f32[2,48,128]{2,1,0:T(8,128)} %inner_rows.1), channel_id=2, replica_groups=mesh['track'=2,'pix'=16] {'track'}, dimensions={0}, use_global_device_ids=true | all-gather | bytes 147456 | tf_op jit(solution)/shard_map/all_gather | solution.py:398
  161.5 0.0 collective-permute-done.before_ref
  161.5 0.0 collective-permute-done.1.after_ref
  161.5 0.6 copy-done.5
  162.1 0.0 copy-done.6
  162.1 1.8 %solve_and_strain.1 = (f32[2,8,512]{2,1,0:T(8,128)}, f32[3,8,512]{2,1,0:T(8,128)}) custom-call(s32[1]{0:T(128)} %bitcast.block_ref, f32[2,3]{1,0:T(2,128)} %los_ref.3, f32[2,2,48,128]{3,2,1,0:T(8,128)} %bitcast.70, f32[2,16,128]{2,1,0:T(8,128)} %get-tuple-element.9.solved_ref, f32[64,128]{1,0:T(8,128)} %reshape.78.north_ref, f32[2,8,128]{2,1,0:T(8,128)} %copy-done.5, ...), custom_call_target="tpu_custom_call" | custom-call | tf_op jit(solution)/shard_map/solve_and_strain/pallas_call | solution.py:352
  (26 shorter events, 0.2 us)
Async XLA Ops:
  5.2 37.0 %all-to-all-start.1 = ((bf16[16,16,2560]{2,1,0:T(8,128)(2,1)}), bf16[16,16,2560]{2,1,0:T(8,128)(2,1)S(1)}, u32[]{:S(2)}, u32[]{:S(2)}) async-start(bf16[16,16,2560]{2,1,0:T(8,128)(2,1)} %pack_edges.1), calls=%async_computation.1 | async-start | bytes 2621440 | tf_op jit(solution)/shard_map/all_to_all | solution.py:369
  11.4 7.1 %copy-start.8 = (s32[1,256,2]{1,2,0:T(2,128)S(1)}, s32[1,256,2]{1,2,0:T(2,128)}, u32[]{:S(2)}) copy-start(s32[1,256,2]{1,2,0:T(2,128)} %param.10) | copy-start | bytes 6148
  19.3 29.2 %copy-start.4 = (f32[8,1024]{1,0:T(8,128)S(1)}, f32[8,1024]{1,0:T(8,128)}, u32[]{:S(2)}) copy-start(f32[8,1024]{1,0:T(8,128)} %param.15) | copy-start | bytes 98308
  42.2 1.1 copy-start.1
  43.3 104.8 %all-to-all-start = ((bf16[16,16,5888]{2,1,0:T(8,128)(2,1)}), bf16[16,16,5888]{2,1,0:T(8,128)(2,1)S(1)}, u32[]{:S(2)}, u32[]{:S(2)}) async-start(bf16[16,16,5888]{2,1,0:T(8,128)(2,1)} %pack_inner.1), calls=%async_computation | async-start | bytes 6029312 | tf_op jit(solution)/shard_map/all_to_all | solution.py:372
  51.5 0.7 copy-start.3
  84.3 43.8 %copy-start.7 = (f32[2,3]{1,0:T(2,128)S(1)}, f32[2,3]{1,0:T(2,128)}, u32[]{:S(2)}) copy-start(f32[2,3]{1,0:T(2,128)} %los_ref.3) | copy-start | bytes 76
  87.7 0.7 copy-start.2
  141.6 19.9 %collective-permute-start = (f32[2,8,128]{2,1,0:T(8,128)}, f32[2,8,128]{2,1,0:T(8,128)S(1)}, u32[]{:S(2)}, u32[]{:S(2)}) collective-permute-start(f32[2,8,128]{2,1,0:T(8,128)} %get-tuple-element.10), channel_id=1, source_target_pairs={{0,1},{1,2},{2,3},{3,4},{4,5},{5,6},{6,7},{7,8},{8,9},{9,10},{10,1... | collective-permute-start | bytes 24584 | tf_op jit(solution)/shard_map/ppermute | solution.py:395
  143.5 18.0 %collective-permute-start.1 = (f32[2,8,128]{2,1,0:T(8,128)}, f32[2,8,128]{2,1,0:T(8,128)S(1)}, u32[]{:S(2)}, u32[]{:S(2)}) collective-permute-start(f32[2,8,128]{2,1,0:T(8,128)} %get-tuple-element.11), channel_id=1, source_target_pairs={{1,0},{2,1},{3,2},{4,3},{5,4},{6,5},{7,6},{8,7},{9,8},{10,9},{11,1... | collective-permute-start | bytes 24584 | tf_op jit(solution)/shard_map/ppermute | solution.py:396
  148.1 1.6 copy-start
  161.5 0.6 copy-start.5
  161.5 0.6 copy-start.6

commit v3 on v2

v3 whole, which is shorter than its diff:
```python
import functools

import jax
import jax.numpy as jnp
from jax import lax
from jax.experimental import pallas as pl
from jax.experimental.pallas import tpu as pltpu
from jax.sharding import PartitionSpec as P

EPOCHS = 200
ROWS = 208
HALO = 128
CTILE = 128
MBLK = 128
LANES = 128
TILE = 256
PIECE = 1024


prior_var = 0.1
ridge_term = 0.5
medium = 24 * 1024 * 1024


def spread(flags, j, shape):
    return jnp.broadcast_to(flags[:, j : j + 1], shape).astype(jnp.bfloat16)


def part_flags(flags_ref, first):
    lead = pl.multiple_of(first // LANES * LANES, LANES)
    flags = (flags_ref[:, pl.ds(lead, LANES)] == 1).astype(jnp.float32)
    return pltpu.roll(flags, (LANES - (first - lead)) % LANES, 1)


def pack_edges_kernel(tiles, flags_ref, phases_ref, out_ref, near_ref, in_sem):
    parts, ifgs, _ = out_ref.shape
    blocks = flags_ref.shape[1]
    span = blocks // parts
    reach = tiles + 1
    bound = 2 * reach * MBLK
    ends = []
    for b, low, at in ((0, 0, reach), (parts, blocks - reach, 0)):
        ends.append(
            pltpu.make_async_copy(
                phases_ref.at[:, pl.ds(low * MBLK, reach * MBLK)], near_ref.at[b, :, pl.ds(at * MBLK, reach * MBLK)], in_sem.at[b]
            )
        )

    def between(b):
        low = pl.multiple_of((span * b - reach) * MBLK, MBLK)
        return pltpu.make_async_copy(phases_ref.at[:, pl.ds(low, bound)], near_ref.at[b], in_sem.at[b])

    ends[0].start()

    @pl.loop(1, parts)
    def _(b):
        between(b).start()

    ends[1].start()
    empty = jnp.zeros((ifgs, reach * MBLK), jnp.bfloat16)
    near_ref[0, :, : reach * MBLK] = empty
    near_ref[parts, :, reach * MBLK :] = empty
    ends[0].wait()

    @pl.loop(0, parts)
    def _(p):
        @pl.when(p < parts - 1)
        def _():
            between(p + 1).wait()

        @pl.when(p == parts - 1)
        def _():
            ends[1].wait()

        first = p * span
        flags = part_flags(flags_ref, first)
        earlier = part_flags(flags_ref, jnp.maximum(first - 1, 0))
        later = part_flags(flags_ref, jnp.minimum(first + span, blocks - 1))
        shape = (ifgs, MBLK)
        for half in range(2):
            for k in range(tiles + 2):
                block = k - 1 if half == 0 else span - reach + k
                if block < 0:
                    keep = spread(earlier, 0, shape)
                elif block == span:
                    keep = spread(later, 0, shape)
                else:
                    keep = spread(flags, block, shape)
                at = (reach - 1 + k if half == 0 else k) * MBLK
                to = (half * (tiles + 2) + k) * MBLK
                out_ref[p, :, to : to + MBLK] = near_ref[p + half, :, at : at + MBLK] * keep


def pack_edges(phases, flags, parts, tiles):
    ifgs = phases.shape[0]
    vmem = pl.BlockSpec(memory_space=pltpu.VMEM)
    return pl.pallas_call(
        functools.partial(pack_edges_kernel, tiles),
        in_specs=[vmem, pl.BlockSpec(memory_space=pltpu.HBM)],
        out_specs=vmem,
        out_shape=jax.ShapeDtypeStruct((parts, ifgs, 2 * (tiles + 2) * MBLK), jnp.bfloat16),
        scratch_shapes=[
            pltpu.VMEM((parts + 1, ifgs, 2 * (tiles + 1) * MBLK), jnp.bfloat16),
            pltpu.SemaphoreType.DMA((parts + 1,)),
        ],
        compiler_params=pltpu.CompilerParams(vmem_limit_bytes=medium),
        name="pack_edges",
    )(flags, phases)


def pack_inner_kernel(reach, flags_ref, phases_ref, out_ref, held_ref, ready_ref, in_sem, out_sem):
    parts, ifgs, width = out_ref.shape
    span = flags_ref.shape[1] // parts

    def inward(p):
        low = pl.multiple_of((p * span + reach) * MBLK, MBLK)
        return pltpu.make_async_copy(phases_ref.at[:, pl.ds(low, width)], held_ref.at[p], in_sem.at[p])

    def outward(p):
        return pltpu.make_async_copy(ready_ref.at[p], out_ref.at[p], out_sem.at[p])

    @pl.loop(0, parts)
    def _(p):
        inward(p).start()

    @pl.loop(0, parts)
    def _(p):
        inward(p).wait()
        flags = part_flags(flags_ref, p * span)
        for k in range(width // MBLK):
            at = slice(k * MBLK, (k + 1) * MBLK)
            ready_ref[p, :, at] = held_ref[p, :, at] * spread(flags, reach + k, (ifgs, MBLK))
        outward(p).start()

    @pl.loop(0, parts)
    def _(p):
        outward(p).wait()


def pack_inner(phases, flags, parts, tiles):
    ifgs = phases.shape[0]
    reach = tiles + 1
    width = (flags.shape[1] // parts - 2 * reach) * MBLK
    hbm = pl.BlockSpec(memory_space=pltpu.HBM)
    return pl.pallas_call(
        functools.partial(pack_inner_kernel, reach),
        in_specs=[pl.BlockSpec(memory_space=pltpu.VMEM), hbm],
        out_specs=hbm,
        out_shape=jax.ShapeDtypeStruct((parts, ifgs, width), jnp.bfloat16),
        scratch_shapes=[
            pltpu.VMEM((parts, ifgs, width), jnp.bfloat16),
            pltpu.VMEM((parts, ifgs, width), jnp.bfloat16),
            pltpu.SemaphoreType.DMA((parts,)),
            pltpu.SemaphoreType.DMA((parts,)),
        ],
        compiler_params=pltpu.CompilerParams(vmem_limit_bytes=medium),
        name="pack_inner",
    )(flags, phases)


def exact_dot(a, b):
    return jnp.dot(a, b, precision=lax.Precision.HIGHEST, preferred_element_type=jnp.float32)


def pseudo_kernel(pairs_ref, design_ref, out_ref, normal_ref, inverse_ref):
    ifgs = pairs_ref.shape[1]
    size = normal_ref.shape[0]
    epoch = lax.broadcasted_iota(jnp.int32, (size, ifgs), 0)
    across = (epoch == pairs_ref[1:2, :]).astype(jnp.float32) - (epoch == pairs_ref[0:1, :]).astype(jnp.float32)
    down = across.T
    design_ref[...] = down[:, :ROWS].astype(jnp.bfloat16)
    eye = (
        lax.broadcasted_iota(jnp.int32, (size, size), 0) == lax.broadcasted_iota(jnp.int32, (size, size), 1)
    ).astype(jnp.float32)
    normal = eye + jnp.dot(
        across.astype(jnp.bfloat16), down.astype(jnp.bfloat16), preferred_element_type=jnp.float32
    )
    normal_ref[...] = normal
    inverse_ref[...] = eye / jnp.where(eye == 1.0, normal, 1.0)

    def unfinished(state):
        step, gap = state
        return jnp.logical_and(step < 24, gap > 1e-5)

    def improve(state):
        step, _ = state
        inverse = inverse_ref[...]
        rest = eye - exact_dot(normal_ref[...], inverse)
        inverse_ref[...] = inverse + exact_dot(inverse, rest)
        return step + 1, jnp.max(jnp.abs(rest))

    lax.while_loop(unfinished, improve, (jnp.int32(0), jnp.float32(1.0)))
    pseudo = exact_dot(inverse_ref[...], across)[:ROWS].astype(jnp.bfloat16).astype(jnp.float32)
    place = lax.broadcasted_iota(jnp.int32, (ROWS, ifgs), 0)
    centred = place.astype(jnp.float32) - (EPOCHS - 1) / 2.0
    square = sum((e - (EPOCHS - 1) / 2.0) ** 2 for e in range(EPOCHS))
    slope = centred * (EPOCHS - 1) / square
    row = jnp.sum(pseudo * jnp.where(place < EPOCHS, slope, 0.0), axis=0, keepdims=True)
    high = row.astype(jnp.bfloat16).astype(jnp.float32)
    rest = row - high
    middle = rest.astype(jnp.bfloat16).astype(jnp.float32)
    low = rest - middle
    extra = place - EPOCHS
    terms = jnp.where(extra == 0, high, jnp.where(extra == 1, middle, jnp.where(extra == 2, low, 0.0)))
    out_ref[...] = jnp.where(extra < 0, pseudo, terms).astype(jnp.bfloat16)


def setup_track(pair_rows):
    ifgs = pair_rows.shape[0]
    size = 256
    vmem = pl.BlockSpec(memory_space=pltpu.VMEM)
    return pl.pallas_call(
        pseudo_kernel,
        in_specs=[vmem],
        out_specs=[vmem] * 2,
        out_shape=[jax.ShapeDtypeStruct((ifgs, ROWS), jnp.bfloat16), jax.ShapeDtypeStruct((ROWS, ifgs), jnp.bfloat16)],
        scratch_shapes=[pltpu.VMEM((size, size), jnp.float32), pltpu.VMEM((size, size), jnp.float32)],
        compiler_params=pltpu.CompilerParams(vmem_limit_bytes=medium),
        name="pseudo_inverse",
    )(pair_rows.T)


def invert_tiles(stack_ref, first, width, pseudo_ref, design_ref, fields_ref, base):
    for start in range(0, width, TILE):
        stack = stack_ref[:, pl.ds(pl.multiple_of(first + start, LANES), TILE)]
        series = jnp.dot(pseudo_ref[...], stack, preferred_element_type=jnp.float32)
        velocity = jnp.sum(series[EPOCHS:], axis=0, keepdims=True)
        fitted = jnp.dot(design_ref[...], series.astype(jnp.bfloat16), preferred_element_type=jnp.float32)
        misfit = stack.astype(jnp.float32) - fitted
        variance = jnp.sum(misfit * misfit, axis=0, keepdims=True) / stack.shape[0]
        for k in range(TILE // LANES):
            row = pl.ds(base + start // LANES + k, 1)
            fields_ref[0, row, :] = velocity[:, k * LANES : (k + 1) * LANES]
            fields_ref[1, row, :] = variance[:, k * LANES : (k + 1) * LANES]


def pick(source, lane):
    return jnp.take_along_axis(source, lane, axis=1, mode="promise_in_bounds")


def resample(fields_ref, base, cell, to, index_ref, weight_ref, cover_ref, north_ref, north_c, out_ref):
    lanes = lax.broadcasted_iota(jnp.int32, (8, LANES), 1)
    here = pl.ds(cell, 8)
    near = [[fields_ref[f, pl.ds(base + k, 8), :] for k in range(3)] for f in range(2)]
    sums = [jnp.zeros((8, LANES), jnp.float32)] * 2
    total = jnp.zeros((8, LANES), jnp.float32)
    for b in range(index_ref.shape[0]):
        weight = weight_ref[b, here, :]
        place = lanes + index_ref[b, here, :] + HALO
        lane = place & (LANES - 1)
        which = place >> 7
        total = total + weight
        for f in range(2):
            low, mid, high = (pick(near[f][k], lane) for k in range(3))
            taken = jnp.where(which == 0, low, jnp.where(which == 1, mid, high))
            sums[f] = sums[f] + taken * weight
    cover = cover_ref[here, :].astype(jnp.float32)
    out_ref[0, pl.ds(to, 8), :] = cover / (sums[1] / total + prior_var)
    out_ref[1, pl.ds(to, 8), :] = sums[0] / total - north_c * north_ref[here, :]


def edges_kernel(
    tiles, here_ref, los_ref, stack_ref, pseudo_ref, design_ref, index_ref, weight_ref, cover_ref, north_ref, out_ref, seam_ref, fields_ref
):
    rows = index_ref.shape[1]
    width = stack_ref.shape[1] // 2

    @pl.loop(0, 2)
    def _(half):
        invert_tiles(stack_ref, half * width, width, pseudo_ref, design_ref, fields_ref, half * (tiles + 2))

    seam_ref[...] = fields_ref[:, tiles : tiles + 4, :]
    north_c = los_ref[here_ref[0], 1]
    for half in range(2):
        for r in range(0, tiles, 8):
            resample(
                fields_ref, half * (tiles + 2) + r, half * (rows - tiles) + r, half * tiles + r,
                index_ref, weight_ref, cover_ref, north_ref, north_c, out_ref,
            )


def edges(here, los, stack, pseudo, design, cells, tiles):
    rows = 2 * (tiles + 2)
    vmem = pl.BlockSpec(memory_space=pltpu.VMEM)
    return pl.pallas_call(
        functools.partial(edges_kernel, tiles),
        in_specs=[pl.BlockSpec(memory_space=pltpu.SMEM)] * 2 + [vmem] * 7,
        out_specs=[vmem] * 2,
        out_shape=[
            jax.ShapeDtypeStruct((2, 2 * tiles, LANES), jnp.float32),
            jax.ShapeDtypeStruct((2, 4, LANES), jnp.float32),
        ],
        scratch_shapes=[pltpu.VMEM((2, -(-rows // 8) * 8, LANES), jnp.float32)],
        compiler_params=pltpu.CompilerParams(vmem_limit_bytes=medium),
        name="edge_rows",
    )(here, los, stack, pseudo, design, *cells)


def inner_kernel(
    tiles, here_ref, los_ref, stack_ref, seam_ref, pseudo_ref, design_ref, index_ref, weight_ref, cover_ref, north_ref, out_ref,
    fields_ref, held_ref, sem,
):
    ifgs, width = stack_ref.shape
    pieces = -(-width // PIECE)
    last = width - (pieces - 1) * PIECE

    def piece(k, size):
        part = pl.ds(pl.multiple_of(k * PIECE, LANES), size)
        return pltpu.make_async_copy(stack_ref.at[:, part], held_ref.at[:, part], sem.at[k])

    for k in range(pieces):
        piece(k, PIECE if k < pieces - 1 else last).start()
    pixel_rows = width // LANES
    fields_ref[:, 0:2, :] = seam_ref[:, 0:2, :]
    fields_ref[:, pixel_rows + 2 : pixel_rows + 4, :] = seam_ref[:, 2:4, :]

    @pl.loop(0, pieces)
    def _(k):
        @pl.when(k < pieces - 1)
        def _():
            piece(k, PIECE).wait()

        @pl.when(k == pieces - 1)
        def _():
            piece(pieces - 1, last).wait()

        first = jnp.minimum(k * PIECE, width - PIECE)
        invert_tiles(held_ref, first, PIECE, pseudo_ref, design_ref, fields_ref, 2 + first // LANES)

    north_c = los_ref[here_ref[0], 1]

    @pl.loop(0, out_ref.shape[1], step=8)
    def _(r):
        r = pl.multiple_of(r, 8)
        resample(fields_ref, r, tiles + r, r, index_ref, weight_ref, cover_ref, north_ref, north_c, out_ref)


def inner(here, los, stack, seam, pseudo, design, cells, tiles):
    ifgs, width = stack.shape
    rows = cells[0].shape[1] - 2 * tiles
    vmem = pl.BlockSpec(memory_space=pltpu.VMEM)
    return pl.pallas_call(
        functools.partial(inner_kernel, tiles),
        in_specs=[pl.BlockSpec(memory_space=pltpu.SMEM)] * 2 + [pl.BlockSpec(memory_space=pltpu.HBM)] + [vmem] * 7,
        out_specs=vmem,
        out_shape=jax.ShapeDtypeStruct((2, rows, LANES), jnp.float32),
        scratch_shapes=[
            pltpu.VMEM((2, -(-(rows + 2) // 8) * 8, LANES), jnp.float32),
            pltpu.VMEM((ifgs, width), jnp.bfloat16),
            pltpu.SemaphoreType.DMA((-(-width // PIECE),)),
        ],
        compiler_params=pltpu.CompilerParams(vmem_limit_bytes=medium),
        name="inner_rows",
    )(here, los, stack, seam, pseudo, design, *cells)


def solve_cells(vals_ref, los_ref):
    a11 = a12 = a22 = b1 = b2 = 0.0
    for t in range(vals_ref.shape[0]):
        weight, target = vals_ref[t, 0], vals_ref[t, 1]
        east_c, up_c = los_ref[t, 0], los_ref[t, 2]
        by_east, by_up = weight * east_c, weight * up_c
        a11 = a11 + by_east * east_c
        a12 = a12 + by_east * up_c
        a22 = a22 + by_up * up_c
        b1 = b1 + by_east * target
        b2 = b2 + by_up * target
    a11 = a11 + ridge_term
    a22 = a22 + ridge_term
    determ = a11 * a22 - a12 * a12
    return (a22 * b1 - a12 * b2) / determ, (a11 * b2 - a12 * b1) / determ


def solve_kernel(tiles, vals_ref, north_ref, los_ref, solved_ref, first_ref, last_ref):
    east, up = solve_cells(vals_ref, los_ref)
    solved_ref[0] = east
    solved_ref[1] = up
    first_ref[0] = east[:tiles]
    first_ref[1] = north_ref[:tiles, :]
    last_ref[0] = east[tiles:]
    last_ref[1] = north_ref[north_ref.shape[0] - tiles :, :]


def solve_edges(vals, north, los, tiles):
    edge = jax.ShapeDtypeStruct((2, tiles, LANES), jnp.float32)
    vmem = pl.BlockSpec(memory_space=pltpu.VMEM)
    return pl.pallas_call(
        functools.partial(solve_kernel, tiles),
        in_specs=[vmem, vmem, pl.BlockSpec(memory_space=pltpu.SMEM)],
        out_specs=[vmem] * 3,
        out_shape=[jax.ShapeDtypeStruct((2, 2 * tiles, LANES), jnp.float32), edge, edge],
        name="solve_edges",
    )(vals, north, los)


def final_kernel(
    tiles, own, block_ref, los_ref, vals_ref, solved_ref, north_ref, before_ref, after_ref, east_up_ref, strain_ref, work_ref
):
    rows = north_ref.shape[0]
    lane = lax.broadcasted_iota(jnp.int32, (rows, LANES), 1)
    tile = lax.broadcasted_iota(jnp.int32, (rows, LANES), 0) % tiles

    def across(field):
        right = jnp.where(tile == tiles - 1, 0.0, pltpu.roll(field, rows - 1, 0))
        left = jnp.where(tile == 0, 0.0, pltpu.roll(field, 1, 0))
        following = jnp.where(lane == LANES - 1, pltpu.roll(right, LANES - 1, 1), pltpu.roll(field, LANES - 1, 1))
        previous = jnp.where(lane == 0, pltpu.roll(left, 1, 1), pltpu.roll(field, 1, 1))
        return following - previous

    def down(field, which):
        below = jnp.concatenate([field[tiles:], after_ref[which]], axis=0)
        above = jnp.concatenate([before_ref[which], field[: rows - tiles]], axis=0)
        return below - above

    east, up = (
        jnp.concatenate([solved_ref[k, :tiles], middle, solved_ref[k, tiles:]], axis=0)
        for k, middle in enumerate(solve_cells(vals_ref, los_ref))
    )
    north = north_ref[...]
    work_ref[0] = east
    work_ref[1] = up
    work_ref[2] = across(east) / 2.0
    work_ref[3] = down(north, 1) / 2.0
    work_ref[4] = (down(east, 0) + across(north)) / 4.0
    start = block_ref[0] * own
    for field in range(5):
        target, at = (east_up_ref, field) if field < 2 else (strain_ref, field - 2)
        for i in range(rows // tiles):
            for j in range(own):
                target[at, i : i + 1, j * LANES : (j + 1) * LANES] = work_ref[field, pl.ds(i * tiles + start + j, 1), :]


def final(block, los, vals, solved, north, before, after, tiles, own):
    rows = north.shape[0]
    shape = (rows // tiles, own * LANES)
    vmem = pl.BlockSpec(memory_space=pltpu.VMEM)
    return pl.pallas_call(
        functools.partial(final_kernel, tiles, own),
        in_specs=[pl.BlockSpec(memory_space=pltpu.SMEM)] * 2 + [vmem] * 5,
        out_specs=[vmem] * 2,
        out_shape=[jax.ShapeDtypeStruct((2, *shape), jnp.float32), jax.ShapeDtypeStruct((3, *shape), jnp.float32)],
        scratch_shapes=[pltpu.VMEM((5, rows, LANES), jnp.float32)],
        name="solve_and_strain",
    )(block, los, vals, solved, north, before, after)


def per_device(phases, coherent, pairs, res_index, res_weight, coverage, los, north):
    parts = lax.axis_size("pix")
    tracks = lax.axis_size("track")
    here = lax.axis_index("track")
    grid_rows, columns = north.shape
    tiles = columns // CTILE
    rows = grid_rows * tiles
    track = here.astype(jnp.int32)[None]
    edge_stack = lax.all_to_all(
        pack_edges(phases[0], coherent[0], parts, tiles), "pix", split_axis=0, concat_axis=0, tiled=True
    )
    inner_stack = lax.all_to_all(
        pack_inner(phases[0], coherent[0], parts, tiles), "pix", split_axis=0, concat_axis=0, tiled=True
    )
    design, pseudo = setup_track(pairs[0])
    north_cells = north.reshape(rows, LANES)
    cells = (
        res_index.reshape(-1, rows, LANES),
        res_weight.reshape(-1, rows, LANES),
        coverage.reshape(rows, 1),
        north_cells,
    )

    def flat(stack):
        return stack.reshape(-1, stack.shape[2])

    edge_vals, seam = edges(track, los, flat(edge_stack), pseudo, design, cells, tiles)
    edge_vals = lax.all_gather(edge_vals, "track", axis=0)
    solved, first, last = solve_edges(edge_vals, north_cells, los, tiles)
    onward = [(i, i + 1) for i in range(parts - 1)]
    back = [(j, i) for i, j in onward]
    before = lax.ppermute(last, "pix", onward)
    after = lax.ppermute(first, "pix", back)
    inner_vals = inner(track, los, flat(inner_stack), seam, pseudo, design, cells, tiles)
    inner_vals = lax.all_gather(inner_vals, "track", axis=0)
    return tuple(final(track, los, inner_vals, solved, north_cells, before, after, tiles, tiles // tracks))


def solution(mesh):
    in_specs = (
        P("track", "pix", None),
        P("track", "pix", None),
        P("track", None, None),
        P("track", None, "pix"),
        P("track", None, "pix"),
        P("track", "pix", None),
        P(),
        P("pix", None),
    )
    out_specs = (P(None, "pix", "track"), P(None, "pix", "track"))
    return jax.shard_map(
        per_device, mesh=mesh, in_specs=in_specs, out_specs=out_specs, check_vma=False
    )
```

time: 166 us -> 134 us (0.81)
  other arithmetic: 60.4 us -> 0 us
  waiting for transfers between devices: 22.9 us -> 61.9 us
  matrix products: 9.06 us -> 0 us
  Pallas kernels: 26.7 us -> 30.6 us
    another operation x14 -> x0, other arithmetic: 53.2 us -> none  [the longest x7 32.1 us: setup_track(): factor = jnp.linalg.cholesky(normal)]
    all_to_all x1, waiting for transfers between devices: 0.01 us -> 40 us  [per_device(): lax.all_to_all(pack_inner(phases[0], coherent[0], parts, tiles), 'pix', s...]
    another operation x8 -> x0, matrix products: 8.49 us -> none  [the longest x6 6.53 us: setup_track(): pseudo = jax.scipy.linalg.cho_solve((factor, True), design.T)]
    unnamed x20 -> x40, local copies, waits for them, and re-layouts: 6.39 us -> 12.1 us
    slice x11 -> x0, local copies, waits for them, and re-layouts: 4.85 us -> none  [the longest x6 4 us: per_device(): at_inner = [a[..., tiles:rows - tiles, :] for a in per_cell]]
    pallas_call x4, Pallas kernels: 18.9 us -> 22.2 us  [the longest x1 8.36 us: setup_track(): pl.pallas_call(pseudo_kernel, in_specs=[vmem], out_specs=[vmem] * 2, out_...]
    div x2 -> x0, other arithmetic: 3.16 us -> none  [the longest x1 2.19 us: setup_track(): slope = centred * (EPOCHS - 1) / jnp.sum(centred * centred)]
    concatenate x4 -> x0, other arithmetic: 1.92 us -> none  [per_device(): jnp.concatenate([a[..., :tiles, :], a[..., rows - tiles:, :]], axis=-2)]
  transfers between devices with their start and end apart: 4 -> 4, of which waited for: 1 -> 2; matrix products, arithmetic and copies ran while one was open for 49% -> 2% of each run, Pallas kernels for 12% -> 18%
where the time goes in v3:
time: 134 us; the launch traced here: 133 us
  waiting for transfers between devices  61.9 us (46%)
  Pallas kernels  30.6 us (23%)
  starting transfers between devices  17.3 us (13%)
  local copies, waits for them, and re-layouts  13.6 us (10%)
  blocking collectives  9.4 us (7%)
    all_to_all x1, waiting for transfers between devices, per_device(): lax.all_to_all(pack_inner(phases[0], coherent[0], parts, tiles), 'pix', s...  40 us
    all_to_all x1, waiting for transfers between devices, per_device(): lax.all_to_all(pack_edges(phases[0], coherent[0], parts, tiles), 'pix', s...  21.8 us
    unnamed x40, local copies, waits for them, and re-layouts  12.1 us
    pallas_call x1, Pallas kernels, setup_track(): pl.pallas_call(pseudo_kernel, in_specs=[vmem], out_specs=[vmem] * 2, out_...  8.36 us
    pallas_call x1, Pallas kernels, pack_inner(): pl.pallas_call(functools.partial(pack_inner_kernel, reach), in_specs=[pl....  6.69 us
    all_to_all x1, starting transfers between devices, per_device(): lax.all_to_all(pack_edges(phases[0], coherent[0], parts, tiles), 'pix', s...  6.17 us
    pallas_call x1, Pallas kernels, inner(): pl.pallas_call(functools.partial(inner_kernel, tiles), in_specs=[pl.Block...  5.15 us
    pallas_call x1, Pallas kernels, pack_edges(): pl.pallas_call(functools.partial(pack_edges_kernel, tiles), in_specs=[vme...  5.13 us
  transfers between devices with their start and end apart: 4, of which 2 were waited for; matrix products, arithmetic and copies ran while one was open for 2% of the time, Pallas kernels for 18%

profile of v3, /device:TPU:16, one launch (start us, length us, event | category | flops | bytes accessed | tf_op | source)
XLA Modules:
  0.0 133.5 jit_solution(1909936116491298709)
XLA Ops:
  0.6 0.0 copy-start
  0.6 2.2 %copy-done = bf16[1,16,131072]{2,1,0:T(8,128)(2,1)S(1)} copy-done((bf16[1,16,131072]{2,1,0:T(8,128)(2,1)S(1)}, bf16[1,16,131072]{2,1,0:T(8,128)(2,1)}, u32[]{:S(2)}) %copy-start) | copy-done | bytes 4194328
  2.8 0.0 copy-start.8
  2.8 0.8 copy-done.8
  3.7 0.0 copy-start.9
  3.7 5.1 %pack_edges.1 = bf16[16,16,2560]{2,1,0:T(8,128)(2,1)} custom-call(s32[16,1024]{1,0:T(8,128)S(1)} %bitcast.28, bf16[16,131072]{1,0:T(8,128)(2,1)S(1)} %bitcast.20), custom_call_target="tpu_custom_call" | custom-call | tf_op jit(solution)/shard_map/pack_edges/pallas_call | solution.py:97
  8.8 6.2 %all-to-all-start.1 = ((bf16[16,16,2560]{2,1,0:T(8,128)(2,1)}), bf16[16,16,2560]{2,1,0:T(8,128)(2,1)S(1)}, u32[]{:S(2)}, u32[]{:S(2)}) async-start(bf16[16,16,2560]{2,1,0:T(8,128)(2,1)} %pack_edges.1), calls=%async_computation.1 | async-start | bytes 2621440 | tf_op jit(solution)/shard_map/all_to_all | solution.py:455
  15.0 0.0 copy-done.9
  15.0 0.0 copy-start.1
  15.0 2.2 %copy-done.1 = bf16[1,16,131072]{2,1,0:T(8,128)(2,1)S(1)} copy-done((bf16[1,16,131072]{2,1,0:T(8,128)(2,1)S(1)}, bf16[1,16,131072]{2,1,0:T(8,128)(2,1)}, u32[]{:S(2)}) %copy-start.1) | copy-done | bytes 4194328
  17.2 6.7 %pack_inner.1 = bf16[16,16,5888]{2,1,0:T(8,128)(2,1)} custom-call(s32[16,1024]{1,0:T(8,128)S(1)} %bitcast.29, bf16[16,131072]{1,0:T(8,128)(2,1)S(1)} %bitcast.21), custom_call_target="tpu_custom_call" | custom-call | tf_op jit(solution)/shard_map/pack_inner/pallas_call | solution.py:145
  23.9 0.0 copy-start.14
  23.9 0.0 copy-start.15
  23.9 0.0 copy-start.18
  23.9 0.0 copy-start.10
  23.9 0.0 copy-start.11
  23.9 21.8 %all-to-all-done.1 = bf16[16,16,2560]{2,1,0:T(8,128)(2,1)S(1)} async-done(((bf16[16,16,2560]{2,1,0:T(8,128)(2,1)}), bf16[16,16,2560]{2,1,0:T(8,128)(2,1)S(1)}, u32[]{:S(2)}, u32[]{:S(2)}) %all-to-all-start.1) | async-done | bytes 1310752 | tf_op jit(solution)/shard_map/all_to_all | solution.py:455
  45.8 0.0 copy-start.2
  45.8 1.1 copy-done.2
  46.8 4.6 %all-to-all-start = ((bf16[16,16,5888]{2,1,0:T(8,128)(2,1)}), bf16[16,16,5888]{2,1,0:T(8,128)(2,1)S(1)}, u32[]{:S(2)}, u32[]{:S(2)}) async-start(bf16[16,16,5888]{2,1,0:T(8,128)(2,1)} %pack_inner.1), calls=%async_computation | async-start | bytes 6029312 | tf_op jit(solution)/shard_map/all_to_all | solution.py:458
  51.5 0.0 copy-done.14
  51.5 8.4 %pseudo_inverse.1 = (bf16[256,208]{1,0:T(8,128)(2,1)S(1)}, bf16[208,256]{1,0:T(8,128)(2,1)S(1)}) custom-call(s32[2,256]{1,0:T(2,128)S(1)} %bitcast.30), custom_call_target="tpu_custom_call" | custom-call | tf_op jit(solution)/shard_map/pseudo_inverse/pallas_call | solution.py:212
  59.8 0.0 copy-done.15
  59.9 0.9 copy.18
  60.8 0.0 copy-done.18
  60.8 0.7 reshape.30.cover_ref
  61.5 0.8 reshape.27.north_ref
  62.3 0.0 copy-start.4
  62.3 0.0 copy-done.10
  62.3 0.0 copy-start.3
  62.3 1.3 copy-done.3
  63.6 0.0 copy-start.6
  63.6 0.8 copy-done.6
  64.4 2.0 %edge_rows.1 = (f32[2,16,128]{2,1,0:T(8,128)S(1)}, f32[2,4,128]{2,1,0:T(4,128)S(1)}) custom-call(s32[1]{0:T(128)} %bitcast.here_ref.block_ref, f32[2,3]{1,0:T(2,128)S(1)} %copy-done.10, bf16[256,2560]{1,0:T(8,128)(2,1)S(1)} %bitcast.23, bf16[208,256]{1,0:T(8,128)(2,1)S(1)} %get-tuple-element.9.pseudo_ref, bf16[256,208]{1,0:T(8,128)(2,1)S(1)} %get-tuple-element.10.design_ref, ...), custom_call_target="tpu_custom_call" | custom-call | tf_op jit(solution)/shard_map/edge_rows/pallas_call | solution.py:285
  66.4 0.0 copy-start.12
  66.4 4.5 %all-gather.1 = f32[4,16,128]{2,1,0:T(8,128)} all-gather(f32[2,16,128]{2,1,0:T(8,128)S(1)} %get-tuple-element.12), channel_id=3, replica_groups=mesh['track'=2,'pix'=16] {'track'}, dimensions={0}, use_global_device_ids=true | all-gather | bytes 49152 | tf_op jit(solution)/shard_map/all_gather | solution.py:474
  70.9 0.0 copy-done.12
  70.9 0.0 copy-done.4
  70.9 1.4 %solve_edges.1 = (f32[2,16,128]{2,1,0:T(8,128)}, f32[2,8,128]{2,1,0:T(8,128)}, f32[2,8,128]{2,1,0:T(8,128)}) custom-call(f32[2,2,16,128]{3,2,1,0:T(8,128)} %bitcast.34, f32[64,128]{1,0:T(8,128)} %copy-done.4, f32[2,3]{1,0:T(2,128)} %los_ref.7), custom_call_target="tpu_custom_call" | custom-call | tf_op jit(solution)/shard_map/solve_edges/pallas_call | solution.py:387
  72.4 1.9 %collective-permute-start = (f32[2,8,128]{2,1,0:T(8,128)}, f32[2,8,128]{2,1,0:T(8,128)S(1)}, u32[]{:S(2)}, u32[]{:S(2)}) collective-permute-start(f32[2,8,128]{2,1,0:T(8,128)} %get-tuple-element.14), channel_id=1, source_target_pairs={{0,1},{1,2},{2,3},{3,4},{4,5},{5,6},{6,7},{7,8},{8,9},{9,10},{10,1... | collective-permute-start | bytes 24584 | tf_op jit(solution)/shard_map/ppermute | solution.py:478
  74.3 4.5 %collective-permute-start.1 = (f32[2,8,128]{2,1,0:T(8,128)}, f32[2,8,128]{2,1,0:T(8,128)S(1)}, u32[]{:S(2)}, u32[]{:S(2)}) collective-permute-start(f32[2,8,128]{2,1,0:T(8,128)} %get-tuple-element.15), channel_id=1, source_target_pairs={{1,0},{2,1},{3,2},{4,3},{5,4},{6,5},{7,6},{8,7},{9,8},{10,9},{11,1... | collective-permute-start | bytes 24584 | tf_op jit(solution)/shard_map/ppermute | solution.py:479
  78.8 40.0 %all-to-all-done = bf16[16,16,5888]{2,1,0:T(8,128)(2,1)S(1)} async-done(((bf16[16,16,5888]{2,1,0:T(8,128)(2,1)}), bf16[16,16,5888]{2,1,0:T(8,128)(2,1)S(1)}, u32[]{:S(2)}, u32[]{:S(2)}) %all-to-all-start) | async-done | bytes 3014688 | tf_op jit(solution)/shard_map/all_to_all | solution.py:458
  118.9 0.0 copy-done.11
  118.9 0.0 copy-start.5
  118.9 0.8 copy-done.5
  119.6 0.0 copy-start.7
  119.6 0.8 copy-done.7
  120.4 0.0 copy-start.13
  120.4 0.7 copy-done.13
  121.1 5.1 %inner_rows.1 = f32[2,48,128]{2,1,0:T(8,128)S(1)} custom-call(s32[1]{0:T(128)} %bitcast.here_ref.block_ref, f32[2,3]{1,0:T(2,128)S(1)} %copy-done.11, bf16[256,5888]{1,0:T(8,128)(2,1)S(1)} %bitcast.22, f32[2,4,128]{2,1,0:T(4,128)S(1)} %copy-done.13, bf16[208,256]{1,0:T(8,128)(2,1)S(1)} %get-tuple-element.9.pseudo_ref, ...), custom_call_target="tpu_custom_call" | custom-call | tf_op jit(solution)/shard_map/inner_rows/pallas_call | solution.py:342
  126.2 4.9 %all-gather = f32[4,48,128]{2,1,0:T(8,128)} all-gather(f32[2,48,128]{2,1,0:T(8,128)S(1)} %inner_rows.1), channel_id=2, replica_groups=mesh['track'=2,'pix'=16] {'track'}, dimensions={0}, use_global_device_ids=true | all-gather | bytes 147456 | tf_op jit(solution)/shard_map/all_gather | solution.py:481
  131.1 0.0 collective-permute-done.before_ref
  131.1 0.0 copy-start.16
  131.1 0.0 collective-permute-done.1.after_ref
  131.1 0.0 copy-start.17
  131.1 0.6 copy-done.16
  131.7 0.0 copy-done.17
  131.7 1.8 %solve_and_strain.1 = (f32[2,8,512]{2,1,0:T(8,128)}, f32[3,8,512]{2,1,0:T(8,128)}) custom-call(s32[1]{0:T(128)} %bitcast.here_ref.block_ref, f32[2,3]{1,0:T(2,128)} %los_ref.7, f32[2,2,48,128]{3,2,1,0:T(8,128)} %bitcast.31, f32[2,16,128]{2,1,0:T(8,128)} %get-tuple-element.13.solved_ref, f32[64,128]{1,0:T(8,128)} %copy-done.4, f32[2,8,128]{2,1,0:T(8,128)} %copy-done.16, ...), custom_call_target="tpu_custom_call" | custom-call | tf_op jit(solution)/shard_map/solve_and_strain/pallas_call | solution.py:437
  (1 shorter events, 0.0 us)
Async XLA Ops:
  0.6 2.2 %copy-start = (bf16[1,16,131072]{2,1,0:T(8,128)(2,1)S(1)}, bf16[1,16,131072]{2,1,0:T(8,128)(2,1)}, u32[]{:S(2)}) copy-start(bf16[1,16,131072]{2,1,0:T(8,128)(2,1)} %param.8) | copy-start | bytes 12582916
  2.8 0.8 copy-start.8
  3.7 11.3 %copy-start.9 = (s32[1,16,1024]{2,1,0:T(8,128)S(1)}, s32[1,16,1024]{2,1,0:T(8,128)}, u32[]{:S(2)}) copy-start(s32[1,16,1024]{2,1,0:T(8,128)} %param.9) | copy-start | bytes 196612
  8.8 37.0 %all-to-all-start.1 = ((bf16[16,16,2560]{2,1,0:T(8,128)(2,1)}), bf16[16,16,2560]{2,1,0:T(8,128)(2,1)S(1)}, u32[]{:S(2)}, u32[]{:S(2)}) async-start(bf16[16,16,2560]{2,1,0:T(8,128)(2,1)} %pack_edges.1), calls=%async_computation.1 | async-start | bytes 2621440 | tf_op jit(solution)/shard_map/all_to_all | solution.py:455
  15.0 2.2 %copy-start.1 = (bf16[1,16,131072]{2,1,0:T(8,128)(2,1)S(1)}, bf16[1,16,131072]{2,1,0:T(8,128)(2,1)}, u32[]{:S(2)}) copy-start(bf16[1,16,131072]{2,1,0:T(8,128)(2,1)} %param.8) | copy-start | bytes 12582916
  23.9 27.6 %copy-start.14 = (s32[1,256,2]{1,2,0:T(2,128)S(1)}, s32[1,256,2]{1,2,0:T(2,128)}, u32[]{:S(2)}) copy-start(s32[1,256,2]{1,2,0:T(2,128)} %param.10) | copy-start | bytes 6148
  23.9 36.0 %copy-start.15 = (s32[1,4,8192]{2,1,0:T(4,128)S(1)}, s32[1,4,8192]{2,1,0:T(4,128)}, u32[]{:S(2)}) copy-start(s32[1,4,8192]{2,1,0:T(4,128)} %param.11) | copy-start | bytes 393220
  23.9 36.9 %copy-start.18 = (s32[1,8,8]{2,1,0:T(8,128)S(1)}, s32[1,8,8]{2,1,0:T(8,128)}, u32[]{:S(2)}) copy-start(s32[1,8,8]{2,1,0:T(8,128)} %param.13) | copy-start | bytes 772
  23.9 38.4 %copy-start.10 = (f32[2,3]{1,0:T(2,128)S(1)}, f32[2,3]{1,0:T(2,128)}, u32[]{:S(2)}) copy-start(f32[2,3]{1,0:T(2,128)} %los_ref.7) | copy-start | bytes 76
  23.9 95.0 %copy-start.11 = (f32[2,3]{1,0:T(2,128)S(1)}, f32[2,3]{1,0:T(2,128)}, u32[]{:S(2)}) copy-start(f32[2,3]{1,0:T(2,128)} %los_ref.7) | copy-start | bytes 76
  45.8 1.1 copy-start.2
  46.8 72.0 %all-to-all-start = ((bf16[16,16,5888]{2,1,0:T(8,128)(2,1)}), bf16[16,16,5888]{2,1,0:T(8,128)(2,1)S(1)}, u32[]{:S(2)}, u32[]{:S(2)}) async-start(bf16[16,16,5888]{2,1,0:T(8,128)(2,1)} %pack_inner.1), calls=%async_computation | async-start | bytes 6029312 | tf_op jit(solution)/shard_map/all_to_all | solution.py:458
  62.3 8.7 %copy-start.4 = (f32[64,128]{1,0:T(8,128)}, f32[64,128]{1,0:T(8,128)S(1)}, u32[]{:S(2)}) copy-start(f32[64,128]{1,0:T(8,128)S(1)} %reshape.27.north_ref) | copy-start | bytes 98308
  62.3 1.3 copy-start.3
  63.6 0.8 copy-start.6
  66.4 4.5 %copy-start.12 = (f32[2,4,128]{2,1,0:T(4,128)}, f32[2,4,128]{2,1,0:T(4,128)S(1)}, u32[]{:S(2)}) copy-start(f32[2,4,128]{2,1,0:T(4,128)S(1)} %get-tuple-element.11.seam_ref) | copy-start | bytes 12292
  72.4 58.7 %collective-permute-start = (f32[2,8,128]{2,1,0:T(8,128)}, f32[2,8,128]{2,1,0:T(8,128)S(1)}, u32[]{:S(2)}, u32[]{:S(2)}) collective-permute-start(f32[2,8,128]{2,1,0:T(8,128)} %get-tuple-element.14), channel_id=1, source_target_pairs={{0,1},{1,2},{2,3},{3,4},{4,5},{5,6},{6,7},{7,8},{8,9},{9,10},{10,1... | collective-permute-start | bytes 24584 | tf_op jit(solution)/shard_map/ppermute | solution.py:478
  74.3 56.8 %collective-permute-start.1 = (f32[2,8,128]{2,1,0:T(8,128)}, f32[2,8,128]{2,1,0:T(8,128)S(1)}, u32[]{:S(2)}, u32[]{:S(2)}) collective-permute-start(f32[2,8,128]{2,1,0:T(8,128)} %get-tuple-element.15), channel_id=1, source_target_pairs={{1,0},{2,1},{3,2},{4,3},{5,4},{6,5},{7,6},{8,7},{9,8},{10,9},{11,1... | collective-permute-start | bytes 24584 | tf_op jit(solution)/shard_map/ppermute | solution.py:479
  118.9 0.8 copy-start.5
  119.6 0.8 copy-start.7
  120.4 0.7 copy-start.13
  131.1 0.6 copy-start.16
  131.1 0.6 copy-start.17

commit v4 on v3

--- a/solution.py
+++ b/solution.py
@@ -15,11 +15,17 @@
 LANES = 128
 TILE = 256
 PIECE = 1024
+GROUP = 4
+EDGE_COST = 50_000_000_000
 
 
 prior_var = 0.1
 ridge_term = 0.5
 medium = 24 * 1024 * 1024
+
+
+def stay(array):
+    return pltpu.with_memory_space_constraint(array, pltpu.HBM)
 
 
 def spread(flags, j, shape):
@@ -32,12 +38,16 @@
     return pltpu.roll(flags, (LANES - (first - lead)) % LANES, 1)
 
 
-def pack_edges_kernel(tiles, flags_ref, phases_ref, out_ref, near_ref, in_sem):
-    parts, ifgs, _ = out_ref.shape
-    blocks = flags_ref.shape[1]
+def pack_edges_kernel(tiles, group, place_ref, flags_hbm, phases_ref, *refs):
+    *out_refs, flags_ref, near_ref, flag_sem, in_sem = refs
+    planes = len(out_refs)
+    parts = planes * group
+    ifgs, blocks = flags_ref.shape
     span = blocks // parts
     reach = tiles + 1
     bound = 2 * reach * MBLK
+    flag_copy = pltpu.make_async_copy(flags_hbm, flags_ref, flag_sem)
+    flag_copy.start()
     ends = []
     for b, low, at in ((0, 0, reach), (parts, blocks - reach, 0)):
         ends.append(
@@ -60,68 +70,97 @@
     empty = jnp.zeros((ifgs, reach * MBLK), jnp.bfloat16)
     near_ref[0, :, : reach * MBLK] = empty
     near_ref[parts, :, reach * MBLK :] = empty
+    flag_copy.wait()
     ends[0].wait()
 
-    @pl.loop(0, parts)
-    def _(p):
-        @pl.when(p < parts - 1)
-        def _():
-            between(p + 1).wait()
-
-        @pl.when(p == parts - 1)
-        def _():
-            ends[1].wait()
-
-        first = p * span
-        flags = part_flags(flags_ref, first)
-        earlier = part_flags(flags_ref, jnp.maximum(first - 1, 0))
-        later = part_flags(flags_ref, jnp.minimum(first + span, blocks - 1))
-        shape = (ifgs, MBLK)
-        for half in range(2):
-            for k in range(tiles + 2):
-                block = k - 1 if half == 0 else span - reach + k
-                if block < 0:
-                    keep = spread(earlier, 0, shape)
-                elif block == span:
-                    keep = spread(later, 0, shape)
-                else:
-                    keep = spread(flags, block, shape)
-                at = (reach - 1 + k if half == 0 else k) * MBLK
-                to = (half * (tiles + 2) + k) * MBLK
-                out_ref[p, :, to : to + MBLK] = near_ref[p + half, :, at : at + MBLK] * keep
-
-
-def pack_edges(phases, flags, parts, tiles):
+    @pl.loop(1, parts)
+    def _(b):
+        between(b).wait()
+
+    ends[1].wait()
+    for s in range(planes):
+        first_part = lax.rem(place_ref[0] + s, planes) * group
+
+        @pl.loop(0, group, unroll=2)
+        def _(g):
+            p = first_part + g
+            first = p * span
+            flags = part_flags(flags_ref, first)
+            earlier = part_flags(flags_ref, jnp.maximum(first - 1, 0))
+            later = part_flags(flags_ref, jnp.minimum(first + span, blocks - 1))
+            shape = (ifgs, MBLK)
+            for half in range(2):
+                for k in range(tiles + 2):
+                    block = k - 1 if half == 0 else span - reach + k
+                    if block < 0:
+                        keep = spread(earlier, 0, shape)
+                    elif block == span:
+                        keep = spread(later, 0, shape)
+                    else:
+                        keep = spread(flags, block, shape)
+                    at = (reach - 1 + k if half == 0 else k) * MBLK
+                    to = (half * (tiles + 2) + k) * MBLK
+                    out_refs[s][g, :, to : to + MBLK] = near_ref[p + half, :, at : at + MBLK] * keep
+
+
+def pack_edges(place, phases, flags, parts, group, tiles):
     ifgs = phases.shape[0]
-    vmem = pl.BlockSpec(memory_space=pltpu.VMEM)
-    return pl.pallas_call(
-        functools.partial(pack_edges_kernel, tiles),
-        in_specs=[vmem, pl.BlockSpec(memory_space=pltpu.HBM)],
-        out_specs=vmem,
-        out_shape=jax.ShapeDtypeStruct((parts, ifgs, 2 * (tiles + 2) * MBLK), jnp.bfloat16),
+    planes = parts // group
+    hbm = pl.BlockSpec(memory_space=pltpu.HBM)
+    width = 2 * (tiles + 2) * MBLK
+    return pl.pallas_call(
+        functools.partial(pack_edges_kernel, tiles, group),
+        in_specs=[pl.BlockSpec(memory_space=pltpu.SMEM), hbm, hbm],
+        out_specs=[pl.BlockSpec(memory_space=pltpu.VMEM)] * planes,
+        out_shape=[jax.ShapeDtypeStruct((group, ifgs, width), jnp.bfloat16)] * planes,
         scratch_shapes=[
+            pltpu.VMEM(flags.shape, jnp.int32),
             pltpu.VMEM((parts + 1, ifgs, 2 * (tiles + 1) * MBLK), jnp.bfloat16),
+            pltpu.SemaphoreType.DMA,
             pltpu.SemaphoreType.DMA((parts + 1,)),
         ],
         compiler_params=pltpu.CompilerParams(vmem_limit_bytes=medium),
         name="pack_edges",
-    )(flags, phases)
-
-
-def pack_inner_kernel(reach, flags_ref, phases_ref, out_ref, held_ref, ready_ref, in_sem, out_sem):
+    )(place, stay(flags), stay(phases))
+
+
+def regroup_kernel(planes, group, place_ref, after_ref, *refs):
+    in_refs, out_refs = refs[:planes], refs[planes:]
+    for j in range(group):
+        column = lax.rem(place_ref[1] + j, group)
+        for s in range(planes):
+            out_refs[j][s] = in_refs[s][column]
+
+
+def regroup(place, after, pieces, group):
+    planes = len(pieces)
+    vmem = pl.BlockSpec(memory_space=pltpu.VMEM)
+    shape = (planes, *pieces[0].shape[1:])
+    return pl.pallas_call(
+        functools.partial(regroup_kernel, planes, group),
+        in_specs=[pl.BlockSpec(memory_space=pltpu.SMEM)] + [vmem] * (planes + 1),
+        out_specs=[vmem] * group,
+        out_shape=[jax.ShapeDtypeStruct(shape, jnp.bfloat16)] * group,
+        compiler_params=pltpu.CompilerParams(vmem_limit_bytes=medium),
+        name="regroup",
+    )(place, after, *pieces)
+
+
+def pack_inner_kernel(reach, flags_hbm, phases_ref, out_ref, flags_ref, held_ref, flag_sem, in_sem):
     parts, ifgs, width = out_ref.shape
     span = flags_ref.shape[1] // parts
+    flag_copy = pltpu.make_async_copy(flags_hbm, flags_ref, flag_sem)
+    flag_copy.start()
 
     def inward(p):
         low = pl.multiple_of((p * span + reach) * MBLK, MBLK)
         return pltpu.make_async_copy(phases_ref.at[:, pl.ds(low, width)], held_ref.at[p], in_sem.at[p])
 
-    def outward(p):
-        return pltpu.make_async_copy(ready_ref.at[p], out_ref.at[p], out_sem.at[p])
-
     @pl.loop(0, parts)
     def _(p):
         inward(p).start()
+
+    flag_copy.wait()
 
     @pl.loop(0, parts)
     def _(p):
@@ -129,12 +168,7 @@
         flags = part_flags(flags_ref, p * span)
         for k in range(width // MBLK):
             at = slice(k * MBLK, (k + 1) * MBLK)
-            ready_ref[p, :, at] = held_ref[p, :, at] * spread(flags, reach + k, (ifgs, MBLK))
-        outward(p).start()
-
-    @pl.loop(0, parts)
-    def _(p):
-        outward(p).wait()
+            out_ref[p, :, at] = held_ref[p, :, at] * spread(flags, reach + k, (ifgs, MBLK))
 
 
 def pack_inner(phases, flags, parts, tiles):
@@ -144,31 +178,34 @@
     hbm = pl.BlockSpec(memory_space=pltpu.HBM)
     return pl.pallas_call(
         functools.partial(pack_inner_kernel, reach),
-        in_specs=[pl.BlockSpec(memory_space=pltpu.VMEM), hbm],
-        out_specs=hbm,
+        in_specs=[hbm, hbm],
+        out_specs=pl.BlockSpec(memory_space=pltpu.VMEM),
         out_shape=jax.ShapeDtypeStruct((parts, ifgs, width), jnp.bfloat16),
         scratch_shapes=[
+            pltpu.VMEM(flags.shape, jnp.int32),
             pltpu.VMEM((parts, ifgs, width), jnp.bfloat16),
-            pltpu.VMEM((parts, ifgs, width), jnp.bfloat16),
-            pltpu.SemaphoreType.DMA((parts,)),
+            pltpu.SemaphoreType.DMA,
             pltpu.SemaphoreType.DMA((parts,)),
         ],
         compiler_params=pltpu.CompilerParams(vmem_limit_bytes=medium),
         name="pack_inner",
-    )(flags, phases)
+    )(stay(flags), stay(phases))
 
 
 def exact_dot(a, b):
     return jnp.dot(a, b, precision=lax.Precision.HIGHEST, preferred_element_type=jnp.float32)
 
 
-def pseudo_kernel(pairs_ref, design_ref, out_ref, normal_ref, inverse_ref):
+def pseudo_kernel(pairs_ref, other_ref, design_ref, out_ref, other_design_ref, other_out_ref, normal_ref, inverse_ref):
     ifgs = pairs_ref.shape[1]
     size = normal_ref.shape[0]
     epoch = lax.broadcasted_iota(jnp.int32, (size, ifgs), 0)
-    across = (epoch == pairs_ref[1:2, :]).astype(jnp.float32) - (epoch == pairs_ref[0:1, :]).astype(jnp.float32)
+
+    def ends(ref):
+        return (epoch == ref[1:2, :]).astype(jnp.float32) - (epoch == ref[0:1, :]).astype(jnp.float32)
+
+    across = ends(pairs_ref)
     down = across.T
-    design_ref[...] = down[:, :ROWS].astype(jnp.bfloat16)
     eye = (
         lax.broadcasted_iota(jnp.int32, (size, size), 0) == lax.broadcasted_iota(jnp.int32, (size, size), 1)
     ).astype(jnp.float32)
@@ -190,39 +227,43 @@
         return step + 1, jnp.max(jnp.abs(rest))
 
     lax.while_loop(unfinished, improve, (jnp.int32(0), jnp.float32(1.0)))
-    pseudo = exact_dot(inverse_ref[...], across)[:ROWS].astype(jnp.bfloat16).astype(jnp.float32)
     place = lax.broadcasted_iota(jnp.int32, (ROWS, ifgs), 0)
     centred = place.astype(jnp.float32) - (EPOCHS - 1) / 2.0
     square = sum((e - (EPOCHS - 1) / 2.0) ** 2 for e in range(EPOCHS))
-    slope = centred * (EPOCHS - 1) / square
-    row = jnp.sum(pseudo * jnp.where(place < EPOCHS, slope, 0.0), axis=0, keepdims=True)
-    high = row.astype(jnp.bfloat16).astype(jnp.float32)
-    rest = row - high
-    middle = rest.astype(jnp.bfloat16).astype(jnp.float32)
-    low = rest - middle
+    slope = jnp.where(place < EPOCHS, centred * (EPOCHS - 1) / square, 0.0)
     extra = place - EPOCHS
-    terms = jnp.where(extra == 0, high, jnp.where(extra == 1, middle, jnp.where(extra == 2, low, 0.0)))
-    out_ref[...] = jnp.where(extra < 0, pseudo, terms).astype(jnp.bfloat16)
-
-
-def setup_track(pair_rows):
+    for ref, to_design_ref, to_ref in ((pairs_ref, design_ref, out_ref), (other_ref, other_design_ref, other_out_ref)):
+        across = ends(ref)
+        to_design_ref[...] = across.T[:, :ROWS].astype(jnp.bfloat16)
+        pseudo = exact_dot(inverse_ref[...], across)[:ROWS].astype(jnp.bfloat16).astype(jnp.float32)
+        row = jnp.sum(pseudo * slope, axis=0, keepdims=True)
+        high = row.astype(jnp.bfloat16).astype(jnp.float32)
+        rest = row - high
+        middle = rest.astype(jnp.bfloat16).astype(jnp.float32)
+        low = rest - middle
+        terms = jnp.where(extra == 0, high, jnp.where(extra == 1, middle, jnp.where(extra == 2, low, 0.0)))
+        to_ref[...] = jnp.where(extra < 0, pseudo, terms).astype(jnp.bfloat16)
+
+
+def setup_track(pair_rows, other_rows):
     ifgs = pair_rows.shape[0]
     size = 256
     vmem = pl.BlockSpec(memory_space=pltpu.VMEM)
     return pl.pallas_call(
         pseudo_kernel,
-        in_specs=[vmem],
-        out_specs=[vmem] * 2,
-        out_shape=[jax.ShapeDtypeStruct((ifgs, ROWS), jnp.bfloat16), jax.ShapeDtypeStruct((ROWS, ifgs), jnp.bfloat16)],
+        in_specs=[vmem] * 2,
+        out_specs=[vmem] * 4,
+        out_shape=[jax.ShapeDtypeStruct((ifgs, ROWS), jnp.bfloat16), jax.ShapeDtypeStruct((ROWS, ifgs), jnp.bfloat16)] * 2,
         scratch_shapes=[pltpu.VMEM((size, size), jnp.float32), pltpu.VMEM((size, size), jnp.float32)],
         compiler_params=pltpu.CompilerParams(vmem_limit_bytes=medium),
         name="pseudo_inverse",
-    )(pair_rows.T)
-
-
-def invert_tiles(stack_ref, first, width, pseudo_ref, design_ref, fields_ref, base):
+    )(pair_rows.T, other_rows.T)
+
+
+def invert_tiles(stack_refs, first, width, pseudo_ref, design_ref, fields_ref, base):
     for start in range(0, width, TILE):
-        stack = stack_ref[:, pl.ds(pl.multiple_of(first + start, LANES), TILE)]
+        here = pl.ds(pl.multiple_of(first + start, LANES), TILE)
+        stack = jnp.concatenate([ref[:, here] for ref in stack_refs], axis=0)
         series = jnp.dot(pseudo_ref[...], stack, preferred_element_type=jnp.float32)
         velocity = jnp.sum(series[EPOCHS:], axis=0, keepdims=True)
         fitted = jnp.dot(design_ref[...], series.astype(jnp.bfloat16), preferred_element_type=jnp.float32)
@@ -260,14 +301,16 @@
 
 
 def edges_kernel(
-    tiles, here_ref, los_ref, stack_ref, pseudo_ref, design_ref, index_ref, weight_ref, cover_ref, north_ref, out_ref, seam_ref, fields_ref
+    tiles, group, here_ref, los_ref, *refs
 ):
+    stack_refs = refs[:group]
+    pseudo_ref, design_ref, index_ref, weight_ref, cover_ref, north_ref, out_ref, seam_ref, fields_ref = refs[group:]
     rows = index_ref.shape[1]
-    width = stack_ref.shape[1] // 2
+    width = stack_refs[0].shape[1] // 2
 
     @pl.loop(0, 2)
     def _(half):
-        invert_tiles(stack_ref, half * width, width, pseudo_ref, design_ref, fields_ref, half * (tiles + 2))
+        invert_tiles(stack_refs, half * width, width, pseudo_ref, design_ref, fields_ref, half * (tiles + 2))
 
     seam_ref[...] = fields_ref[:, tiles : tiles + 4, :]
     north_c = los_ref[here_ref[0], 1]
@@ -279,12 +322,12 @@
             )
 
 
-def edges(here, los, stack, pseudo, design, cells, tiles):
+def edges(here, los, stacks, pseudo, design, cells, tiles):
     rows = 2 * (tiles + 2)
     vmem = pl.BlockSpec(memory_space=pltpu.VMEM)
     return pl.pallas_call(
-        functools.partial(edges_kernel, tiles),
-        in_specs=[pl.BlockSpec(memory_space=pltpu.SMEM)] * 2 + [vmem] * 7,
+        functools.partial(edges_kernel, tiles, len(stacks)),
+        in_specs=[pl.BlockSpec(memory_space=pltpu.SMEM)] * 2 + [vmem] * (len(stacks) + 6),
         out_specs=[vmem] * 2,
         out_shape=[
             jax.ShapeDtypeStruct((2, 2 * tiles, LANES), jnp.float32),
@@ -292,40 +335,24 @@
         ],
         scratch_shapes=[pltpu.VMEM((2, -(-rows // 8) * 8, LANES), jnp.float32)],
         compiler_params=pltpu.CompilerParams(vmem_limit_bytes=medium),
+        cost_estimate=pl.CostEstimate(flops=EDGE_COST, bytes_accessed=0, transcendentals=0),
         name="edge_rows",
-    )(here, los, stack, pseudo, design, *cells)
+    )(here, los, *stacks, pseudo, design, *cells)
 
 
 def inner_kernel(
     tiles, here_ref, los_ref, stack_ref, seam_ref, pseudo_ref, design_ref, index_ref, weight_ref, cover_ref, north_ref, out_ref,
-    fields_ref, held_ref, sem,
+    fields_ref,
 ):
-    ifgs, width = stack_ref.shape
-    pieces = -(-width // PIECE)
-    last = width - (pieces - 1) * PIECE
-
-    def piece(k, size):
-        part = pl.ds(pl.multiple_of(k * PIECE, LANES), size)
-        return pltpu.make_async_copy(stack_ref.at[:, part], held_ref.at[:, part], sem.at[k])
-
-    for k in range(pieces):
-        piece(k, PIECE if k < pieces - 1 else last).start()
+    width = stack_ref.shape[1]
     pixel_rows = width // LANES
     fields_ref[:, 0:2, :] = seam_ref[:, 0:2, :]
     fields_ref[:, pixel_rows + 2 : pixel_rows + 4, :] = seam_ref[:, 2:4, :]
 
-    @pl.loop(0, pieces)
+    @pl.loop(0, -(-width // PIECE))
     def _(k):
-        @pl.when(k < pieces - 1)
-        def _():
-            piece(k, PIECE).wait()
-
-        @pl.when(k == pieces - 1)
-        def _():
-            piece(pieces - 1, last).wait()
-
         first = jnp.minimum(k * PIECE, width - PIECE)
-        invert_tiles(held_ref, first, PIECE, pseudo_ref, design_ref, fields_ref, 2 + first // LANES)
+        invert_tiles([stack_ref], first, PIECE, pseudo_ref, design_ref, fields_ref, 2 + first // LANES)
 
     north_c = los_ref[here_ref[0], 1]
 
@@ -336,19 +363,14 @@
 
 
 def inner(here, los, stack, seam, pseudo, design, cells, tiles):
-    ifgs, width = stack.shape
     rows = cells[0].shape[1] - 2 * tiles
     vmem = pl.BlockSpec(memory_space=pltpu.VMEM)
     return pl.pallas_call(
         functools.partial(inner_kernel, tiles),
-        in_specs=[pl.BlockSpec(memory_space=pltpu.SMEM)] * 2 + [pl.BlockSpec(memory_space=pltpu.HBM)] + [vmem] * 7,
+        in_specs=[pl.BlockSpec(memory_space=pltpu.SMEM)] * 2 + [vmem] * 8,
         out_specs=vmem,
         out_shape=jax.ShapeDtypeStruct((2, rows, LANES), jnp.float32),
-        scratch_shapes=[
-            pltpu.VMEM((2, -(-(rows + 2) // 8) * 8, LANES), jnp.float32),
-            pltpu.VMEM((ifgs, width), jnp.bfloat16),
-            pltpu.SemaphoreType.DMA((-(-width // PIECE),)),
-        ],
+        scratch_shapes=[pltpu.VMEM((2, -(-(rows + 2) // 8) * 8, LANES), jnp.float32)],
         compiler_params=pltpu.CompilerParams(vmem_limit_bytes=medium),
         name="inner_rows",
     )(here, los, stack, seam, pseudo, design, *cells)
@@ -452,13 +474,28 @@
     tiles = columns // CTILE
     rows = grid_rows * tiles
     track = here.astype(jnp.int32)[None]
-    edge_stack = lax.all_to_all(
-        pack_edges(phases[0], coherent[0], parts, tiles), "pix", split_axis=0, concat_axis=0, tiled=True
+    group = GROUP if parts % GROUP == 0 else parts
+    planes = parts // group
+    plane, column = jnp.divmod(lax.axis_index("pix").astype(jnp.int32), group)
+    place = jnp.stack([plane, column])
+    packed = pack_edges(place, phases[0], coherent[0], parts, group, tiles)
+    steps_j, steps_s = jnp.meshgrid(jnp.arange(group), jnp.arange(planes), indexing="ij")
+    sources = ((plane - steps_s) % planes * group + (column - steps_j) % group).reshape(-1)
+    edge_pairs = jnp.take(pairs[0].reshape(parts, -1, 2), sources, axis=0).reshape(-1, 2)
+    design, pseudo, edge_design, edge_pseudo = setup_track(pairs[0], edge_pairs)
+    arrived = [packed[0]]
+    for s in range(1, planes):
+        far = [(z * group + c, (z + s) % planes * group + c) for z in range(planes) for c in range(group)]
+        arrived.append(lax.ppermute(packed[s], "pix", far))
+    by_column = regroup(place, edge_pseudo, arrived, group)
+    pieces = [by_column[0]]
+    for j in range(1, group):
+        near = [(z * group + c, z * group + (c + j) % group) for z in range(planes) for c in range(group)]
+        pieces.append(lax.ppermute(by_column[j], "pix", near))
+    later_flags, *_ = lax.optimization_barrier((coherent[0], packed[0]))
+    inner_stack = lax.all_to_all(
+        pack_inner(phases[0], later_flags, parts, tiles), "pix", split_axis=0, concat_axis=0, tiled=True
     )
-    inner_stack = lax.all_to_all(
-        pack_inner(phases[0], coherent[0], parts, tiles), "pix", split_axis=0, concat_axis=0, tiled=True
-    )
-    design, pseudo = setup_track(pairs[0])
     north_cells = north.reshape(rows, LANES)
     cells = (
         res_index.reshape(-1, rows, LANES),
@@ -468,9 +505,9 @@
     )
 
     def flat(stack):
-        return stack.reshape(-1, stack.shape[2])
-
-    edge_vals, seam = edges(track, los, flat(edge_stack), pseudo, design, cells, tiles)
+        return stack.reshape(-1, stack.shape[-1])
+
+    edge_vals, seam = edges(track, los, [flat(piece) for piece in pieces], edge_pseudo, edge_design, cells, tiles)
     edge_vals = lax.all_gather(edge_vals, "track", axis=0)
     solved, first, last = solve_edges(edge_vals, north_cells, los, tiles)
     onward = [(i, i + 1) for i in range(parts - 1)]

time: 134 us -> 116 us (0.87)
  waiting for transfers between devices: 61.9 us -> 45.1 us
  local copies, waits for them, and re-layouts: 13.6 us -> 9.7 us
  Pallas kernels: 30.6 us -> 32.7 us
    all_to_all x2 -> x1, waiting for transfers between devices: 61.9 us -> 3.22 us  [per_device(): lax.all_to_all(pack_inner(phases[0], later_flags, parts, tiles), 'pix', s...]
    ppermute x0 -> x6, waiting for transfers between devices: none -> 41.8 us  [the longest x3 22.7 us: per_device(): pieces.append(lax.ppermute(by_column[j], 'pix', near))]
    ppermute x0 -> x6, starting transfers between devices: none -> 4.96 us  [the longest x3 3.17 us: per_device(): arrived.append(lax.ppermute(packed[s], 'pix', far))]
    all_to_all x2 -> x1, starting transfers between devices: 10.8 us -> 6.45 us  [per_device(): lax.all_to_all(pack_inner(phases[0], later_flags, parts, tiles), 'pix', s...]
    unnamed x40 -> x36, local copies, waits for them, and re-layouts: 12.1 us -> 8.28 us
    pallas_call x4 -> x5, Pallas kernels: 22.2 us -> 24.6 us  [the longest x1 8.72 us: setup_track(): pl.pallas_call(pseudo_kernel, in_specs=[vmem] * 2, out_specs=[vmem] * 4,...]
  transfers between devices with their start and end apart: 4 -> 9, of which waited for: 2 -> 5; matrix products, arithmetic and copies ran while one was open for 2% -> 3% of each run, Pallas kernels for 18% -> 23%
where the time goes in v4:
time: 116 us
  waiting for transfers between devices  45.1 us (39%)
  Pallas kernels  32.7 us (28%)
  starting transfers between devices  17.9 us (15%)
  local copies, waits for them, and re-layouts  9.7 us (8%)
  blocking collectives  9.4 us (8%)
    ppermute x3, waiting for transfers between devices, per_device(): pieces.append(lax.ppermute(by_column[j], 'pix', near))  22.7 us
    ppermute x3, waiting for transfers between devices, per_device(): arrived.append(lax.ppermute(packed[s], 'pix', far))  19.1 us
    pallas_call x1, Pallas kernels, setup_track(): pl.pallas_call(pseudo_kernel, in_specs=[vmem] * 2, out_specs=[vmem] * 4,...  8.72 us
    unnamed x36, local copies, waits for them, and re-layouts  8.28 us
    all_to_all x1, starting transfers between devices, per_device(): lax.all_to_all(pack_inner(phases[0], later_flags, parts, tiles), 'pix', s...  6.45 us
    pallas_call x1, Pallas kernels, pack_inner(): pl.pallas_call(functools.partial(pack_inner_kernel, reach), in_specs=[hbm...  6.41 us
    all_gather x1, blocking collectives, per_device(): inner_vals = lax.all_gather(inner_vals, 'track', axis=0)  4.87 us
    pallas_call x1, Pallas kernels, inner(): pl.pallas_call(functools.partial(inner_kernel, tiles), in_specs=[pl.Block...  4.87 us
  transfers between devices with their start and end apart: 9, of which 5 were waited for; matrix products, arithmetic and copies ran while one was open for 3% of the time, Pallas kernels for 23%

profile of v4, /device:TPU:16, one launch (start us, length us, event | category | flops | bytes accessed | tf_op | source)
XLA Modules:
  0.0 115.7 jit_solution(9626237818973046901)
XLA Ops:
  0.7 0.1 pad_add_fusion.place_ref
  0.7 4.6 %pack_edges.1 = (bf16[4,16,2560]{2,1,0:T(8,128)(2,1)S(1)}, bf16[4,16,2560]{2,1,0:T(8,128)(2,1)}, bf16[4,16,2560]{2,1,0:T(8,128)(2,1)}, bf16[4,16,2560]{2,1,0:T(8,128)(2,1)}) custom-call(s32[2]{0:T(128)S(1)} %pad_add_fusion.place_ref, s32[16,1024]{1,0:T(8,128)} %bitcast.43, bf16[16,131072]{1,0:T(8,128)(2,1)} %bitcast.40), custom_call_target="tpu_custom_call" | custom-call | tf_op jit(solution)/shard_map/pack_edges/pallas_call | solution.py:111
  5.4 1.6 %collective-permute-start = (bf16[4,16,2560]{2,1,0:T(8,128)(2,1)}, bf16[4,16,2560]{2,1,0:T(8,128)(2,1)}, u32[]{:S(2)}, u32[]{:S(2)}) collective-permute-start(bf16[4,16,2560]{2,1,0:T(8,128)(2,1)} %get-tuple-element.23), channel_id=1, source_target_pairs={{0,4},{1,5},{2,6},{3,7},{4,8},{5,9},{6,10},{7,11},{8,12},{9,13},{1... | collective-permute-start | bytes 983048 | tf_op jit(solution)/shard_map/ppermute | solution.py:489
  7.0 0.3 collective-permute-start.1
  7.3 1.2 %collective-permute-start.2 = (bf16[4,16,2560]{2,1,0:T(8,128)(2,1)}, bf16[4,16,2560]{2,1,0:T(8,128)(2,1)}, u32[]{:S(2)}, u32[]{:S(2)}) collective-permute-start(bf16[4,16,2560]{2,1,0:T(8,128)(2,1)} %get-tuple-element.25), channel_id=1, source_target_pairs={{0,12},{1,13},{2,14},{3,15},{4,0},{5,1},{6,2},{7,3},{8,4},{9,5},{1... | collective-permute-start | bytes 983048 | tf_op jit(solution)/shard_map/ppermute | solution.py:489
  8.5 6.4 %pack_inner.1 = bf16[16,16,5888]{2,1,0:T(8,128)(2,1)} custom-call(s32[16,1024]{1,0:T(8,128)} %bitcast.44, bf16[16,131072]{1,0:T(8,128)(2,1)} %bitcast.41), custom_call_target="tpu_custom_call" | custom-call | tf_op jit(solution)/shard_map/pack_inner/pallas_call | solution.py:179
  14.9 0.0 copy-start.8
  15.0 0.0 copy-start.13
  15.0 0.0 copy-start.16
  15.0 0.0 copy-start.6
  15.0 6.4 %all-to-all-start = ((bf16[16,16,5888]{2,1,0:T(8,128)(2,1)}), bf16[16,16,5888]{2,1,0:T(8,128)(2,1)S(1)}, u32[]{:S(2)}, u32[]{:S(2)}) async-start(bf16[16,16,5888]{2,1,0:T(8,128)(2,1)} %pack_inner.1), calls=%async_computation | async-start | bytes 6029312 | tf_op jit(solution)/shard_map/all_to_all | solution.py:496
  21.5 0.1 broadcast_in_dim.34
  21.5 0.1 broadcast_in_dim.40
  21.6 0.1 broadcast_in_dim.39
  21.7 0.1 broadcast_in_dim.35
  21.8 0.1 broadcast_in_dim.33
  21.9 0.0 copy-done.8
  21.9 0.1 reshape_squeeze.3
  22.0 0.6 gather_fusion
  22.6 0.1 gather.7
  22.7 0.1 broadcast_in_dim.36
  22.8 0.1 broadcast_in_dim.37
  22.9 8.7 %pseudo_inverse.1 = (bf16[256,208]{1,0:T(8,128)(2,1)S(1)}, bf16[208,256]{1,0:T(8,128)(2,1)S(1)}, bf16[256,208]{1,0:T(8,128)(2,1)S(1)}, bf16[208,256]{1,0:T(8,128)(2,1)S(1)}) custom-call(s32[2,256]{1,0:T(2,128)S(1)} %bitcast.38, s32[2,256]{1,0:T(2,128)S(1)} %select_bitcast_fusion.other_ref), custom_call_target="tpu_custom_call" | custom-call | tf_op jit(solution)/shard_map/pseudo_inverse/pallas_call | solution.py:252
  31.6 0.0 copy-start.4
  31.6 0.6 copy-done.4
  32.3 0.0 collective-permute-done.refs_1_
  32.3 0.0 collective-permute-done.1.refs_2_
  32.3 19.1 %collective-permute-done.2.refs_3_ = bf16[4,16,2560]{2,1,0:T(8,128)(2,1)} collective-permute-done((bf16[4,16,2560]{2,1,0:T(8,128)(2,1)}, bf16[4,16,2560]{2,1,0:T(8,128)(2,1)}, u32[]{:S(2)}, u32[]{:S(2)}) %collective-permute-start.2) | collective-permute-done | bytes 327712 | tf_op jit(solution)/shard_map/ppermute | solution.py:489
  51.4 2.2 %regroup.1 = (bf16[4,16,2560]{2,1,0:T(8,128)(2,1)S(1)}, bf16[4,16,2560]{2,1,0:T(8,128)(2,1)}, bf16[4,16,2560]{2,1,0:T(8,128)(2,1)}, bf16[4,16,2560]{2,1,0:T(8,128)(2,1)}) custom-call(s32[2]{0:T(128)S(1)} %pad_add_fusion.place_ref, bf16[208,256]{1,0:T(8,128)(2,1)S(1)} %get-tuple-element.22.after_ref.refs_4_, ...), custom_call_target="tpu_custom_call" | custom-call | tf_op jit(solution)/shard_map/regroup/pallas_call | solution.py:139
  53.6 0.7 copy-done.9
  54.4 0.0 collective-permute-start.3
  54.4 0.0 collective-permute-start.4
  54.4 0.0 copy-done.2
  54.4 0.0 copy-done.11
  54.4 1.8 %collective-permute-start.5 = (bf16[4,16,2560]{2,1,0:T(8,128)(2,1)}, bf16[4,16,2560]{2,1,0:T(8,128)(2,1)}, u32[]{:S(2)}, u32[]{:S(2)}) collective-permute-start(bf16[4,16,2560]{2,1,0:T(8,128)(2,1)} %get-tuple-element.29), channel_id=1, source_target_pairs={{0,3},{1,0},{2,1},{3,2},{4,7},{5,4},{6,5},{7,6},{8,11},{9,8},{10,9... | collective-permute-start | bytes 983048 | tf_op jit(solution)/shard_map/ppermute | solution.py:494
  56.2 0.0 copy-done.13
  56.2 0.0 copy-start
  56.2 0.9 copy.27
  57.1 0.9 copy.28
  58.0 0.0 copy-done.16
  58.1 0.1 reshape.183.refs_8_.cover_ref
  58.1 14.2 %collective-permute-done.3 = bf16[4,16,2560]{2,1,0:T(8,128)(2,1)} collective-permute-done((bf16[4,16,2560]{2,1,0:T(8,128)(2,1)}, bf16[4,16,2560]{2,1,0:T(8,128)(2,1)}, u32[]{:S(2)}, u32[]{:S(2)}) %collective-permute-start.3) | collective-permute-done | bytes 327712 | tf_op jit(solution)/shard_map/ppermute | solution.py:494
  72.3 0.6 collective-permute-done.4
  72.9 7.9 %collective-permute-done.5 = bf16[4,16,2560]{2,1,0:T(8,128)(2,1)} collective-permute-done((bf16[4,16,2560]{2,1,0:T(8,128)(2,1)}, bf16[4,16,2560]{2,1,0:T(8,128)(2,1)}, u32[]{:S(2)}, u32[]{:S(2)}) %collective-permute-start.5) | collective-permute-done | bytes 327712 | tf_op jit(solution)/shard_map/ppermute | solution.py:494
  80.8 0.0 copy-done.6
  80.8 0.9 copy-done.3
  81.7 1.0 copy-done.10
  82.7 0.9 copy-done.12
  83.6 2.6 %edge_rows.1 = (f32[2,16,128]{2,1,0:T(8,128)S(1)}, f32[2,4,128]{2,1,0:T(4,128)S(1)}) custom-call(s32[1]{0:T(128)} %bitcast.here_ref.block_ref, f32[2,3]{1,0:T(2,128)S(1)} %copy-done.6, bf16[64,2560]{1,0:T(8,128)(2,1)S(1)} %bitcast.39, bf16[64,2560]{1,0:T(8,128)(2,1)} %bitcast.11.refs_1_, bf16[64,2560]{1,0:T(8,128)(2,1)} %bitcast.12.refs_2_, ...), custom_call_target="tpu_custom_call" | custom-call | flops 49999998976 | tf_op jit(solution)/shard_map/edge_rows/pallas_call | solution.py:328
  86.3 0.0 copy-done
  86.3 4.5 %all-gather.1 = f32[4,16,128]{2,1,0:T(8,128)} all-gather(f32[2,16,128]{2,1,0:T(8,128)S(1)} %get-tuple-element.34), channel_id=3, replica_groups=mesh['track'=2,'pix'=16] {'track'}, dimensions={0}, use_global_device_ids=true | all-gather | bytes 49152 | tf_op jit(solution)/shard_map/all_gather | solution.py:511
  90.8 1.4 %solve_edges.1 = (f32[2,16,128]{2,1,0:T(8,128)}, f32[2,8,128]{2,1,0:T(8,128)}, f32[2,8,128]{2,1,0:T(8,128)}) custom-call(f32[2,2,16,128]{3,2,1,0:T(8,128)} %bitcast.47, f32[64,128]{1,0:T(8,128)} %copy-done, f32[2,3]{1,0:T(2,128)} %los_ref.7), custom_call_target="tpu_custom_call" | custom-call | tf_op jit(solution)/shard_map/solve_edges/pallas_call | solution.py:409
  92.2 1.9 %collective-permute-start.6 = (f32[2,8,128]{2,1,0:T(8,128)}, f32[2,8,128]{2,1,0:T(8,128)S(1)}, u32[]{:S(2)}, u32[]{:S(2)}) collective-permute-start(f32[2,8,128]{2,1,0:T(8,128)} %get-tuple-element.36), channel_id=1, source_target_pairs={{0,1},{1,2},{2,3},{3,4},{4,5},{5,6},{6,7},{7,8},{8,9},{9,10},{10,1... | collective-permute-start | bytes 24584 | tf_op jit(solution)/shard_map/ppermute | solution.py:515
  94.2 4.5 %collective-permute-start.7 = (f32[2,8,128]{2,1,0:T(8,128)}, f32[2,8,128]{2,1,0:T(8,128)S(1)}, u32[]{:S(2)}, u32[]{:S(2)}) collective-permute-start(f32[2,8,128]{2,1,0:T(8,128)} %get-tuple-element.37), channel_id=1, source_target_pairs={{1,0},{2,1},{3,2},{4,3},{5,4},{6,5},{7,6},{8,7},{9,8},{10,9},{11,1... | collective-permute-start | bytes 24584 | tf_op jit(solution)/shard_map/ppermute | solution.py:516
  98.7 3.2 %all-to-all-done = bf16[16,16,5888]{2,1,0:T(8,128)(2,1)S(1)} async-done(((bf16[16,16,5888]{2,1,0:T(8,128)(2,1)}), bf16[16,16,5888]{2,1,0:T(8,128)(2,1)S(1)}, u32[]{:S(2)}, u32[]{:S(2)}) %all-to-all-start) | async-done | bytes 3014688 | tf_op jit(solution)/shard_map/all_to_all | solution.py:496
  101.9 0.8 copy-done.1
  102.7 0.9 copy-done.5
  103.6 4.9 %inner_rows.1 = f32[2,48,128]{2,1,0:T(8,128)S(1)} custom-call(s32[1]{0:T(128)} %bitcast.here_ref.block_ref, f32[2,3]{1,0:T(2,128)S(1)} %copy-done.7, bf16[256,5888]{1,0:T(8,128)(2,1)S(1)} %bitcast.33, f32[2,4,128]{2,1,0:T(4,128)S(1)} %get-tuple-element.31.seam_ref, bf16[208,256]{1,0:T(8,128)(2,1)S(1)} %copy-done.5, ...), custom_call_target="tpu_custom_call" | custom-call | tf_op jit(solution)/shard_map/inner_rows/pallas_call | solution.py:368
  108.5 4.9 %all-gather = f32[4,48,128]{2,1,0:T(8,128)} all-gather(f32[2,48,128]{2,1,0:T(8,128)S(1)} %inner_rows.1), channel_id=2, replica_groups=mesh['track'=2,'pix'=16] {'track'}, dimensions={0}, use_global_device_ids=true | all-gather | bytes 147456 | tf_op jit(solution)/shard_map/all_gather | solution.py:518
  113.3 0.0 collective-permute-done.6.before_ref
  113.3 0.0 collective-permute-done.7.after_ref
  113.4 0.6 copy-done.14
  113.9 0.0 copy-done.15
  113.9 1.8 %solve_and_strain.1 = (f32[2,8,512]{2,1,0:T(8,128)}, f32[3,8,512]{2,1,0:T(8,128)}) custom-call(s32[1]{0:T(128)} %bitcast.here_ref.block_ref, f32[2,3]{1,0:T(2,128)} %los_ref.7, f32[2,2,48,128]{3,2,1,0:T(8,128)} %bitcast.42, f32[2,16,128]{2,1,0:T(8,128)} %get-tuple-element.35.solved_ref, f32[64,128]{1,0:T(8,128)} %copy-done, f32[2,8,128]{2,1,0:T(8,128)} %copy-done.14, ...), custom_call_target="tpu_custom_call" | custom-call | tf_op jit(solution)/shard_map/solve_and_strain/pallas_call | solution.py:459
  (22 shorter events, 0.1 us)
Async XLA Ops:
  5.4 26.9 %collective-permute-start = (bf16[4,16,2560]{2,1,0:T(8,128)(2,1)}, bf16[4,16,2560]{2,1,0:T(8,128)(2,1)}, u32[]{:S(2)}, u32[]{:S(2)}) collective-permute-start(bf16[4,16,2560]{2,1,0:T(8,128)(2,1)} %get-tuple-element.23), channel_id=1, source_target_pairs={{0,4},{1,5},{2,6},{3,7},{4,8},{5,9},{6,10},{7,11},{8,12},{9,13},{1... | collective-permute-start | bytes 983048 | tf_op jit(solution)/shard_map/ppermute | solution.py:489
  7.0 25.3 %collective-permute-start.1 = (bf16[4,16,2560]{2,1,0:T(8,128)(2,1)}, bf16[4,16,2560]{2,1,0:T(8,128)(2,1)}, u32[]{:S(2)}, u32[]{:S(2)}) collective-permute-start(bf16[4,16,2560]{2,1,0:T(8,128)(2,1)} %get-tuple-element.24), channel_id=1, source_target_pairs={{0,8},{1,9},{2,10},{3,11},{4,12},{5,13},{6,14},{7,15},{8,0},{9,1},... | collective-permute-start | bytes 983048 | tf_op jit(solution)/shard_map/ppermute | solution.py:489
  7.3 44.1 %collective-permute-start.2 = (bf16[4,16,2560]{2,1,0:T(8,128)(2,1)}, bf16[4,16,2560]{2,1,0:T(8,128)(2,1)}, u32[]{:S(2)}, u32[]{:S(2)}) collective-permute-start(bf16[4,16,2560]{2,1,0:T(8,128)(2,1)} %get-tuple-element.25), channel_id=1, source_target_pairs={{0,12},{1,13},{2,14},{3,15},{4,0},{5,1},{6,2},{7,3},{8,4},{9,5},{1... | collective-permute-start | bytes 983048 | tf_op jit(solution)/shard_map/ppermute | solution.py:489
  14.9 6.9 %copy-start.8 = (s32[1,256,2]{1,2,0:T(2,128)S(1)}, s32[1,256,2]{1,2,0:T(2,128)}, u32[]{:S(2)}) copy-start(s32[1,256,2]{1,2,0:T(2,128)} %param.10) | copy-start | bytes 6148
  15.0 41.2 %copy-start.13 = (f32[8,1024]{1,0:T(8,128)S(1)}, f32[8,1024]{1,0:T(8,128)}, u32[]{:S(2)}) copy-start(f32[8,1024]{1,0:T(8,128)} %param.15) | copy-start | bytes 98308
  15.0 43.1 %copy-start.16 = (s32[1,8,8]{2,1,0:T(8,128)S(1)}, s32[1,8,8]{2,1,0:T(8,128)}, u32[]{:S(2)}) copy-start(s32[1,8,8]{2,1,0:T(8,128)} %param.13) | copy-start | bytes 772
  15.0 65.8 %copy-start.6 = (f32[2,3]{1,0:T(2,128)S(1)}, f32[2,3]{1,0:T(2,128)}, u32[]{:S(2)}) copy-start(f32[2,3]{1,0:T(2,128)} %los_ref.7) | copy-start | bytes 76
  15.0 86.9 %all-to-all-start = ((bf16[16,16,5888]{2,1,0:T(8,128)(2,1)}), bf16[16,16,5888]{2,1,0:T(8,128)(2,1)S(1)}, u32[]{:S(2)}, u32[]{:S(2)}) async-start(bf16[16,16,5888]{2,1,0:T(8,128)(2,1)} %pack_inner.1), calls=%async_computation | async-start | bytes 6029312 | tf_op jit(solution)/shard_map/all_to_all | solution.py:496
  31.6 0.6 copy-start.4
  32.3 22.1 %copy-start.2 = (bf16[208,256]{1,0:T(8,128)(2,1)}, bf16[208,256]{1,0:T(8,128)(2,1)S(1)}, u32[]{:S(2)}) copy-start(bf16[208,256]{1,0:T(8,128)(2,1)S(1)} %get-tuple-element.22.after_ref.refs_4_) | copy-start | bytes 319492
  32.3 22.1 %copy-start.11 = (bf16[256,208]{1,0:T(8,128)(2,1)}, bf16[256,208]{1,0:T(8,128)(2,1)S(1)}, u32[]{:S(2)}) copy-start(bf16[256,208]{1,0:T(8,128)(2,1)S(1)} %get-tuple-element.30.refs_5_) | copy-start | bytes 319492
  53.6 0.8 copy-start.9
  54.4 17.9 %collective-permute-start.3 = (bf16[4,16,2560]{2,1,0:T(8,128)(2,1)}, bf16[4,16,2560]{2,1,0:T(8,128)(2,1)}, u32[]{:S(2)}, u32[]{:S(2)}) collective-permute-start(bf16[4,16,2560]{2,1,0:T(8,128)(2,1)} %get-tuple-element.27), channel_id=1, source_target_pairs={{0,1},{1,2},{2,3},{3,0},{4,5},{5,6},{6,7},{7,4},{8,9},{9,10},{10,1... | collective-permute-start | bytes 983048 | tf_op jit(solution)/shard_map/ppermute | solution.py:494
  54.4 18.5 %collective-permute-start.4 = (bf16[4,16,2560]{2,1,0:T(8,128)(2,1)}, bf16[4,16,2560]{2,1,0:T(8,128)(2,1)}, u32[]{:S(2)}, u32[]{:S(2)}) collective-permute-start(bf16[4,16,2560]{2,1,0:T(8,128)(2,1)} %get-tuple-element.28), channel_id=1, source_target_pairs={{0,2},{1,3},{2,0},{3,1},{4,6},{5,7},{6,4},{7,5},{8,10},{9,11},{10,... | collective-permute-start | bytes 983048 | tf_op jit(solution)/shard_map/ppermute | solution.py:494
  54.4 26.4 %collective-permute-start.5 = (bf16[4,16,2560]{2,1,0:T(8,128)(2,1)}, bf16[4,16,2560]{2,1,0:T(8,128)(2,1)}, u32[]{:S(2)}, u32[]{:S(2)}) collective-permute-start(bf16[4,16,2560]{2,1,0:T(8,128)(2,1)} %get-tuple-element.29), channel_id=1, source_target_pairs={{0,3},{1,0},{2,1},{3,2},{4,7},{5,4},{6,5},{7,6},{8,11},{9,8},{10,9... | collective-permute-start | bytes 983048 | tf_op jit(solution)/shard_map/ppermute | solution.py:494
  56.2 30.1 %copy-start = (f32[64,128]{1,0:T(8,128)}, f32[64,128]{1,0:T(8,128)S(1)}, u32[]{:S(2)}) copy-start(f32[64,128]{1,0:T(8,128)S(1)} %reshape.172.refs_9_.north_ref) | copy-start | bytes 98308
  80.8 0.9 copy-start.3
  81.7 1.0 copy-start.10
  82.7 0.9 copy-start.12
  83.6 18.3 %copy-start.7 = (f32[2,3]{1,0:T(2,128)S(1)}, f32[2,3]{1,0:T(2,128)}, u32[]{:S(2)}) copy-start(f32[2,3]{1,0:T(2,128)} %los_ref.7) | copy-start | bytes 76
  92.2 21.1 %collective-permute-start.6 = (f32[2,8,128]{2,1,0:T(8,128)}, f32[2,8,128]{2,1,0:T(8,128)S(1)}, u32[]{:S(2)}, u32[]{:S(2)}) collective-permute-start(f32[2,8,128]{2,1,0:T(8,128)} %get-tuple-element.36), channel_id=1, source_target_pairs={{0,1},{1,2},{2,3},{3,4},{4,5},{5,6},{6,7},{7,8},{8,9},{9,10},{10,1... | collective-permute-start | bytes 24584 | tf_op jit(solution)/shard_map/ppermute | solution.py:515
  94.2 19.2 %collective-permute-start.7 = (f32[2,8,128]{2,1,0:T(8,128)}, f32[2,8,128]{2,1,0:T(8,128)S(1)}, u32[]{:S(2)}, u32[]{:S(2)}) collective-permute-start(f32[2,8,128]{2,1,0:T(8,128)} %get-tuple-element.37), channel_id=1, source_target_pairs={{1,0},{2,1},{3,2},{4,3},{5,4},{6,5},{7,6},{8,7},{9,8},{10,9},{11,1... | collective-permute-start | bytes 24584 | tf_op jit(solution)/shard_map/ppermute | solution.py:516
  101.9 0.8 copy-start.1
  102.7 0.9 copy-start.5
  113.3 0.6 copy-start.14
  113.3 0.6 copy-start.15

commit v5 on v4

--- a/solution.py
+++ b/solution.py
@@ -8,7 +8,7 @@
 from jax.sharding import PartitionSpec as P
 
 EPOCHS = 200
-ROWS = 208
+EXTRA = 16
 HALO = 128
 CTILE = 128
 MBLK = 128
@@ -38,7 +38,7 @@
     return pltpu.roll(flags, (LANES - (first - lead)) % LANES, 1)
 
 
-def pack_edges_kernel(tiles, group, place_ref, flags_hbm, phases_ref, *refs):
+def pack_edges_kernel(tiles, group, flags_hbm, phases_ref, *refs):
     *out_refs, flags_ref, near_ref, flag_sem, in_sem = refs
     planes = len(out_refs)
     parts = planes * group
@@ -71,24 +71,17 @@
     near_ref[0, :, : reach * MBLK] = empty
     near_ref[parts, :, reach * MBLK :] = empty
     flag_copy.wait()
-    ends[0].wait()
-
-    @pl.loop(1, parts)
-    def _(b):
-        between(b).wait()
-
-    ends[1].wait()
+    plane = lax.axis_index("pix") // group
+    shape = (ifgs, MBLK)
     for s in range(planes):
-        first_part = lax.rem(place_ref[0] + s, planes) * group
+        first_part = lax.rem(plane + s, planes) * group
 
         @pl.loop(0, group, unroll=2)
         def _(g):
-            p = first_part + g
-            first = p * span
+            first = (first_part + g) * span
             flags = part_flags(flags_ref, first)
             earlier = part_flags(flags_ref, jnp.maximum(first - 1, 0))
             later = part_flags(flags_ref, jnp.minimum(first + span, blocks - 1))
-            shape = (ifgs, MBLK)
             for half in range(2):
                 for k in range(tiles + 2):
                     block = k - 1 if half == 0 else span - reach + k
@@ -98,19 +91,36 @@
                         keep = spread(later, 0, shape)
                     else:
                         keep = spread(flags, block, shape)
-                    at = (reach - 1 + k if half == 0 else k) * MBLK
                     to = (half * (tiles + 2) + k) * MBLK
-                    out_refs[s][g, :, to : to + MBLK] = near_ref[p + half, :, at : at + MBLK] * keep
-
-
-def pack_edges(place, phases, flags, parts, group, tiles):
+                    out_refs[s][g, :, to : to + MBLK] = keep
+
+    ends[0].wait()
+
+    @pl.loop(1, parts)
+    def _(b):
+        between(b).wait()
+
+    ends[1].wait()
+    wide = (tiles + 2) * MBLK
+    for s in range(planes):
+        first_part = lax.rem(plane + s, planes) * group
+
+        @pl.loop(0, group, unroll=2)
+        def _(g):
+            for half in range(2):
+                at = (reach - 1 if half == 0 else 0) * MBLK
+                to = half * wide
+                out_refs[s][g, :, to : to + wide] *= near_ref[first_part + g + half, :, at : at + wide]
+
+
+def pack_edges(phases, flags, parts, group, tiles):
     ifgs = phases.shape[0]
     planes = parts // group
     hbm = pl.BlockSpec(memory_space=pltpu.HBM)
     width = 2 * (tiles + 2) * MBLK
     return pl.pallas_call(
         functools.partial(pack_edges_kernel, tiles, group),
-        in_specs=[pl.BlockSpec(memory_space=pltpu.SMEM), hbm, hbm],
+        in_specs=[hbm, hbm],
         out_specs=[pl.BlockSpec(memory_space=pltpu.VMEM)] * planes,
         out_shape=[jax.ShapeDtypeStruct((group, ifgs, width), jnp.bfloat16)] * planes,
         scratch_shapes=[
@@ -121,29 +131,29 @@
         ],
         compiler_params=pltpu.CompilerParams(vmem_limit_bytes=medium),
         name="pack_edges",
-    )(place, stay(flags), stay(phases))
-
-
-def regroup_kernel(planes, group, place_ref, after_ref, *refs):
+    )(stay(flags), stay(phases))
+
+
+def regroup_kernel(planes, group, after_ref, *refs):
     in_refs, out_refs = refs[:planes], refs[planes:]
     for j in range(group):
-        column = lax.rem(place_ref[1] + j, group)
+        column = lax.rem(lax.axis_index("pix") + j, group)
         for s in range(planes):
             out_refs[j][s] = in_refs[s][column]
 
 
-def regroup(place, after, pieces, group):
+def regroup(after, pieces, group):
     planes = len(pieces)
     vmem = pl.BlockSpec(memory_space=pltpu.VMEM)
     shape = (planes, *pieces[0].shape[1:])
     return pl.pallas_call(
         functools.partial(regroup_kernel, planes, group),
-        in_specs=[pl.BlockSpec(memory_space=pltpu.SMEM)] + [vmem] * (planes + 1),
+        in_specs=[vmem] * (planes + 1),
         out_specs=[vmem] * group,
         out_shape=[jax.ShapeDtypeStruct(shape, jnp.bfloat16)] * group,
         compiler_params=pltpu.CompilerParams(vmem_limit_bytes=medium),
         name="regroup",
-    )(place, after, *pieces)
+    )(after, *pieces)
 
 
 def pack_inner_kernel(reach, flags_hbm, phases_ref, out_ref, flags_ref, held_ref, flag_sem, in_sem):
@@ -164,11 +174,14 @@
 
     @pl.loop(0, parts)
     def _(p):
-        inward(p).wait()
         flags = part_flags(flags_ref, p * span)
         for k in range(width // MBLK):
-            at = slice(k * MBLK, (k + 1) * MBLK)
-            out_ref[p, :, at] = held_ref[p, :, at] * spread(flags, reach + k, (ifgs, MBLK))
+            out_ref[p, :, k * MBLK : (k + 1) * MBLK] = spread(flags, reach + k, (ifgs, MBLK))
+
+    @pl.loop(0, parts)
+    def _(p):
+        inward(p).wait()
+        out_ref[p] *= held_ref[p]
 
 
 def pack_inner(phases, flags, parts, tiles):
@@ -196,7 +209,7 @@
     return jnp.dot(a, b, precision=lax.Precision.HIGHEST, preferred_element_type=jnp.float32)
 
 
-def pseudo_kernel(pairs_ref, other_ref, design_ref, out_ref, other_design_ref, other_out_ref, normal_ref, inverse_ref):
+def operator_kernel(pairs_ref, other_ref, out_ref, other_out_ref, normal_ref, inverse_ref):
     ifgs = pairs_ref.shape[1]
     size = normal_ref.shape[0]
     epoch = lax.broadcasted_iota(jnp.int32, (size, ifgs), 0)
@@ -227,48 +240,49 @@
         return step + 1, jnp.max(jnp.abs(rest))
 
     lax.while_loop(unfinished, improve, (jnp.int32(0), jnp.float32(1.0)))
-    place = lax.broadcasted_iota(jnp.int32, (ROWS, ifgs), 0)
+    place = lax.broadcasted_iota(jnp.int32, (size, ifgs), 0)
     centred = place.astype(jnp.float32) - (EPOCHS - 1) / 2.0
     square = sum((e - (EPOCHS - 1) / 2.0) ** 2 for e in range(EPOCHS))
     slope = jnp.where(place < EPOCHS, centred * (EPOCHS - 1) / square, 0.0)
-    extra = place - EPOCHS
-    for ref, to_design_ref, to_ref in ((pairs_ref, design_ref, out_ref), (other_ref, other_design_ref, other_out_ref)):
+    same = lax.broadcasted_iota(jnp.int32, (ifgs, ifgs), 0) == lax.broadcasted_iota(jnp.int32, (ifgs, ifgs), 1)
+    extra = lax.broadcasted_iota(jnp.int32, (EXTRA, ifgs), 0)
+    for ref, to_ref in ((pairs_ref, out_ref), (other_ref, other_out_ref)):
         across = ends(ref)
-        to_design_ref[...] = across.T[:, :ROWS].astype(jnp.bfloat16)
-        pseudo = exact_dot(inverse_ref[...], across)[:ROWS].astype(jnp.bfloat16).astype(jnp.float32)
-        row = jnp.sum(pseudo * slope, axis=0, keepdims=True)
+        pseudo = exact_dot(inverse_ref[...], across).astype(jnp.bfloat16)
+        fitted = jnp.dot(across.T.astype(jnp.bfloat16), pseudo, preferred_element_type=jnp.float32)
+        to_ref[:ifgs, :] = (same.astype(jnp.float32) - fitted).astype(jnp.bfloat16)
+        row = jnp.sum(pseudo.astype(jnp.float32) * slope, axis=0, keepdims=True)
         high = row.astype(jnp.bfloat16).astype(jnp.float32)
         rest = row - high
         middle = rest.astype(jnp.bfloat16).astype(jnp.float32)
         low = rest - middle
         terms = jnp.where(extra == 0, high, jnp.where(extra == 1, middle, jnp.where(extra == 2, low, 0.0)))
-        to_ref[...] = jnp.where(extra < 0, pseudo, terms).astype(jnp.bfloat16)
+        to_ref[ifgs:, :] = terms.astype(jnp.bfloat16)
 
 
 def setup_track(pair_rows, other_rows):
     ifgs = pair_rows.shape[0]
-    size = 256
+    size = -(-EPOCHS // LANES) * LANES
     vmem = pl.BlockSpec(memory_space=pltpu.VMEM)
     return pl.pallas_call(
-        pseudo_kernel,
+        operator_kernel,
         in_specs=[vmem] * 2,
-        out_specs=[vmem] * 4,
-        out_shape=[jax.ShapeDtypeStruct((ifgs, ROWS), jnp.bfloat16), jax.ShapeDtypeStruct((ROWS, ifgs), jnp.bfloat16)] * 2,
+        out_specs=[vmem] * 2,
+        out_shape=[jax.ShapeDtypeStruct((ifgs + EXTRA, ifgs), jnp.bfloat16)] * 2,
         scratch_shapes=[pltpu.VMEM((size, size), jnp.float32), pltpu.VMEM((size, size), jnp.float32)],
         compiler_params=pltpu.CompilerParams(vmem_limit_bytes=medium),
-        name="pseudo_inverse",
+        name="misfit_operator",
     )(pair_rows.T, other_rows.T)
 
 
-def invert_tiles(stack_refs, first, width, pseudo_ref, design_ref, fields_ref, base):
+def invert_tiles(stack_refs, first, width, operator_ref, fields_ref, base):
+    ifgs = operator_ref.shape[1]
     for start in range(0, width, TILE):
         here = pl.ds(pl.multiple_of(first + start, LANES), TILE)
         stack = jnp.concatenate([ref[:, here] for ref in stack_refs], axis=0)
-        series = jnp.dot(pseudo_ref[...], stack, preferred_element_type=jnp.float32)
-        velocity = jnp.sum(series[EPOCHS:], axis=0, keepdims=True)
-        fitted = jnp.dot(design_ref[...], series.astype(jnp.bfloat16), preferred_element_type=jnp.float32)
-        misfit = stack.astype(jnp.float32) - fitted
-        variance = jnp.sum(misfit * misfit, axis=0, keepdims=True) / stack.shape[0]
+        product = jnp.dot(operator_ref[...], stack, preferred_element_type=jnp.float32)
+        velocity = jnp.sum(product[ifgs : ifgs + 8], axis=0, keepdims=True)
+        variance = jnp.sum(product[:ifgs] * product[:ifgs], axis=0, keepdims=True) / ifgs
         for k in range(TILE // LANES):
             row = pl.ds(base + start // LANES + k, 1)
             fields_ref[0, row, :] = velocity[:, k * LANES : (k + 1) * LANES]
@@ -301,19 +315,19 @@
 
 
 def edges_kernel(
-    tiles, group, here_ref, los_ref, *refs
+    tiles, group, los_ref, *refs
 ):
     stack_refs = refs[:group]
-    pseudo_ref, design_ref, index_ref, weight_ref, cover_ref, north_ref, out_ref, seam_ref, fields_ref = refs[group:]
+    operator_ref, index_ref, weight_ref, cover_ref, north_ref, out_ref, seam_ref, fields_ref = refs[group:]
     rows = index_ref.shape[1]
     width = stack_refs[0].shape[1] // 2
 
     @pl.loop(0, 2)
     def _(half):
-        invert_tiles(stack_refs, half * width, width, pseudo_ref, design_ref, fields_ref, half * (tiles + 2))
+        invert_tiles(stack_refs, half * width, width, operator_ref, fields_ref, half * (tiles + 2))
 
     seam_ref[...] = fields_ref[:, tiles : tiles + 4, :]
-    north_c = los_ref[here_ref[0], 1]
+    north_c = los_ref[lax.axis_index("track"), 1]
     for half in range(2):
         for r in range(0, tiles, 8):
             resample(
@@ -322,12 +336,12 @@
             )
 
 
-def edges(here, los, stacks, pseudo, design, cells, tiles):
+def edges(los, stacks, operator, cells, tiles):
     rows = 2 * (tiles + 2)
     vmem = pl.BlockSpec(memory_space=pltpu.VMEM)
     return pl.pallas_call(
         functools.partial(edges_kernel, tiles, len(stacks)),
-        in_specs=[pl.BlockSpec(memory_space=pltpu.SMEM)] * 2 + [vmem] * (len(stacks) + 6),
+        in_specs=[pl.BlockSpec(memory_space=pltpu.SMEM)] + [vmem] * (len(stacks) + 5),
         out_specs=[vmem] * 2,
         out_shape=[
             jax.ShapeDtypeStruct((2, 2 * tiles, LANES), jnp.float32),
@@ -337,11 +351,11 @@
         compiler_params=pltpu.CompilerParams(vmem_limit_bytes=medium),
         cost_estimate=pl.CostEstimate(flops=EDGE_COST, bytes_accessed=0, transcendentals=0),
         name="edge_rows",
-    )(here, los, *stacks, pseudo, design, *cells)
+    )(los, *stacks, operator, *cells)
 
 
 def inner_kernel(
-    tiles, here_ref, los_ref, stack_ref, seam_ref, pseudo_ref, design_ref, index_ref, weight_ref, cover_ref, north_ref, out_ref,
+    tiles, los_ref, stack_ref, seam_ref, operator_ref, index_ref, weight_ref, cover_ref, north_ref, out_ref,
     fields_ref,
 ):
     width = stack_ref.shape[1]
@@ -352,9 +366,9 @@
     @pl.loop(0, -(-width // PIECE))
     def _(k):
         first = jnp.minimum(k * PIECE, width - PIECE)
-        invert_tiles([stack_ref], first, PIECE, pseudo_ref, design_ref, fields_ref, 2 + first // LANES)
-
-    north_c = los_ref[here_ref[0], 1]
+        invert_tiles([stack_ref], first, PIECE, operator_ref, fields_ref, 2 + first // LANES)
+
+    north_c = los_ref[lax.axis_index("track"), 1]
 
     @pl.loop(0, out_ref.shape[1], step=8)
     def _(r):
@@ -362,18 +376,18 @@
         resample(fields_ref, r, tiles + r, r, index_ref, weight_ref, cover_ref, north_ref, north_c, out_ref)
 
 
-def inner(here, los, stack, seam, pseudo, design, cells, tiles):
+def inner(los, stack, seam, operator, cells, tiles):
     rows = cells[0].shape[1] - 2 * tiles
     vmem = pl.BlockSpec(memory_space=pltpu.VMEM)
     return pl.pallas_call(
         functools.partial(inner_kernel, tiles),
-        in_specs=[pl.BlockSpec(memory_space=pltpu.SMEM)] * 2 + [vmem] * 8,
+        in_specs=[pl.BlockSpec(memory_space=pltpu.SMEM)] + [vmem] * 7,
         out_specs=vmem,
         out_shape=jax.ShapeDtypeStruct((2, rows, LANES), jnp.float32),
         scratch_shapes=[pltpu.VMEM((2, -(-(rows + 2) // 8) * 8, LANES), jnp.float32)],
         compiler_params=pltpu.CompilerParams(vmem_limit_bytes=medium),
         name="inner_rows",
-    )(here, los, stack, seam, pseudo, design, *cells)
+    )(los, stack, seam, operator, *cells)
 
 
 def solve_cells(vals_ref, los_ref):
@@ -411,12 +425,13 @@
         in_specs=[vmem, vmem, pl.BlockSpec(memory_space=pltpu.SMEM)],
         out_specs=[vmem] * 3,
         out_shape=[jax.ShapeDtypeStruct((2, 2 * tiles, LANES), jnp.float32), edge, edge],
+        compiler_params=pltpu.CompilerParams(vmem_limit_bytes=medium),
         name="solve_edges",
     )(vals, north, los)
 
 
 def final_kernel(
-    tiles, own, block_ref, los_ref, vals_ref, solved_ref, north_ref, before_ref, after_ref, east_up_ref, strain_ref, work_ref
+    tiles, own, los_ref, vals_ref, solved_ref, north_ref, before_ref, after_ref, east_up_ref, strain_ref, work_ref
 ):
     rows = north_ref.shape[0]
     lane = lax.broadcasted_iota(jnp.int32, (rows, LANES), 1)
@@ -444,7 +459,7 @@
     work_ref[2] = across(east) / 2.0
     work_ref[3] = down(north, 1) / 2.0
     work_ref[4] = (down(east, 0) + across(north)) / 4.0
-    start = block_ref[0] * own
+    start = lax.axis_index("track") * own
     for field in range(5):
         target, at = (east_up_ref, field) if field < 2 else (strain_ref, field - 2)
         for i in range(rows // tiles):
@@ -452,42 +467,40 @@
                 target[at, i : i + 1, j * LANES : (j + 1) * LANES] = work_ref[field, pl.ds(i * tiles + start + j, 1), :]
 
 
-def final(block, los, vals, solved, north, before, after, tiles, own):
+def final(los, vals, solved, north, before, after, tiles, own):
     rows = north.shape[0]
     shape = (rows // tiles, own * LANES)
     vmem = pl.BlockSpec(memory_space=pltpu.VMEM)
     return pl.pallas_call(
         functools.partial(final_kernel, tiles, own),
-        in_specs=[pl.BlockSpec(memory_space=pltpu.SMEM)] * 2 + [vmem] * 5,
+        in_specs=[pl.BlockSpec(memory_space=pltpu.SMEM)] + [vmem] * 5,
         out_specs=[vmem] * 2,
         out_shape=[jax.ShapeDtypeStruct((2, *shape), jnp.float32), jax.ShapeDtypeStruct((3, *shape), jnp.float32)],
         scratch_shapes=[pltpu.VMEM((5, rows, LANES), jnp.float32)],
+        compiler_params=pltpu.CompilerParams(vmem_limit_bytes=medium),
         name="solve_and_strain",
-    )(block, los, vals, solved, north, before, after)
+    )(los, vals, solved, north, before, after)
 
 
 def per_device(phases, coherent, pairs, res_index, res_weight, coverage, los, north):
     parts = lax.axis_size("pix")
     tracks = lax.axis_size("track")
-    here = lax.axis_index("track")
     grid_rows, columns = north.shape
     tiles = columns // CTILE
     rows = grid_rows * tiles
-    track = here.astype(jnp.int32)[None]
     group = GROUP if parts % GROUP == 0 else parts
     planes = parts // group
     plane, column = jnp.divmod(lax.axis_index("pix").astype(jnp.int32), group)
-    place = jnp.stack([plane, column])
-    packed = pack_edges(place, phases[0], coherent[0], parts, group, tiles)
+    packed = pack_edges(phases[0], coherent[0], parts, group, tiles)
     steps_j, steps_s = jnp.meshgrid(jnp.arange(group), jnp.arange(planes), indexing="ij")
     sources = ((plane - steps_s) % planes * group + (column - steps_j) % group).reshape(-1)
     edge_pairs = jnp.take(pairs[0].reshape(parts, -1, 2), sources, axis=0).reshape(-1, 2)
-    design, pseudo, edge_design, edge_pseudo = setup_track(pairs[0], edge_pairs)
+    operator, edge_operator = setup_track(pairs[0], edge_pairs)
     arrived = [packed[0]]
     for s in range(1, planes):
         far = [(z * group + c, (z + s) % planes * group + c) for z in range(planes) for c in range(group)]
         arrived.append(lax.ppermute(packed[s], "pix", far))
-    by_column = regroup(place, edge_pseudo, arrived, group)
+    by_column = regroup(edge_operator, arrived, group)
     pieces = [by_column[0]]
     for j in range(1, group):
         near = [(z * group + c, z * group + (c + j) % group) for z in range(planes) for c in range(group)]
@@ -507,16 +520,16 @@
     def flat(stack):
         return stack.reshape(-1, stack.shape[-1])
 
-    edge_vals, seam = edges(track, los, [flat(piece) for piece in pieces], edge_pseudo, edge_design, cells, tiles)
+    edge_vals, seam = edges(los, [flat(piece) for piece in pieces], edge_operator, cells, tiles)
     edge_vals = lax.all_gather(edge_vals, "track", axis=0)
     solved, first, last = solve_edges(edge_vals, north_cells, los, tiles)
     onward = [(i, i + 1) for i in range(parts - 1)]
     back = [(j, i) for i, j in onward]
     before = lax.ppermute(last, "pix", onward)
     after = lax.ppermute(first, "pix", back)
-    inner_vals = inner(track, los, flat(inner_stack), seam, pseudo, design, cells, tiles)
+    inner_vals = inner(los, flat(inner_stack), seam, operator, cells, tiles)
     inner_vals = lax.all_gather(inner_vals, "track", axis=0)
-    return tuple(final(track, los, inner_vals, solved, north_cells, before, after, tiles, tiles // tracks))
+    return tuple(final(los, inner_vals, solved, north_cells, before, after, tiles, tiles // tracks))
 
 
 def solution(mesh):

time: 116 us -> 111 us (0.957)
  local copies, waits for them, and re-layouts: 9.7 us -> 5.9 us
  Pallas kernels: 32.7 us -> 29.5 us
  waiting for transfers between devices: 45.1 us -> 47.6 us
    unnamed x36 -> x18, local copies, waits for them, and re-layouts: 8.28 us -> 4.47 us
    all_to_all x1, waiting for transfers between devices: 3.22 us -> 5.83 us  [per_device(): lax.all_to_all(pack_inner(phases[0], later_flags, parts, tiles), 'pix', s...]
    pallas_call x1, Pallas kernels: 4.87 us -> 3.29 us  [inner(): pl.pallas_call(functools.partial(inner_kernel, tiles), in_specs=[pl.Block...]
  transfers between devices with their start and end apart: 9 -> 9, of which waited for: 5 -> 5; matrix products, arithmetic and copies ran while one was open for 3% -> 3% of each run, Pallas kernels for 23% -> 22%
where the time goes in v5:
time: 111 us
  waiting for transfers between devices  47.6 us (43%)
  Pallas kernels  29.5 us (27%)
  starting transfers between devices  17.7 us (16%)
  blocking collectives  9.18 us (8%)
  local copies, waits for them, and re-layouts  5.9 us (5%)
    ppermute x3, waiting for transfers between devices, per_device(): pieces.append(lax.ppermute(by_column[j], 'pix', near))  22.8 us
    ppermute x3, waiting for transfers between devices, per_device(): arrived.append(lax.ppermute(packed[s], 'pix', far))  18.9 us
    pallas_call x1, Pallas kernels, setup_track(): pl.pallas_call(operator_kernel, in_specs=[vmem] * 2, out_specs=[vmem] * 2...  9.37 us
    pallas_call x1, Pallas kernels, pack_inner(): pl.pallas_call(functools.partial(pack_inner_kernel, reach), in_specs=[hbm...  6.63 us
    all_to_all x1, starting transfers between devices, per_device(): lax.all_to_all(pack_inner(phases[0], later_flags, parts, tiles), 'pix', s...  6.45 us
    all_to_all x1, waiting for transfers between devices, per_device(): lax.all_to_all(pack_inner(phases[0], later_flags, parts, tiles), 'pix', s...  5.83 us
    all_gather x1, blocking collectives, per_device(): inner_vals = lax.all_gather(inner_vals, 'track', axis=0)  4.77 us
    ppermute x1, starting transfers between devices, per_device(): after = lax.ppermute(first, 'pix', back)  4.54 us
  transfers between devices with their start and end apart: 9, of which 5 were waited for; matrix products, arithmetic and copies ran while one was open for 3% of the time, Pallas kernels for 22%

profile of v5, /device:TPU:16, one launch (start us, length us, event | category | flops | bytes accessed | tf_op | source)
XLA Modules:
  0.0 110.7 jit_solution(14566846843946649925)
XLA Ops:
  0.6 4.0 %pack_edges.1 = (bf16[4,16,2560]{2,1,0:T(8,128)(2,1)S(1)}, bf16[4,16,2560]{2,1,0:T(8,128)(2,1)}, bf16[4,16,2560]{2,1,0:T(8,128)(2,1)}, bf16[4,16,2560]{2,1,0:T(8,128)(2,1)}) custom-call(s32[16,1024]{1,0:T(8,128)} %bitcast.41, bf16[16,131072]{1,0:T(8,128)(2,1)} %bitcast.39), custom_call_target="tpu_custom_call" | custom-call | tf_op jit(solution)/shard_map/pack_edges/pallas_call | solution.py:121
  4.6 1.6 %collective-permute-start = (bf16[4,16,2560]{2,1,0:T(8,128)(2,1)}, bf16[4,16,2560]{2,1,0:T(8,128)(2,1)}, u32[]{:S(2)}, u32[]{:S(2)}) collective-permute-start(bf16[4,16,2560]{2,1,0:T(8,128)(2,1)} %get-tuple-element.21), channel_id=1, source_target_pairs={{0,4},{1,5},{2,6},{3,7},{4,8},{5,9},{6,10},{7,11},{8,12},{9,13},{1... | collective-permute-start | bytes 983048 | tf_op jit(solution)/shard_map/ppermute | solution.py:502
  6.3 0.3 collective-permute-start.1
  6.6 1.2 %collective-permute-start.2 = (bf16[4,16,2560]{2,1,0:T(8,128)(2,1)}, bf16[4,16,2560]{2,1,0:T(8,128)(2,1)}, u32[]{:S(2)}, u32[]{:S(2)}) collective-permute-start(bf16[4,16,2560]{2,1,0:T(8,128)(2,1)} %get-tuple-element.23), channel_id=1, source_target_pairs={{0,12},{1,13},{2,14},{3,15},{4,0},{5,1},{6,2},{7,3},{8,4},{9,5},{1... | collective-permute-start | bytes 983048 | tf_op jit(solution)/shard_map/ppermute | solution.py:502
  7.8 6.6 %pack_inner.1 = bf16[16,16,5888]{2,1,0:T(8,128)(2,1)} custom-call(s32[16,1024]{1,0:T(8,128)} %bitcast.42, bf16[16,131072]{1,0:T(8,128)(2,1)} %bitcast.40), custom_call_target="tpu_custom_call" | custom-call | tf_op jit(solution)/shard_map/pack_inner/pallas_call | solution.py:192
  14.4 0.0 copy-start.3
  14.5 0.0 copy-start.6
  14.5 0.0 copy-start.7
  14.5 0.0 copy-start.2
  14.5 6.4 %all-to-all-start = ((bf16[16,16,5888]{2,1,0:T(8,128)(2,1)}), bf16[16,16,5888]{2,1,0:T(8,128)(2,1)S(1)}, u32[]{:S(2)}, u32[]{:S(2)}) async-start(bf16[16,16,5888]{2,1,0:T(8,128)(2,1)} %pack_inner.1), calls=%async_computation | async-start | bytes 6029312 | tf_op jit(solution)/shard_map/all_to_all | solution.py:509
  20.9 0.1 broadcast_in_dim.30
  21.0 0.1 broadcast_in_dim.36
  21.1 0.1 broadcast_in_dim.35
  21.2 0.1 broadcast_in_dim.31
  21.3 0.1 broadcast_in_dim.29
  21.4 0.0 copy-done.3
  21.4 0.1 reshape_squeeze.3
  21.5 0.6 gather_fusion
  22.1 0.1 gather.7
  22.2 0.1 broadcast_in_dim.32
  22.3 0.1 broadcast_in_dim.33
  22.4 9.4 %misfit_operator.1 = (bf16[272,256]{1,0:T(8,128)(2,1)S(1)}, bf16[272,256]{1,0:T(8,128)(2,1)S(1)}) custom-call(s32[2,256]{1,0:T(2,128)S(1)} %bitcast.37, s32[2,256]{1,0:T(2,128)S(1)} %select_bitcast_fusion.other_ref), custom_call_target="tpu_custom_call" | custom-call | tf_op jit(solution)/shard_map/misfit_operator/pallas_call | solution.py:267
  31.8 0.0 copy-start
  31.8 0.0 collective-permute-done.refs_1_
  31.8 0.0 collective-permute-done.1.refs_2_
  31.8 18.9 %collective-permute-done.2.refs_3_ = bf16[4,16,2560]{2,1,0:T(8,128)(2,1)} collective-permute-done((bf16[4,16,2560]{2,1,0:T(8,128)(2,1)}, bf16[4,16,2560]{2,1,0:T(8,128)(2,1)}, u32[]{:S(2)}, u32[]{:S(2)}) %collective-permute-start.2) | collective-permute-done | bytes 327712 | tf_op jit(solution)/shard_map/ppermute | solution.py:502
  50.7 2.2 %regroup.1 = (bf16[4,16,2560]{2,1,0:T(8,128)(2,1)S(1)}, bf16[4,16,2560]{2,1,0:T(8,128)(2,1)}, bf16[4,16,2560]{2,1,0:T(8,128)(2,1)}, bf16[4,16,2560]{2,1,0:T(8,128)(2,1)}) custom-call(bf16[272,256]{1,0:T(8,128)(2,1)S(1)} %get-tuple-element.20.after_ref.refs_4_, bf16[4,16,2560]{2,1,0:T(8,128)(2,1)S(1)} %get-tuple-element.18.refs_0_, ...), custom_call_target="tpu_custom_call" | custom-call | tf_op jit(solution)/shard_map/regroup/pallas_call | solution.py:149
  52.9 0.0 copy-start.4
  52.9 0.7 copy-done.4
  53.6 0.0 collective-permute-start.5
  53.6 0.5 collective-permute-start.3
  54.1 0.0 copy-done
  54.1 1.1 collective-permute-start.4
  55.2 0.0 copy-done.6
  55.2 0.9 copy.27
  56.1 0.9 copy.28
  57.0 0.0 copy-done.7
  57.1 0.1 reshape.183.refs_7_.cover_ref
  57.1 10.9 %collective-permute-done.5 = bf16[4,16,2560]{2,1,0:T(8,128)(2,1)} collective-permute-done((bf16[4,16,2560]{2,1,0:T(8,128)(2,1)}, bf16[4,16,2560]{2,1,0:T(8,128)(2,1)}, u32[]{:S(2)}, u32[]{:S(2)}) %collective-permute-start.5) | collective-permute-done | bytes 327712 | tf_op jit(solution)/shard_map/ppermute | solution.py:507
  68.0 3.8 %collective-permute-done.3 = bf16[4,16,2560]{2,1,0:T(8,128)(2,1)} collective-permute-done((bf16[4,16,2560]{2,1,0:T(8,128)(2,1)}, bf16[4,16,2560]{2,1,0:T(8,128)(2,1)}, u32[]{:S(2)}, u32[]{:S(2)}) %collective-permute-start.3) | collective-permute-done | bytes 327712 | tf_op jit(solution)/shard_map/ppermute | solution.py:507
  71.8 8.2 %collective-permute-done.4 = bf16[4,16,2560]{2,1,0:T(8,128)(2,1)} collective-permute-done((bf16[4,16,2560]{2,1,0:T(8,128)(2,1)}, bf16[4,16,2560]{2,1,0:T(8,128)(2,1)}, u32[]{:S(2)}, u32[]{:S(2)}) %collective-permute-start.4) | collective-permute-done | bytes 327712 | tf_op jit(solution)/shard_map/ppermute | solution.py:507
  80.0 0.0 copy-done.2
  80.0 0.0 copy-start.1
  80.0 0.9 copy-done.1
  80.9 0.0 copy-start.5
  80.9 1.0 copy-done.5
  81.8 2.1 %edge_rows.1 = (f32[2,16,128]{2,1,0:T(8,128)S(1)}, f32[2,4,128]{2,1,0:T(4,128)S(1)}) custom-call(f32[2,3]{1,0:T(2,128)S(1)} %copy-done.2, bf16[64,2560]{1,0:T(8,128)(2,1)S(1)} %bitcast.38, bf16[64,2560]{1,0:T(8,128)(2,1)} %bitcast.8.refs_1_, bf16[64,2560]{1,0:T(8,128)(2,1)} %bitcast.9.refs_2_, bf16[64,2560]{1,0:T(8,128)(2,1)} %bitcast.10.refs_3_, ...), custom_call_target="tpu_custom_call" | custom-call | flops 49999998976 | tf_op jit(solution)/shard_map/edge_rows/pallas_call | solution.py:342
  83.9 4.4 %all-gather.1 = f32[4,16,128]{2,1,0:T(8,128)S(1)} all-gather(f32[2,16,128]{2,1,0:T(8,128)S(1)} %get-tuple-element.30), channel_id=3, replica_groups=mesh['track'=2,'pix'=16] {'track'}, dimensions={0}, use_global_device_ids=true | all-gather | bytes 49152 | tf_op jit(solution)/shard_map/all_gather | solution.py:524
  88.3 0.6 solve_edges.1
  88.9 1.9 %collective-permute-start.6 = (f32[2,8,128]{2,1,0:T(8,128)S(1)}, f32[2,8,128]{2,1,0:T(8,128)S(1)}, u32[]{:S(2)}, u32[]{:S(2)}) collective-permute-start(f32[2,8,128]{2,1,0:T(8,128)S(1)} %get-tuple-element.32), channel_id=1, source_target_pairs={{0,1},{1,2},{2,3},{3,4},{4,5},{5,6},{6,7},{7,8},{8,9},{9,10},{10,1... | collective-permute-start | bytes 24584 | tf_op jit(solution)/shard_map/ppermute | solution.py:528
  90.8 4.5 %collective-permute-start.7 = (f32[2,8,128]{2,1,0:T(8,128)S(1)}, f32[2,8,128]{2,1,0:T(8,128)S(1)}, u32[]{:S(2)}, u32[]{:S(2)}) collective-permute-start(f32[2,8,128]{2,1,0:T(8,128)S(1)} %get-tuple-element.33), channel_id=1, source_target_pairs={{1,0},{2,1},{3,2},{4,3},{5,4},{6,5},{7,6},{8,7},{9,8},{10,9},{11,1... | collective-permute-start | bytes 24584 | tf_op jit(solution)/shard_map/ppermute | solution.py:529
  95.4 5.8 %all-to-all-done = bf16[16,16,5888]{2,1,0:T(8,128)(2,1)S(1)} async-done(((bf16[16,16,5888]{2,1,0:T(8,128)(2,1)}), bf16[16,16,5888]{2,1,0:T(8,128)(2,1)S(1)}, u32[]{:S(2)}, u32[]{:S(2)}) %all-to-all-start) | async-done | bytes 3014688 | tf_op jit(solution)/shard_map/all_to_all | solution.py:509
  101.2 3.3 %inner_rows.1 = f32[2,48,128]{2,1,0:T(8,128)S(1)} custom-call(f32[2,3]{1,0:T(2,128)S(1)} %copy-done.2, bf16[256,5888]{1,0:T(8,128)(2,1)S(1)} %bitcast.30, f32[2,4,128]{2,1,0:T(4,128)S(1)} %get-tuple-element.28.seam_ref, bf16[272,256]{1,0:T(8,128)(2,1)S(1)} %get-tuple-element.29.operator_ref, s32[4,64,128]{2,1,0:T(8,128)S(1)} %bitcast.34, ...), custom_call_target="tpu_custom_call" | custom-call | tf_op jit(solution)/shard_map/inner_rows/pallas_call | solution.py:382
  104.5 4.8 %all-gather = f32[4,48,128]{2,1,0:T(8,128)S(1)} all-gather(f32[2,48,128]{2,1,0:T(8,128)S(1)} %inner_rows.1), channel_id=2, replica_groups=mesh['track'=2,'pix'=16] {'track'}, dimensions={0}, use_global_device_ids=true | all-gather | bytes 147456 | tf_op jit(solution)/shard_map/all_gather | solution.py:531
  109.3 0.0 collective-permute-done.6.before_ref
  109.3 0.0 collective-permute-done.7.after_ref
  109.3 1.4 %solve_and_strain.1 = (f32[2,8,512]{2,1,0:T(8,128)}, f32[3,8,512]{2,1,0:T(8,128)}) custom-call(f32[2,3]{1,0:T(2,128)S(1)} %copy-done.2, f32[2,2,48,128]{3,2,1,0:T(8,128)S(1)} %bitcast.35, f32[2,16,128]{2,1,0:T(8,128)S(1)} %get-tuple-element.31.solved_ref, f32[64,128]{1,0:T(8,128)S(1)} %reshape.172.refs_8_.north_ref, ...), custom_call_target="tpu_custom_call" | custom-call | tf_op jit(solution)/shard_map/solve_and_strain/pallas_call | solution.py:474
  (10 shorter events, 0.1 us)
Async XLA Ops:
  4.6 27.1 %collective-permute-start = (bf16[4,16,2560]{2,1,0:T(8,128)(2,1)}, bf16[4,16,2560]{2,1,0:T(8,128)(2,1)}, u32[]{:S(2)}, u32[]{:S(2)}) collective-permute-start(bf16[4,16,2560]{2,1,0:T(8,128)(2,1)} %get-tuple-element.21), channel_id=1, source_target_pairs={{0,4},{1,5},{2,6},{3,7},{4,8},{5,9},{6,10},{7,11},{8,12},{9,13},{1... | collective-permute-start | bytes 983048 | tf_op jit(solution)/shard_map/ppermute | solution.py:502
  6.3 25.5 %collective-permute-start.1 = (bf16[4,16,2560]{2,1,0:T(8,128)(2,1)}, bf16[4,16,2560]{2,1,0:T(8,128)(2,1)}, u32[]{:S(2)}, u32[]{:S(2)}) collective-permute-start(bf16[4,16,2560]{2,1,0:T(8,128)(2,1)} %get-tuple-element.22), channel_id=1, source_target_pairs={{0,8},{1,9},{2,10},{3,11},{4,12},{5,13},{6,14},{7,15},{8,0},{9,1},... | collective-permute-start | bytes 983048 | tf_op jit(solution)/shard_map/ppermute | solution.py:502
  6.6 44.1 %collective-permute-start.2 = (bf16[4,16,2560]{2,1,0:T(8,128)(2,1)}, bf16[4,16,2560]{2,1,0:T(8,128)(2,1)}, u32[]{:S(2)}, u32[]{:S(2)}) collective-permute-start(bf16[4,16,2560]{2,1,0:T(8,128)(2,1)} %get-tuple-element.23), channel_id=1, source_target_pairs={{0,12},{1,13},{2,14},{3,15},{4,0},{5,1},{6,2},{7,3},{8,4},{9,5},{1... | collective-permute-start | bytes 983048 | tf_op jit(solution)/shard_map/ppermute | solution.py:502
  14.4 6.9 %copy-start.3 = (s32[1,256,2]{1,2,0:T(2,128)S(1)}, s32[1,256,2]{1,2,0:T(2,128)}, u32[]{:S(2)}) copy-start(s32[1,256,2]{1,2,0:T(2,128)} %param.10) | copy-start | bytes 6148
  14.5 40.7 %copy-start.6 = (f32[8,1024]{1,0:T(8,128)S(1)}, f32[8,1024]{1,0:T(8,128)}, u32[]{:S(2)}) copy-start(f32[8,1024]{1,0:T(8,128)} %param.15) | copy-start | bytes 98308
  14.5 42.6 %copy-start.7 = (s32[1,8,8]{2,1,0:T(8,128)S(1)}, s32[1,8,8]{2,1,0:T(8,128)}, u32[]{:S(2)}) copy-start(s32[1,8,8]{2,1,0:T(8,128)} %param.13) | copy-start | bytes 772
  14.5 65.5 %copy-start.2 = (f32[2,3]{1,0:T(2,128)S(1)}, f32[2,3]{1,0:T(2,128)}, u32[]{:S(2)}) copy-start(f32[2,3]{1,0:T(2,128)} %los_ref.7) | copy-start | bytes 76
  14.5 86.7 %all-to-all-start = ((bf16[16,16,5888]{2,1,0:T(8,128)(2,1)}), bf16[16,16,5888]{2,1,0:T(8,128)(2,1)S(1)}, u32[]{:S(2)}, u32[]{:S(2)}) async-start(bf16[16,16,5888]{2,1,0:T(8,128)(2,1)} %pack_inner.1), calls=%async_computation | async-start | bytes 6029312 | tf_op jit(solution)/shard_map/all_to_all | solution.py:509
  31.8 22.4 %copy-start = (bf16[272,256]{1,0:T(8,128)(2,1)}, bf16[272,256]{1,0:T(8,128)(2,1)S(1)}, u32[]{:S(2)}) copy-start(bf16[272,256]{1,0:T(8,128)(2,1)S(1)} %get-tuple-element.20.after_ref.refs_4_) | copy-start | bytes 417796
  52.9 0.7 copy-start.4
  53.6 14.4 %collective-permute-start.5 = (bf16[4,16,2560]{2,1,0:T(8,128)(2,1)}, bf16[4,16,2560]{2,1,0:T(8,128)(2,1)}, u32[]{:S(2)}, u32[]{:S(2)}) collective-permute-start(bf16[4,16,2560]{2,1,0:T(8,128)(2,1)} %get-tuple-element.27), channel_id=1, source_target_pairs={{0,3},{1,0},{2,1},{3,2},{4,7},{5,4},{6,5},{7,6},{8,11},{9,8},{10,9... | collective-permute-start | bytes 983048 | tf_op jit(solution)/shard_map/ppermute | solution.py:507
  53.6 18.2 %collective-permute-start.3 = (bf16[4,16,2560]{2,1,0:T(8,128)(2,1)}, bf16[4,16,2560]{2,1,0:T(8,128)(2,1)}, u32[]{:S(2)}, u32[]{:S(2)}) collective-permute-start(bf16[4,16,2560]{2,1,0:T(8,128)(2,1)} %get-tuple-element.25), channel_id=1, source_target_pairs={{0,1},{1,2},{2,3},{3,0},{4,5},{5,6},{6,7},{7,4},{8,9},{9,10},{10,1... | collective-permute-start | bytes 983048 | tf_op jit(solution)/shard_map/ppermute | solution.py:507
  54.1 25.8 %collective-permute-start.4 = (bf16[4,16,2560]{2,1,0:T(8,128)(2,1)}, bf16[4,16,2560]{2,1,0:T(8,128)(2,1)}, u32[]{:S(2)}, u32[]{:S(2)}) collective-permute-start(bf16[4,16,2560]{2,1,0:T(8,128)(2,1)} %get-tuple-element.26), channel_id=1, source_target_pairs={{0,2},{1,3},{2,0},{3,1},{4,6},{5,7},{6,4},{7,5},{8,10},{9,11},{10,... | collective-permute-start | bytes 983048 | tf_op jit(solution)/shard_map/ppermute | solution.py:507
  80.0 0.9 copy-start.1
  80.9 1.0 copy-start.5
  88.9 20.4 %collective-permute-start.6 = (f32[2,8,128]{2,1,0:T(8,128)S(1)}, f32[2,8,128]{2,1,0:T(8,128)S(1)}, u32[]{:S(2)}, u32[]{:S(2)}) collective-permute-start(f32[2,8,128]{2,1,0:T(8,128)S(1)} %get-tuple-element.32), channel_id=1, source_target_pairs={{0,1},{1,2},{2,3},{3,4},{4,5},{5,6},{6,7},{7,8},{8,9},{9,10},{10,1... | collective-permute-start | bytes 24584 | tf_op jit(solution)/shard_map/ppermute | solution.py:528
  90.8 18.4 %collective-permute-start.7 = (f32[2,8,128]{2,1,0:T(8,128)S(1)}, f32[2,8,128]{2,1,0:T(8,128)S(1)}, u32[]{:S(2)}, u32[]{:S(2)}) collective-permute-start(f32[2,8,128]{2,1,0:T(8,128)S(1)} %get-tuple-element.33), channel_id=1, source_target_pairs={{1,0},{2,1},{3,2},{4,3},{5,4},{6,5},{7,6},{8,7},{9,8},{10,9},{11,1... | collective-permute-start | bytes 24584 | tf_op jit(solution)/shard_map/ppermute | solution.py:529

commit v6 on v5

v6 whole, which is shorter than its diff:
```python
import functools

import jax
import jax.numpy as jnp
from jax import lax
from jax.experimental import pallas as pl
from jax.experimental.pallas import tpu as pltpu
from jax.sharding import PartitionSpec as P

EPOCHS = 200
EXTRA = 16
HALO = 128
CTILE = 128
MBLK = 128
LANES = 128
TILE = 256
GROUP = 4
EDGE_COST = 54_000_000_000


prior_var = 0.1
ridge_term = 0.5
medium = 24 * 1024 * 1024


def stay(array):
    return pltpu.with_memory_space_constraint(array, pltpu.HBM)


def expand_masks(flags_ref, stacked_ref, firsts, wanted, tile_out):
    ifgs = flags_ref.shape[0]
    for n, first in enumerate(firsts):
        stacked_ref[n * ifgs : (n + 1) * ifgs, :] = part_flags(flags_ref, first)
    stacked = stacked_ref[...].astype(jnp.bfloat16)
    block = lax.broadcasted_iota(jnp.int32, (LANES, 2 * MBLK), 0)
    right = lax.broadcasted_iota(jnp.int32, (LANES, 2 * MBLK), 1) >= MBLK
    for start in range(0, len(wanted), 2):
        here = jnp.where(right, wanted[start + 1], wanted[start])
        ones = (block == here).astype(jnp.bfloat16)
        keep = jnp.dot(stacked, ones, preferred_element_type=jnp.float32).astype(jnp.bfloat16)
        for n in range(len(firsts)):
            tile_out(n, start * MBLK, keep[n * ifgs : (n + 1) * ifgs])


def part_flags(flags_ref, first):
    lead = pl.multiple_of(first // LANES * LANES, LANES)
    flags = (flags_ref[:, pl.ds(lead, LANES)] == 1).astype(jnp.float32)
    return pltpu.roll(flags, (LANES - (first - lead)) % LANES, 1)


def partner(index, step, size):
    return index ^ step if size & (size - 1) == 0 else (index + step) % size


def partner_back(index, step, size):
    return index ^ step if size & (size - 1) == 0 else (index - step + size) % size


def pack_edges_kernel(tiles, group, flags_hbm, phases_ref, *refs):
    *out_refs, flags_ref, stacked_ref, near_ref, flag_sem, in_sem = refs
    planes = len(out_refs)
    parts = planes * group
    ifgs, blocks = flags_ref.shape
    span = blocks // parts
    reach = tiles + 1
    half = reach * MBLK
    flag_copy = pltpu.make_async_copy(flags_hbm, flags_ref, flag_sem)
    flag_copy.start()
    ends = [
        pltpu.make_async_copy(phases_ref.at[:, pl.ds(0, half)], near_ref.at[0, :, pl.ds(half, half)], in_sem.at[0]),
        pltpu.make_async_copy(
            phases_ref.at[:, pl.ds(blocks * MBLK - half, half)], near_ref.at[parts, :, pl.ds(0, half)], in_sem.at[parts]
        ),
    ]

    def between(b):
        low = pl.multiple_of((span * b - reach) * MBLK, MBLK)
        return pltpu.make_async_copy(phases_ref.at[:, pl.ds(low, 2 * half)], near_ref.at[b], in_sem.at[b])

    ends[0].start()

    @pl.loop(1, parts)
    def _(b):
        between(b).start()

    ends[1].start()
    flag_copy.wait()
    plane = lax.axis_index("pix") // group
    firsts = [(partner(plane, s, planes) * group + g) * span for s in range(planes) for g in range(group)]

    def tile_out(n, start, keep):
        out_refs[n // group][n % group, :, start : start + 2 * MBLK] = keep

    wanted = [k if k < reach else span - 2 * reach + k for k in range(2 * reach)]
    expand_masks(flags_ref, stacked_ref, firsts, wanted, tile_out)
    ends[0].wait()

    @pl.loop(1, parts)
    def _(b):
        between(b).wait()

    ends[1].wait()
    for s in range(planes):
        first_part = partner(plane, s, planes) * group

        @pl.loop(0, group, unroll=2)
        def _(g):
            out_refs[s][g, :, :half] *= near_ref[first_part + g, :, half:]
            out_refs[s][g, :, half:] *= near_ref[first_part + g + 1, :, :half]


def pack_edges(phases, flags, parts, group, tiles):
    ifgs = phases.shape[0]
    planes = parts // group
    hbm = pl.BlockSpec(memory_space=pltpu.HBM)
    width = 2 * (tiles + 1) * MBLK
    return pl.pallas_call(
        functools.partial(pack_edges_kernel, tiles, group),
        in_specs=[hbm, hbm],
        out_specs=[pl.BlockSpec(memory_space=pltpu.VMEM)] * planes,
        out_shape=[jax.ShapeDtypeStruct((group, ifgs, width), jnp.bfloat16)] * planes,
        scratch_shapes=[
            pltpu.VMEM(flags.shape, jnp.int32),
            pltpu.VMEM((parts * ifgs, LANES), jnp.float32),
            pltpu.VMEM((parts + 1, ifgs, 2 * (tiles + 1) * MBLK), jnp.bfloat16),
            pltpu.SemaphoreType.DMA,
            pltpu.SemaphoreType.DMA((parts + 1,)),
        ],
        compiler_params=pltpu.CompilerParams(vmem_limit_bytes=medium),
        name="pack_edges",
    )(stay(flags), stay(phases))


def regroup_kernel(planes, group, after_ref, *refs):
    in_refs, out_refs = refs[:planes], refs[planes:]
    for j in range(group):
        column = partner(lax.rem(lax.axis_index("pix"), group), j, group)
        for s in range(planes):
            out_refs[j][s] = in_refs[s][column]


def regroup(after, pieces, group):
    planes = len(pieces)
    vmem = pl.BlockSpec(memory_space=pltpu.VMEM)
    shape = (planes, *pieces[0].shape[1:])
    return pl.pallas_call(
        functools.partial(regroup_kernel, planes, group),
        in_specs=[vmem] * (planes + 1),
        out_specs=[vmem] * group,
        out_shape=[jax.ShapeDtypeStruct(shape, jnp.bfloat16)] * group,
        compiler_params=pltpu.CompilerParams(vmem_limit_bytes=medium),
        name="regroup",
    )(after, *pieces)


def pack_inner_kernel(reach, flags_hbm, phases_ref, out_ref, flags_ref, stacked_ref, held_ref, flag_sem, in_sem):
    parts, ifgs, width = out_ref.shape
    span = flags_ref.shape[1] // parts
    flag_copy = pltpu.make_async_copy(flags_hbm, flags_ref, flag_sem)
    flag_copy.start()

    def inward(p):
        low = pl.multiple_of((p * span + reach) * MBLK, MBLK)
        return pltpu.make_async_copy(phases_ref.at[:, pl.ds(low, width)], held_ref.at[p], in_sem.at[p])

    @pl.loop(0, parts)
    def _(p):
        inward(p).start()

    flag_copy.wait()

    def tile_out(n, start, keep):
        out_ref[n, :, start : start + 2 * MBLK] = keep

    wanted = list(range(reach, span - reach))
    expand_masks(flags_ref, stacked_ref, [p * span for p in range(parts)], wanted, tile_out)

    @pl.loop(0, parts)
    def _(p):
        inward(p).wait()
        out_ref[p] *= held_ref[p]


def pack_inner(phases, flags, parts, tiles):
    ifgs = phases.shape[0]
    reach = tiles + 1
    width = (flags.shape[1] // parts - 2 * reach) * MBLK
    hbm = pl.BlockSpec(memory_space=pltpu.HBM)
    return pl.pallas_call(
        functools.partial(pack_inner_kernel, reach),
        in_specs=[hbm, hbm],
        out_specs=pl.BlockSpec(memory_space=pltpu.VMEM),
        out_shape=jax.ShapeDtypeStruct((parts, ifgs, width), jnp.bfloat16),
        scratch_shapes=[
            pltpu.VMEM(flags.shape, jnp.int32),
            pltpu.VMEM((parts * ifgs, LANES), jnp.float32),
            pltpu.VMEM((parts, ifgs, width), jnp.bfloat16),
            pltpu.SemaphoreType.DMA,
            pltpu.SemaphoreType.DMA((parts,)),
        ],
        compiler_params=pltpu.CompilerParams(vmem_limit_bytes=medium),
        name="pack_inner",
    )(stay(flags), stay(phases))


def exact_dot(a, b):
    return jnp.dot(a, b, precision=lax.Precision.HIGHEST, preferred_element_type=jnp.float32)


def operator_kernel(pairs_ref, other_ref, out_ref, other_out_ref, normal_ref, inverse_ref):
    ifgs = pairs_ref.shape[1]
    size = normal_ref.shape[0]
    epoch = lax.broadcasted_iota(jnp.int32, (size, ifgs), 0)

    def ends(ref):
        return (epoch == ref[1:2, :]).astype(jnp.float32) - (epoch == ref[0:1, :]).astype(jnp.float32)

    across = ends(pairs_ref)
    down = across.T
    eye = (
        lax.broadcasted_iota(jnp.int32, (size, size), 0) == lax.broadcasted_iota(jnp.int32, (size, size), 1)
    ).astype(jnp.float32)
    normal = eye + jnp.dot(
        across.astype(jnp.bfloat16), down.astype(jnp.bfloat16), preferred_element_type=jnp.float32
    )
    normal_ref[...] = normal
    inverse_ref[...] = eye / jnp.where(eye == 1.0, normal, 1.0)

    def unfinished(state):
        step, gap = state
        return jnp.logical_and(step < 24, gap > 1e-5)

    def improve(state):
        step, _ = state
        inverse = inverse_ref[...]
        rest = eye - exact_dot(normal_ref[...], inverse)
        inverse_ref[...] = inverse + exact_dot(inverse, rest)
        return step + 1, jnp.max(jnp.abs(rest))

    lax.while_loop(unfinished, improve, (jnp.int32(0), jnp.float32(1.0)))
    place = lax.broadcasted_iota(jnp.int32, (size, ifgs), 0)
    centred = place.astype(jnp.float32) - (EPOCHS - 1) / 2.0
    square = sum((e - (EPOCHS - 1) / 2.0) ** 2 for e in range(EPOCHS))
    slope = jnp.where(place < EPOCHS, centred * (EPOCHS - 1) / square, 0.0)
    same = lax.broadcasted_iota(jnp.int32, (ifgs, ifgs), 0) == lax.broadcasted_iota(jnp.int32, (ifgs, ifgs), 1)
    extra = lax.broadcasted_iota(jnp.int32, (EXTRA, ifgs), 0)
    for ref, to_ref in ((pairs_ref, out_ref), (other_ref, other_out_ref)):
        across = ends(ref)
        pseudo = exact_dot(inverse_ref[...], across).astype(jnp.bfloat16)
        fitted = jnp.dot(across.T.astype(jnp.bfloat16), pseudo, preferred_element_type=jnp.float32)
        to_ref[:ifgs, :] = (same.astype(jnp.float32) - fitted).astype(jnp.bfloat16)
        row = jnp.sum(pseudo.astype(jnp.float32) * slope, axis=0, keepdims=True)
        high = row.astype(jnp.bfloat16).astype(jnp.float32)
        rest = row - high
        middle = rest.astype(jnp.bfloat16).astype(jnp.float32)
        low = rest - middle
        terms = jnp.where(extra == 0, high, jnp.where(extra == 1, middle, jnp.where(extra == 2, low, 0.0)))
        to_ref[ifgs:, :] = terms.astype(jnp.bfloat16)


def setup_track(pair_rows, other_rows):
    ifgs = pair_rows.shape[0]
    size = -(-EPOCHS // LANES) * LANES
    vmem = pl.BlockSpec(memory_space=pltpu.VMEM)
    return pl.pallas_call(
        operator_kernel,
        in_specs=[vmem] * 2,
        out_specs=[vmem] * 2,
        out_shape=[jax.ShapeDtypeStruct((ifgs + EXTRA, ifgs), jnp.bfloat16)] * 2,
        scratch_shapes=[pltpu.VMEM((size, size), jnp.float32), pltpu.VMEM((size, size), jnp.float32)],
        compiler_params=pltpu.CompilerParams(vmem_limit_bytes=medium),
        name="misfit_operator",
    )(pair_rows.T, other_rows.T)


def invert_tiles(stack_refs, first, width, operator_ref, fields_ref, base):
    ifgs = operator_ref.shape[1]
    for start in range(0, width, TILE):
        here = pl.ds(pl.multiple_of(first + start, LANES), TILE)
        stack = jnp.concatenate([ref[:, here] for ref in stack_refs], axis=0)
        product = jnp.dot(operator_ref[...], stack, preferred_element_type=jnp.float32)
        velocity = jnp.sum(product[ifgs : ifgs + 8], axis=0, keepdims=True)
        variance = jnp.sum(product[:ifgs] * product[:ifgs], axis=0, keepdims=True) / ifgs
        for k in range(TILE // LANES):
            row = pl.ds(base + start // LANES + k, 1)
            fields_ref[0, row, :] = velocity[:, k * LANES : (k + 1) * LANES]
            fields_ref[1, row, :] = variance[:, k * LANES : (k + 1) * LANES]


def pick(source, lane):
    return jnp.take_along_axis(source, lane, axis=1, mode="promise_in_bounds")


def resample(near, cell, index_ref, weight_ref):
    lanes = lax.broadcasted_iota(jnp.int32, (8, LANES), 1)
    here = pl.ds(cell, 8)
    sums = [jnp.zeros((8, LANES), jnp.float32)] * 2
    total = jnp.zeros((8, LANES), jnp.float32)
    for b in range(index_ref.shape[0]):
        weight = weight_ref[b, here, :]
        place = lanes + index_ref[b, here, :] + HALO
        lane = place & (LANES - 1)
        which = place >> 7
        total = total + weight
        for f in range(2):
            low, mid, high = (pick(near[f][k], lane) for k in range(3))
            taken = jnp.where(which == 0, low, jnp.where(which == 1, mid, high))
            sums[f] = sums[f] + taken * weight
    return sums[0] / total, sums[1] / total, total


def boundary(row, offsets, weights, sources, wanted):
    lanes = lax.broadcasted_iota(jnp.int32, (8, LANES), 1)
    rows = lax.broadcasted_iota(jnp.int32, (8, LANES), 0)
    sums = [jnp.zeros((8, LANES), jnp.float32)] * 2
    for offset, weight in zip(offsets, weights):
        place = lanes + offset + HALO
        lane = place & (LANES - 1)
        keep = jnp.where(jnp.logical_and(place >> 7 == wanted, rows == row), weight, 0.0)
        for f in range(2):
            sums[f] = sums[f] + pick(jnp.broadcast_to(sources[f], (8, LANES)), lane) * keep
    return sums


def store_cells(out_ref, at, velocity, variance, cover, north, north_c):
    out_ref[0, at : at + 8, :] = cover / (variance + prior_var)
    out_ref[1, at : at + 8, :] = velocity - north_c * north


def edges_kernel(tiles, group, *refs):
    stack_refs = refs[:group]
    operator_ref, index_ref, weight_ref, cover_ref, north_ref, seam_ref, own_ref, ends_ref, back_ref, onward_ref, fields_ref = refs[group:]
    width = stack_refs[0].shape[1]
    count = width // LANES
    taps, rows, _ = index_ref.shape
    none = jnp.zeros((2, 1, LANES), jnp.float32)
    fields_ref[:, :1, :] = none
    fields_ref[:, count + 1 : count + 2, :] = none
    invert_tiles(stack_refs, 0, width, operator_ref, fields_ref, 1)
    seam_ref[...] = fields_ref[:, tiles : tiles + 4, :]
    ends_ref[:, :1, :] = fields_ref[:, 1:2, :]
    ends_ref[:, 1:, :] = fields_ref[:, count : count + 1, :]
    for half, to_ref in enumerate((back_ref, onward_ref)):
        first = half * (rows - tiles)
        to_ref[:tiles, :] = north_ref[first : first + tiles, :]
        to_ref[tiles : 2 * tiles, :] = jnp.broadcast_to(cover_ref[first : first + tiles, :].astype(jnp.float32), (tiles, LANES))
        for r in range(0, tiles, 8):
            base = half * (tiles + 2) + r
            near = [[fields_ref[f, base + k : base + k + 8, :] for k in range(3)] for f in range(2)]
            velocity, variance, total = resample(near, first + r, index_ref, weight_ref)
            for f, values in enumerate((velocity, variance)):
                own_ref[f, half * tiles + r : half * tiles + r + 8, :] = values
                to_ref[(2 + f) * tiles + r : (2 + f) * tiles + r + 8, :] = values
            if r == (tiles - 8 if half else 0):
                outer = total[7:] if half else total[:1]
        outermost = first + (tiles - 1 if half else 0)
        at = 4 * tiles
        for b in range(taps):
            to_ref[at + b : at + b + 1, :] = index_ref[b, outermost : outermost + 1, :].astype(jnp.float32)
            to_ref[at + taps + b : at + taps + b + 1, :] = weight_ref[b, outermost : outermost + 1, :] / outer
        at += 2 * taps
        for f in range(2):
            to_ref[at + f : at + f + 1, :] = ends_ref[f, half : half + 1, :]
        left = to_ref.shape[0] - at - 2
        to_ref[at + 2 :, :] = jnp.zeros((left, LANES), jnp.float32)


def edges(stacks, operator, cells, tiles):
    rows = 2 * (tiles + 1)
    payload = -(-(4 * tiles + 2 * cells[0].shape[0] + 2) // 8) * 8
    shapes = [(2, 4, LANES), (2, 2 * tiles, LANES), (2, 2, LANES), (payload, LANES), (payload, LANES)]
    vmem = pl.BlockSpec(memory_space=pltpu.VMEM)
    return pl.pallas_call(
        functools.partial(edges_kernel, tiles, len(stacks)),
        in_specs=[vmem] * (len(stacks) + 5),
        out_specs=[vmem] * 5,
        out_shape=[jax.ShapeDtypeStruct(shape, jnp.float32) for shape in shapes],
        scratch_shapes=[pltpu.VMEM((2, -(-(rows + 2) // 8) * 8, LANES), jnp.float32)],
        compiler_params=pltpu.CompilerParams(vmem_limit_bytes=medium),
        cost_estimate=pl.CostEstimate(flops=EDGE_COST, bytes_accessed=0, transcendentals=0),
        name="edge_rows",
    )(*stacks, operator, *cells)


def inner_kernel(
    tiles, los_ref, stack_ref, seam_ref, own_ref, ends_ref, before_ref, after_ref, operator_ref, index_ref, weight_ref, cover_ref,
    north_ref, out_ref, fields_ref,
):
    width = stack_ref.shape[1]
    taps, rows, _ = index_ref.shape
    north_c = los_ref[lax.axis_index("track"), 1]
    pixel_rows = width // LANES
    fields_ref[:, 0:2, :] = seam_ref[:, 0:2, :]
    fields_ref[:, pixel_rows + 2 : pixel_rows + 4, :] = seam_ref[:, 2:4, :]
    for half, from_ref in enumerate((before_ref, after_ref)):
        edge = half * (tiles - 8)
        row = 7 * half
        outermost = half * (rows - 1)
        total = sum(weight_ref[b, outermost : outermost + 1, :] for b in range(taps))
        at = 4 * tiles
        theirs = [from_ref[at + 2 * taps + f : at + 2 * taps + f + 1, :] for f in range(2)]
        mine = [ends_ref[f, half : half + 1, :] for f in range(2)]
        to_own = boundary(
            row,
            [index_ref[b, outermost : outermost + 1, :] for b in range(taps)],
            [weight_ref[b, outermost : outermost + 1, :] / total for b in range(taps)],
            theirs,
            2 * half,
        )
        to_other = boundary(
            7 - row,
            [from_ref[at + b : at + b + 1, :].astype(jnp.int32) for b in range(taps)],
            [from_ref[at + taps + b : at + taps + b + 1, :] for b in range(taps)],
            mine,
            2 - 2 * half,
        )
        for r in range(0, tiles, 8):
            first = half * (rows - tiles) + r
            values = [own_ref[f, half * tiles + r : half * tiles + r + 8, :] for f in range(2)]
            if r == edge:
                values = [value + more for value, more in zip(values, to_own)]
            cover = cover_ref[first : first + 8, :].astype(jnp.float32)
            store_cells(out_ref, tiles + first, *values, cover, north_ref[first : first + 8, :], north_c)
            values = [from_ref[(2 + f) * tiles + r : (2 + f) * tiles + r + 8, :] for f in range(2)]
            if r == tiles - 8 - edge:
                values = [value + more for value, more in zip(values, to_other)]
            cover = from_ref[tiles + r : tiles + r + 8, :]
            store_cells(out_ref, half * (rows + tiles) + r, *values, cover, from_ref[r : r + 8, :], north_c)
    invert_tiles([stack_ref], 0, width, operator_ref, fields_ref, 2)
    for r in range(0, rows - 2 * tiles, 8):
        near = [[fields_ref[f, r + k : r + k + 8, :] for k in range(3)] for f in range(2)]
        first = tiles + r
        velocity, variance, _ = resample(near, first, index_ref, weight_ref)
        cover = cover_ref[first : first + 8, :].astype(jnp.float32)
        store_cells(out_ref, tiles + first, velocity, variance, cover, north_ref[first : first + 8, :], north_c)


def inner(los, stack, seam, own, ends, before, after, operator, cells, tiles):
    rows = cells[0].shape[1]
    vmem = pl.BlockSpec(memory_space=pltpu.VMEM)
    return pl.pallas_call(
        functools.partial(inner_kernel, tiles),
        in_specs=[pl.BlockSpec(memory_space=pltpu.SMEM)] + [vmem] * 11,
        out_specs=vmem,
        out_shape=jax.ShapeDtypeStruct((2, rows + 2 * tiles, LANES), jnp.float32),
        scratch_shapes=[pltpu.VMEM((2, -(-(rows - 2 * tiles + 2) // 8) * 8, LANES), jnp.float32)],
        compiler_params=pltpu.CompilerParams(vmem_limit_bytes=medium),
        name="inner_rows",
    )(los, stack, seam, own, ends, before, after, operator, *cells)


def solve_cells(vals_ref, los_ref):
    a11 = a12 = a22 = b1 = b2 = 0.0
    for t in range(vals_ref.shape[0]):
        weight, target = vals_ref[t, 0], vals_ref[t, 1]
        east_c, up_c = los_ref[t, 0], los_ref[t, 2]
        by_east, by_up = weight * east_c, weight * up_c
        a11 = a11 + by_east * east_c
        a12 = a12 + by_east * up_c
        a22 = a22 + by_up * up_c
        b1 = b1 + by_east * target
        b2 = b2 + by_up * target
    a11 = a11 + ridge_term
    a22 = a22 + ridge_term
    determ = a11 * a22 - a12 * a12
    return (a22 * b1 - a12 * b2) / determ, (a11 * b2 - a12 * b1) / determ


def final_kernel(tiles, own, los_ref, vals_ref, north_ref, before_ref, after_ref, east_up_ref, strain_ref, work_ref):
    rows = north_ref.shape[0]
    lane = lax.broadcasted_iota(jnp.int32, (rows, LANES), 1)
    tile = lax.broadcasted_iota(jnp.int32, (rows, LANES), 0) % tiles

    def across(field):
        right = jnp.where(tile == tiles - 1, 0.0, pltpu.roll(field, rows - 1, 0))
        left = jnp.where(tile == 0, 0.0, pltpu.roll(field, 1, 0))
        following = jnp.where(lane == LANES - 1, pltpu.roll(right, LANES - 1, 1), pltpu.roll(field, LANES - 1, 1))
        previous = jnp.where(lane == 0, pltpu.roll(left, 1, 1), pltpu.roll(field, 1, 1))
        return following - previous

    wide_east, wide_up = solve_cells(vals_ref, los_ref)
    wide_north = jnp.concatenate([before_ref[:tiles, :], north_ref[...], after_ref[:tiles, :]], axis=0)
    east, north = (wide[tiles : tiles + rows] for wide in (wide_east, wide_north))
    work_ref[0] = east
    work_ref[1] = wide_up[tiles : tiles + rows]
    work_ref[2] = across(east) / 2.0
    work_ref[3] = (wide_north[2 * tiles :] - wide_north[:rows]) / 2.0
    work_ref[4] = (wide_east[2 * tiles :] - wide_east[:rows] + across(north)) / 4.0
    start = lax.axis_index("track") * own
    for field in range(5):
        target, at = (east_up_ref, field) if field < 2 else (strain_ref, field - 2)
        for i in range(rows // tiles):
            for j in range(own):
                target[at, i : i + 1, j * LANES : (j + 1) * LANES] = work_ref[field, pl.ds(i * tiles + start + j, 1), :]


def final(los, vals, north, before, after, tiles, own):
    rows = north.shape[0]
    shape = (rows // tiles, own * LANES)
    vmem = pl.BlockSpec(memory_space=pltpu.VMEM)
    return pl.pallas_call(
        functools.partial(final_kernel, tiles, own),
        in_specs=[pl.BlockSpec(memory_space=pltpu.SMEM)] + [vmem] * 4,
        out_specs=[vmem] * 2,
        out_shape=[jax.ShapeDtypeStruct((2, *shape), jnp.float32), jax.ShapeDtypeStruct((3, *shape), jnp.float32)],
        scratch_shapes=[pltpu.VMEM((5, rows, LANES), jnp.float32)],
        compiler_params=pltpu.CompilerParams(vmem_limit_bytes=medium),
        name="solve_and_strain",
    )(los, vals, north, before, after)


def per_device(phases, coherent, pairs, res_index, res_weight, coverage, los, north):
    parts = lax.axis_size("pix")
    tracks = lax.axis_size("track")
    grid_rows, columns = north.shape
    tiles = columns // CTILE
    rows = grid_rows * tiles
    group = GROUP if parts % GROUP == 0 else parts
    planes = parts // group
    plane, column = jnp.divmod(lax.axis_index("pix").astype(jnp.int32), group)
    packed = pack_edges(phases[0], coherent[0], parts, group, tiles)
    later_pairs, _ = lax.optimization_barrier((pairs[0], packed[0]))
    steps_j, steps_s = jnp.meshgrid(jnp.arange(group), jnp.arange(planes), indexing="ij")
    sources = (partner_back(plane, steps_s, planes) * group + partner_back(column, steps_j, group)).reshape(-1)
    edge_pairs = jnp.take(later_pairs.reshape(parts, -1, 2), sources, axis=0).reshape(-1, 2)
    operator, edge_operator = setup_track(later_pairs, edge_pairs)
    ids = [(z, c) for z in range(planes) for c in range(group)]
    arrived = [packed[0]]
    for s in range(1, planes):
        far = [(z * group + c, partner(z, s, planes) * group + c) for z, c in ids]
        arrived.append(lax.ppermute(packed[s], "pix", far))
    by_column = regroup(edge_operator, arrived, group)
    pieces = [by_column[0]]
    for j in range(1, group):
        near = [(z * group + c, z * group + partner(c, j, group)) for z, c in ids]
        pieces.append(lax.ppermute(by_column[j], "pix", near))
    later_flags, *_ = lax.optimization_barrier((coherent[0], packed[0], operator))
    inner_stack = lax.all_to_all(
        pack_inner(phases[0], later_flags, parts, tiles), "pix", split_axis=0, concat_axis=0, tiled=True
    )
    north_cells = north.reshape(rows, LANES)
    cells = (
        res_index.reshape(-1, rows, LANES),
        res_weight.reshape(-1, rows, LANES),
        coverage.reshape(rows, 1),
        north_cells,
    )

    def flat(stack):
        return stack.reshape(-1, stack.shape[-1])

    onward = [(i, i + 1) for i in range(parts - 1)]
    back = [(j, i) for i, j in onward]
    seam, own, ends, for_before, for_after = edges([flat(piece) for piece in pieces], edge_operator, cells, tiles)
    before = lax.ppermute(for_after, "pix", onward)
    after = lax.ppermute(for_before, "pix", back)
    vals = inner(los, flat(inner_stack), seam, own, ends, before, after, operator, cells, tiles)
    vals = lax.all_gather(vals, "track", axis=0)
    return tuple(final(los, vals, north_cells, before, after, tiles, tiles // tracks))


def solution(mesh):
    in_specs = (
        P("track", "pix", None),
        P("track", "pix", None),
        P("track", None, None),
        P("track", None, "pix"),
        P("track", None, "pix"),
        P("track", "pix", None),
        P(),
        P("pix", None),
    )
    out_specs = (P(None, "pix", "track"), P(None, "pix", "track"))
    return jax.shard_map(
        per_device, mesh=mesh, in_specs=in_specs, out_specs=out_specs, check_vma=False
    )
```

time: 111 us -> 108 us (0.973)
  starting transfers between devices: 17.7 us -> 28.9 us
  waiting for transfers between devices: 47.6 us -> 40.9 us
  Pallas kernels: 29.5 us -> 23.1 us
  blocking collectives: 9.18 us -> 5.12 us
  local copies, waits for them, and re-layouts: 5.9 us -> 8.46 us
    ppermute x3, waiting for transfers between devices: 18.9 us -> 4.82 us  [per_device(): arrived.append(lax.ppermute(packed[s], 'pix', far))]
    ppermute x2, waiting for transfers between devices: 0.01 us -> 13.6 us  [the longest x1 13.6 us: per_device(): before = lax.ppermute(for_after, 'pix', onward)]
    ppermute x2, starting transfers between devices: 6.46 us -> 16.4 us  [the longest x1 14.5 us: per_device(): after = lax.ppermute(for_before, 'pix', back)]
    all_to_all x1, waiting for transfers between devices: 5.83 us -> 1.16 us  [per_device(): lax.all_to_all(pack_inner(phases[0], later_flags, parts, tiles), 'pix', s...]
    all_gather x2 -> x1, blocking collectives: 9.18 us -> 5.12 us  [per_device(): vals = lax.all_gather(vals, 'track', axis=0)]
    unnamed x18 -> x24, local copies, waits for them, and re-layouts: 4.47 us -> 7.28 us
    pallas_call x1, Pallas kernels: 6.63 us -> 3.96 us  [pack_inner(): pl.pallas_call(functools.partial(pack_inner_kernel, reach), in_specs=[hbm...]
    pallas_call x1, Pallas kernels: 3.29 us -> 1.69 us  [inner(): pl.pallas_call(functools.partial(inner_kernel, tiles), in_specs=[pl.Block...]
  transfers between devices with their start and end apart: 9 -> 9, of which waited for: 5 -> 5; matrix products, arithmetic and copies ran while one was open for 3% -> 3% of each run, Pallas kernels for 22% -> 16%
where the time goes in v6:
time: 108 us; the launch traced here: 107 us
  waiting for transfers between devices  40.9 us (38%)
  starting transfers between devices  28.9 us (27%)
  Pallas kernels  23.1 us (21%)
  local copies, waits for them, and re-layouts  8.46 us (8%)
  blocking collectives  5.12 us (5%)
    ppermute x3, waiting for transfers between devices, per_device(): pieces.append(lax.ppermute(by_column[j], 'pix', near))  21.3 us
    ppermute x1, starting transfers between devices, per_device(): after = lax.ppermute(for_before, 'pix', back)  14.5 us
    ppermute x1, waiting for transfers between devices, per_device(): before = lax.ppermute(for_after, 'pix', onward)  13.6 us
    pallas_call x1, Pallas kernels, setup_track(): pl.pallas_call(operator_kernel, in_specs=[vmem] * 2, out_specs=[vmem] * 2...  9.36 us
    unnamed x24, local copies, waits for them, and re-layouts  7.28 us
    all_to_all x1, starting transfers between devices, per_device(): lax.all_to_all(pack_inner(phases[0], later_flags, parts, tiles), 'pix', s...  7.07 us
    all_gather x1, blocking collectives, per_device(): vals = lax.all_gather(vals, 'track', axis=0)  5.12 us
    ppermute x3, waiting for transfers between devices, per_device(): arrived.append(lax.ppermute(packed[s], 'pix', far))  4.82 us
  transfers between devices with their start and end apart: 9, of which 5 were waited for; matrix products, arithmetic and copies ran while one was open for 3% of the time, Pallas kernels for 16%

profile of v6, /device:TPU:16, one launch (start us, length us, event | category | flops | bytes accessed | tf_op | source)
XLA Modules:
  0.0 107.4 jit_solution(507098219194655524)
XLA Ops:
  0.6 0.0 copy-start.3
  0.6 2.8 %pack_edges.1 = (bf16[4,16,2304]{2,1,0:T(8,128)(2,1)S(1)}, bf16[4,16,2304]{2,1,0:T(8,128)(2,1)}, bf16[4,16,2304]{2,1,0:T(8,128)(2,1)}, bf16[4,16,2304]{2,1,0:T(8,128)(2,1)}) custom-call(s32[16,1024]{1,0:T(8,128)} %bitcast.39, bf16[16,131072]{1,0:T(8,128)(2,1)} %bitcast.37), custom_call_target="tpu_custom_call" | custom-call | tf_op jit(solution)/shard_map/pack_edges/pallas_call | solution.py:117
  3.5 1.6 %collective-permute-start = (bf16[4,16,2304]{2,1,0:T(8,128)(2,1)}, bf16[4,16,2304]{2,1,0:T(8,128)(2,1)}, u32[]{:S(2)}, u32[]{:S(2)}) collective-permute-start(bf16[4,16,2304]{2,1,0:T(8,128)(2,1)} %get-tuple-element.24), channel_id=1, source_target_pairs={{0,4},{1,5},{2,6},{3,7},{4,0},{5,1},{6,2},{7,3},{8,12},{9,13},{10,... | collective-permute-start | bytes 884744 | tf_op jit(solution)/shard_map/ppermute | solution.py:531
  5.1 0.3 collective-permute-start.1
  5.4 1.6 %collective-permute-start.2 = (bf16[4,16,2304]{2,1,0:T(8,128)(2,1)}, bf16[4,16,2304]{2,1,0:T(8,128)(2,1)}, u32[]{:S(2)}, u32[]{:S(2)}) collective-permute-start(bf16[4,16,2304]{2,1,0:T(8,128)(2,1)} %get-tuple-element.26), channel_id=1, source_target_pairs={{0,12},{1,13},{2,14},{3,15},{4,8},{5,9},{6,10},{7,11},{8,4},{9,5},... | collective-permute-start | bytes 884744 | tf_op jit(solution)/shard_map/ppermute | solution.py:531
  7.0 0.1 broadcast_add_fusion
  7.1 0.1 add.44
  7.2 0.1 add.42
  7.3 0.1 broadcast_in_dim.22
  7.4 0.1 broadcast_in_dim.23
  7.5 0.0 copy-done.3
  7.5 0.1 reshape.83
  7.6 0.6 gather_fusion
  8.2 0.1 gather.7
  8.2 9.4 %misfit_operator.1 = (bf16[272,256]{1,0:T(8,128)(2,1)S(1)}, bf16[272,256]{1,0:T(8,128)(2,1)S(1)}) custom-call(s32[2,256]{1,0:T(2,128)S(1)} %bitcast.35, s32[2,256]{1,0:T(2,128)S(1)} %select_bitcast_fusion.other_ref), custom_call_target="tpu_custom_call" | custom-call | tf_op jit(solution)/shard_map/misfit_operator/pallas_call | solution.py:265
  17.6 0.0 copy-start
  17.6 0.7 copy-done
  18.3 4.0 %pack_inner.1 = bf16[16,16,5888]{2,1,0:T(8,128)(2,1)} custom-call(s32[16,1024]{1,0:T(8,128)} %bitcast.40, bf16[16,131072]{1,0:T(8,128)(2,1)} %bitcast.38), custom_call_target="tpu_custom_call" | custom-call | tf_op jit(solution)/shard_map/pack_inner/pallas_call | solution.py:189
  22.3 0.0 copy-start.9
  22.3 0.0 copy-start.10
  22.3 7.1 %all-to-all-start = ((bf16[16,16,5888]{2,1,0:T(8,128)(2,1)}), bf16[16,16,5888]{2,1,0:T(8,128)(2,1)S(1)}, u32[]{:S(2)}, u32[]{:S(2)}) async-start(bf16[16,16,5888]{2,1,0:T(8,128)(2,1)} %pack_inner.1), calls=%async_computation | async-start | bytes 6029312 | tf_op jit(solution)/shard_map/all_to_all | solution.py:538
  29.4 0.0 collective-permute-done.refs_1_
  29.4 0.0 collective-permute-done.1.refs_2_
  29.4 4.8 %collective-permute-done.2.refs_3_ = bf16[4,16,2304]{2,1,0:T(8,128)(2,1)} collective-permute-done((bf16[4,16,2304]{2,1,0:T(8,128)(2,1)}, bf16[4,16,2304]{2,1,0:T(8,128)(2,1)}, u32[]{:S(2)}, u32[]{:S(2)}) %collective-permute-start.2) | collective-permute-done | bytes 294944 | tf_op jit(solution)/shard_map/ppermute | solution.py:531
  34.2 0.0 copy-start.1
  34.2 0.9 copy-done.1
  35.1 2.1 %regroup.1 = (bf16[4,16,2304]{2,1,0:T(8,128)(2,1)S(1)}, bf16[4,16,2304]{2,1,0:T(8,128)(2,1)}, bf16[4,16,2304]{2,1,0:T(8,128)(2,1)}, bf16[4,16,2304]{2,1,0:T(8,128)(2,1)}) custom-call(bf16[272,256]{1,0:T(8,128)(2,1)S(1)} %copy-done.1, bf16[4,16,2304]{2,1,0:T(8,128)(2,1)S(1)} %get-tuple-element.19.refs_0_, bf16[4,16,2304]{2,1,0:T(8,128)(2,1)} %collective-permute-done.refs_1_, ...), custom_call_target="tpu_custom_call" | custom-call | tf_op jit(solution)/shard_map/regroup/pallas_call | solution.py:146
  37.2 0.0 copy-start.7
  37.2 0.7 copy-done.7
  37.9 0.0 collective-permute-start.3
  37.9 1.5 %collective-permute-start.4 = (bf16[4,16,2304]{2,1,0:T(8,128)(2,1)}, bf16[4,16,2304]{2,1,0:T(8,128)(2,1)}, u32[]{:S(2)}, u32[]{:S(2)}) collective-permute-start(bf16[4,16,2304]{2,1,0:T(8,128)(2,1)} %get-tuple-element.29), channel_id=1, source_target_pairs={{0,2},{1,3},{2,0},{3,1},{4,6},{5,7},{6,4},{7,5},{8,10},{9,11},{10,... | collective-permute-start | bytes 884744 | tf_op jit(solution)/shard_map/ppermute | solution.py:536
  39.4 0.4 collective-permute-start.5
  39.8 0.0 copy-done.9
  39.8 0.0 copy-done.10
  39.8 0.1 reshape.102.refs_7_.cover_ref
  39.9 0.9 copy.25
  40.8 0.9 copy.24
  41.7 0.0 collective-permute-done.3
  41.8 13.3 %collective-permute-done.4 = bf16[4,16,2304]{2,1,0:T(8,128)(2,1)} collective-permute-done((bf16[4,16,2304]{2,1,0:T(8,128)(2,1)}, bf16[4,16,2304]{2,1,0:T(8,128)(2,1)}, u32[]{:S(2)}, u32[]{:S(2)}) %collective-permute-start.4) | collective-permute-done | bytes 294944 | tf_op jit(solution)/shard_map/ppermute | solution.py:536
  55.1 8.0 %collective-permute-done.5 = bf16[4,16,2304]{2,1,0:T(8,128)(2,1)} collective-permute-done((bf16[4,16,2304]{2,1,0:T(8,128)(2,1)}, bf16[4,16,2304]{2,1,0:T(8,128)(2,1)}, u32[]{:S(2)}, u32[]{:S(2)}) %collective-permute-start.5) | collective-permute-done | bytes 294944 | tf_op jit(solution)/shard_map/ppermute | solution.py:536
  63.0 0.0 copy-start.2
  63.1 0.9 copy-done.2
  64.0 0.0 copy-start.8
  64.0 1.0 copy-done.8
  64.9 0.0 copy-start.4
  64.9 1.8 %edge_rows.1 = (f32[2,4,128]{2,1,0:T(4,128)S(1)}, f32[2,16,128]{2,1,0:T(8,128)S(1)}, f32[2,2,128]{2,1,0:T(2,128)S(1)}, f32[48,128]{1,0:T(8,128)S(1)}, f32[48,128]{1,0:T(8,128)S(1)}) custom-call(bf16[64,2304]{1,0:T(8,128)(2,1)S(1)} %bitcast.36, bf16[64,2304]{1,0:T(8,128)(2,1)} %bitcast.8.refs_1_, bf16[64,2304]{1,0:T(8,128)(2,1)} %bitcast.9.refs_2_, ...), custom_call_target="tpu_custom_call" | custom-call | flops 54000001024 | tf_op jit(solution)/shard_map/edge_rows/pallas_call | solution.py:373
  66.7 0.0 copy-start.5
  66.7 0.6 copy-done.5
  67.3 1.9 %collective-permute-start.6 = (f32[48,128]{1,0:T(8,128)S(1)}, f32[48,128]{1,0:T(8,128)S(1)}, u32[]{:S(2)}, u32[]{:S(2)}) collective-permute-start(f32[48,128]{1,0:T(8,128)S(1)} %get-tuple-element.34), channel_id=1, source_target_pairs={{0,1},{1,2},{2,3},{3,4},{4,5},{5,6},{6,7},{7,8},{8,9},{9,10},{10,1... | collective-permute-start | bytes 73736 | tf_op jit(solution)/shard_map/ppermute | solution.py:555
  69.2 14.5 %collective-permute-start.7 = (f32[48,128]{1,0:T(8,128)S(1)}, f32[48,128]{1,0:T(8,128)S(1)}, u32[]{:S(2)}, u32[]{:S(2)}) collective-permute-start(f32[48,128]{1,0:T(8,128)S(1)} %get-tuple-element.35), channel_id=1, source_target_pairs={{1,0},{2,1},{3,2},{4,3},{5,4},{6,5},{7,6},{8,7},{9,8},{10,9},{11,1... | collective-permute-start | bytes 73736 | tf_op jit(solution)/shard_map/ppermute | solution.py:556
  83.7 13.6 %collective-permute-done.6.before_ref = f32[48,128]{1,0:T(8,128)S(1)} collective-permute-done((f32[48,128]{1,0:T(8,128)S(1)}, f32[48,128]{1,0:T(8,128)S(1)}, u32[]{:S(2)}, u32[]{:S(2)}) %collective-permute-start.6) | collective-permute-done | bytes 24608 | tf_op jit(solution)/shard_map/ppermute | solution.py:555
  97.3 0.0 collective-permute-done.7.after_ref
  97.3 1.2 %all-to-all-done = bf16[16,16,5888]{2,1,0:T(8,128)(2,1)S(1)} async-done(((bf16[16,16,5888]{2,1,0:T(8,128)(2,1)}), bf16[16,16,5888]{2,1,0:T(8,128)(2,1)S(1)}, u32[]{:S(2)}, u32[]{:S(2)}) %all-to-all-start) | async-done | bytes 3014688 | tf_op jit(solution)/shard_map/all_to_all | solution.py:538
  98.5 0.0 copy-done.4
  98.5 0.0 copy-start.6
  98.5 0.7 copy-done.6
  99.2 1.7 %inner_rows.1 = f32[2,80,128]{2,1,0:T(8,128)S(1)} custom-call(f32[2,3]{1,0:T(2,128)S(1)} %copy-done.4, bf16[256,5888]{1,0:T(8,128)(2,1)S(1)} %bitcast.28, f32[2,4,128]{2,1,0:T(4,128)S(1)} %get-tuple-element.31.seam_ref, f32[2,16,128]{2,1,0:T(8,128)S(1)} %get-tuple-element.32.own_ref, f32[2,2,128]{2,1,0:T(2,128)S(1)} %copy-done.6, ...), custom_call_target="tpu_custom_call" | custom-call | tf_op jit(solution)/shard_map/inner_rows/pallas_call | solution.py:441
  100.8 5.1 %all-gather = f32[4,80,128]{2,1,0:T(8,128)S(1)} all-gather(f32[2,80,128]{2,1,0:T(8,128)S(1)} %inner_rows.1), channel_id=2, replica_groups=mesh['track'=2,'pix'=16] {'track'}, dimensions={0}, use_global_device_ids=true | all-gather | bytes 245760 | tf_op jit(solution)/shard_map/all_gather | solution.py:558
  106.0 1.4 %solve_and_strain.1 = (f32[2,8,512]{2,1,0:T(8,128)}, f32[3,8,512]{2,1,0:T(8,128)}) custom-call(f32[2,3]{1,0:T(2,128)S(1)} %copy-done.4, f32[2,2,80,128]{3,2,1,0:T(8,128)S(1)} %bitcast.29, f32[64,128]{1,0:T(8,128)S(1)} %reshape.92.refs_8_.north_ref, f32[48,128]{1,0:T(8,128)S(1)} %collective-permute-done.6.before_ref, ...), custom_call_target="tpu_custom_call" | custom-call | tf_op jit(solution)/shard_map/solve_and_strain/pallas_call | solution.py:501
  (8 shorter events, 0.1 us)
Async XLA Ops:
  0.6 6.8 %copy-start.3 = (s32[1,256,2]{1,2,0:T(2,128)S(1)}, s32[1,256,2]{1,2,0:T(2,128)}, u32[]{:S(2)}) copy-start(s32[1,256,2]{1,2,0:T(2,128)} %param.10) | copy-start | bytes 6148
  3.5 25.9 %collective-permute-start = (bf16[4,16,2304]{2,1,0:T(8,128)(2,1)}, bf16[4,16,2304]{2,1,0:T(8,128)(2,1)}, u32[]{:S(2)}, u32[]{:S(2)}) collective-permute-start(bf16[4,16,2304]{2,1,0:T(8,128)(2,1)} %get-tuple-element.24), channel_id=1, source_target_pairs={{0,4},{1,5},{2,6},{3,7},{4,0},{5,1},{6,2},{7,3},{8,12},{9,13},{10,... | collective-permute-start | bytes 884744 | tf_op jit(solution)/shard_map/ppermute | solution.py:531
  5.1 24.3 %collective-permute-start.1 = (bf16[4,16,2304]{2,1,0:T(8,128)(2,1)}, bf16[4,16,2304]{2,1,0:T(8,128)(2,1)}, u32[]{:S(2)}, u32[]{:S(2)}) collective-permute-start(bf16[4,16,2304]{2,1,0:T(8,128)(2,1)} %get-tuple-element.25), channel_id=1, source_target_pairs={{0,8},{1,9},{2,10},{3,11},{4,12},{5,13},{6,14},{7,15},{8,0},{9,1},... | collective-permute-start | bytes 884744 | tf_op jit(solution)/shard_map/ppermute | solution.py:531
  5.4 28.8 %collective-permute-start.2 = (bf16[4,16,2304]{2,1,0:T(8,128)(2,1)}, bf16[4,16,2304]{2,1,0:T(8,128)(2,1)}, u32[]{:S(2)}, u32[]{:S(2)}) collective-permute-start(bf16[4,16,2304]{2,1,0:T(8,128)(2,1)} %get-tuple-element.26), channel_id=1, source_target_pairs={{0,12},{1,13},{2,14},{3,15},{4,8},{5,9},{6,10},{7,11},{8,4},{9,5},... | collective-permute-start | bytes 884744 | tf_op jit(solution)/shard_map/ppermute | solution.py:531
  17.6 0.7 copy-start
  22.3 17.5 %copy-start.9 = (f32[8,1024]{1,0:T(8,128)S(1)}, f32[8,1024]{1,0:T(8,128)}, u32[]{:S(2)}) copy-start(f32[8,1024]{1,0:T(8,128)} %param.15) | copy-start | bytes 98308
  22.3 17.5 %copy-start.10 = (s32[1,8,8]{2,1,0:T(8,128)S(1)}, s32[1,8,8]{2,1,0:T(8,128)}, u32[]{:S(2)}) copy-start(s32[1,8,8]{2,1,0:T(8,128)} %param.13) | copy-start | bytes 772
  22.3 76.2 %all-to-all-start = ((bf16[16,16,5888]{2,1,0:T(8,128)(2,1)}), bf16[16,16,5888]{2,1,0:T(8,128)(2,1)S(1)}, u32[]{:S(2)}, u32[]{:S(2)}) async-start(bf16[16,16,5888]{2,1,0:T(8,128)(2,1)} %pack_inner.1), calls=%async_computation | async-start | bytes 6029312 | tf_op jit(solution)/shard_map/all_to_all | solution.py:538
  34.2 0.9 copy-start.1
  37.2 0.7 copy-start.7
  37.9 3.8 %collective-permute-start.3 = (bf16[4,16,2304]{2,1,0:T(8,128)(2,1)}, bf16[4,16,2304]{2,1,0:T(8,128)(2,1)}, u32[]{:S(2)}, u32[]{:S(2)}) collective-permute-start(bf16[4,16,2304]{2,1,0:T(8,128)(2,1)} %get-tuple-element.28), channel_id=1, source_target_pairs={{0,1},{1,0},{2,3},{3,2},{4,5},{5,4},{6,7},{7,6},{8,9},{9,8},{10,11... | collective-permute-start | bytes 884744 | tf_op jit(solution)/shard_map/ppermute | solution.py:536
  37.9 17.1 %collective-permute-start.4 = (bf16[4,16,2304]{2,1,0:T(8,128)(2,1)}, bf16[4,16,2304]{2,1,0:T(8,128)(2,1)}, u32[]{:S(2)}, u32[]{:S(2)}) collective-permute-start(bf16[4,16,2304]{2,1,0:T(8,128)(2,1)} %get-tuple-element.29), channel_id=1, source_target_pairs={{0,2},{1,3},{2,0},{3,1},{4,6},{5,7},{6,4},{7,5},{8,10},{9,11},{10,... | collective-permute-start | bytes 884744 | tf_op jit(solution)/shard_map/ppermute | solution.py:536
  39.4 23.6 %collective-permute-start.5 = (bf16[4,16,2304]{2,1,0:T(8,128)(2,1)}, bf16[4,16,2304]{2,1,0:T(8,128)(2,1)}, u32[]{:S(2)}, u32[]{:S(2)}) collective-permute-start(bf16[4,16,2304]{2,1,0:T(8,128)(2,1)} %get-tuple-element.30), channel_id=1, source_target_pairs={{0,3},{1,2},{2,1},{3,0},{4,7},{5,6},{6,5},{7,4},{8,11},{9,10},{10,... | collective-permute-start | bytes 884744 | tf_op jit(solution)/shard_map/ppermute | solution.py:536
  63.0 0.9 copy-start.2
  64.0 1.0 copy-start.8
  64.9 33.5 %copy-start.4 = (f32[2,3]{1,0:T(2,128)S(1)}, f32[2,3]{1,0:T(2,128)}, u32[]{:S(2)}) copy-start(f32[2,3]{1,0:T(2,128)} %los_ref.3) | copy-start | bytes 76
  66.7 0.6 copy-start.5
  67.3 30.0 %collective-permute-start.6 = (f32[48,128]{1,0:T(8,128)S(1)}, f32[48,128]{1,0:T(8,128)S(1)}, u32[]{:S(2)}, u32[]{:S(2)}) collective-permute-start(f32[48,128]{1,0:T(8,128)S(1)} %get-tuple-element.34), channel_id=1, source_target_pairs={{0,1},{1,2},{2,3},{3,4},{4,5},{5,6},{6,7},{7,8},{8,9},{9,10},{10,1... | collective-permute-start | bytes 73736 | tf_op jit(solution)/shard_map/ppermute | solution.py:555
  69.2 28.1 %collective-permute-start.7 = (f32[48,128]{1,0:T(8,128)S(1)}, f32[48,128]{1,0:T(8,128)S(1)}, u32[]{:S(2)}, u32[]{:S(2)}) collective-permute-start(f32[48,128]{1,0:T(8,128)S(1)} %get-tuple-element.35), channel_id=1, source_target_pairs={{1,0},{2,1},{3,2},{4,3},{5,4},{6,5},{7,6},{8,7},{9,8},{10,9},{11,1... | collective-permute-start | bytes 73736 | tf_op jit(solution)/shard_map/ppermute | solution.py:556
  98.5 0.7 copy-start.6

commit v7 on v6

--- a/solution.py
+++ b/solution.py
@@ -16,6 +16,8 @@
 TILE = 256
 GROUP = 4
 EDGE_COST = 54_000_000_000
+
+token = jax.ShapeDtypeStruct((8, LANES), jnp.float32)
 
 
 prior_var = 0.1
@@ -57,7 +59,8 @@
 
 
 def pack_edges_kernel(tiles, group, flags_hbm, phases_ref, *refs):
-    *out_refs, flags_ref, stacked_ref, near_ref, flag_sem, in_sem = refs
+    *out_refs, token_ref, flags_ref, stacked_ref, near_ref, flag_sem, in_sem = refs
+    token_ref[...] = jnp.zeros_like(token_ref)
     planes = len(out_refs)
     parts = planes * group
     ifgs, blocks = flags_ref.shape
@@ -117,8 +120,8 @@
     return pl.pallas_call(
         functools.partial(pack_edges_kernel, tiles, group),
         in_specs=[hbm, hbm],
-        out_specs=[pl.BlockSpec(memory_space=pltpu.VMEM)] * planes,
-        out_shape=[jax.ShapeDtypeStruct((group, ifgs, width), jnp.bfloat16)] * planes,
+        out_specs=[pl.BlockSpec(memory_space=pltpu.VMEM)] * (planes + 1),
+        out_shape=[jax.ShapeDtypeStruct((group, ifgs, width), jnp.bfloat16)] * planes + [token],
         scratch_shapes=[
             pltpu.VMEM(flags.shape, jnp.int32),
             pltpu.VMEM((parts * ifgs, LANES), jnp.float32),
@@ -207,7 +210,8 @@
     return jnp.dot(a, b, precision=lax.Precision.HIGHEST, preferred_element_type=jnp.float32)
 
 
-def operator_kernel(pairs_ref, other_ref, out_ref, other_out_ref, normal_ref, inverse_ref):
+def operator_kernel(pairs_ref, other_ref, out_ref, other_out_ref, token_ref, normal_ref, inverse_ref):
+    token_ref[...] = jnp.zeros_like(token_ref)
     ifgs = pairs_ref.shape[1]
     size = normal_ref.shape[0]
     epoch = lax.broadcasted_iota(jnp.int32, (size, ifgs), 0)
@@ -265,8 +269,8 @@
     return pl.pallas_call(
         operator_kernel,
         in_specs=[vmem] * 2,
-        out_specs=[vmem] * 2,
-        out_shape=[jax.ShapeDtypeStruct((ifgs + EXTRA, ifgs), jnp.bfloat16)] * 2,
+        out_specs=[vmem] * 3,
+        out_shape=[jax.ShapeDtypeStruct((ifgs + EXTRA, ifgs), jnp.bfloat16)] * 2 + [token],
         scratch_shapes=[pltpu.VMEM((size, size), jnp.float32), pltpu.VMEM((size, size), jnp.float32)],
         compiler_params=pltpu.CompilerParams(vmem_limit_bytes=medium),
         name="misfit_operator",
@@ -327,105 +331,159 @@
     out_ref[1, at : at + 8, :] = velocity - north_c * north
 
 
-def edges_kernel(tiles, group, *refs):
+def fixed_kernel(tiles, index_ref, weight_ref, cover_ref, north_ref, back_ref, onward_ref):
+    taps, rows, _ = index_ref.shape
+    place = lax.broadcasted_iota(jnp.int32, (tiles, LANES), 0) == lax.broadcasted_iota(jnp.int32, (tiles, LANES), 1)
+    for half, to_ref in enumerate((back_ref, onward_ref)):
+        edge = slice(half * (rows - tiles), half * (rows - tiles) + tiles)
+        outermost = half * (rows - 1)
+        row = slice(outermost, outermost + 1)
+        to_ref[:tiles, :] = north_ref[edge, :]
+        total = sum(weight_ref[b, row, :] for b in range(taps))
+        for b in range(taps):
+            to_ref[tiles + b : tiles + b + 1, :] = index_ref[b, row, :].astype(jnp.float32)
+            to_ref[tiles + taps + b : tiles + taps + b + 1, :] = weight_ref[b, row, :] / total
+        at = tiles + 2 * taps
+        cover = jnp.where(place, jnp.broadcast_to(cover_ref[edge, :].astype(jnp.float32), (tiles, LANES)), 0.0)
+        to_ref[at : at + 1, :] = jnp.sum(cover, axis=0, keepdims=True)
+        to_ref[at + 1 :, :] = jnp.zeros((to_ref.shape[0] - at - 1, LANES), jnp.float32)
+
+
+def fixed(cells, tiles):
+    rows = -(-(tiles + 2 * cells[0].shape[0] + 1) // 8) * 8
+    vmem = pl.BlockSpec(memory_space=pltpu.VMEM)
+    return pl.pallas_call(
+        functools.partial(fixed_kernel, tiles),
+        in_specs=[vmem] * 4,
+        out_specs=[vmem] * 2,
+        out_shape=[jax.ShapeDtypeStruct((rows, LANES), jnp.float32)] * 2,
+        compiler_params=pltpu.CompilerParams(vmem_limit_bytes=medium),
+        name="edge_inputs",
+    )(*cells)
+
+
+def edges_kernel(tiles, group, los_ref, *refs):
     stack_refs = refs[:group]
-    operator_ref, index_ref, weight_ref, cover_ref, north_ref, seam_ref, own_ref, ends_ref, back_ref, onward_ref, fields_ref = refs[group:]
+    operator_ref, index_ref, weight_ref, *fixed_refs, kept_ref, back_ref, onward_ref, fields_ref = refs[group:]
     width = stack_refs[0].shape[1]
     count = width // LANES
-    taps, rows, _ = index_ref.shape
+    rows = index_ref.shape[1]
     none = jnp.zeros((2, 1, LANES), jnp.float32)
     fields_ref[:, :1, :] = none
     fields_ref[:, count + 1 : count + 2, :] = none
     invert_tiles(stack_refs, 0, width, operator_ref, fields_ref, 1)
-    seam_ref[...] = fields_ref[:, tiles : tiles + 4, :]
-    ends_ref[:, :1, :] = fields_ref[:, 1:2, :]
-    ends_ref[:, 1:, :] = fields_ref[:, count : count + 1, :]
-    for half, to_ref in enumerate((back_ref, onward_ref)):
+    seam = 2 * tiles
+    kept_ref[:, seam : seam + 4, :] = fields_ref[:, tiles : tiles + 4, :]
+    kept_ref[:, seam + 4 : seam + 5, :] = fields_ref[:, 1:2, :]
+    kept_ref[:, seam + 5 : seam + 6, :] = fields_ref[:, count : count + 1, :]
+    kept_ref[:, seam + 6 :, :] = jnp.zeros((2, kept_ref.shape[1] - seam - 6, LANES), jnp.float32)
+    tracks = los_ref.shape[0]
+    scalars = [los_ref[t, part] for part in (0, 2) for t in range(tracks)] + [los_ref[lax.axis_index("track"), 1]]
+    for k, scalar in enumerate(scalars):
+        row = seam + 8 + k
+        kept_ref[0, row : row + 1, :] = jnp.full((1, LANES), scalar, jnp.float32)
+    for half, (fixed_ref, to_ref) in enumerate(zip(fixed_refs, (back_ref, onward_ref))):
         first = half * (rows - tiles)
-        to_ref[:tiles, :] = north_ref[first : first + tiles, :]
-        to_ref[tiles : 2 * tiles, :] = jnp.broadcast_to(cover_ref[first : first + tiles, :].astype(jnp.float32), (tiles, LANES))
+        after = to_ref.shape[0] - fixed_ref.shape[0]
+        to_ref[after:, :] = fixed_ref[...]
         for r in range(0, tiles, 8):
             base = half * (tiles + 2) + r
             near = [[fields_ref[f, base + k : base + k + 8, :] for k in range(3)] for f in range(2)]
-            velocity, variance, total = resample(near, first + r, index_ref, weight_ref)
+            velocity, variance, _ = resample(near, first + r, index_ref, weight_ref)
             for f, values in enumerate((velocity, variance)):
-                own_ref[f, half * tiles + r : half * tiles + r + 8, :] = values
-                to_ref[(2 + f) * tiles + r : (2 + f) * tiles + r + 8, :] = values
-            if r == (tiles - 8 if half else 0):
-                outer = total[7:] if half else total[:1]
-        outermost = first + (tiles - 1 if half else 0)
-        at = 4 * tiles
-        for b in range(taps):
-            to_ref[at + b : at + b + 1, :] = index_ref[b, outermost : outermost + 1, :].astype(jnp.float32)
-            to_ref[at + taps + b : at + taps + b + 1, :] = weight_ref[b, outermost : outermost + 1, :] / outer
-        at += 2 * taps
+                kept_ref[f, half * tiles + r : half * tiles + r + 8, :] = values
+                to_ref[f * tiles + r : f * tiles + r + 8, :] = values
         for f in range(2):
-            to_ref[at + f : at + f + 1, :] = ends_ref[f, half : half + 1, :]
-        left = to_ref.shape[0] - at - 2
-        to_ref[at + 2 :, :] = jnp.zeros((left, LANES), jnp.float32)
-
-
-def edges(stacks, operator, cells, tiles):
+            to_ref[seam + f : seam + f + 1, :] = kept_ref[f, seam + 4 + half : seam + 5 + half, :]
+        to_ref[seam + 2 : after, :] = jnp.zeros((after - seam - 2, LANES), jnp.float32)
+
+
+def edges(los, stacks, operator, cells, both_fixed, tiles):
     rows = 2 * (tiles + 1)
-    payload = -(-(4 * tiles + 2 * cells[0].shape[0] + 2) // 8) * 8
-    shapes = [(2, 4, LANES), (2, 2 * tiles, LANES), (2, 2, LANES), (payload, LANES), (payload, LANES)]
+    payload = -(-(2 * tiles + 2) // 8) * 8 + both_fixed[0].shape[0]
+    sight = -(-(2 * los.shape[0] + 1) // 8) * 8
+    shapes = [(2, 2 * tiles + 8 + sight, LANES), (payload, LANES), (payload, LANES)]
     vmem = pl.BlockSpec(memory_space=pltpu.VMEM)
     return pl.pallas_call(
         functools.partial(edges_kernel, tiles, len(stacks)),
-        in_specs=[vmem] * (len(stacks) + 5),
-        out_specs=[vmem] * 5,
+        in_specs=[pl.BlockSpec(memory_space=pltpu.SMEM)] + [vmem] * (len(stacks) + 5),
+        out_specs=[vmem] * 3,
         out_shape=[jax.ShapeDtypeStruct(shape, jnp.float32) for shape in shapes],
         scratch_shapes=[pltpu.VMEM((2, -(-(rows + 2) // 8) * 8, LANES), jnp.float32)],
         compiler_params=pltpu.CompilerParams(vmem_limit_bytes=medium),
         cost_estimate=pl.CostEstimate(flops=EDGE_COST, bytes_accessed=0, transcendentals=0),
         name="edge_rows",
-    )(*stacks, operator, *cells)
-
-
-def inner_kernel(
-    tiles, los_ref, stack_ref, seam_ref, own_ref, ends_ref, before_ref, after_ref, operator_ref, index_ref, weight_ref, cover_ref,
-    north_ref, out_ref, fields_ref,
+    )(los, *stacks, operator, *cells[:2], *both_fixed)
+
+
+def finish_kernel(
+    tiles, tracks, kept_ref, before_ref, after_ref, index_ref, weight_ref, cover_ref, north_ref, out_ref
 ):
-    width = stack_ref.shape[1]
     taps, rows, _ = index_ref.shape
-    north_c = los_ref[lax.axis_index("track"), 1]
-    pixel_rows = width // LANES
-    fields_ref[:, 0:2, :] = seam_ref[:, 0:2, :]
-    fields_ref[:, pixel_rows + 2 : pixel_rows + 4, :] = seam_ref[:, 2:4, :]
+    seam = 2 * tiles
+    north_c = kept_ref[0, seam + 8 + 2 * tracks : seam + 9 + 2 * tracks, :]
+    place = lax.broadcasted_iota(jnp.int32, (8, LANES), 0) - lax.broadcasted_iota(jnp.int32, (8, LANES), 1)
     for half, from_ref in enumerate((before_ref, after_ref)):
+        fixed_ref = from_ref.at[-(-(seam + 2) // 8) * 8 :]
         edge = half * (tiles - 8)
         row = 7 * half
         outermost = half * (rows - 1)
         total = sum(weight_ref[b, outermost : outermost + 1, :] for b in range(taps))
-        at = 4 * tiles
-        theirs = [from_ref[at + 2 * taps + f : at + 2 * taps + f + 1, :] for f in range(2)]
-        mine = [ends_ref[f, half : half + 1, :] for f in range(2)]
         to_own = boundary(
             row,
             [index_ref[b, outermost : outermost + 1, :] for b in range(taps)],
             [weight_ref[b, outermost : outermost + 1, :] / total for b in range(taps)],
-            theirs,
+            [from_ref[seam + f : seam + f + 1, :] for f in range(2)],
             2 * half,
         )
         to_other = boundary(
             7 - row,
-            [from_ref[at + b : at + b + 1, :].astype(jnp.int32) for b in range(taps)],
-            [from_ref[at + taps + b : at + taps + b + 1, :] for b in range(taps)],
-            mine,
+            [fixed_ref[tiles + b : tiles + b + 1, :].astype(jnp.int32) for b in range(taps)],
+            [fixed_ref[tiles + taps + b : tiles + taps + b + 1, :] for b in range(taps)],
+            [kept_ref[f, seam + 4 + half : seam + 5 + half, :] for f in range(2)],
             2 - 2 * half,
         )
+        covers = fixed_ref[tiles + 2 * taps : tiles + 2 * taps + 1, :]
         for r in range(0, tiles, 8):
             first = half * (rows - tiles) + r
-            values = [own_ref[f, half * tiles + r : half * tiles + r + 8, :] for f in range(2)]
+            values = [kept_ref[f, half * tiles + r : half * tiles + r + 8, :] for f in range(2)]
             if r == edge:
                 values = [value + more for value, more in zip(values, to_own)]
             cover = cover_ref[first : first + 8, :].astype(jnp.float32)
-            store_cells(out_ref, tiles + first, *values, cover, north_ref[first : first + 8, :], north_c)
-            values = [from_ref[(2 + f) * tiles + r : (2 + f) * tiles + r + 8, :] for f in range(2)]
+            store_cells(out_ref, (1 + half) * tiles + r, *values, cover, north_ref[first : first + 8, :], north_c)
+            values = [from_ref[f * tiles + r : f * tiles + r + 8, :] for f in range(2)]
             if r == tiles - 8 - edge:
                 values = [value + more for value, more in zip(values, to_other)]
-            cover = from_ref[tiles + r : tiles + r + 8, :]
-            store_cells(out_ref, half * (rows + tiles) + r, *values, cover, from_ref[r : r + 8, :], north_c)
+            cover = jnp.sum(jnp.where(place == -r, jnp.broadcast_to(covers, (8, LANES)), 0.0), axis=1, keepdims=True)
+            store_cells(out_ref, 3 * half * tiles + r, *values, cover, fixed_ref[r : r + 8, :], north_c)
+    out_ref[:, 4 * tiles :, :] = kept_ref[:, seam:, :]
+
+
+def finish(kept, before, after, cells, tiles, tracks):
+    vmem = pl.BlockSpec(memory_space=pltpu.VMEM)
+    return pl.pallas_call(
+        functools.partial(finish_kernel, tiles, tracks),
+        in_specs=[vmem] * 7,
+        out_specs=vmem,
+        out_shape=jax.ShapeDtypeStruct((2, kept.shape[1] + 2 * tiles, LANES), jnp.float32),
+        compiler_params=pltpu.CompilerParams(vmem_limit_bytes=medium),
+        name="edge_cells",
+    )(kept, before, after, *cells)
+
+
+def inner_kernel(
+    tiles, tracks, stack_ref, edge_ref, operator_ref, index_ref, weight_ref, cover_ref, north_ref, out_ref, sight_ref, fields_ref
+):
+    width = stack_ref.shape[1]
+    rows = index_ref.shape[1]
+    seam = 4 * tiles
+    sight_ref[...] = edge_ref[0, seam + 8 :, :]
+    north_c = edge_ref[0, seam + 8 + 2 * tracks : seam + 9 + 2 * tracks, :]
+    pixel_rows = width // LANES
+    fields_ref[:, 0:2, :] = edge_ref[:, seam : seam + 2, :]
+    fields_ref[:, pixel_rows + 2 : pixel_rows + 4, :] = edge_ref[:, seam + 2 : seam + 4, :]
+    out_ref[:, : 2 * tiles, :] = edge_ref[:, : 2 * tiles, :]
+    out_ref[:, rows:, :] = edge_ref[:, 2 * tiles : 4 * tiles, :]
     invert_tiles([stack_ref], 0, width, operator_ref, fields_ref, 2)
     for r in range(0, rows - 2 * tiles, 8):
         near = [[fields_ref[f, r + k : r + k + 8, :] for k in range(3)] for f in range(2)]
@@ -435,25 +493,28 @@
         store_cells(out_ref, tiles + first, velocity, variance, cover, north_ref[first : first + 8, :], north_c)
 
 
-def inner(los, stack, seam, own, ends, before, after, operator, cells, tiles):
+def inner(stack, edge, operator, cells, tiles, tracks):
     rows = cells[0].shape[1]
     vmem = pl.BlockSpec(memory_space=pltpu.VMEM)
     return pl.pallas_call(
-        functools.partial(inner_kernel, tiles),
-        in_specs=[pl.BlockSpec(memory_space=pltpu.SMEM)] + [vmem] * 11,
-        out_specs=vmem,
-        out_shape=jax.ShapeDtypeStruct((2, rows + 2 * tiles, LANES), jnp.float32),
+        functools.partial(inner_kernel, tiles, tracks),
+        in_specs=[vmem] * 7,
+        out_specs=[vmem] * 2,
+        out_shape=[
+            jax.ShapeDtypeStruct((2, rows + 2 * tiles, LANES), jnp.float32),
+            jax.ShapeDtypeStruct((edge.shape[1] - 4 * tiles - 8, LANES), jnp.float32),
+        ],
         scratch_shapes=[pltpu.VMEM((2, -(-(rows - 2 * tiles + 2) // 8) * 8, LANES), jnp.float32)],
         compiler_params=pltpu.CompilerParams(vmem_limit_bytes=medium),
         name="inner_rows",
-    )(los, stack, seam, own, ends, before, after, operator, *cells)
-
-
-def solve_cells(vals_ref, los_ref):
+    )(stack, edge, operator, *cells)
+
+
+def solve_cells(of_tracks, sight_ref, tracks):
     a11 = a12 = a22 = b1 = b2 = 0.0
-    for t in range(vals_ref.shape[0]):
-        weight, target = vals_ref[t, 0], vals_ref[t, 1]
-        east_c, up_c = los_ref[t, 0], los_ref[t, 2]
+    for t, values_ref in of_tracks:
+        weight, target = values_ref[0], values_ref[1]
+        east_c, up_c = sight_ref[pl.ds(t, 1), :], sight_ref[pl.ds(tracks + t, 1), :]
         by_east, by_up = weight * east_c, weight * up_c
         a11 = a11 + by_east * east_c
         a12 = a12 + by_east * up_c
@@ -466,7 +527,7 @@
     return (a22 * b1 - a12 * b2) / determ, (a11 * b2 - a12 * b1) / determ
 
 
-def final_kernel(tiles, own, los_ref, vals_ref, north_ref, before_ref, after_ref, east_up_ref, strain_ref, work_ref):
+def final_kernel(tiles, own, tracks, sight_ref, own_ref, other_ref, north_ref, before_ref, after_ref, east_up_ref, strain_ref, work_ref):
     rows = north_ref.shape[0]
     lane = lax.broadcasted_iota(jnp.int32, (rows, LANES), 1)
     tile = lax.broadcasted_iota(jnp.int32, (rows, LANES), 0) % tiles
@@ -478,15 +539,21 @@
         previous = jnp.where(lane == 0, pltpu.roll(left, 1, 1), pltpu.roll(field, 1, 1))
         return following - previous
 
-    wide_east, wide_up = solve_cells(vals_ref, los_ref)
-    wide_north = jnp.concatenate([before_ref[:tiles, :], north_ref[...], after_ref[:tiles, :]], axis=0)
+    here = lax.axis_index("track")
+    if other_ref.shape[0] == 1:
+        of_tracks = [(here, own_ref), (1 - here, other_ref.at[0])]
+    else:
+        of_tracks = [(t, other_ref.at[t]) for t in range(other_ref.shape[0])]
+    wide_east, wide_up = solve_cells(of_tracks, sight_ref, tracks)
+    at = -(-(2 * tiles + 2) // 8) * 8
+    wide_north = jnp.concatenate([before_ref[at : at + tiles, :], north_ref[...], after_ref[at : at + tiles, :]], axis=0)
     east, north = (wide[tiles : tiles + rows] for wide in (wide_east, wide_north))
     work_ref[0] = east
     work_ref[1] = wide_up[tiles : tiles + rows]
     work_ref[2] = across(east) / 2.0
     work_ref[3] = (wide_north[2 * tiles :] - wide_north[:rows]) / 2.0
     work_ref[4] = (wide_east[2 * tiles :] - wide_east[:rows] + across(north)) / 4.0
-    start = lax.axis_index("track") * own
+    start = here * own
     for field in range(5):
         target, at = (east_up_ref, field) if field < 2 else (strain_ref, field - 2)
         for i in range(rows // tiles):
@@ -494,19 +561,19 @@
                 target[at, i : i + 1, j * LANES : (j + 1) * LANES] = work_ref[field, pl.ds(i * tiles + start + j, 1), :]
 
 
-def final(los, vals, north, before, after, tiles, own):
+def final(sight, vals, others, north, before, after, tiles, own, tracks):
     rows = north.shape[0]
     shape = (rows // tiles, own * LANES)
     vmem = pl.BlockSpec(memory_space=pltpu.VMEM)
     return pl.pallas_call(
-        functools.partial(final_kernel, tiles, own),
-        in_specs=[pl.BlockSpec(memory_space=pltpu.SMEM)] + [vmem] * 4,
+        functools.partial(final_kernel, tiles, own, tracks),
+        in_specs=[vmem] * 6,
         out_specs=[vmem] * 2,
         out_shape=[jax.ShapeDtypeStruct((2, *shape), jnp.float32), jax.ShapeDtypeStruct((3, *shape), jnp.float32)],
         scratch_shapes=[pltpu.VMEM((5, rows, LANES), jnp.float32)],
         compiler_params=pltpu.CompilerParams(vmem_limit_bytes=medium),
         name="solve_and_strain",
-    )(los, vals, north, before, after)
+    )(sight, vals, others, north, before, after)
 
 
 def per_device(phases, coherent, pairs, res_index, res_weight, coverage, los, north):
@@ -518,23 +585,23 @@
     group = GROUP if parts % GROUP == 0 else parts
     planes = parts // group
     plane, column = jnp.divmod(lax.axis_index("pix").astype(jnp.int32), group)
-    packed = pack_edges(phases[0], coherent[0], parts, group, tiles)
-    later_pairs, _ = lax.optimization_barrier((pairs[0], packed[0]))
+    *packed, packed_token = pack_edges(phases[0], coherent[0], parts, group, tiles)
+    later_pairs, _ = lax.optimization_barrier((pairs[0], packed_token))
     steps_j, steps_s = jnp.meshgrid(jnp.arange(group), jnp.arange(planes), indexing="ij")
     sources = (partner_back(plane, steps_s, planes) * group + partner_back(column, steps_j, group)).reshape(-1)
     edge_pairs = jnp.take(later_pairs.reshape(parts, -1, 2), sources, axis=0).reshape(-1, 2)
-    operator, edge_operator = setup_track(later_pairs, edge_pairs)
+    operator, edge_operator, formed_token = setup_track(later_pairs, edge_pairs)
     ids = [(z, c) for z in range(planes) for c in range(group)]
-    arrived = [packed[0]]
-    for s in range(1, planes):
+    arrived = [packed[0]] * planes
+    for s in reversed(range(1, planes)):
         far = [(z * group + c, partner(z, s, planes) * group + c) for z, c in ids]
-        arrived.append(lax.ppermute(packed[s], "pix", far))
-    by_column = regroup(edge_operator, arrived, group)
+        arrived[s] = lax.ppermute(packed[s], "pix", far)
+    by_column = regroup(formed_token, arrived, group)
     pieces = [by_column[0]]
     for j in range(1, group):
         near = [(z * group + c, z * group + partner(c, j, group)) for z, c in ids]
         pieces.append(lax.ppermute(by_column[j], "pix", near))
-    later_flags, *_ = lax.optimization_barrier((coherent[0], packed[0], operator))
+    later_flags, *_ = lax.optimization_barrier((coherent[0], formed_token))
     inner_stack = lax.all_to_all(
         pack_inner(phases[0], later_flags, parts, tiles), "pix", split_axis=0, concat_axis=0, tiled=True
     )
@@ -551,12 +618,18 @@
 
     onward = [(i, i + 1) for i in range(parts - 1)]
     back = [(j, i) for i, j in onward]
-    seam, own, ends, for_before, for_after = edges([flat(piece) for piece in pieces], edge_operator, cells, tiles)
+    kept, for_before, for_after = edges(
+        los, [flat(piece) for piece in pieces], edge_operator, cells, fixed(cells, tiles), tiles
+    )
     before = lax.ppermute(for_after, "pix", onward)
     after = lax.ppermute(for_before, "pix", back)
-    vals = inner(los, flat(inner_stack), seam, own, ends, before, after, operator, cells, tiles)
-    vals = lax.all_gather(vals, "track", axis=0)
-    return tuple(final(los, vals, north_cells, before, after, tiles, tiles // tracks))
+    edge_vals = finish(kept, before, after, cells, tiles, tracks)
+    vals, sight = inner(flat(inner_stack), edge_vals, operator, cells, tiles, tracks)
+    if tracks == 2:
+        others = lax.ppermute(vals, "track", [(0, 1), (1, 0)])[None]
+    else:
+        others = lax.all_gather(vals, "track", axis=0)
+    return tuple(final(sight, vals, others, north_cells, before, after, tiles, tiles // tracks, tracks))
 
 
 def solution(mesh):

time: 108 us -> 105 us (0.972)
  waiting for transfers between devices: 40.9 us -> 54.3 us
  starting transfers between devices: 28.9 us -> 20.7 us
  blocking collectives: 5.12 us -> 0 us
  local copies, waits for them, and re-layouts: 8.46 us -> 6.92 us
    ppermute x1, waiting for transfers between devices: 13.6 us -> 24 us  [per_device(): before = lax.ppermute(for_after, 'pix', onward)]
    ppermute x1, starting transfers between devices: 14.5 us -> 4.54 us  [per_device(): after = lax.ppermute(for_before, 'pix', back)]
    all_gather x1 -> x0, blocking collectives: 5.12 us -> none  [per_device(): vals = lax.all_gather(vals, 'track', axis=0)]
    ppermute x3 -> x4, waiting for transfers between devices: 4.82 us -> 7.52 us  [the longest x3 4.59 us: per_device(): arrived[s] = lax.ppermute(packed[s], 'pix', far)]
    ppermute x3 -> x4, starting transfers between devices: 3.55 us -> 5.13 us  [the longest x3 3.55 us: per_device(): arrived[s] = lax.ppermute(packed[s], 'pix', far)]
    unnamed x24 -> x22, local copies, waits for them, and re-layouts: 7.28 us -> 5.73 us
    pallas_call x3 -> x5, Pallas kernels: 12.4 us -> 11.6 us  [the longest x1 9.37 us: setup_track(): pl.pallas_call(operator_kernel, in_specs=[vmem] * 2, out_specs=[vmem] * 3...]
  transfers between devices with their start and end apart: 9 -> 10, of which waited for: 5 -> 6; matrix products, arithmetic and copies ran while one was open for 3% -> 3% of each run, Pallas kernels for 16% -> 17%
where the time goes in v7:
time: 105 us
  waiting for transfers between devices  54.3 us (52%)
  Pallas kernels  22.2 us (21%)
  starting transfers between devices  20.7 us (20%)
  local copies, waits for them, and re-layouts  6.92 us (7%)
    ppermute x1, waiting for transfers between devices, per_device(): before = lax.ppermute(for_after, 'pix', onward)  24 us
    ppermute x3, waiting for transfers between devices, per_device(): pieces.append(lax.ppermute(by_column[j], 'pix', near))  22.4 us
    pallas_call x1, Pallas kernels, setup_track(): pl.pallas_call(operator_kernel, in_specs=[vmem] * 2, out_specs=[vmem] * 3...  9.37 us
    all_to_all x1, starting transfers between devices, per_device(): lax.all_to_all(pack_inner(phases[0], later_flags, parts, tiles), 'pix', s...  7.2 us
    unnamed x22, local copies, waits for them, and re-layouts  5.73 us
    ppermute x3, waiting for transfers between devices, per_device(): arrived[s] = lax.ppermute(packed[s], 'pix', far)  4.59 us
    ppermute x1, starting transfers between devices, per_device(): after = lax.ppermute(for_before, 'pix', back)  4.54 us
    pallas_call x1, Pallas kernels, pack_inner(): pl.pallas_call(functools.partial(pack_inner_kernel, reach), in_specs=[hbm...  3.95 us
  transfers between devices with their start and end apart: 10, of which 6 were waited for; matrix products, arithmetic and copies ran while one was open for 3% of the time, Pallas kernels for 17%

profile of v7, /device:TPU:16, one launch (start us, length us, event | category | flops | bytes accessed | tf_op | source)
XLA Modules:
  0.0 105.0 jit_solution(6779408404834927904)
XLA Ops:
  0.6 0.0 copy-start.2
  0.6 2.8 %pack_edges.1 = (bf16[4,16,2304]{2,1,0:T(8,128)(2,1)S(1)}, bf16[4,16,2304]{2,1,0:T(8,128)(2,1)}, bf16[4,16,2304]{2,1,0:T(8,128)(2,1)}, bf16[4,16,2304]{2,1,0:T(8,128)(2,1)}, f32[8,128]{1,0:T(8,128)}) custom-call(s32[16,1024]{1,0:T(8,128)} %bitcast.43, bf16[16,131072]{1,0:T(8,128)(2,1)} %bitcast.41), custom_call_target="tpu_custom_call" | custom-call | tf_op jit(solution)/shard_map/pack_edges/pallas_call | solution.py:120
  3.5 1.6 %collective-permute-start = (bf16[4,16,2304]{2,1,0:T(8,128)(2,1)}, bf16[4,16,2304]{2,1,0:T(8,128)(2,1)}, u32[]{:S(2)}, u32[]{:S(2)}) collective-permute-start(bf16[4,16,2304]{2,1,0:T(8,128)(2,1)} %get-tuple-element.24), channel_id=1, source_target_pairs={{0,4},{1,5},{2,6},{3,7},{4,0},{5,1},{6,2},{7,3},{8,12},{9,13},{10,... | collective-permute-start | bytes 884744 | tf_op jit(solution)/shard_map/ppermute | solution.py:598
  5.1 0.3 collective-permute-start.1
  5.4 1.6 %collective-permute-start.2 = (bf16[4,16,2304]{2,1,0:T(8,128)(2,1)}, bf16[4,16,2304]{2,1,0:T(8,128)(2,1)}, u32[]{:S(2)}, u32[]{:S(2)}) collective-permute-start(bf16[4,16,2304]{2,1,0:T(8,128)(2,1)} %get-tuple-element.26), channel_id=1, source_target_pairs={{0,12},{1,13},{2,14},{3,15},{4,8},{5,9},{6,10},{7,11},{8,4},{9,5},... | collective-permute-start | bytes 884744 | tf_op jit(solution)/shard_map/ppermute | solution.py:598
  7.0 0.1 broadcast_add_fusion
  7.1 0.1 add.44
  7.2 0.1 add.42
  7.3 0.0 copy-done.2
  7.3 0.1 reshape.83
  7.4 0.6 gather_fusion
  8.0 0.1 gather.7
  8.1 0.1 broadcast_in_dim.25
  8.2 0.1 broadcast_in_dim.26
  8.3 9.4 %misfit_operator.1 = (bf16[272,256]{1,0:T(8,128)(2,1)S(1)}, bf16[272,256]{1,0:T(8,128)(2,1)S(1)}, f32[8,128]{1,0:T(8,128)S(1)}) custom-call(s32[2,256]{1,0:T(2,128)S(1)} %bitcast.39, s32[2,256]{1,0:T(2,128)S(1)} %select_bitcast_fusion.other_ref), custom_call_target="tpu_custom_call" | custom-call | tf_op jit(solution)/shard_map/misfit_operator/pallas_call | solution.py:269
  17.6 0.0 copy-start.5
  17.6 0.7 copy-done.5
  18.3 3.9 %pack_inner.1 = bf16[16,16,5888]{2,1,0:T(8,128)(2,1)} custom-call(s32[16,1024]{1,0:T(8,128)} %bitcast.44, bf16[16,131072]{1,0:T(8,128)(2,1)} %bitcast.42), custom_call_target="tpu_custom_call" | custom-call | tf_op jit(solution)/shard_map/pack_inner/pallas_call | solution.py:192
  22.3 0.0 copy-start.9
  22.3 0.0 copy-start.8
  22.3 0.0 copy-start.7
  22.3 7.2 %all-to-all-start = ((bf16[16,16,5888]{2,1,0:T(8,128)(2,1)}), bf16[16,16,5888]{2,1,0:T(8,128)(2,1)S(1)}, u32[]{:S(2)}, u32[]{:S(2)}) async-start(bf16[16,16,5888]{2,1,0:T(8,128)(2,1)} %pack_inner.1), calls=%async_computation | async-start | bytes 6029312 | tf_op jit(solution)/shard_map/all_to_all | solution.py:605
  29.5 0.0 collective-permute-done.refs_1_
  29.5 0.0 collective-permute-done.1.refs_2_
  29.5 4.6 %collective-permute-done.2.refs_3_ = bf16[4,16,2304]{2,1,0:T(8,128)(2,1)} collective-permute-done((bf16[4,16,2304]{2,1,0:T(8,128)(2,1)}, bf16[4,16,2304]{2,1,0:T(8,128)(2,1)}, u32[]{:S(2)}, u32[]{:S(2)}) %collective-permute-start.2) | collective-permute-done | bytes 294944 | tf_op jit(solution)/shard_map/ppermute | solution.py:598
  34.1 2.1 %regroup.1 = (bf16[4,16,2304]{2,1,0:T(8,128)(2,1)S(1)}, bf16[4,16,2304]{2,1,0:T(8,128)(2,1)}, bf16[4,16,2304]{2,1,0:T(8,128)(2,1)}, bf16[4,16,2304]{2,1,0:T(8,128)(2,1)}) custom-call(f32[8,128]{1,0:T(8,128)S(1)} %get-tuple-element.21.after_ref, bf16[4,16,2304]{2,1,0:T(8,128)(2,1)S(1)} %get-tuple-element.23.refs_0_, ...), custom_call_target="tpu_custom_call" | custom-call | tf_op jit(solution)/shard_map/regroup/pallas_call | solution.py:149
  36.2 0.0 copy-start.3
  36.2 0.7 copy-done.3
  36.9 0.0 collective-permute-start.3
  36.9 1.6 %collective-permute-start.4 = (bf16[4,16,2304]{2,1,0:T(8,128)(2,1)}, bf16[4,16,2304]{2,1,0:T(8,128)(2,1)}, u32[]{:S(2)}, u32[]{:S(2)}) collective-permute-start(bf16[4,16,2304]{2,1,0:T(8,128)(2,1)} %get-tuple-element.29), channel_id=1, source_target_pairs={{0,2},{1,3},{2,0},{3,1},{4,6},{5,7},{6,4},{7,5},{8,10},{9,11},{10,... | collective-permute-start | bytes 884744 | tf_op jit(solution)/shard_map/ppermute | solution.py:603
  38.5 0.3 collective-permute-start.5
  38.8 0.9 copy.23
  39.7 0.9 copy.22
  40.6 0.0 copy-done.9
  40.7 0.1 reshape.101.cover_ref
  40.7 0.0 copy-done.8
  40.7 0.1 edge_inputs.1
  40.8 0.0 collective-permute-done.3
  40.8 14.4 %collective-permute-done.4 = bf16[4,16,2304]{2,1,0:T(8,128)(2,1)} collective-permute-done((bf16[4,16,2304]{2,1,0:T(8,128)(2,1)}, bf16[4,16,2304]{2,1,0:T(8,128)(2,1)}, u32[]{:S(2)}, u32[]{:S(2)}) %collective-permute-start.4) | collective-permute-done | bytes 294944 | tf_op jit(solution)/shard_map/ppermute | solution.py:603
  55.2 8.0 %collective-permute-done.5 = bf16[4,16,2304]{2,1,0:T(8,128)(2,1)} collective-permute-done((bf16[4,16,2304]{2,1,0:T(8,128)(2,1)}, bf16[4,16,2304]{2,1,0:T(8,128)(2,1)}, u32[]{:S(2)}, u32[]{:S(2)}) %collective-permute-start.5) | collective-permute-done | bytes 294944 | tf_op jit(solution)/shard_map/ppermute | solution.py:603
  63.2 0.0 copy-done.7
  63.2 0.0 copy-start.4
  63.2 1.0 copy-done.4
  64.2 0.0 copy-start.6
  64.2 0.9 copy-done.6
  65.1 1.8 %edge_rows.1 = (f32[2,32,128]{2,1,0:T(8,128)S(1)}, f32[48,128]{1,0:T(8,128)S(1)}, f32[48,128]{1,0:T(8,128)S(1)}) custom-call(f32[2,3]{1,0:T(2,128)S(1)} %copy-done.7, bf16[64,2304]{1,0:T(8,128)(2,1)S(1)} %bitcast.40, bf16[64,2304]{1,0:T(8,128)(2,1)} %bitcast.8.refs_1_, bf16[64,2304]{1,0:T(8,128)(2,1)} %bitcast.9.refs_2_, bf16[64,2304]{1,0:T(8,128)(2,1)} %bitcast.10.refs_3_, ...), custom_call_target="tpu_custom_call" | custom-call | flops 54000001024 | tf_op jit(solution)/shard_map/edge_rows/pallas_call | solution.py:407
  66.8 1.9 %collective-permute-start.6 = (f32[48,128]{1,0:T(8,128)S(1)}, f32[48,128]{1,0:T(8,128)S(1)}, u32[]{:S(2)}, u32[]{:S(2)}) collective-permute-start(f32[48,128]{1,0:T(8,128)S(1)} %get-tuple-element.35), channel_id=1, source_target_pairs={{0,1},{1,2},{2,3},{3,4},{4,5},{5,6},{6,7},{7,8},{8,9},{9,10},{10,1... | collective-permute-start | bytes 73736 | tf_op jit(solution)/shard_map/ppermute | solution.py:624
  68.8 4.5 %collective-permute-start.7 = (f32[48,128]{1,0:T(8,128)S(1)}, f32[48,128]{1,0:T(8,128)S(1)}, u32[]{:S(2)}, u32[]{:S(2)}) collective-permute-start(f32[48,128]{1,0:T(8,128)S(1)} %get-tuple-element.36), channel_id=1, source_target_pairs={{1,0},{2,1},{3,2},{4,3},{5,4},{6,5},{7,6},{8,7},{9,8},{10,9},{11,1... | collective-permute-start | bytes 73736 | tf_op jit(solution)/shard_map/ppermute | solution.py:625
  73.3 24.0 %collective-permute-done.6.before_ref = f32[48,128]{1,0:T(8,128)S(1)} collective-permute-done((f32[48,128]{1,0:T(8,128)S(1)}, f32[48,128]{1,0:T(8,128)S(1)}, u32[]{:S(2)}, u32[]{:S(2)}) %collective-permute-start.6) | collective-permute-done | bytes 24608 | tf_op jit(solution)/shard_map/ppermute | solution.py:624
  97.4 0.0 collective-permute-done.7.after_ref
  97.4 0.2 edge_cells.1.edge_ref
  97.5 0.0 copy-start
  97.5 0.6 copy-done
  98.2 0.4 all-to-all-done
  98.5 0.0 copy-start.1
  98.5 1.1 %inner_rows.1 = (f32[2,80,128]{2,1,0:T(8,128)S(1)}, f32[8,128]{1,0:T(8,128)S(1)}) custom-call(bf16[256,5888]{1,0:T(8,128)(2,1)S(1)} %bitcast.28, f32[2,48,128]{2,1,0:T(8,128)S(1)} %edge_cells.1.edge_ref, bf16[272,256]{1,0:T(8,128)(2,1)S(1)} %get-tuple-element.37.operator_ref, s32[4,64,128]{2,1,0:T(8,128)S(1)} %bitcast.32, f32[4,64,128]{2,1,0:T(8,128)S(1)} %bitcast.36, ...), custom_call_target="tpu_custom_call" | custom-call | tf_op jit(solution)/shard_map/inner_rows/pallas_call | solution.py:499
  99.7 1.6 %collective-permute-start.8 = (f32[2,80,128]{2,1,0:T(8,128)S(1)}, f32[2,80,128]{2,1,0:T(8,128)S(1)}, u32[]{:S(2)}, u32[]{:S(2)}) collective-permute-start(f32[2,80,128]{2,1,0:T(8,128)S(1)} %get-tuple-element.39.own_ref), channel_id=1, source_target_pairs={{0,16},{16,0},{1,17},{17,1},{2,18},{18,2},{3,19},{19,3},{4,20},{20... | collective-permute-start | bytes 245768 | tf_op jit(solution)/shard_map/ppermute | solution.py:629
  101.2 2.9 %collective-permute-done.8 = f32[2,80,128]{2,1,0:T(8,128)S(1)} collective-permute-done((f32[2,80,128]{2,1,0:T(8,128)S(1)}, f32[2,80,128]{2,1,0:T(8,128)S(1)}, u32[]{:S(2)}, u32[]{:S(2)}) %collective-permute-start.8) | collective-permute-done | bytes 81952 | tf_op jit(solution)/shard_map/ppermute | solution.py:629
  104.2 0.0 copy-done.1
  104.2 0.8 solve_and_strain.1
  (8 shorter events, 0.1 us)
Async XLA Ops:
  0.6 6.6 %copy-start.2 = (s32[1,256,2]{1,2,0:T(2,128)S(1)}, s32[1,256,2]{1,2,0:T(2,128)}, u32[]{:S(2)}) copy-start(s32[1,256,2]{1,2,0:T(2,128)} %param.10) | copy-start | bytes 6148
  3.5 26.0 %collective-permute-start = (bf16[4,16,2304]{2,1,0:T(8,128)(2,1)}, bf16[4,16,2304]{2,1,0:T(8,128)(2,1)}, u32[]{:S(2)}, u32[]{:S(2)}) collective-permute-start(bf16[4,16,2304]{2,1,0:T(8,128)(2,1)} %get-tuple-element.24), channel_id=1, source_target_pairs={{0,4},{1,5},{2,6},{3,7},{4,0},{5,1},{6,2},{7,3},{8,12},{9,13},{10,... | collective-permute-start | bytes 884744 | tf_op jit(solution)/shard_map/ppermute | solution.py:598
  5.1 24.4 %collective-permute-start.1 = (bf16[4,16,2304]{2,1,0:T(8,128)(2,1)}, bf16[4,16,2304]{2,1,0:T(8,128)(2,1)}, u32[]{:S(2)}, u32[]{:S(2)}) collective-permute-start(bf16[4,16,2304]{2,1,0:T(8,128)(2,1)} %get-tuple-element.25), channel_id=1, source_target_pairs={{0,8},{1,9},{2,10},{3,11},{4,12},{5,13},{6,14},{7,15},{8,0},{9,1},... | collective-permute-start | bytes 884744 | tf_op jit(solution)/shard_map/ppermute | solution.py:598
  5.4 28.7 %collective-permute-start.2 = (bf16[4,16,2304]{2,1,0:T(8,128)(2,1)}, bf16[4,16,2304]{2,1,0:T(8,128)(2,1)}, u32[]{:S(2)}, u32[]{:S(2)}) collective-permute-start(bf16[4,16,2304]{2,1,0:T(8,128)(2,1)} %get-tuple-element.26), channel_id=1, source_target_pairs={{0,12},{1,13},{2,14},{3,15},{4,8},{5,9},{6,10},{7,11},{8,4},{9,5},... | collective-permute-start | bytes 884744 | tf_op jit(solution)/shard_map/ppermute | solution.py:598
  17.6 0.7 copy-start.5
  22.3 18.4 %copy-start.9 = (s32[1,8,8]{2,1,0:T(8,128)S(1)}, s32[1,8,8]{2,1,0:T(8,128)}, u32[]{:S(2)}) copy-start(s32[1,8,8]{2,1,0:T(8,128)} %param.13) | copy-start | bytes 772
  22.3 18.4 %copy-start.8 = (f32[8,1024]{1,0:T(8,128)S(1)}, f32[8,1024]{1,0:T(8,128)}, u32[]{:S(2)}) copy-start(f32[8,1024]{1,0:T(8,128)} %param.15) | copy-start | bytes 98308
  22.3 40.9 %copy-start.7 = (f32[2,3]{1,0:T(2,128)S(1)}, f32[2,3]{1,0:T(2,128)}, u32[]{:S(2)}) copy-start(f32[2,3]{1,0:T(2,128)} %los_ref.1) | copy-start | bytes 76
  22.3 76.2 %all-to-all-start = ((bf16[16,16,5888]{2,1,0:T(8,128)(2,1)}), bf16[16,16,5888]{2,1,0:T(8,128)(2,1)S(1)}, u32[]{:S(2)}, u32[]{:S(2)}) async-start(bf16[16,16,5888]{2,1,0:T(8,128)(2,1)} %pack_inner.1), calls=%async_computation | async-start | bytes 6029312 | tf_op jit(solution)/shard_map/all_to_all | solution.py:605
  36.2 0.7 copy-start.3
  36.9 3.9 %collective-permute-start.3 = (bf16[4,16,2304]{2,1,0:T(8,128)(2,1)}, bf16[4,16,2304]{2,1,0:T(8,128)(2,1)}, u32[]{:S(2)}, u32[]{:S(2)}) collective-permute-start(bf16[4,16,2304]{2,1,0:T(8,128)(2,1)} %get-tuple-element.28), channel_id=1, source_target_pairs={{0,1},{1,0},{2,3},{3,2},{4,5},{5,4},{6,7},{7,6},{8,9},{9,8},{10,11... | collective-permute-start | bytes 884744 | tf_op jit(solution)/shard_map/ppermute | solution.py:603
  36.9 18.3 %collective-permute-start.4 = (bf16[4,16,2304]{2,1,0:T(8,128)(2,1)}, bf16[4,16,2304]{2,1,0:T(8,128)(2,1)}, u32[]{:S(2)}, u32[]{:S(2)}) collective-permute-start(bf16[4,16,2304]{2,1,0:T(8,128)(2,1)} %get-tuple-element.29), channel_id=1, source_target_pairs={{0,2},{1,3},{2,0},{3,1},{4,6},{5,7},{6,4},{7,5},{8,10},{9,11},{10,... | collective-permute-start | bytes 884744 | tf_op jit(solution)/shard_map/ppermute | solution.py:603
  38.5 24.7 %collective-permute-start.5 = (bf16[4,16,2304]{2,1,0:T(8,128)(2,1)}, bf16[4,16,2304]{2,1,0:T(8,128)(2,1)}, u32[]{:S(2)}, u32[]{:S(2)}) collective-permute-start(bf16[4,16,2304]{2,1,0:T(8,128)(2,1)} %get-tuple-element.30), channel_id=1, source_target_pairs={{0,3},{1,2},{2,1},{3,0},{4,7},{5,6},{6,5},{7,4},{8,11},{9,10},{10,... | collective-permute-start | bytes 884744 | tf_op jit(solution)/shard_map/ppermute | solution.py:603
  63.2 1.0 copy-start.4
  64.2 0.9 copy-start.6
  66.8 30.5 %collective-permute-start.6 = (f32[48,128]{1,0:T(8,128)S(1)}, f32[48,128]{1,0:T(8,128)S(1)}, u32[]{:S(2)}, u32[]{:S(2)}) collective-permute-start(f32[48,128]{1,0:T(8,128)S(1)} %get-tuple-element.35), channel_id=1, source_target_pairs={{0,1},{1,2},{2,3},{3,4},{4,5},{5,6},{6,7},{7,8},{8,9},{9,10},{10,1... | collective-permute-start | bytes 73736 | tf_op jit(solution)/shard_map/ppermute | solution.py:624
  68.8 28.6 %collective-permute-start.7 = (f32[48,128]{1,0:T(8,128)S(1)}, f32[48,128]{1,0:T(8,128)S(1)}, u32[]{:S(2)}, u32[]{:S(2)}) collective-permute-start(f32[48,128]{1,0:T(8,128)S(1)} %get-tuple-element.36), channel_id=1, source_target_pairs={{1,0},{2,1},{3,2},{4,3},{5,4},{6,5},{7,6},{8,7},{9,8},{10,9},{11,1... | collective-permute-start | bytes 73736 | tf_op jit(solution)/shard_map/ppermute | solution.py:625
  97.5 0.6 copy-start
  98.5 5.7 %copy-start.1 = (f32[48,128]{1,0:T(8,128)S(1)}, f32[48,128]{1,0:T(8,128)}, u32[]{:S(2)}) copy-start(f32[48,128]{1,0:T(8,128)} %copy-done) | copy-start | bytes 73732
  99.7 4.5 %collective-permute-start.8 = (f32[2,80,128]{2,1,0:T(8,128)S(1)}, f32[2,80,128]{2,1,0:T(8,128)S(1)}, u32[]{:S(2)}, u32[]{:S(2)}) collective-permute-start(f32[2,80,128]{2,1,0:T(8,128)S(1)} %get-tuple-element.39.own_ref), channel_id=1, source_target_pairs={{0,16},{16,0},{1,17},{17,1},{2,18},{18,2},{3,19},{19,3},{4,20},{20... | collective-permute-start | bytes 245768 | tf_op jit(solution)/shard_map/ppermute | solution.py:629

commit v8 on v7

--- a/solution.py
+++ b/solution.py
@@ -89,7 +89,7 @@
     ends[1].start()
     flag_copy.wait()
     plane = lax.axis_index("pix") // group
-    firsts = [(partner(plane, s, planes) * group + g) * span for s in range(planes) for g in range(group)]
+    firsts = [(partner(plane, -s % planes, planes) * group + g) * span for s in range(planes) for g in range(group)]
 
     def tile_out(n, start, keep):
         out_refs[n // group][n % group, :, start : start + 2 * MBLK] = keep
@@ -104,7 +104,7 @@
 
     ends[1].wait()
     for s in range(planes):
-        first_part = partner(plane, s, planes) * group
+        first_part = partner(plane, -s % planes, planes) * group
 
         @pl.loop(0, group, unroll=2)
         def _(g):
@@ -472,8 +472,9 @@
 
 
 def inner_kernel(
-    tiles, tracks, stack_ref, edge_ref, operator_ref, index_ref, weight_ref, cover_ref, north_ref, out_ref, sight_ref, fields_ref
+    tiles, tracks, span, stack_ref, edge_ref, operator_ref, index_ref, weight_ref, cover_ref, north_ref, *refs
 ):
+    *to_refs, sight_ref, fields_ref, out_ref = refs
     width = stack_ref.shape[1]
     rows = index_ref.shape[1]
     seam = 4 * tiles
@@ -493,18 +494,31 @@
         store_cells(out_ref, tiles + first, velocity, variance, cover, north_ref[first : first + 8, :], north_c)
 
 
-def inner(stack, edge, operator, cells, tiles, tracks):
+    here = lax.axis_index("track")
+    lines = rows // tiles + 2
+    for half, to_ref in zip((here, 1 - here), to_refs):
+        start = half * (tiles - span)
+        for i in range(lines):
+            to_ref[:, i * span : (i + 1) * span, :] = out_ref[:, pl.ds(i * tiles + start, span), :]
+        left = to_ref.shape[1] - lines * span
+        if left:
+            to_ref[:, lines * span :, :] = jnp.zeros((2, left, LANES), jnp.float32)
+
+
+def inner(stack, edge, operator, cells, tiles, tracks, span, copies):
     rows = cells[0].shape[1]
+    compact = -(-(rows // tiles + 2) * span // 8) * 8
     vmem = pl.BlockSpec(memory_space=pltpu.VMEM)
     return pl.pallas_call(
-        functools.partial(inner_kernel, tiles, tracks),
+        functools.partial(inner_kernel, tiles, tracks, span),
         in_specs=[vmem] * 7,
-        out_specs=[vmem] * 2,
-        out_shape=[
-            jax.ShapeDtypeStruct((2, rows + 2 * tiles, LANES), jnp.float32),
-            jax.ShapeDtypeStruct((edge.shape[1] - 4 * tiles - 8, LANES), jnp.float32),
+        out_specs=[vmem] * (copies + 1),
+        out_shape=[jax.ShapeDtypeStruct((2, compact, LANES), jnp.float32)] * copies
+        + [jax.ShapeDtypeStruct((edge.shape[1] - 4 * tiles - 8, LANES), jnp.float32)],
+        scratch_shapes=[
+            pltpu.VMEM((2, -(-(rows - 2 * tiles + 2) // 8) * 8, LANES), jnp.float32),
+            pltpu.VMEM((2, rows + 2 * tiles, LANES), jnp.float32),
         ],
-        scratch_shapes=[pltpu.VMEM((2, -(-(rows - 2 * tiles + 2) // 8) * 8, LANES), jnp.float32)],
         compiler_params=pltpu.CompilerParams(vmem_limit_bytes=medium),
         name="inner_rows",
     )(stack, edge, operator, *cells)
@@ -527,50 +541,58 @@
     return (a22 * b1 - a12 * b2) / determ, (a11 * b2 - a12 * b1) / determ
 
 
-def final_kernel(tiles, own, tracks, sight_ref, own_ref, other_ref, north_ref, before_ref, after_ref, east_up_ref, strain_ref, work_ref):
-    rows = north_ref.shape[0]
+def final_kernel(
+    tiles, span, own, tracks, sight_ref, own_ref, other_ref, north_ref, before_ref, after_ref, east_up_ref, strain_ref, work_ref, line_ref
+):
+    lines = north_ref.shape[0] // tiles
+    rows = lines * span
+    here = lax.axis_index("track")
+    start = here * (tiles - span)
+    at = -(-(2 * tiles + 2) // 8) * 8 + start
+    line_ref[:span, :] = before_ref[pl.ds(at, span), :]
+    for i in range(lines):
+        line_ref[(i + 1) * span : (i + 2) * span, :] = north_ref[pl.ds(i * tiles + start, span), :]
+    line_ref[rows + span : rows + 2 * span, :] = after_ref[pl.ds(at, span), :]
     lane = lax.broadcasted_iota(jnp.int32, (rows, LANES), 1)
-    tile = lax.broadcasted_iota(jnp.int32, (rows, LANES), 0) % tiles
+    tile = lax.broadcasted_iota(jnp.int32, (rows, LANES), 0) % span
 
     def across(field):
-        right = jnp.where(tile == tiles - 1, 0.0, pltpu.roll(field, rows - 1, 0))
+        right = jnp.where(tile == span - 1, 0.0, pltpu.roll(field, rows - 1, 0))
         left = jnp.where(tile == 0, 0.0, pltpu.roll(field, 1, 0))
         following = jnp.where(lane == LANES - 1, pltpu.roll(right, LANES - 1, 1), pltpu.roll(field, LANES - 1, 1))
         previous = jnp.where(lane == 0, pltpu.roll(left, 1, 1), pltpu.roll(field, 1, 1))
         return following - previous
 
-    here = lax.axis_index("track")
     if other_ref.shape[0] == 1:
         of_tracks = [(here, own_ref), (1 - here, other_ref.at[0])]
     else:
         of_tracks = [(t, other_ref.at[t]) for t in range(other_ref.shape[0])]
     wide_east, wide_up = solve_cells(of_tracks, sight_ref, tracks)
-    at = -(-(2 * tiles + 2) // 8) * 8
-    wide_north = jnp.concatenate([before_ref[at : at + tiles, :], north_ref[...], after_ref[at : at + tiles, :]], axis=0)
-    east, north = (wide[tiles : tiles + rows] for wide in (wide_east, wide_north))
+    wide_north = line_ref[...]
+    east, up, north = (wide[span : span + rows] for wide in (wide_east, wide_up, wide_north))
     work_ref[0] = east
-    work_ref[1] = wide_up[tiles : tiles + rows]
+    work_ref[1] = up
     work_ref[2] = across(east) / 2.0
-    work_ref[3] = (wide_north[2 * tiles :] - wide_north[:rows]) / 2.0
-    work_ref[4] = (wide_east[2 * tiles :] - wide_east[:rows] + across(north)) / 4.0
-    start = here * own
+    work_ref[3] = (wide_north[2 * span : 2 * span + rows] - wide_north[:rows]) / 2.0
+    work_ref[4] = (wide_east[2 * span : 2 * span + rows] - wide_east[:rows] + across(north)) / 4.0
+    first = here * own - start
     for field in range(5):
         target, at = (east_up_ref, field) if field < 2 else (strain_ref, field - 2)
-        for i in range(rows // tiles):
+        for i in range(lines):
             for j in range(own):
-                target[at, i : i + 1, j * LANES : (j + 1) * LANES] = work_ref[field, pl.ds(i * tiles + start + j, 1), :]
-
-
-def final(sight, vals, others, north, before, after, tiles, own, tracks):
-    rows = north.shape[0]
-    shape = (rows // tiles, own * LANES)
+                target[at, i : i + 1, j * LANES : (j + 1) * LANES] = work_ref[field, pl.ds(i * span + first + j, 1), :]
+
+
+def final(sight, vals, others, north, before, after, tiles, span, own, tracks):
+    lines = north.shape[0] // tiles
+    shape = (lines, own * LANES)
     vmem = pl.BlockSpec(memory_space=pltpu.VMEM)
     return pl.pallas_call(
-        functools.partial(final_kernel, tiles, own, tracks),
+        functools.partial(final_kernel, tiles, span, own, tracks),
         in_specs=[vmem] * 6,
         out_specs=[vmem] * 2,
         out_shape=[jax.ShapeDtypeStruct((2, *shape), jnp.float32), jax.ShapeDtypeStruct((3, *shape), jnp.float32)],
-        scratch_shapes=[pltpu.VMEM((5, rows, LANES), jnp.float32)],
+        scratch_shapes=[pltpu.VMEM((5, lines * span, LANES), jnp.float32), pltpu.VMEM(vals.shape[1:], jnp.float32)],
         compiler_params=pltpu.CompilerParams(vmem_limit_bytes=medium),
         name="solve_and_strain",
     )(sight, vals, others, north, before, after)
@@ -588,13 +610,13 @@
     *packed, packed_token = pack_edges(phases[0], coherent[0], parts, group, tiles)
     later_pairs, _ = lax.optimization_barrier((pairs[0], packed_token))
     steps_j, steps_s = jnp.meshgrid(jnp.arange(group), jnp.arange(planes), indexing="ij")
-    sources = (partner_back(plane, steps_s, planes) * group + partner_back(column, steps_j, group)).reshape(-1)
+    sources = (partner_back(plane, -steps_s % planes, planes) * group + partner_back(column, steps_j, group)).reshape(-1)
     edge_pairs = jnp.take(later_pairs.reshape(parts, -1, 2), sources, axis=0).reshape(-1, 2)
     operator, edge_operator, formed_token = setup_track(later_pairs, edge_pairs)
     ids = [(z, c) for z in range(planes) for c in range(group)]
     arrived = [packed[0]] * planes
-    for s in reversed(range(1, planes)):
-        far = [(z * group + c, partner(z, s, planes) * group + c) for z, c in ids]
+    for s in range(1, planes):
+        far = [(z * group + c, partner(z, planes - s, planes) * group + c) for z, c in ids]
         arrived[s] = lax.ppermute(packed[s], "pix", far)
     by_column = regroup(formed_token, arrived, group)
     pieces = [by_column[0]]
@@ -624,12 +646,16 @@
     before = lax.ppermute(for_after, "pix", onward)
     after = lax.ppermute(for_before, "pix", back)
     edge_vals = finish(kept, before, after, cells, tiles, tracks)
-    vals, sight = inner(flat(inner_stack), edge_vals, operator, cells, tiles, tracks)
+    own_tiles = tiles // tracks
     if tracks == 2:
-        others = lax.ppermute(vals, "track", [(0, 1), (1, 0)])[None]
+        span = own_tiles + 1
+        vals, for_other, sight = inner(flat(inner_stack), edge_vals, operator, cells, tiles, tracks, span, 2)
+        others = lax.ppermute(for_other, "track", [(0, 1), (1, 0)])[None]
     else:
+        span = tiles
+        vals, sight = inner(flat(inner_stack), edge_vals, operator, cells, tiles, tracks, span, 1)
         others = lax.all_gather(vals, "track", axis=0)
-    return tuple(final(sight, vals, others, north_cells, before, after, tiles, tiles // tracks, tracks))
+    return tuple(final(sight, vals, others, north_cells, before, after, tiles, span, own_tiles, tracks))
 
 
 def solution(mesh):

time: 105 us -> 105 us (level)
  waiting for transfers between devices: 54.3 us -> 52.8 us
    ppermute x3, waiting for transfers between devices: 4.59 us -> 0.01 us  [per_device(): arrived[s] = lax.ppermute(packed[s], 'pix', far)]
    ppermute x3, waiting for transfers between devices: 22.4 us -> 26.9 us  [per_device(): pieces.append(lax.ppermute(by_column[j], 'pix', near))]
    ppermute x1, starting transfers between devices: 1.92 us -> 4.95 us  [per_device(): before = lax.ppermute(for_after, 'pix', onward)]
    ppermute x1, starting transfers between devices: 4.54 us -> 1.92 us  [per_device(): after = lax.ppermute(for_before, 'pix', back)]
  transfers between devices with their start and end apart: 10 -> 10, of which waited for: 6 -> 4; matrix products, arithmetic and copies ran while one was open for 3% -> 3% of each run, Pallas kernels for 17% -> 17%
where the time goes in v8:
time: 105 us; the launch traced here: 104 us
  waiting for transfers between devices  52.8 us (50%)
  Pallas kernels  22.3 us (21%)
  starting transfers between devices  21.1 us (20%)
  local copies, waits for them, and re-layouts  7.18 us (7%)
    ppermute x3, waiting for transfers between devices, per_device(): pieces.append(lax.ppermute(by_column[j], 'pix', near))  26.9 us
    ppermute x1, waiting for transfers between devices, per_device(): before = lax.ppermute(for_after, 'pix', onward)  23.2 us
    pallas_call x1, Pallas kernels, setup_track(): pl.pallas_call(operator_kernel, in_specs=[vmem] * 2, out_specs=[vmem] * 3...  9.37 us
    all_to_all x1, starting transfers between devices, per_device(): lax.all_to_all(pack_inner(phases[0], later_flags, parts, tiles), 'pix', s...  6.75 us
    unnamed x22, local copies, waits for them, and re-layouts  5.75 us
    ppermute x1, starting transfers between devices, per_device(): before = lax.ppermute(for_after, 'pix', onward)  4.95 us
    ppermute x3, starting transfers between devices, per_device(): arrived[s] = lax.ppermute(packed[s], 'pix', far)  4 us
    pallas_call x1, Pallas kernels, pack_inner(): pl.pallas_call(functools.partial(pack_inner_kernel, reach), in_specs=[hbm...  3.95 us
  transfers between devices with their start and end apart: 10, of which 4 were waited for; matrix products, arithmetic and copies ran while one was open for 3% of the time, Pallas kernels for 17%

profile of v8, /device:TPU:16, one launch (start us, length us, event | category | flops | bytes accessed | tf_op | source)
XLA Modules:
  0.0 104.2 jit_solution(18368711746713281757)
XLA Ops:
  0.6 0.0 copy-start.2
  0.6 2.8 %pack_edges.1 = (bf16[4,16,2304]{2,1,0:T(8,128)(2,1)S(1)}, bf16[4,16,2304]{2,1,0:T(8,128)(2,1)}, bf16[4,16,2304]{2,1,0:T(8,128)(2,1)}, bf16[4,16,2304]{2,1,0:T(8,128)(2,1)}, f32[8,128]{1,0:T(8,128)}) custom-call(s32[16,1024]{1,0:T(8,128)} %bitcast.43, bf16[16,131072]{1,0:T(8,128)(2,1)} %bitcast.41), custom_call_target="tpu_custom_call" | custom-call | tf_op jit(solution)/shard_map/pack_edges/pallas_call | solution.py:120
  3.5 0.5 collective-permute-start
  4.0 3.5 %collective-permute-start.1 = (bf16[4,16,2304]{2,1,0:T(8,128)(2,1)}, bf16[4,16,2304]{2,1,0:T(8,128)(2,1)}, u32[]{:S(2)}, u32[]{:S(2)}) collective-permute-start(bf16[4,16,2304]{2,1,0:T(8,128)(2,1)} %get-tuple-element.26), channel_id=1, source_target_pairs={{0,8},{1,9},{2,10},{3,11},{4,12},{5,13},{6,14},{7,15},{8,0},{9,1},... | collective-permute-start | bytes 884744 | tf_op jit(solution)/shard_map/ppermute | solution.py:620
  7.5 0.0 collective-permute-start.2
  7.5 0.1 broadcast_in_dim.35
  7.6 0.1 broadcast_in_dim.41
  7.6 0.1 broadcast_in_dim.36
  7.7 0.1 broadcast_in_dim.40
  7.8 0.1 broadcast_in_dim.34
  7.9 0.0 copy-done.2
  7.9 0.1 reshape.125
  8.1 0.6 gather_fusion
  8.6 0.1 gather.7
  8.7 0.1 broadcast_in_dim.37
  8.8 0.1 broadcast_in_dim.38
  8.9 9.4 %misfit_operator.1 = (bf16[272,256]{1,0:T(8,128)(2,1)S(1)}, bf16[272,256]{1,0:T(8,128)(2,1)S(1)}, f32[8,128]{1,0:T(8,128)S(1)}) custom-call(s32[2,256]{1,0:T(2,128)S(1)} %bitcast.39, s32[2,256]{1,0:T(2,128)S(1)} %select_bitcast_fusion.other_ref), custom_call_target="tpu_custom_call" | custom-call | tf_op jit(solution)/shard_map/misfit_operator/pallas_call | solution.py:269
  18.3 0.0 copy-start.5
  18.3 0.7 copy-done.5
  19.0 4.0 %pack_inner.1 = bf16[16,16,5888]{2,1,0:T(8,128)(2,1)} custom-call(s32[16,1024]{1,0:T(8,128)} %bitcast.44, bf16[16,131072]{1,0:T(8,128)(2,1)} %bitcast.42), custom_call_target="tpu_custom_call" | custom-call | tf_op jit(solution)/shard_map/pack_inner/pallas_call | solution.py:192
  23.0 0.0 copy-start.9
  23.0 0.0 copy-start.8
  23.0 0.0 copy-start.7
  23.0 6.7 %all-to-all-start = ((bf16[16,16,5888]{2,1,0:T(8,128)(2,1)}), bf16[16,16,5888]{2,1,0:T(8,128)(2,1)S(1)}, u32[]{:S(2)}, u32[]{:S(2)}) async-start(bf16[16,16,5888]{2,1,0:T(8,128)(2,1)} %pack_inner.1), calls=%async_computation | async-start | bytes 6029312 | tf_op jit(solution)/shard_map/all_to_all | solution.py:627
  29.7 0.0 collective-permute-done.refs_1_
  29.7 0.0 collective-permute-done.1.refs_2_
  29.8 0.0 collective-permute-done.2.refs_3_
  29.8 2.1 %regroup.1 = (bf16[4,16,2304]{2,1,0:T(8,128)(2,1)S(1)}, bf16[4,16,2304]{2,1,0:T(8,128)(2,1)}, bf16[4,16,2304]{2,1,0:T(8,128)(2,1)}, bf16[4,16,2304]{2,1,0:T(8,128)(2,1)}) custom-call(f32[8,128]{1,0:T(8,128)S(1)} %get-tuple-element.22.after_ref, bf16[4,16,2304]{2,1,0:T(8,128)(2,1)S(1)} %get-tuple-element.24.refs_0_, ...), custom_call_target="tpu_custom_call" | custom-call | tf_op jit(solution)/shard_map/regroup/pallas_call | solution.py:149
  31.9 0.0 copy-start.3
  31.9 0.7 copy-done.3
  32.6 0.1 collective-permute-start.3
  32.8 1.5 %collective-permute-start.4 = (bf16[4,16,2304]{2,1,0:T(8,128)(2,1)}, bf16[4,16,2304]{2,1,0:T(8,128)(2,1)}, u32[]{:S(2)}, u32[]{:S(2)}) collective-permute-start(bf16[4,16,2304]{2,1,0:T(8,128)(2,1)} %get-tuple-element.30), channel_id=1, source_target_pairs={{0,2},{1,3},{2,0},{3,1},{4,6},{5,7},{6,4},{7,5},{8,10},{9,11},{10,... | collective-permute-start | bytes 884744 | tf_op jit(solution)/shard_map/ppermute | solution.py:625
  34.2 0.2 collective-permute-start.5
  34.5 0.9 copy.23
  35.4 0.9 copy.22
  36.3 0.0 copy-done.9
  36.3 0.1 reshape.143.cover_ref
  36.4 0.0 copy-done.8
  36.4 0.1 edge_inputs.1
  36.5 0.0 collective-permute-done.3
  36.5 21.1 %collective-permute-done.4 = bf16[4,16,2304]{2,1,0:T(8,128)(2,1)} collective-permute-done((bf16[4,16,2304]{2,1,0:T(8,128)(2,1)}, bf16[4,16,2304]{2,1,0:T(8,128)(2,1)}, u32[]{:S(2)}, u32[]{:S(2)}) %collective-permute-start.4) | collective-permute-done | bytes 294944 | tf_op jit(solution)/shard_map/ppermute | solution.py:625
  57.6 5.8 %collective-permute-done.5 = bf16[4,16,2304]{2,1,0:T(8,128)(2,1)} collective-permute-done((bf16[4,16,2304]{2,1,0:T(8,128)(2,1)}, bf16[4,16,2304]{2,1,0:T(8,128)(2,1)}, u32[]{:S(2)}, u32[]{:S(2)}) %collective-permute-start.5) | collective-permute-done | bytes 294944 | tf_op jit(solution)/shard_map/ppermute | solution.py:625
  63.4 0.0 copy-done.7
  63.4 0.0 copy-start.4
  63.4 1.0 copy-done.4
  64.4 0.0 copy-start.6
  64.4 0.9 copy-done.6
  65.3 1.8 %edge_rows.1 = (f32[2,32,128]{2,1,0:T(8,128)S(1)}, f32[48,128]{1,0:T(8,128)S(1)}, f32[48,128]{1,0:T(8,128)S(1)}) custom-call(f32[2,3]{1,0:T(2,128)S(1)} %copy-done.7, bf16[64,2304]{1,0:T(8,128)(2,1)S(1)} %bitcast.40, bf16[64,2304]{1,0:T(8,128)(2,1)} %bitcast.8.refs_1_, bf16[64,2304]{1,0:T(8,128)(2,1)} %bitcast.9.refs_2_, bf16[64,2304]{1,0:T(8,128)(2,1)} %bitcast.10.refs_3_, ...), custom_call_target="tpu_custom_call" | custom-call | flops 54000001024 | tf_op jit(solution)/shard_map/edge_rows/pallas_call | solution.py:407
  67.1 5.0 %collective-permute-start.6 = (f32[48,128]{1,0:T(8,128)S(1)}, f32[48,128]{1,0:T(8,128)S(1)}, u32[]{:S(2)}, u32[]{:S(2)}) collective-permute-start(f32[48,128]{1,0:T(8,128)S(1)} %get-tuple-element.36), channel_id=1, source_target_pairs={{0,1},{1,2},{2,3},{3,4},{4,5},{5,6},{6,7},{7,8},{8,9},{9,10},{10,1... | collective-permute-start | bytes 73736 | tf_op jit(solution)/shard_map/ppermute | solution.py:646
  72.0 1.9 %collective-permute-start.7 = (f32[48,128]{1,0:T(8,128)S(1)}, f32[48,128]{1,0:T(8,128)S(1)}, u32[]{:S(2)}, u32[]{:S(2)}) collective-permute-start(f32[48,128]{1,0:T(8,128)S(1)} %get-tuple-element.37), channel_id=1, source_target_pairs={{1,0},{2,1},{3,2},{4,3},{5,4},{6,5},{7,6},{8,7},{9,8},{10,9},{11,1... | collective-permute-start | bytes 73736 | tf_op jit(solution)/shard_map/ppermute | solution.py:647
  74.0 23.2 %collective-permute-done.6.before_ref = f32[48,128]{1,0:T(8,128)S(1)} collective-permute-done((f32[48,128]{1,0:T(8,128)S(1)}, f32[48,128]{1,0:T(8,128)S(1)}, u32[]{:S(2)}, u32[]{:S(2)}) %collective-permute-start.6) | collective-permute-done | bytes 24608 | tf_op jit(solution)/shard_map/ppermute | solution.py:646
  97.1 0.0 collective-permute-done.7.after_ref
  97.1 0.2 edge_cells.1.edge_ref
  97.3 0.0 copy-start
  97.3 0.6 copy-done
  97.9 0.0 all-to-all-done
  97.9 0.0 copy-start.1
  97.9 1.2 %inner_rows.1 = (f32[2,56,128]{2,1,0:T(8,128)S(1)}, f32[2,56,128]{2,1,0:T(8,128)S(1)}, f32[8,128]{1,0:T(8,128)S(1)}) custom-call(bf16[256,5888]{1,0:T(8,128)(2,1)S(1)} %bitcast.28, f32[2,48,128]{2,1,0:T(8,128)S(1)} %edge_cells.1.edge_ref, bf16[272,256]{1,0:T(8,128)(2,1)S(1)} %get-tuple-element.38.operator_ref, s32[4,64,128]{2,1,0:T(8,128)S(1)} %bitcast.32, ...), custom_call_target="tpu_custom_call" | custom-call | tf_op jit(solution)/shard_map/inner_rows/pallas_call | solution.py:512
  99.1 1.6 %collective-permute-start.8 = (f32[2,56,128]{2,1,0:T(8,128)S(1)}, f32[2,56,128]{2,1,0:T(8,128)S(1)}, u32[]{:S(2)}, u32[]{:S(2)}) collective-permute-start(f32[2,56,128]{2,1,0:T(8,128)S(1)} %get-tuple-element.41), channel_id=1, source_target_pairs={{0,16},{16,0},{1,17},{17,1},{2,18},{18,2},{3,19},{19,3},{4,20},{20... | collective-permute-start | bytes 172040 | tf_op jit(solution)/shard_map/ppermute | solution.py:653
  100.7 2.7 %collective-permute-done.8 = f32[2,56,128]{2,1,0:T(8,128)S(1)} collective-permute-done((f32[2,56,128]{2,1,0:T(8,128)S(1)}, f32[2,56,128]{2,1,0:T(8,128)S(1)}, u32[]{:S(2)}, u32[]{:S(2)}) %collective-permute-start.8) | collective-permute-done | bytes 57376 | tf_op jit(solution)/shard_map/ppermute | solution.py:653
  103.4 0.0 copy-done.1
  103.4 0.8 solve_and_strain.1
  (10 shorter events, 0.1 us)
Async XLA Ops:
  0.6 7.3 %copy-start.2 = (s32[1,256,2]{1,2,0:T(2,128)S(1)}, s32[1,256,2]{1,2,0:T(2,128)}, u32[]{:S(2)}) copy-start(s32[1,256,2]{1,2,0:T(2,128)} %param.10) | copy-start | bytes 6148
  3.5 26.3 %collective-permute-start = (bf16[4,16,2304]{2,1,0:T(8,128)(2,1)}, bf16[4,16,2304]{2,1,0:T(8,128)(2,1)}, u32[]{:S(2)}, u32[]{:S(2)}) collective-permute-start(bf16[4,16,2304]{2,1,0:T(8,128)(2,1)} %get-tuple-element.25), channel_id=1, source_target_pairs={{0,12},{1,13},{2,14},{3,15},{4,8},{5,9},{6,10},{7,11},{8,4},{9,5},... | collective-permute-start | bytes 884744 | tf_op jit(solution)/shard_map/ppermute | solution.py:620
  4.0 25.8 %collective-permute-start.1 = (bf16[4,16,2304]{2,1,0:T(8,128)(2,1)}, bf16[4,16,2304]{2,1,0:T(8,128)(2,1)}, u32[]{:S(2)}, u32[]{:S(2)}) collective-permute-start(bf16[4,16,2304]{2,1,0:T(8,128)(2,1)} %get-tuple-element.26), channel_id=1, source_target_pairs={{0,8},{1,9},{2,10},{3,11},{4,12},{5,13},{6,14},{7,15},{8,0},{9,1},... | collective-permute-start | bytes 884744 | tf_op jit(solution)/shard_map/ppermute | solution.py:620
  7.5 22.3 %collective-permute-start.2 = (bf16[4,16,2304]{2,1,0:T(8,128)(2,1)}, bf16[4,16,2304]{2,1,0:T(8,128)(2,1)}, u32[]{:S(2)}, u32[]{:S(2)}) collective-permute-start(bf16[4,16,2304]{2,1,0:T(8,128)(2,1)} %get-tuple-element.27), channel_id=1, source_target_pairs={{0,4},{1,5},{2,6},{3,7},{4,0},{5,1},{6,2},{7,3},{8,12},{9,13},{10,... | collective-permute-start | bytes 884744 | tf_op jit(solution)/shard_map/ppermute | solution.py:620
  18.3 0.7 copy-start.5
  23.0 13.4 %copy-start.9 = (s32[1,8,8]{2,1,0:T(8,128)S(1)}, s32[1,8,8]{2,1,0:T(8,128)}, u32[]{:S(2)}) copy-start(s32[1,8,8]{2,1,0:T(8,128)} %param.13) | copy-start | bytes 772
  23.0 13.4 %copy-start.8 = (f32[8,1024]{1,0:T(8,128)S(1)}, f32[8,1024]{1,0:T(8,128)}, u32[]{:S(2)}) copy-start(f32[8,1024]{1,0:T(8,128)} %param.15) | copy-start | bytes 98308
  23.0 40.4 %copy-start.7 = (f32[2,3]{1,0:T(2,128)S(1)}, f32[2,3]{1,0:T(2,128)}, u32[]{:S(2)}) copy-start(f32[2,3]{1,0:T(2,128)} %los_ref.1) | copy-start | bytes 76
  23.0 75.0 %all-to-all-start = ((bf16[16,16,5888]{2,1,0:T(8,128)(2,1)}), bf16[16,16,5888]{2,1,0:T(8,128)(2,1)S(1)}, u32[]{:S(2)}, u32[]{:S(2)}) async-start(bf16[16,16,5888]{2,1,0:T(8,128)(2,1)} %pack_inner.1), calls=%async_computation | async-start | bytes 6029312 | tf_op jit(solution)/shard_map/all_to_all | solution.py:627
  31.9 0.7 copy-start.3
  32.6 3.9 %collective-permute-start.3 = (bf16[4,16,2304]{2,1,0:T(8,128)(2,1)}, bf16[4,16,2304]{2,1,0:T(8,128)(2,1)}, u32[]{:S(2)}, u32[]{:S(2)}) collective-permute-start(bf16[4,16,2304]{2,1,0:T(8,128)(2,1)} %get-tuple-element.29), channel_id=1, source_target_pairs={{0,1},{1,0},{2,3},{3,2},{4,5},{5,4},{6,7},{7,6},{8,9},{9,8},{10,11... | collective-permute-start | bytes 884744 | tf_op jit(solution)/shard_map/ppermute | solution.py:625
  32.8 24.8 %collective-permute-start.4 = (bf16[4,16,2304]{2,1,0:T(8,128)(2,1)}, bf16[4,16,2304]{2,1,0:T(8,128)(2,1)}, u32[]{:S(2)}, u32[]{:S(2)}) collective-permute-start(bf16[4,16,2304]{2,1,0:T(8,128)(2,1)} %get-tuple-element.30), channel_id=1, source_target_pairs={{0,2},{1,3},{2,0},{3,1},{4,6},{5,7},{6,4},{7,5},{8,10},{9,11},{10,... | collective-permute-start | bytes 884744 | tf_op jit(solution)/shard_map/ppermute | solution.py:625
  34.2 29.2 %collective-permute-start.5 = (bf16[4,16,2304]{2,1,0:T(8,128)(2,1)}, bf16[4,16,2304]{2,1,0:T(8,128)(2,1)}, u32[]{:S(2)}, u32[]{:S(2)}) collective-permute-start(bf16[4,16,2304]{2,1,0:T(8,128)(2,1)} %get-tuple-element.31), channel_id=1, source_target_pairs={{0,3},{1,2},{2,1},{3,0},{4,7},{5,6},{6,5},{7,4},{8,11},{9,10},{10,... | collective-permute-start | bytes 884744 | tf_op jit(solution)/shard_map/ppermute | solution.py:625
  63.4 1.0 copy-start.4
  64.4 0.9 copy-start.6
  67.1 30.1 %collective-permute-start.6 = (f32[48,128]{1,0:T(8,128)S(1)}, f32[48,128]{1,0:T(8,128)S(1)}, u32[]{:S(2)}, u32[]{:S(2)}) collective-permute-start(f32[48,128]{1,0:T(8,128)S(1)} %get-tuple-element.36), channel_id=1, source_target_pairs={{0,1},{1,2},{2,3},{3,4},{4,5},{5,6},{6,7},{7,8},{8,9},{9,10},{10,1... | collective-permute-start | bytes 73736 | tf_op jit(solution)/shard_map/ppermute | solution.py:646
  72.0 25.1 %collective-permute-start.7 = (f32[48,128]{1,0:T(8,128)S(1)}, f32[48,128]{1,0:T(8,128)S(1)}, u32[]{:S(2)}, u32[]{:S(2)}) collective-permute-start(f32[48,128]{1,0:T(8,128)S(1)} %get-tuple-element.37), channel_id=1, source_target_pairs={{1,0},{2,1},{3,2},{4,3},{5,4},{6,5},{7,6},{8,7},{9,8},{10,9},{11,1... | collective-permute-start | bytes 73736 | tf_op jit(solution)/shard_map/ppermute | solution.py:647
  97.3 0.6 copy-start
  97.9 5.4 %copy-start.1 = (f32[48,128]{1,0:T(8,128)S(1)}, f32[48,128]{1,0:T(8,128)}, u32[]{:S(2)}) copy-start(f32[48,128]{1,0:T(8,128)} %copy-done) | copy-start | bytes 73732
  99.1 4.2 %collective-permute-start.8 = (f32[2,56,128]{2,1,0:T(8,128)S(1)}, f32[2,56,128]{2,1,0:T(8,128)S(1)}, u32[]{:S(2)}, u32[]{:S(2)}) collective-permute-start(f32[2,56,128]{2,1,0:T(8,128)S(1)} %get-tuple-element.41), channel_id=1, source_target_pairs={{0,16},{16,0},{1,17},{17,1},{2,18},{18,2},{3,19},{19,3},{4,20},{20... | collective-permute-start | bytes 172040 | tf_op jit(solution)/shard_map/ppermute | solution.py:653

commit v9 on v8

--- a/solution.py
+++ b/solution.py
@@ -206,14 +206,22 @@
     )(stay(flags), stay(phases))
 
 
-def exact_dot(a, b):
-    return jnp.dot(a, b, precision=lax.Precision.HIGHEST, preferred_element_type=jnp.float32)
-
-
-def operator_kernel(pairs_ref, other_ref, out_ref, other_out_ref, token_ref, normal_ref, inverse_ref):
+def split(a, terms):
+    parts = []
+    for _ in range(terms):
+        parts.append(a.astype(jnp.bfloat16))
+        a = a - parts[-1].astype(jnp.float32)
+    return parts
+
+
+def sum_dots(pairs):
+    return sum(jnp.dot(a, b, preferred_element_type=jnp.float32) for a, b in pairs)
+
+
+def operator_kernel(pairs_ref, other_ref, out_ref, other_out_ref, token_ref, laplacian_ref, inverse_ref):
     token_ref[...] = jnp.zeros_like(token_ref)
     ifgs = pairs_ref.shape[1]
-    size = normal_ref.shape[0]
+    size = inverse_ref.shape[0]
     epoch = lax.broadcasted_iota(jnp.int32, (size, ifgs), 0)
 
     def ends(ref):
@@ -224,11 +232,12 @@
     eye = (
         lax.broadcasted_iota(jnp.int32, (size, size), 0) == lax.broadcasted_iota(jnp.int32, (size, size), 1)
     ).astype(jnp.float32)
-    normal = eye + jnp.dot(
-        across.astype(jnp.bfloat16), down.astype(jnp.bfloat16), preferred_element_type=jnp.float32
-    )
-    normal_ref[...] = normal
-    inverse_ref[...] = eye / jnp.where(eye == 1.0, normal, 1.0)
+    laplacian = jnp.dot(across.astype(jnp.bfloat16), down.astype(jnp.bfloat16), preferred_element_type=jnp.float32)
+    normal = eye + laplacian
+    laplacian_ref[...] = laplacian.astype(jnp.bfloat16)
+    first = eye / jnp.where(eye == 1.0, normal, 1.0)
+    scaled = jnp.sum(first, axis=1, keepdims=True) * normal * jnp.sum(first, axis=0, keepdims=True)
+    inverse_ref[...] = 2.0 * first - scaled
 
     def unfinished(state):
         step, gap = state
@@ -237,8 +246,10 @@
     def improve(state):
         step, _ = state
         inverse = inverse_ref[...]
-        rest = eye - exact_dot(normal_ref[...], inverse)
-        inverse_ref[...] = inverse + exact_dot(inverse, rest)
+        parts = split(inverse, 3)
+        rest = eye - inverse - sum_dots((laplacian_ref[...], part) for part in parts)
+        high, low = split(rest, 2)
+        inverse_ref[...] = inverse + sum_dots(((parts[0], low), (parts[1], high), (parts[0], high)))
         return step + 1, jnp.max(jnp.abs(rest))
 
     lax.while_loop(unfinished, improve, (jnp.int32(0), jnp.float32(1.0)))
@@ -250,7 +261,8 @@
     extra = lax.broadcasted_iota(jnp.int32, (EXTRA, ifgs), 0)
     for ref, to_ref in ((pairs_ref, out_ref), (other_ref, other_out_ref)):
         across = ends(ref)
-        pseudo = exact_dot(inverse_ref[...], across).astype(jnp.bfloat16)
+        ones = across.astype(jnp.bfloat16)
+        pseudo = sum_dots((part, ones) for part in split(inverse_ref[...], 3)).astype(jnp.bfloat16)
         fitted = jnp.dot(across.T.astype(jnp.bfloat16), pseudo, preferred_element_type=jnp.float32)
         to_ref[:ifgs, :] = (same.astype(jnp.float32) - fitted).astype(jnp.bfloat16)
         row = jnp.sum(pseudo.astype(jnp.float32) * slope, axis=0, keepdims=True)
@@ -271,7 +283,7 @@
         in_specs=[vmem] * 2,
         out_specs=[vmem] * 3,
         out_shape=[jax.ShapeDtypeStruct((ifgs + EXTRA, ifgs), jnp.bfloat16)] * 2 + [token],
-        scratch_shapes=[pltpu.VMEM((size, size), jnp.float32), pltpu.VMEM((size, size), jnp.float32)],
+        scratch_shapes=[pltpu.VMEM((size, size), jnp.bfloat16), pltpu.VMEM((size, size), jnp.float32)],
         compiler_params=pltpu.CompilerParams(vmem_limit_bytes=medium),
         name="misfit_operator",
     )(pair_rows.T, other_rows.T)

time: 105 us -> 104 us (level)
  Pallas kernels: 22.3 us -> 18.3 us
  waiting for transfers between devices: 52.8 us -> 55 us
  starting transfers between devices: 21.1 us -> 22.3 us
    ppermute x3, waiting for transfers between devices: 0.01 us -> 21 us  [per_device(): arrived[s] = lax.ppermute(packed[s], 'pix', far)]
    ppermute x1, waiting for transfers between devices: 23.2 us -> 11.4 us  [per_device(): before = lax.ppermute(for_after, 'pix', onward)]
    ppermute x3, waiting for transfers between devices: 26.9 us -> 19.9 us  [per_device(): pieces.append(lax.ppermute(by_column[j], 'pix', near))]
    ppermute x1, starting transfers between devices: 1.92 us -> 5.98 us  [per_device(): after = lax.ppermute(for_before, 'pix', back)]
    pallas_call x1, Pallas kernels: 9.37 us -> 5.42 us  [setup_track(): pl.pallas_call(operator_kernel, in_specs=[vmem] * 2, out_specs=[vmem] * 3...]
    ppermute x1, starting transfers between devices: 4.95 us -> 2.12 us  [per_device(): before = lax.ppermute(for_after, 'pix', onward)]
  transfers between devices with their start and end apart: 10 -> 10, of which waited for: 4 -> 7; matrix products, arithmetic and copies ran while one was open for 3% -> 3% of each run, Pallas kernels for 17% -> 13%
where the time goes in v9:
time: 104 us
  waiting for transfers between devices  55 us (53%)
  starting transfers between devices  22.3 us (21%)
  Pallas kernels  18.3 us (18%)
  local copies, waits for them, and re-layouts  7.18 us (7%)
    ppermute x3, waiting for transfers between devices, per_device(): arrived[s] = lax.ppermute(packed[s], 'pix', far)  21 us
    ppermute x3, waiting for transfers between devices, per_device(): pieces.append(lax.ppermute(by_column[j], 'pix', near))  19.9 us
    ppermute x1, waiting for transfers between devices, per_device(): before = lax.ppermute(for_after, 'pix', onward)  11.4 us
    all_to_all x1, starting transfers between devices, per_device(): lax.all_to_all(pack_inner(phases[0], later_flags, parts, tiles), 'pix', s...  6.75 us
    ppermute x1, starting transfers between devices, per_device(): after = lax.ppermute(for_before, 'pix', back)  5.98 us
    unnamed x22, local copies, waits for them, and re-layouts  5.75 us
    pallas_call x1, Pallas kernels, setup_track(): pl.pallas_call(operator_kernel, in_specs=[vmem] * 2, out_specs=[vmem] * 3...  5.42 us
    ppermute x3, starting transfers between devices, per_device(): arrived[s] = lax.ppermute(packed[s], 'pix', far)  4 us
  transfers between devices with their start and end apart: 10, of which 7 were waited for; matrix products, arithmetic and copies ran while one was open for 3% of the time, Pallas kernels for 13%

profile of v9, /device:TPU:16, one launch (start us, length us, event | category | flops | bytes accessed | tf_op | source)
XLA Modules:
  0.0 103.7 jit_solution(11118266710127625914)
XLA Ops:
  0.6 0.0 copy-start.2
  0.6 2.8 %pack_edges.1 = (bf16[4,16,2304]{2,1,0:T(8,128)(2,1)S(1)}, bf16[4,16,2304]{2,1,0:T(8,128)(2,1)}, bf16[4,16,2304]{2,1,0:T(8,128)(2,1)}, bf16[4,16,2304]{2,1,0:T(8,128)(2,1)}, f32[8,128]{1,0:T(8,128)}) custom-call(s32[16,1024]{1,0:T(8,128)} %bitcast.43, bf16[16,131072]{1,0:T(8,128)(2,1)} %bitcast.41), custom_call_target="tpu_custom_call" | custom-call | tf_op jit(solution)/shard_map/pack_edges/pallas_call | solution.py:120
  3.5 0.5 collective-permute-start
  4.0 3.5 %collective-permute-start.1 = (bf16[4,16,2304]{2,1,0:T(8,128)(2,1)}, bf16[4,16,2304]{2,1,0:T(8,128)(2,1)}, u32[]{:S(2)}, u32[]{:S(2)}) collective-permute-start(bf16[4,16,2304]{2,1,0:T(8,128)(2,1)} %get-tuple-element.26), channel_id=1, source_target_pairs={{0,8},{1,9},{2,10},{3,11},{4,12},{5,13},{6,14},{7,15},{8,0},{9,1},... | collective-permute-start | bytes 884744 | tf_op jit(solution)/shard_map/ppermute | solution.py:632
  7.5 0.0 collective-permute-start.2
  7.5 0.1 broadcast_in_dim.35
  7.6 0.1 broadcast_in_dim.41
  7.6 0.1 broadcast_in_dim.36
  7.7 0.1 broadcast_in_dim.40
  7.8 0.1 broadcast_in_dim.34
  7.9 0.0 copy-done.2
  7.9 0.1 reshape.125
  8.1 0.6 gather_fusion
  8.6 0.1 gather.7
  8.7 0.1 broadcast_in_dim.37
  8.8 0.1 broadcast_in_dim.38
  8.9 5.4 %misfit_operator.1 = (bf16[272,256]{1,0:T(8,128)(2,1)S(1)}, bf16[272,256]{1,0:T(8,128)(2,1)S(1)}, f32[8,128]{1,0:T(8,128)S(1)}) custom-call(s32[2,256]{1,0:T(2,128)S(1)} %bitcast.39, s32[2,256]{1,0:T(2,128)S(1)} %select_bitcast_fusion.other_ref), custom_call_target="tpu_custom_call" | custom-call | tf_op jit(solution)/shard_map/misfit_operator/pallas_call | solution.py:281
  14.4 0.0 copy-start.5
  14.4 0.7 copy-done.5
  15.0 4.0 %pack_inner.1 = bf16[16,16,5888]{2,1,0:T(8,128)(2,1)} custom-call(s32[16,1024]{1,0:T(8,128)} %bitcast.44, bf16[16,131072]{1,0:T(8,128)(2,1)} %bitcast.42), custom_call_target="tpu_custom_call" | custom-call | tf_op jit(solution)/shard_map/pack_inner/pallas_call | solution.py:192
  19.0 0.0 copy-start.9
  19.0 0.0 copy-start.8
  19.0 0.0 copy-start.7
  19.0 6.8 %all-to-all-start = ((bf16[16,16,5888]{2,1,0:T(8,128)(2,1)}), bf16[16,16,5888]{2,1,0:T(8,128)(2,1)S(1)}, u32[]{:S(2)}, u32[]{:S(2)}) async-start(bf16[16,16,5888]{2,1,0:T(8,128)(2,1)} %pack_inner.1), calls=%async_computation | async-start | bytes 6029312 | tf_op jit(solution)/shard_map/all_to_all | solution.py:639
  25.8 0.6 collective-permute-done.refs_1_
  26.4 20.4 %collective-permute-done.1.refs_2_ = bf16[4,16,2304]{2,1,0:T(8,128)(2,1)} collective-permute-done((bf16[4,16,2304]{2,1,0:T(8,128)(2,1)}, bf16[4,16,2304]{2,1,0:T(8,128)(2,1)}, u32[]{:S(2)}, u32[]{:S(2)}) %collective-permute-start.1) | collective-permute-done | bytes 294944 | tf_op jit(solution)/shard_map/ppermute | solution.py:632
  46.8 0.0 collective-permute-done.2.refs_3_
  46.8 2.1 %regroup.1 = (bf16[4,16,2304]{2,1,0:T(8,128)(2,1)S(1)}, bf16[4,16,2304]{2,1,0:T(8,128)(2,1)}, bf16[4,16,2304]{2,1,0:T(8,128)(2,1)}, bf16[4,16,2304]{2,1,0:T(8,128)(2,1)}) custom-call(f32[8,128]{1,0:T(8,128)S(1)} %get-tuple-element.22.after_ref, bf16[4,16,2304]{2,1,0:T(8,128)(2,1)S(1)} %get-tuple-element.24.refs_0_, ...), custom_call_target="tpu_custom_call" | custom-call | tf_op jit(solution)/shard_map/regroup/pallas_call | solution.py:149
  48.9 0.0 copy-start.3
  48.9 0.7 copy-done.3
  49.6 0.0 collective-permute-start.3
  49.6 0.0 collective-permute-start.4
  49.6 1.9 %collective-permute-start.5 = (bf16[4,16,2304]{2,1,0:T(8,128)(2,1)}, bf16[4,16,2304]{2,1,0:T(8,128)(2,1)}, u32[]{:S(2)}, u32[]{:S(2)}) collective-permute-start(bf16[4,16,2304]{2,1,0:T(8,128)(2,1)} %get-tuple-element.31), channel_id=1, source_target_pairs={{0,3},{1,2},{2,1},{3,0},{4,7},{5,6},{6,5},{7,4},{8,11},{9,10},{10,... | collective-permute-start | bytes 884744 | tf_op jit(solution)/shard_map/ppermute | solution.py:637
  51.5 0.9 copy.23
  52.4 0.9 copy.22
  53.3 0.0 copy-done.9
  53.3 0.1 reshape.143.cover_ref
  53.4 0.0 copy-done.8
  53.4 0.1 edge_inputs.1
  53.5 0.0 collective-permute-done.3
  53.5 10.3 %collective-permute-done.4 = bf16[4,16,2304]{2,1,0:T(8,128)(2,1)} collective-permute-done((bf16[4,16,2304]{2,1,0:T(8,128)(2,1)}, bf16[4,16,2304]{2,1,0:T(8,128)(2,1)}, u32[]{:S(2)}, u32[]{:S(2)}) %collective-permute-start.4) | collective-permute-done | bytes 294944 | tf_op jit(solution)/shard_map/ppermute | solution.py:637
  63.8 9.6 %collective-permute-done.5 = bf16[4,16,2304]{2,1,0:T(8,128)(2,1)} collective-permute-done((bf16[4,16,2304]{2,1,0:T(8,128)(2,1)}, bf16[4,16,2304]{2,1,0:T(8,128)(2,1)}, u32[]{:S(2)}, u32[]{:S(2)}) %collective-permute-start.5) | collective-permute-done | bytes 294944 | tf_op jit(solution)/shard_map/ppermute | solution.py:637
  73.4 0.0 copy-done.7
  73.4 0.0 copy-start.4
  73.4 1.0 copy-done.4
  74.3 0.0 copy-start.6
  74.3 0.9 copy-done.6
  75.3 1.8 %edge_rows.1 = (f32[2,32,128]{2,1,0:T(8,128)S(1)}, f32[48,128]{1,0:T(8,128)S(1)}, f32[48,128]{1,0:T(8,128)S(1)}) custom-call(f32[2,3]{1,0:T(2,128)S(1)} %copy-done.7, bf16[64,2304]{1,0:T(8,128)(2,1)S(1)} %bitcast.40, bf16[64,2304]{1,0:T(8,128)(2,1)} %bitcast.8.refs_1_, bf16[64,2304]{1,0:T(8,128)(2,1)} %bitcast.9.refs_2_, bf16[64,2304]{1,0:T(8,128)(2,1)} %bitcast.10.refs_3_, ...), custom_call_target="tpu_custom_call" | custom-call | flops 54000001024 | tf_op jit(solution)/shard_map/edge_rows/pallas_call | solution.py:419
  77.0 2.1 %collective-permute-start.6 = (f32[48,128]{1,0:T(8,128)S(1)}, f32[48,128]{1,0:T(8,128)S(1)}, u32[]{:S(2)}, u32[]{:S(2)}) collective-permute-start(f32[48,128]{1,0:T(8,128)S(1)} %get-tuple-element.36), channel_id=1, source_target_pairs={{0,1},{1,2},{2,3},{3,4},{4,5},{5,6},{6,7},{7,8},{8,9},{9,10},{10,1... | collective-permute-start | bytes 73736 | tf_op jit(solution)/shard_map/ppermute | solution.py:658
  79.2 6.0 %collective-permute-start.7 = (f32[48,128]{1,0:T(8,128)S(1)}, f32[48,128]{1,0:T(8,128)S(1)}, u32[]{:S(2)}, u32[]{:S(2)}) collective-permute-start(f32[48,128]{1,0:T(8,128)S(1)} %get-tuple-element.37), channel_id=1, source_target_pairs={{1,0},{2,1},{3,2},{4,3},{5,4},{6,5},{7,6},{8,7},{9,8},{10,9},{11,1... | collective-permute-start | bytes 73736 | tf_op jit(solution)/shard_map/ppermute | solution.py:659
  85.1 11.4 %collective-permute-done.6.before_ref = f32[48,128]{1,0:T(8,128)S(1)} collective-permute-done((f32[48,128]{1,0:T(8,128)S(1)}, f32[48,128]{1,0:T(8,128)S(1)}, u32[]{:S(2)}, u32[]{:S(2)}) %collective-permute-start.6) | collective-permute-done | bytes 24608 | tf_op jit(solution)/shard_map/ppermute | solution.py:658
  96.5 0.0 collective-permute-done.7.after_ref
  96.5 0.2 edge_cells.1.edge_ref
  96.7 0.0 copy-start
  96.7 0.6 copy-done
  97.3 0.1 all-to-all-done
  97.4 0.0 copy-start.1
  97.4 1.2 %inner_rows.1 = (f32[2,56,128]{2,1,0:T(8,128)S(1)}, f32[2,56,128]{2,1,0:T(8,128)S(1)}, f32[8,128]{1,0:T(8,128)S(1)}) custom-call(bf16[256,5888]{1,0:T(8,128)(2,1)S(1)} %bitcast.28, f32[2,48,128]{2,1,0:T(8,128)S(1)} %edge_cells.1.edge_ref, bf16[272,256]{1,0:T(8,128)(2,1)S(1)} %get-tuple-element.38.operator_ref, s32[4,64,128]{2,1,0:T(8,128)S(1)} %bitcast.32, ...), custom_call_target="tpu_custom_call" | custom-call | tf_op jit(solution)/shard_map/inner_rows/pallas_call | solution.py:524
  98.6 1.6 %collective-permute-start.8 = (f32[2,56,128]{2,1,0:T(8,128)S(1)}, f32[2,56,128]{2,1,0:T(8,128)S(1)}, u32[]{:S(2)}, u32[]{:S(2)}) collective-permute-start(f32[2,56,128]{2,1,0:T(8,128)S(1)} %get-tuple-element.41), channel_id=1, source_target_pairs={{0,16},{16,0},{1,17},{17,1},{2,18},{18,2},{3,19},{19,3},{4,20},{20... | collective-permute-start | bytes 172040 | tf_op jit(solution)/shard_map/ppermute | solution.py:665
  100.2 2.7 %collective-permute-done.8 = f32[2,56,128]{2,1,0:T(8,128)S(1)} collective-permute-done((f32[2,56,128]{2,1,0:T(8,128)S(1)}, f32[2,56,128]{2,1,0:T(8,128)S(1)}, u32[]{:S(2)}, u32[]{:S(2)}) %collective-permute-start.8) | collective-permute-done | bytes 57376 | tf_op jit(solution)/shard_map/ppermute | solution.py:665
  102.8 0.0 copy-done.1
  102.8 0.8 solve_and_strain.1
  (10 shorter events, 0.1 us)
Async XLA Ops:
  0.6 7.3 %copy-start.2 = (s32[1,256,2]{1,2,0:T(2,128)S(1)}, s32[1,256,2]{1,2,0:T(2,128)}, u32[]{:S(2)}) copy-start(s32[1,256,2]{1,2,0:T(2,128)} %param.10) | copy-start | bytes 6148
  3.5 22.9 %collective-permute-start = (bf16[4,16,2304]{2,1,0:T(8,128)(2,1)}, bf16[4,16,2304]{2,1,0:T(8,128)(2,1)}, u32[]{:S(2)}, u32[]{:S(2)}) collective-permute-start(bf16[4,16,2304]{2,1,0:T(8,128)(2,1)} %get-tuple-element.25), channel_id=1, source_target_pairs={{0,12},{1,13},{2,14},{3,15},{4,8},{5,9},{6,10},{7,11},{8,4},{9,5},... | collective-permute-start | bytes 884744 | tf_op jit(solution)/shard_map/ppermute | solution.py:632
  4.0 42.8 %collective-permute-start.1 = (bf16[4,16,2304]{2,1,0:T(8,128)(2,1)}, bf16[4,16,2304]{2,1,0:T(8,128)(2,1)}, u32[]{:S(2)}, u32[]{:S(2)}) collective-permute-start(bf16[4,16,2304]{2,1,0:T(8,128)(2,1)} %get-tuple-element.26), channel_id=1, source_target_pairs={{0,8},{1,9},{2,10},{3,11},{4,12},{5,13},{6,14},{7,15},{8,0},{9,1},... | collective-permute-start | bytes 884744 | tf_op jit(solution)/shard_map/ppermute | solution.py:632
  7.5 39.3 %collective-permute-start.2 = (bf16[4,16,2304]{2,1,0:T(8,128)(2,1)}, bf16[4,16,2304]{2,1,0:T(8,128)(2,1)}, u32[]{:S(2)}, u32[]{:S(2)}) collective-permute-start(bf16[4,16,2304]{2,1,0:T(8,128)(2,1)} %get-tuple-element.27), channel_id=1, source_target_pairs={{0,4},{1,5},{2,6},{3,7},{4,0},{5,1},{6,2},{7,3},{8,12},{9,13},{10,... | collective-permute-start | bytes 884744 | tf_op jit(solution)/shard_map/ppermute | solution.py:632
  14.4 0.7 copy-start.5
  19.0 34.3 %copy-start.9 = (s32[1,8,8]{2,1,0:T(8,128)S(1)}, s32[1,8,8]{2,1,0:T(8,128)}, u32[]{:S(2)}) copy-start(s32[1,8,8]{2,1,0:T(8,128)} %param.13) | copy-start | bytes 772
  19.0 34.4 %copy-start.8 = (f32[8,1024]{1,0:T(8,128)S(1)}, f32[8,1024]{1,0:T(8,128)}, u32[]{:S(2)}) copy-start(f32[8,1024]{1,0:T(8,128)} %param.15) | copy-start | bytes 98308
  19.0 54.4 %copy-start.7 = (f32[2,3]{1,0:T(2,128)S(1)}, f32[2,3]{1,0:T(2,128)}, u32[]{:S(2)}) copy-start(f32[2,3]{1,0:T(2,128)} %los_ref.1) | copy-start | bytes 76
  19.0 78.4 %all-to-all-start = ((bf16[16,16,5888]{2,1,0:T(8,128)(2,1)}), bf16[16,16,5888]{2,1,0:T(8,128)(2,1)S(1)}, u32[]{:S(2)}, u32[]{:S(2)}) async-start(bf16[16,16,5888]{2,1,0:T(8,128)(2,1)} %pack_inner.1), calls=%async_computation | async-start | bytes 6029312 | tf_op jit(solution)/shard_map/all_to_all | solution.py:639
  48.9 0.7 copy-start.3
  49.6 3.9 %collective-permute-start.3 = (bf16[4,16,2304]{2,1,0:T(8,128)(2,1)}, bf16[4,16,2304]{2,1,0:T(8,128)(2,1)}, u32[]{:S(2)}, u32[]{:S(2)}) collective-permute-start(bf16[4,16,2304]{2,1,0:T(8,128)(2,1)} %get-tuple-element.29), channel_id=1, source_target_pairs={{0,1},{1,0},{2,3},{3,2},{4,5},{5,4},{6,7},{7,6},{8,9},{9,8},{10,11... | collective-permute-start | bytes 884744 | tf_op jit(solution)/shard_map/ppermute | solution.py:637
  49.6 14.2 %collective-permute-start.4 = (bf16[4,16,2304]{2,1,0:T(8,128)(2,1)}, bf16[4,16,2304]{2,1,0:T(8,128)(2,1)}, u32[]{:S(2)}, u32[]{:S(2)}) collective-permute-start(bf16[4,16,2304]{2,1,0:T(8,128)(2,1)} %get-tuple-element.30), channel_id=1, source_target_pairs={{0,2},{1,3},{2,0},{3,1},{4,6},{5,7},{6,4},{7,5},{8,10},{9,11},{10,... | collective-permute-start | bytes 884744 | tf_op jit(solution)/shard_map/ppermute | solution.py:637
  49.6 23.7 %collective-permute-start.5 = (bf16[4,16,2304]{2,1,0:T(8,128)(2,1)}, bf16[4,16,2304]{2,1,0:T(8,128)(2,1)}, u32[]{:S(2)}, u32[]{:S(2)}) collective-permute-start(bf16[4,16,2304]{2,1,0:T(8,128)(2,1)} %get-tuple-element.31), channel_id=1, source_target_pairs={{0,3},{1,2},{2,1},{3,0},{4,7},{5,6},{6,5},{7,4},{8,11},{9,10},{10,... | collective-permute-start | bytes 884744 | tf_op jit(solution)/shard_map/ppermute | solution.py:637
  73.4 1.0 copy-start.4
  74.3 0.9 copy-start.6
  77.0 19.5 %collective-permute-start.6 = (f32[48,128]{1,0:T(8,128)S(1)}, f32[48,128]{1,0:T(8,128)S(1)}, u32[]{:S(2)}, u32[]{:S(2)}) collective-permute-start(f32[48,128]{1,0:T(8,128)S(1)} %get-tuple-element.36), channel_id=1, source_target_pairs={{0,1},{1,2},{2,3},{3,4},{4,5},{5,6},{6,7},{7,8},{8,9},{9,10},{10,1... | collective-permute-start | bytes 73736 | tf_op jit(solution)/shard_map/ppermute | solution.py:658
  79.2 17.4 %collective-permute-start.7 = (f32[48,128]{1,0:T(8,128)S(1)}, f32[48,128]{1,0:T(8,128)S(1)}, u32[]{:S(2)}, u32[]{:S(2)}) collective-permute-start(f32[48,128]{1,0:T(8,128)S(1)} %get-tuple-element.37), channel_id=1, source_target_pairs={{1,0},{2,1},{3,2},{4,3},{5,4},{6,5},{7,6},{8,7},{9,8},{10,9},{11,1... | collective-permute-start | bytes 73736 | tf_op jit(solution)/shard_map/ppermute | solution.py:659
  96.7 0.6 copy-start
  97.4 5.4 %copy-start.1 = (f32[48,128]{1,0:T(8,128)S(1)}, f32[48,128]{1,0:T(8,128)}, u32[]{:S(2)}) copy-start(f32[48,128]{1,0:T(8,128)} %copy-done) | copy-start | bytes 73732
  98.6 4.2 %collective-permute-start.8 = (f32[2,56,128]{2,1,0:T(8,128)S(1)}, f32[2,56,128]{2,1,0:T(8,128)S(1)}, u32[]{:S(2)}, u32[]{:S(2)}) collective-permute-start(f32[2,56,128]{2,1,0:T(8,128)S(1)} %get-tuple-element.41), channel_id=1, source_target_pairs={{0,16},{16,0},{1,17},{17,1},{2,18},{18,2},{3,19},{19,3},{4,20},{20... | collective-permute-start | bytes 172040 | tf_op jit(solution)/shard_map/ppermute | solution.py:665

commit v10 on v9

--- a/solution.py
+++ b/solution.py
@@ -58,76 +58,72 @@
     return index ^ step if size & (size - 1) == 0 else (index - step + size) % size
 
 
-def pack_edges_kernel(tiles, group, flags_hbm, phases_ref, *refs):
+def pack_edges_kernel(tiles, group, steps, flags_hbm, phases_ref, *refs):
     *out_refs, token_ref, flags_ref, stacked_ref, near_ref, flag_sem, in_sem = refs
     token_ref[...] = jnp.zeros_like(token_ref)
-    planes = len(out_refs)
-    parts = planes * group
     ifgs, blocks = flags_ref.shape
-    span = blocks // parts
     reach = tiles + 1
     half = reach * MBLK
+    parts = lax.axis_size("pix")
+    planes = parts // group
+    span = blocks // parts
     flag_copy = pltpu.make_async_copy(flags_hbm, flags_ref, flag_sem)
     flag_copy.start()
-    ends = [
-        pltpu.make_async_copy(phases_ref.at[:, pl.ds(0, half)], near_ref.at[0, :, pl.ds(half, half)], in_sem.at[0]),
-        pltpu.make_async_copy(
-            phases_ref.at[:, pl.ds(blocks * MBLK - half, half)], near_ref.at[parts, :, pl.ds(0, half)], in_sem.at[parts]
-        ),
-    ]
-
-    def between(b):
-        low = pl.multiple_of((span * b - reach) * MBLK, MBLK)
-        return pltpu.make_async_copy(phases_ref.at[:, pl.ds(low, 2 * half)], near_ref.at[b], in_sem.at[b])
-
-    ends[0].start()
-
-    @pl.loop(1, parts)
-    def _(b):
-        between(b).start()
-
-    ends[1].start()
+    plane = lax.axis_index("pix") // group
+    first_parts = [partner(plane, step, planes) * group for step in steps]
+
+    def regions(act):
+        for n, first_part in enumerate(first_parts):
+            for g in range(group + 1):
+                b = first_part + g
+                to_ref, sem = near_ref.at[n, g], in_sem.at[n, g]
+
+                @pl.when(b == 0)
+                def _():
+                    act(pltpu.make_async_copy(phases_ref.at[:, pl.ds(0, half)], to_ref.at[:, pl.ds(half, half)], sem))
+
+                @pl.when(b == parts)
+                def _():
+                    low = blocks * MBLK - half
+                    act(pltpu.make_async_copy(phases_ref.at[:, pl.ds(low, half)], to_ref.at[:, pl.ds(0, half)], sem))
+
+                @pl.when(jnp.logical_and(b > 0, b < parts))
+                def _():
+                    low = pl.multiple_of((span * jnp.clip(b, 1, parts - 1) - reach) * MBLK, MBLK)
+                    act(pltpu.make_async_copy(phases_ref.at[:, pl.ds(low, 2 * half)], to_ref, sem))
+
+    regions(lambda copy: copy.start())
     flag_copy.wait()
-    plane = lax.axis_index("pix") // group
-    firsts = [(partner(plane, -s % planes, planes) * group + g) * span for s in range(planes) for g in range(group)]
+    firsts = [(first_part + g) * span for first_part in first_parts for g in range(group)]
 
     def tile_out(n, start, keep):
         out_refs[n // group][n % group, :, start : start + 2 * MBLK] = keep
 
     wanted = [k if k < reach else span - 2 * reach + k for k in range(2 * reach)]
     expand_masks(flags_ref, stacked_ref, firsts, wanted, tile_out)
-    ends[0].wait()
-
-    @pl.loop(1, parts)
-    def _(b):
-        between(b).wait()
-
-    ends[1].wait()
-    for s in range(planes):
-        first_part = partner(plane, -s % planes, planes) * group
-
-        @pl.loop(0, group, unroll=2)
-        def _(g):
-            out_refs[s][g, :, :half] *= near_ref[first_part + g, :, half:]
-            out_refs[s][g, :, half:] *= near_ref[first_part + g + 1, :, :half]
-
-
-def pack_edges(phases, flags, parts, group, tiles):
+    regions(lambda copy: copy.wait())
+    for n, out_ref in enumerate(out_refs):
+        for g in range(group):
+            out_ref[g, :, :half] *= near_ref[n, g, :, half:]
+            out_ref[g, :, half:] *= near_ref[n, g + 1, :, :half]
+
+
+def pack_edges(phases, flags, group, tiles, steps):
     ifgs = phases.shape[0]
-    planes = parts // group
     hbm = pl.BlockSpec(memory_space=pltpu.HBM)
     width = 2 * (tiles + 1) * MBLK
-    return pl.pallas_call(
-        functools.partial(pack_edges_kernel, tiles, group),
+    count = len(steps)
+    return pl.pallas_call(
+        functools.partial(pack_edges_kernel, tiles, group, steps),
         in_specs=[hbm, hbm],
-        out_specs=[pl.BlockSpec(memory_space=pltpu.VMEM)] * (planes + 1),
-        out_shape=[jax.ShapeDtypeStruct((group, ifgs, width), jnp.bfloat16)] * planes + [token],
+        out_specs=[pl.BlockSpec(memory_space=pltpu.VMEM)] * (count + 1),
+        out_shape=[jax.ShapeDtypeStruct((group, ifgs, width), jnp.bfloat16)] * count + [token],
         scratch_shapes=[
             pltpu.VMEM(flags.shape, jnp.int32),
-            pltpu.VMEM((parts * ifgs, LANES), jnp.float32),
-            pltpu.VMEM((parts + 1, ifgs, 2 * (tiles + 1) * MBLK), jnp.bfloat16),
+            pltpu.VMEM((count * group * ifgs, LANES), jnp.float32),
+            pltpu.VMEM((count, group + 1, ifgs, width), jnp.bfloat16),
             pltpu.SemaphoreType.DMA,
-            pltpu.SemaphoreType.DMA((parts + 1,)),
+            pltpu.SemaphoreType.DMA((count, group + 1)),
         ],
         compiler_params=pltpu.CompilerParams(vmem_limit_bytes=medium),
         name="pack_edges",
@@ -619,7 +615,11 @@
     group = GROUP if parts % GROUP == 0 else parts
     planes = parts // group
     plane, column = jnp.divmod(lax.axis_index("pix").astype(jnp.int32), group)
-    *packed, packed_token = pack_edges(phases[0], coherent[0], parts, group, tiles)
+    steps = [-s % planes for s in range(planes)]
+    first_piece, first_token = pack_edges(phases[0], coherent[0], group, tiles, steps[1:2])
+    rest_flags, _ = lax.optimization_barrier((coherent[0], first_token))
+    own_piece, *others, packed_token = pack_edges(phases[0], rest_flags, group, tiles, steps[:1] + steps[2:])
+    packed = [own_piece, first_piece, *others]
     later_pairs, _ = lax.optimization_barrier((pairs[0], packed_token))
     steps_j, steps_s = jnp.meshgrid(jnp.arange(group), jnp.arange(planes), indexing="ij")
     sources = (partner_back(plane, -steps_s % planes, planes) * group + partner_back(column, steps_j, group)).reshape(-1)
@@ -635,7 +635,7 @@
     for j in range(1, group):
         near = [(z * group + c, z * group + partner(c, j, group)) for z, c in ids]
         pieces.append(lax.ppermute(by_column[j], "pix", near))
-    later_flags, *_ = lax.optimization_barrier((coherent[0], formed_token))
+    later_flags, *_ = lax.optimization_barrier((coherent[0], packed_token))
     inner_stack = lax.all_to_all(
         pack_inner(phases[0], later_flags, parts, tiles), "pix", split_axis=0, concat_axis=0, tiled=True
     )

time: 104 us -> 103 us (level)
  waiting for transfers between devices: 55 us -> 51.8 us
  Pallas kernels: 18.3 us -> 20.3 us
  local copies, waits for them, and re-layouts: 7.18 us -> 8.81 us
  starting transfers between devices: 22.3 us -> 21.1 us
    ppermute x3, waiting for transfers between devices: 21 us -> 17.4 us  [per_device(): arrived[s] = lax.ppermute(packed[s], 'pix', far)]
    pallas_call x1 -> x2, Pallas kernels: 2.83 us -> 4.94 us  [pack_edges(): pl.pallas_call(functools.partial(pack_edges_kernel, tiles, group, steps),...]
    unnamed x22 -> x26, local copies, waits for them, and re-layouts: 5.75 us -> 7.39 us
    ppermute x3, waiting for transfers between devices: 19.9 us -> 21.1 us  [per_device(): pieces.append(lax.ppermute(by_column[j], 'pix', near))]
  transfers between devices with their start and end apart: 10 -> 10, of which waited for: 7 -> 6; matrix products, arithmetic and copies ran while one was open for 3% -> 3% of each run, Pallas kernels for 13% -> 16%
where the time goes in v10:
time: 103 us
  waiting for transfers between devices  51.8 us (50%)
  starting transfers between devices  21.1 us (20%)
  Pallas kernels  20.3 us (20%)
  local copies, waits for them, and re-layouts  8.81 us (9%)
    ppermute x3, waiting for transfers between devices, per_device(): pieces.append(lax.ppermute(by_column[j], 'pix', near))  21.1 us
    ppermute x3, waiting for transfers between devices, per_device(): arrived[s] = lax.ppermute(packed[s], 'pix', far)  17.4 us
    ppermute x1, waiting for transfers between devices, per_device(): before = lax.ppermute(for_after, 'pix', onward)  10.5 us
    unnamed x26, local copies, waits for them, and re-layouts  7.39 us
    all_to_all x1, starting transfers between devices, per_device(): lax.all_to_all(pack_inner(phases[0], later_flags, parts, tiles), 'pix', s...  6.75 us
    pallas_call x1, Pallas kernels, setup_track(): pl.pallas_call(operator_kernel, in_specs=[vmem] * 2, out_specs=[vmem] * 3...  5.42 us
    ppermute x1, starting transfers between devices, per_device(): after = lax.ppermute(for_before, 'pix', back)  5 us
    pallas_call x2, Pallas kernels, pack_edges(): pl.pallas_call(functools.partial(pack_edges_kernel, tiles, group, steps),...  4.94 us
  transfers between devices with their start and end apart: 10, of which 6 were waited for; matrix products, arithmetic and copies ran while one was open for 3% of the time, Pallas kernels for 16%

profile of v10, /device:TPU:16, one launch (start us, length us, event | category | flops | bytes accessed | tf_op | source)
XLA Modules:
  0.0 102.9 jit_solution(349433474547881779)
XLA Ops:
  0.6 2.1 %pack_edges.3 = (bf16[4,16,2304]{2,1,0:T(8,128)(2,1)}, f32[8,128]{1,0:T(8,128)}) custom-call(s32[16,1024]{1,0:T(8,128)} %bitcast.44, bf16[16,131072]{1,0:T(8,128)(2,1)} %bitcast.41), custom_call_target="tpu_custom_call" | custom-call | tf_op jit(solution)/shard_map/pack_edges/pallas_call | solution.py:116
  2.8 0.5 collective-permute-start
  3.3 2.8 %pack_edges.2 = (bf16[4,16,2304]{2,1,0:T(8,128)(2,1)S(1)}, bf16[4,16,2304]{2,1,0:T(8,128)(2,1)}, bf16[4,16,2304]{2,1,0:T(8,128)(2,1)}, f32[8,128]{1,0:T(8,128)}) custom-call(s32[16,1024]{1,0:T(8,128)} %bitcast.45, bf16[16,131072]{1,0:T(8,128)(2,1)} %bitcast.42), custom_call_target="tpu_custom_call" | custom-call | tf_op jit(solution)/shard_map/pack_edges/pallas_call | solution.py:116
  6.1 0.0 copy-start
  6.1 0.7 copy-done
  6.8 3.5 %collective-permute-start.1 = (bf16[4,16,2304]{2,1,0:T(8,128)(2,1)}, bf16[4,16,2304]{2,1,0:T(8,128)(2,1)}, u32[]{:S(2)}, u32[]{:S(2)}) collective-permute-start(bf16[4,16,2304]{2,1,0:T(8,128)(2,1)} %get-tuple-element.30), channel_id=1, source_target_pairs={{0,8},{1,9},{2,10},{3,11},{4,12},{5,13},{6,14},{7,15},{8,0},{9,1},... | collective-permute-start | bytes 884744 | tf_op jit(solution)/shard_map/ppermute | solution.py:632
  10.3 0.0 collective-permute-start.2
  10.3 4.0 %pack_inner.1 = bf16[16,16,5888]{2,1,0:T(8,128)(2,1)} custom-call(s32[16,1024]{1,0:T(8,128)} %bitcast.46, bf16[16,131072]{1,0:T(8,128)(2,1)} %bitcast.43), custom_call_target="tpu_custom_call" | custom-call | tf_op jit(solution)/shard_map/pack_inner/pallas_call | solution.py:188
  14.3 0.0 copy-start.4
  14.3 0.0 copy-start.10
  14.3 0.0 copy-start.11
  14.3 0.0 copy-start.9
  14.3 6.7 %all-to-all-start = ((bf16[16,16,5888]{2,1,0:T(8,128)(2,1)}), bf16[16,16,5888]{2,1,0:T(8,128)(2,1)S(1)}, u32[]{:S(2)}, u32[]{:S(2)}) async-start(bf16[16,16,5888]{2,1,0:T(8,128)(2,1)} %pack_inner.1), calls=%async_computation | async-start | bytes 6029312 | tf_op jit(solution)/shard_map/all_to_all | solution.py:639
  21.1 0.1 broadcast_in_dim.40
  21.1 0.1 broadcast_in_dim.34
  21.2 0.1 broadcast_in_dim.35
  21.3 0.1 broadcast_in_dim.41
  21.4 0.1 broadcast_in_dim.36
  21.5 0.1 broadcast_in_dim.37
  21.6 0.1 broadcast_in_dim.38
  21.7 0.0 copy-done.4
  21.7 0.1 reshape.126
  21.8 0.6 gather_fusion
  22.4 0.1 gather.7
  22.5 5.4 %misfit_operator.1 = (bf16[272,256]{1,0:T(8,128)(2,1)S(1)}, bf16[272,256]{1,0:T(8,128)(2,1)S(1)}, f32[8,128]{1,0:T(8,128)S(1)}) custom-call(s32[2,256]{1,0:T(2,128)S(1)} %bitcast.39, s32[2,256]{1,0:T(2,128)S(1)} %select_bitcast_fusion.other_ref), custom_call_target="tpu_custom_call" | custom-call | tf_op jit(solution)/shard_map/misfit_operator/pallas_call | solution.py:277
  27.9 0.0 copy-start.7
  27.9 0.7 copy-done.7
  28.6 0.0 collective-permute-done.refs_1_
  28.6 17.4 %collective-permute-done.1.refs_2_ = bf16[4,16,2304]{2,1,0:T(8,128)(2,1)} collective-permute-done((bf16[4,16,2304]{2,1,0:T(8,128)(2,1)}, bf16[4,16,2304]{2,1,0:T(8,128)(2,1)}, u32[]{:S(2)}, u32[]{:S(2)}) %collective-permute-start.1) | collective-permute-done | bytes 294944 | tf_op jit(solution)/shard_map/ppermute | solution.py:632
  46.0 0.0 collective-permute-done.2.refs_3_
  46.0 0.0 copy-start.1
  46.0 1.0 copy-done.1
  47.0 2.0 %regroup.1 = (bf16[4,16,2304]{2,1,0:T(8,128)(2,1)S(1)}, bf16[4,16,2304]{2,1,0:T(8,128)(2,1)}, bf16[4,16,2304]{2,1,0:T(8,128)(2,1)}, bf16[4,16,2304]{2,1,0:T(8,128)(2,1)}) custom-call(f32[8,128]{1,0:T(8,128)S(1)} %get-tuple-element.27.after_ref, bf16[4,16,2304]{2,1,0:T(8,128)(2,1)S(1)} %copy-done.1, bf16[4,16,2304]{2,1,0:T(8,128)(2,1)S(1)} %collective-permute-done.refs_1_, ...), custom_call_target="tpu_custom_call" | custom-call | tf_op jit(solution)/shard_map/regroup/pallas_call | solution.py:145
  49.0 0.0 copy-start.5
  49.0 0.7 copy-done.5
  49.7 0.0 collective-permute-start.3
  49.7 0.0 collective-permute-start.4
  49.7 1.9 %collective-permute-start.5 = (bf16[4,16,2304]{2,1,0:T(8,128)(2,1)}, bf16[4,16,2304]{2,1,0:T(8,128)(2,1)}, u32[]{:S(2)}, u32[]{:S(2)}) collective-permute-start(bf16[4,16,2304]{2,1,0:T(8,128)(2,1)} %get-tuple-element.35), channel_id=1, source_target_pairs={{0,3},{1,2},{2,1},{3,0},{4,7},{5,6},{6,5},{7,4},{8,11},{9,10},{10,... | collective-permute-start | bytes 884744 | tf_op jit(solution)/shard_map/ppermute | solution.py:637
  51.5 0.0 copy-done.10
  51.6 0.0 copy-done.11
  51.6 0.1 reshape.143.cover_ref
  51.6 0.9 copy.23
  52.6 0.9 copy.22
  53.5 0.1 edge_inputs.1
  53.6 0.0 collective-permute-done.3
  53.6 14.3 %collective-permute-done.4 = bf16[4,16,2304]{2,1,0:T(8,128)(2,1)} collective-permute-done((bf16[4,16,2304]{2,1,0:T(8,128)(2,1)}, bf16[4,16,2304]{2,1,0:T(8,128)(2,1)}, u32[]{:S(2)}, u32[]{:S(2)}) %collective-permute-start.4) | collective-permute-done | bytes 294944 | tf_op jit(solution)/shard_map/ppermute | solution.py:637
  67.9 6.8 %collective-permute-done.5 = bf16[4,16,2304]{2,1,0:T(8,128)(2,1)} collective-permute-done((bf16[4,16,2304]{2,1,0:T(8,128)(2,1)}, bf16[4,16,2304]{2,1,0:T(8,128)(2,1)}, u32[]{:S(2)}, u32[]{:S(2)}) %collective-permute-start.5) | collective-permute-done | bytes 294944 | tf_op jit(solution)/shard_map/ppermute | solution.py:637
  74.7 0.0 copy-done.9
  74.7 0.0 copy-start.6
  74.7 1.0 copy-done.6
  75.6 0.9 copy-done.8
  76.5 1.8 %edge_rows.1 = (f32[2,32,128]{2,1,0:T(8,128)S(1)}, f32[48,128]{1,0:T(8,128)S(1)}, f32[48,128]{1,0:T(8,128)S(1)}) custom-call(f32[2,3]{1,0:T(2,128)S(1)} %copy-done.9, bf16[64,2304]{1,0:T(8,128)(2,1)S(1)} %bitcast.40, bf16[64,2304]{1,0:T(8,128)(2,1)} %bitcast.8.refs_1_, bf16[64,2304]{1,0:T(8,128)(2,1)} %bitcast.9.refs_2_, bf16[64,2304]{1,0:T(8,128)(2,1)} %bitcast.10.refs_3_, ...), custom_call_target="tpu_custom_call" | custom-call | flops 54000001024 | tf_op jit(solution)/shard_map/edge_rows/pallas_call | solution.py:415
  78.3 1.9 %collective-permute-start.6 = (f32[48,128]{1,0:T(8,128)S(1)}, f32[48,128]{1,0:T(8,128)S(1)}, u32[]{:S(2)}, u32[]{:S(2)}) collective-permute-start(f32[48,128]{1,0:T(8,128)S(1)} %get-tuple-element.40), channel_id=1, source_target_pairs={{0,1},{1,2},{2,3},{3,4},{4,5},{5,6},{6,7},{7,8},{8,9},{9,10},{10,1... | collective-permute-start | bytes 73736 | tf_op jit(solution)/shard_map/ppermute | solution.py:658
  80.2 5.0 %collective-permute-start.7 = (f32[48,128]{1,0:T(8,128)S(1)}, f32[48,128]{1,0:T(8,128)S(1)}, u32[]{:S(2)}, u32[]{:S(2)}) collective-permute-start(f32[48,128]{1,0:T(8,128)S(1)} %get-tuple-element.41), channel_id=1, source_target_pairs={{1,0},{2,1},{3,2},{4,3},{5,4},{6,5},{7,6},{8,7},{9,8},{10,9},{11,1... | collective-permute-start | bytes 73736 | tf_op jit(solution)/shard_map/ppermute | solution.py:659
  85.3 10.5 %collective-permute-done.6.before_ref = f32[48,128]{1,0:T(8,128)S(1)} collective-permute-done((f32[48,128]{1,0:T(8,128)S(1)}, f32[48,128]{1,0:T(8,128)S(1)}, u32[]{:S(2)}, u32[]{:S(2)}) %collective-permute-start.6) | collective-permute-done | bytes 24608 | tf_op jit(solution)/shard_map/ppermute | solution.py:658
  95.8 0.0 collective-permute-done.7.after_ref
  95.8 0.2 edge_cells.1.edge_ref
  96.0 0.6 copy-done.2
  96.6 0.1 all-to-all-done
  96.7 1.2 %inner_rows.1 = (f32[2,56,128]{2,1,0:T(8,128)S(1)}, f32[2,56,128]{2,1,0:T(8,128)S(1)}, f32[8,128]{1,0:T(8,128)S(1)}) custom-call(bf16[256,5888]{1,0:T(8,128)(2,1)S(1)} %bitcast.28, f32[2,48,128]{2,1,0:T(8,128)S(1)} %edge_cells.1.edge_ref, bf16[272,256]{1,0:T(8,128)(2,1)S(1)} %get-tuple-element.42.operator_ref, s32[4,64,128]{2,1,0:T(8,128)S(1)} %bitcast.32, ...), custom_call_target="tpu_custom_call" | custom-call | tf_op jit(solution)/shard_map/inner_rows/pallas_call | solution.py:520
  97.8 1.6 %collective-permute-start.8 = (f32[2,56,128]{2,1,0:T(8,128)S(1)}, f32[2,56,128]{2,1,0:T(8,128)S(1)}, u32[]{:S(2)}, u32[]{:S(2)}) collective-permute-start(f32[2,56,128]{2,1,0:T(8,128)S(1)} %get-tuple-element.45), channel_id=1, source_target_pairs={{0,16},{16,0},{1,17},{17,1},{2,18},{18,2},{3,19},{19,3},{4,20},{20... | collective-permute-start | bytes 172040 | tf_op jit(solution)/shard_map/ppermute | solution.py:665
  99.4 2.7 %collective-permute-done.8 = f32[2,56,128]{2,1,0:T(8,128)S(1)} collective-permute-done((f32[2,56,128]{2,1,0:T(8,128)S(1)}, f32[2,56,128]{2,1,0:T(8,128)S(1)}, u32[]{:S(2)}, u32[]{:S(2)}) %collective-permute-start.8) | collective-permute-done | bytes 57376 | tf_op jit(solution)/shard_map/ppermute | solution.py:665
  102.1 0.0 copy-done.3
  102.1 0.8 solve_and_strain.1
  (13 shorter events, 0.1 us)
Async XLA Ops:
  2.8 25.8 %collective-permute-start = (bf16[4,16,2304]{2,1,0:T(8,128)(2,1)}, bf16[4,16,2304]{2,1,0:T(8,128)(2,1)S(1)}, u32[]{:S(2)}, u32[]{:S(2)}) collective-permute-start(bf16[4,16,2304]{2,1,0:T(8,128)(2,1)} %get-tuple-element.29), channel_id=1, source_target_pairs={{0,12},{1,13},{2,14},{3,15},{4,8},{5,9},{6,10},{7,11},{8,4},{9,5},... | collective-permute-start | bytes 884744 | tf_op jit(solution)/shard_map/ppermute | solution.py:632
  6.1 0.7 copy-start
  6.8 39.2 %collective-permute-start.1 = (bf16[4,16,2304]{2,1,0:T(8,128)(2,1)}, bf16[4,16,2304]{2,1,0:T(8,128)(2,1)}, u32[]{:S(2)}, u32[]{:S(2)}) collective-permute-start(bf16[4,16,2304]{2,1,0:T(8,128)(2,1)} %get-tuple-element.30), channel_id=1, source_target_pairs={{0,8},{1,9},{2,10},{3,11},{4,12},{5,13},{6,14},{7,15},{8,0},{9,1},... | collective-permute-start | bytes 884744 | tf_op jit(solution)/shard_map/ppermute | solution.py:632
  10.3 35.7 %collective-permute-start.2 = (bf16[4,16,2304]{2,1,0:T(8,128)(2,1)}, bf16[4,16,2304]{2,1,0:T(8,128)(2,1)}, u32[]{:S(2)}, u32[]{:S(2)}) collective-permute-start(bf16[4,16,2304]{2,1,0:T(8,128)(2,1)} %get-tuple-element.31), channel_id=1, source_target_pairs={{0,4},{1,5},{2,6},{3,7},{4,0},{5,1},{6,2},{7,3},{8,12},{9,13},{10,... | collective-permute-start | bytes 884744 | tf_op jit(solution)/shard_map/ppermute | solution.py:632
  14.3 7.4 %copy-start.4 = (s32[1,256,2]{1,2,0:T(2,128)S(1)}, s32[1,256,2]{1,2,0:T(2,128)}, u32[]{:S(2)}) copy-start(s32[1,256,2]{1,2,0:T(2,128)} %param.10) | copy-start | bytes 6148
  14.3 37.3 %copy-start.10 = (f32[8,1024]{1,0:T(8,128)S(1)}, f32[8,1024]{1,0:T(8,128)}, u32[]{:S(2)}) copy-start(f32[8,1024]{1,0:T(8,128)} %param.15) | copy-start | bytes 98308
  14.3 37.3 %copy-start.11 = (s32[1,8,8]{2,1,0:T(8,128)S(1)}, s32[1,8,8]{2,1,0:T(8,128)}, u32[]{:S(2)}) copy-start(s32[1,8,8]{2,1,0:T(8,128)} %param.13) | copy-start | bytes 772
  14.3 60.4 %copy-start.9 = (f32[2,3]{1,0:T(2,128)S(1)}, f32[2,3]{1,0:T(2,128)}, u32[]{:S(2)}) copy-start(f32[2,3]{1,0:T(2,128)} %los_ref.1) | copy-start | bytes 76
  14.3 82.4 %all-to-all-start = ((bf16[16,16,5888]{2,1,0:T(8,128)(2,1)}), bf16[16,16,5888]{2,1,0:T(8,128)(2,1)S(1)}, u32[]{:S(2)}, u32[]{:S(2)}) async-start(bf16[16,16,5888]{2,1,0:T(8,128)(2,1)} %pack_inner.1), calls=%async_computation | async-start | bytes 6029312 | tf_op jit(solution)/shard_map/all_to_all | solution.py:639
  27.9 0.7 copy-start.7
  46.0 1.0 copy-start.1
  49.0 0.7 copy-start.5
  49.7 3.9 %collective-permute-start.3 = (bf16[4,16,2304]{2,1,0:T(8,128)(2,1)}, bf16[4,16,2304]{2,1,0:T(8,128)(2,1)}, u32[]{:S(2)}, u32[]{:S(2)}) collective-permute-start(bf16[4,16,2304]{2,1,0:T(8,128)(2,1)} %get-tuple-element.33), channel_id=1, source_target_pairs={{0,1},{1,0},{2,3},{3,2},{4,5},{5,4},{6,7},{7,6},{8,9},{9,8},{10,11... | collective-permute-start | bytes 884744 | tf_op jit(solution)/shard_map/ppermute | solution.py:637
  49.7 18.2 %collective-permute-start.4 = (bf16[4,16,2304]{2,1,0:T(8,128)(2,1)}, bf16[4,16,2304]{2,1,0:T(8,128)(2,1)}, u32[]{:S(2)}, u32[]{:S(2)}) collective-permute-start(bf16[4,16,2304]{2,1,0:T(8,128)(2,1)} %get-tuple-element.34), channel_id=1, source_target_pairs={{0,2},{1,3},{2,0},{3,1},{4,6},{5,7},{6,4},{7,5},{8,10},{9,11},{10,... | collective-permute-start | bytes 884744 | tf_op jit(solution)/shard_map/ppermute | solution.py:637
  49.7 25.0 %collective-permute-start.5 = (bf16[4,16,2304]{2,1,0:T(8,128)(2,1)}, bf16[4,16,2304]{2,1,0:T(8,128)(2,1)}, u32[]{:S(2)}, u32[]{:S(2)}) collective-permute-start(bf16[4,16,2304]{2,1,0:T(8,128)(2,1)} %get-tuple-element.35), channel_id=1, source_target_pairs={{0,3},{1,2},{2,1},{3,0},{4,7},{5,6},{6,5},{7,4},{8,11},{9,10},{10,... | collective-permute-start | bytes 884744 | tf_op jit(solution)/shard_map/ppermute | solution.py:637
  74.7 1.0 copy-start.6
  75.6 0.9 copy-start.8
  78.3 17.5 %collective-permute-start.6 = (f32[48,128]{1,0:T(8,128)S(1)}, f32[48,128]{1,0:T(8,128)S(1)}, u32[]{:S(2)}, u32[]{:S(2)}) collective-permute-start(f32[48,128]{1,0:T(8,128)S(1)} %get-tuple-element.40), channel_id=1, source_target_pairs={{0,1},{1,2},{2,3},{3,4},{4,5},{5,6},{6,7},{7,8},{8,9},{9,10},{10,1... | collective-permute-start | bytes 73736 | tf_op jit(solution)/shard_map/ppermute | solution.py:658
  80.2 15.5 %collective-permute-start.7 = (f32[48,128]{1,0:T(8,128)S(1)}, f32[48,128]{1,0:T(8,128)S(1)}, u32[]{:S(2)}, u32[]{:S(2)}) collective-permute-start(f32[48,128]{1,0:T(8,128)S(1)} %get-tuple-element.41), channel_id=1, source_target_pairs={{1,0},{2,1},{3,2},{4,3},{5,4},{6,5},{7,6},{8,7},{9,8},{10,9},{11,1... | collective-permute-start | bytes 73736 | tf_op jit(solution)/shard_map/ppermute | solution.py:659
  95.9 0.6 copy-start.2
  96.7 5.4 %copy-start.3 = (f32[48,128]{1,0:T(8,128)S(1)}, f32[48,128]{1,0:T(8,128)}, u32[]{:S(2)}) copy-start(f32[48,128]{1,0:T(8,128)} %copy-done.2) | copy-start | bytes 73732
  97.8 4.2 %collective-permute-start.8 = (f32[2,56,128]{2,1,0:T(8,128)S(1)}, f32[2,56,128]{2,1,0:T(8,128)S(1)}, u32[]{:S(2)}, u32[]{:S(2)}) collective-permute-start(f32[2,56,128]{2,1,0:T(8,128)S(1)} %get-tuple-element.45), channel_id=1, source_target_pairs={{0,16},{16,0},{1,17},{17,1},{2,18},{18,2},{3,19},{19,3},{4,20},{20... | collective-permute-start | bytes 172040 | tf_op jit(solution)/shard_map/ppermute | solution.py:665

commit v11 on v10

--- a/solution.py
+++ b/solution.py
@@ -152,15 +152,20 @@
     )(after, *pieces)
 
 
-def pack_inner_kernel(reach, flags_hbm, phases_ref, out_ref, flags_ref, stacked_ref, held_ref, flag_sem, in_sem):
+def snake(n, group):
+    plane, column = n // group, n % group
+    return n + plane % 2 * (group - 1 - 2 * column)
+
+
+def pack_inner_kernel(reach, group, flags_hbm, phases_ref, out_ref, flags_ref, stacked_ref, held_ref, flag_sem, in_sem):
     parts, ifgs, width = out_ref.shape
     span = flags_ref.shape[1] // parts
     flag_copy = pltpu.make_async_copy(flags_hbm, flags_ref, flag_sem)
     flag_copy.start()
 
-    def inward(p):
-        low = pl.multiple_of((p * span + reach) * MBLK, MBLK)
-        return pltpu.make_async_copy(phases_ref.at[:, pl.ds(low, width)], held_ref.at[p], in_sem.at[p])
+    def inward(n):
+        low = pl.multiple_of((snake(n, group) * span + reach) * MBLK, MBLK)
+        return pltpu.make_async_copy(phases_ref.at[:, pl.ds(low, width)], held_ref.at[n], in_sem.at[n])
 
     @pl.loop(0, parts)
     def _(p):
@@ -172,7 +177,7 @@
         out_ref[n, :, start : start + 2 * MBLK] = keep
 
     wanted = list(range(reach, span - reach))
-    expand_masks(flags_ref, stacked_ref, [p * span for p in range(parts)], wanted, tile_out)
+    expand_masks(flags_ref, stacked_ref, [snake(n, group) * span for n in range(parts)], wanted, tile_out)
 
     @pl.loop(0, parts)
     def _(p):
@@ -180,13 +185,13 @@
         out_ref[p] *= held_ref[p]
 
 
-def pack_inner(phases, flags, parts, tiles):
+def pack_inner(phases, flags, parts, group, tiles):
     ifgs = phases.shape[0]
     reach = tiles + 1
     width = (flags.shape[1] // parts - 2 * reach) * MBLK
     hbm = pl.BlockSpec(memory_space=pltpu.HBM)
     return pl.pallas_call(
-        functools.partial(pack_inner_kernel, reach),
+        functools.partial(pack_inner_kernel, reach, group),
         in_specs=[hbm, hbm],
         out_specs=pl.BlockSpec(memory_space=pltpu.VMEM),
         out_shape=jax.ShapeDtypeStruct((parts, ifgs, width), jnp.bfloat16),
@@ -464,7 +469,13 @@
                 values = [value + more for value, more in zip(values, to_other)]
             cover = jnp.sum(jnp.where(place == -r, jnp.broadcast_to(covers, (8, LANES)), 0.0), axis=1, keepdims=True)
             store_cells(out_ref, 3 * half * tiles + r, *values, cover, fixed_ref[r : r + 8, :], north_c)
-    out_ref[:, 4 * tiles :, :] = kept_ref[:, seam:, :]
+    rest = 4 * tiles + kept_ref.shape[1] - seam
+    out_ref[:, 4 * tiles : rest, :] = kept_ref[:, seam:, :]
+    at = -(-(seam + 2) // 8) * 8
+    for half, from_ref in enumerate((before_ref, after_ref)):
+        here = slice(rest + half * tiles, rest + (half + 1) * tiles)
+        out_ref[0, here, :] = from_ref[at : at + tiles, :]
+        out_ref[1, here, :] = jnp.zeros((tiles, LANES), jnp.float32)
 
 
 def finish(kept, before, after, cells, tiles, tracks):
@@ -473,7 +484,7 @@
         functools.partial(finish_kernel, tiles, tracks),
         in_specs=[vmem] * 7,
         out_specs=vmem,
-        out_shape=jax.ShapeDtypeStruct((2, kept.shape[1] + 2 * tiles, LANES), jnp.float32),
+        out_shape=pltpu.VMEM((2, kept.shape[1] + 4 * tiles, LANES), jnp.float32),
         compiler_params=pltpu.CompilerParams(vmem_limit_bytes=medium),
         name="edge_cells",
     )(kept, before, after, *cells)
@@ -529,7 +540,7 @@
         ],
         compiler_params=pltpu.CompilerParams(vmem_limit_bytes=medium),
         name="inner_rows",
-    )(stack, edge, operator, *cells)
+    )(stack, *(pltpu.with_memory_space_constraint(a, pltpu.VMEM) for a in (edge, operator, *cells)))
 
 
 def solve_cells(of_tracks, sight_ref, tracks):
@@ -550,17 +561,17 @@
 
 
 def final_kernel(
-    tiles, span, own, tracks, sight_ref, own_ref, other_ref, north_ref, before_ref, after_ref, east_up_ref, strain_ref, work_ref, line_ref
+    tiles, span, own, tracks, sight_ref, own_ref, other_ref, north_ref, east_up_ref, strain_ref, work_ref, line_ref
 ):
     lines = north_ref.shape[0] // tiles
     rows = lines * span
     here = lax.axis_index("track")
     start = here * (tiles - span)
-    at = -(-(2 * tiles + 2) // 8) * 8 + start
-    line_ref[:span, :] = before_ref[pl.ds(at, span), :]
+    at = sight_ref.shape[0] - 2 * tiles + start
+    line_ref[:span, :] = sight_ref[pl.ds(at, span), :]
     for i in range(lines):
         line_ref[(i + 1) * span : (i + 2) * span, :] = north_ref[pl.ds(i * tiles + start, span), :]
-    line_ref[rows + span : rows + 2 * span, :] = after_ref[pl.ds(at, span), :]
+    line_ref[rows + span : rows + 2 * span, :] = sight_ref[pl.ds(at + tiles, span), :]
     lane = lax.broadcasted_iota(jnp.int32, (rows, LANES), 1)
     tile = lax.broadcasted_iota(jnp.int32, (rows, LANES), 0) % span
 
@@ -591,19 +602,19 @@
                 target[at, i : i + 1, j * LANES : (j + 1) * LANES] = work_ref[field, pl.ds(i * span + first + j, 1), :]
 
 
-def final(sight, vals, others, north, before, after, tiles, span, own, tracks):
+def final(sight, vals, others, north, tiles, span, own, tracks):
     lines = north.shape[0] // tiles
     shape = (lines, own * LANES)
     vmem = pl.BlockSpec(memory_space=pltpu.VMEM)
     return pl.pallas_call(
         functools.partial(final_kernel, tiles, span, own, tracks),
-        in_specs=[vmem] * 6,
+        in_specs=[vmem] * 4,
         out_specs=[vmem] * 2,
         out_shape=[jax.ShapeDtypeStruct((2, *shape), jnp.float32), jax.ShapeDtypeStruct((3, *shape), jnp.float32)],
         scratch_shapes=[pltpu.VMEM((5, lines * span, LANES), jnp.float32), pltpu.VMEM(vals.shape[1:], jnp.float32)],
         compiler_params=pltpu.CompilerParams(vmem_limit_bytes=medium),
         name="solve_and_strain",
-    )(sight, vals, others, north, before, after)
+    )(sight, vals, others, north)
 
 
 def per_device(phases, coherent, pairs, res_index, res_weight, coverage, los, north):
@@ -623,8 +634,11 @@
     later_pairs, _ = lax.optimization_barrier((pairs[0], packed_token))
     steps_j, steps_s = jnp.meshgrid(jnp.arange(group), jnp.arange(planes), indexing="ij")
     sources = (partner_back(plane, -steps_s % planes, planes) * group + partner_back(column, steps_j, group)).reshape(-1)
-    edge_pairs = jnp.take(later_pairs.reshape(parts, -1, 2), sources, axis=0).reshape(-1, 2)
-    operator, edge_operator, formed_token = setup_track(later_pairs, edge_pairs)
+    by_part = later_pairs.reshape(parts, -1, 2)
+    edge_pairs = jnp.take(by_part, sources, axis=0).reshape(-1, 2)
+    order = [snake(n, group) for n in range(parts)]
+    inner_pairs = jnp.concatenate([by_part[p] for p in order], axis=0)
+    operator, edge_operator, formed_token = setup_track(inner_pairs, edge_pairs)
     ids = [(z, c) for z in range(planes) for c in range(group)]
     arrived = [packed[0]] * planes
     for s in range(1, planes):
@@ -637,7 +651,12 @@
         pieces.append(lax.ppermute(by_column[j], "pix", near))
     later_flags, *_ = lax.optimization_barrier((coherent[0], packed_token))
     inner_stack = lax.all_to_all(
-        pack_inner(phases[0], later_flags, parts, tiles), "pix", split_axis=0, concat_axis=0, tiled=True
+        pack_inner(phases[0], later_flags, parts, group, tiles),
+        "pix",
+        split_axis=0,
+        concat_axis=0,
+        tiled=True,
+        axis_index_groups=[order],
     )
     north_cells = north.reshape(rows, LANES)
     cells = (
@@ -667,7 +686,7 @@
         span = tiles
         vals, sight = inner(flat(inner_stack), edge_vals, operator, cells, tiles, tracks, span, 1)
         others = lax.all_gather(vals, "track", axis=0)
-    return tuple(final(sight, vals, others, north_cells, before, after, tiles, span, own_tiles, tracks))
+    return tuple(final(sight, vals, others, north_cells, tiles, span, own_tiles, tracks))
 
 
 def solution(mesh):

time: 103 us -> 103 us (level)
  waiting for transfers between devices: 51.8 us -> 47.6 us
  starting transfers between devices: 21.1 us -> 24.9 us
    ppermute x3, waiting for transfers between devices: 17.4 us -> 13.1 us  [per_device(): arrived[s] = lax.ppermute(packed[s], 'pix', far)]
    ppermute x3, starting transfers between devices: 1.86 us -> 5.67 us  [per_device(): pieces.append(lax.ppermute(by_column[j], 'pix', near))]
    unnamed x26 -> x22, local copies, waits for them, and re-layouts: 7.39 us -> 6.77 us
  transfers between devices with their start and end apart: 10 -> 10, of which waited for: 6 -> 5; matrix products, arithmetic and copies ran while one was open for 3% -> 3% of each run, Pallas kernels for 16% -> 16%
where the time goes in v11:
time: 103 us; the launch traced here: 102 us
  waiting for transfers between devices  47.6 us (46%)
  starting transfers between devices  24.9 us (24%)
  Pallas kernels  20.4 us (20%)
  local copies, waits for them, and re-layouts  8.37 us (8%)
    ppermute x3, waiting for transfers between devices, per_device(): pieces.append(lax.ppermute(by_column[j], 'pix', near))  20.3 us
    ppermute x3, waiting for transfers between devices, per_device(): arrived[s] = lax.ppermute(packed[s], 'pix', far)  13.1 us
    ppermute x1, waiting for transfers between devices, per_device(): before = lax.ppermute(for_after, 'pix', onward)  11.5 us
    unnamed x22, local copies, waits for them, and re-layouts  6.77 us
    all_to_all x1, starting transfers between devices, per_device(): lax.all_to_all(pack_inner(phases[0], later_flags, parts, group, tiles), '...  6.75 us
    ppermute x3, starting transfers between devices, per_device(): pieces.append(lax.ppermute(by_column[j], 'pix', near))  5.67 us
    pallas_call x1, Pallas kernels, setup_track(): pl.pallas_call(operator_kernel, in_specs=[vmem] * 2, out_specs=[vmem] * 3...  5.42 us
    pallas_call x2, Pallas kernels, pack_edges(): pl.pallas_call(functools.partial(pack_edges_kernel, tiles, group, steps),...  4.94 us
  transfers between devices with their start and end apart: 10, of which 5 were waited for; matrix products, arithmetic and copies ran while one was open for 3% of the time, Pallas kernels for 16%

profile of v11, /device:TPU:16, one launch (start us, length us, event | category | flops | bytes accessed | tf_op | source)
XLA Modules:
  0.0 102.1 jit_solution(2181111762724288735)
XLA Ops:
  0.6 2.1 %pack_edges.3 = (bf16[4,16,2304]{2,1,0:T(8,128)(2,1)}, f32[8,128]{1,0:T(8,128)}) custom-call(s32[16,1024]{1,0:T(8,128)} %bitcast.43, bf16[16,131072]{1,0:T(8,128)(2,1)} %bitcast.40), custom_call_target="tpu_custom_call" | custom-call | tf_op jit(solution)/shard_map/pack_edges/pallas_call | solution.py:116
  2.8 0.5 collective-permute-start
  3.3 2.8 %pack_edges.2 = (bf16[4,16,2304]{2,1,0:T(8,128)(2,1)S(1)}, bf16[4,16,2304]{2,1,0:T(8,128)(2,1)}, bf16[4,16,2304]{2,1,0:T(8,128)(2,1)}, f32[8,128]{1,0:T(8,128)}) custom-call(s32[16,1024]{1,0:T(8,128)} %bitcast.44, bf16[16,131072]{1,0:T(8,128)(2,1)} %bitcast.41), custom_call_target="tpu_custom_call" | custom-call | tf_op jit(solution)/shard_map/pack_edges/pallas_call | solution.py:116
  6.1 0.0 copy-start
  6.1 0.7 copy-done
  6.8 3.5 %collective-permute-start.1 = (bf16[4,16,2304]{2,1,0:T(8,128)(2,1)}, bf16[4,16,2304]{2,1,0:T(8,128)(2,1)}, u32[]{:S(2)}, u32[]{:S(2)}) collective-permute-start(bf16[4,16,2304]{2,1,0:T(8,128)(2,1)} %get-tuple-element.30), channel_id=1, source_target_pairs={{0,8},{1,9},{2,10},{3,11},{4,12},{5,13},{6,14},{7,15},{8,0},{9,1},... | collective-permute-start | bytes 884744 | tf_op jit(solution)/shard_map/ppermute | solution.py:646
  10.3 0.0 collective-permute-start.2
  10.3 4.0 %pack_inner.1 = bf16[16,16,5888]{2,1,0:T(8,128)(2,1)} custom-call(s32[16,1024]{1,0:T(8,128)} %bitcast.45, bf16[16,131072]{1,0:T(8,128)(2,1)} %bitcast.42), custom_call_target="tpu_custom_call" | custom-call | tf_op jit(solution)/shard_map/pack_inner/pallas_call | solution.py:193
  14.3 0.0 copy-start.7
  14.3 0.0 copy-start.8
  14.3 0.0 copy-start.9
  14.3 0.0 copy-start.6
  14.3 6.7 %all-to-all-start = ((bf16[16,16,5888]{2,1,0:T(8,128)(2,1)}), bf16[16,16,5888]{2,1,0:T(8,128)(2,1)S(1)}, u32[]{:S(2)}, u32[]{:S(2)}) async-start(bf16[16,16,5888]{2,1,0:T(8,128)(2,1)} %pack_inner.1), calls=%async_computation | async-start | bytes 6029312 | tf_op jit(solution)/shard_map/all_to_all | solution.py:653
  21.1 0.1 broadcast_in_dim.40
  21.1 0.1 broadcast_in_dim.34
  21.2 0.1 broadcast_in_dim.35
  21.3 0.1 broadcast_in_dim.41
  21.4 0.1 broadcast_in_dim.36
  21.5 0.0 copy-done.7
  21.5 0.1 fusion.9
  21.6 0.1 reshape.158
  21.7 0.1 broadcast_in_dim.37
  21.8 0.1 broadcast_in_dim.38
  21.9 0.6 gather_fusion
  22.5 0.1 gather.7
  22.6 0.1 concatenate.4
  22.7 5.4 %misfit_operator.1 = (bf16[272,256]{1,0:T(8,128)(2,1)S(1)}, bf16[272,256]{1,0:T(8,128)(2,1)S(1)}, f32[8,128]{1,0:T(8,128)S(1)}) custom-call(s32[2,256]{1,0:T(2,128)S(1)} %bitcast.38, s32[2,256]{1,0:T(2,128)S(1)} %select_bitcast_fusion.other_ref), custom_call_target="tpu_custom_call" | custom-call | tf_op jit(solution)/shard_map/misfit_operator/pallas_call | solution.py:282
  28.1 0.0 copy-start.4
  28.1 0.7 copy-done.4
  28.8 0.0 collective-permute-done.refs_1_
  28.8 13.1 %collective-permute-done.1.refs_2_ = bf16[4,16,2304]{2,1,0:T(8,128)(2,1)} collective-permute-done((bf16[4,16,2304]{2,1,0:T(8,128)(2,1)}, bf16[4,16,2304]{2,1,0:T(8,128)(2,1)}, u32[]{:S(2)}, u32[]{:S(2)}) %collective-permute-start.1) | collective-permute-done | bytes 294944 | tf_op jit(solution)/shard_map/ppermute | solution.py:646
  41.9 0.0 collective-permute-done.2.refs_3_
  41.9 0.0 copy-start.1
  41.9 1.0 copy-done.1
  42.9 2.0 %regroup.1 = (bf16[4,16,2304]{2,1,0:T(8,128)(2,1)S(1)}, bf16[4,16,2304]{2,1,0:T(8,128)(2,1)}, bf16[4,16,2304]{2,1,0:T(8,128)(2,1)}, bf16[4,16,2304]{2,1,0:T(8,128)(2,1)}) custom-call(f32[8,128]{1,0:T(8,128)S(1)} %get-tuple-element.27.after_ref, bf16[4,16,2304]{2,1,0:T(8,128)(2,1)S(1)} %copy-done.1, bf16[4,16,2304]{2,1,0:T(8,128)(2,1)S(1)} %collective-permute-done.refs_1_, ...), custom_call_target="tpu_custom_call" | custom-call | tf_op jit(solution)/shard_map/regroup/pallas_call | solution.py:145
  44.9 0.0 copy-start.2
  44.9 0.7 copy-done.2
  45.6 0.0 collective-permute-start.3
  45.6 5.5 %collective-permute-start.4 = (bf16[4,16,2304]{2,1,0:T(8,128)(2,1)}, bf16[4,16,2304]{2,1,0:T(8,128)(2,1)}, u32[]{:S(2)}, u32[]{:S(2)}) collective-permute-start(bf16[4,16,2304]{2,1,0:T(8,128)(2,1)} %get-tuple-element.34), channel_id=1, source_target_pairs={{0,2},{1,3},{2,0},{3,1},{4,6},{5,7},{6,4},{7,5},{8,10},{9,11},{10,... | collective-permute-start | bytes 884744 | tf_op jit(solution)/shard_map/ppermute | solution.py:651
  51.1 0.1 collective-permute-start.5
  51.3 0.0 copy-done.8
  51.3 0.0 copy-done.9
  51.3 0.1 reshape.175.cover_ref
  51.4 0.9 copy.23
  52.3 0.9 copy.22
  53.2 0.1 edge_inputs.1
  53.3 0.0 collective-permute-done.3
  53.3 10.1 %collective-permute-done.4 = bf16[4,16,2304]{2,1,0:T(8,128)(2,1)} collective-permute-done((bf16[4,16,2304]{2,1,0:T(8,128)(2,1)}, bf16[4,16,2304]{2,1,0:T(8,128)(2,1)}, u32[]{:S(2)}, u32[]{:S(2)}) %collective-permute-start.4) | collective-permute-done | bytes 294944 | tf_op jit(solution)/shard_map/ppermute | solution.py:651
  63.5 10.2 %collective-permute-done.5 = bf16[4,16,2304]{2,1,0:T(8,128)(2,1)} collective-permute-done((bf16[4,16,2304]{2,1,0:T(8,128)(2,1)}, bf16[4,16,2304]{2,1,0:T(8,128)(2,1)}, u32[]{:S(2)}, u32[]{:S(2)}) %collective-permute-start.5) | collective-permute-done | bytes 294944 | tf_op jit(solution)/shard_map/ppermute | solution.py:651
  73.6 0.0 copy-done.6
  73.6 0.0 copy-start.3
  73.6 1.0 copy-done.3
  74.6 0.9 copy-done.5
  75.5 1.8 %edge_rows.1 = (f32[2,32,128]{2,1,0:T(8,128)S(1)}, f32[48,128]{1,0:T(8,128)S(1)}, f32[48,128]{1,0:T(8,128)S(1)}) custom-call(f32[2,3]{1,0:T(2,128)S(1)} %copy-done.6, bf16[64,2304]{1,0:T(8,128)(2,1)S(1)} %bitcast.39, bf16[64,2304]{1,0:T(8,128)(2,1)} %bitcast.8.refs_1_, bf16[64,2304]{1,0:T(8,128)(2,1)} %bitcast.9.refs_2_, bf16[64,2304]{1,0:T(8,128)(2,1)} %bitcast.10.refs_3_, ...), custom_call_target="tpu_custom_call" | custom-call | flops 54000001024 | tf_op jit(solution)/shard_map/edge_rows/pallas_call | solution.py:420
  77.3 2.0 %collective-permute-start.6 = (f32[48,128]{1,0:T(8,128)S(1)}, f32[48,128]{1,0:T(8,128)S(1)}, u32[]{:S(2)}, u32[]{:S(2)}) collective-permute-start(f32[48,128]{1,0:T(8,128)S(1)} %get-tuple-element.40), channel_id=1, source_target_pairs={{0,1},{1,2},{2,3},{3,4},{4,5},{5,6},{6,7},{7,8},{8,9},{9,10},{10,1... | collective-permute-start | bytes 73736 | tf_op jit(solution)/shard_map/ppermute | solution.py:677
  79.3 4.9 %collective-permute-start.7 = (f32[48,128]{1,0:T(8,128)S(1)}, f32[48,128]{1,0:T(8,128)S(1)}, u32[]{:S(2)}, u32[]{:S(2)}) collective-permute-start(f32[48,128]{1,0:T(8,128)S(1)} %get-tuple-element.41), channel_id=1, source_target_pairs={{1,0},{2,1},{3,2},{4,3},{5,4},{6,5},{7,6},{8,7},{9,8},{10,9},{11,1... | collective-permute-start | bytes 73736 | tf_op jit(solution)/shard_map/ppermute | solution.py:678
  84.2 11.5 %collective-permute-done.6.before_ref = f32[48,128]{1,0:T(8,128)S(1)} collective-permute-done((f32[48,128]{1,0:T(8,128)S(1)}, f32[48,128]{1,0:T(8,128)S(1)}, u32[]{:S(2)}, u32[]{:S(2)}) %collective-permute-start.6) | collective-permute-done | bytes 24608 | tf_op jit(solution)/shard_map/ppermute | solution.py:677
  95.7 0.0 collective-permute-done.7.after_ref
  95.7 0.2 edge_cells.1.edge_ref
  95.9 0.0 all-to-all-done
  95.9 1.2 %inner_rows.1 = (f32[2,56,128]{2,1,0:T(8,128)S(1)}, f32[2,56,128]{2,1,0:T(8,128)S(1)}, f32[24,128]{1,0:T(8,128)S(1)}) custom-call(bf16[256,5888]{1,0:T(8,128)(2,1)S(1)} %bitcast.28, f32[2,64,128]{2,1,0:T(8,128)S(1)} %edge_cells.1.edge_ref, bf16[272,256]{1,0:T(8,128)(2,1)S(1)} %get-tuple-element.42.operator_ref, s32[4,64,128]{2,1,0:T(8,128)S(1)} %bitcast.32, ...), custom_call_target="tpu_custom_call" | custom-call | tf_op jit(solution)/shard_map/inner_rows/pallas_call | solution.py:531
  97.1 1.6 %collective-permute-start.8 = (f32[2,56,128]{2,1,0:T(8,128)S(1)}, f32[2,56,128]{2,1,0:T(8,128)S(1)}, u32[]{:S(2)}, u32[]{:S(2)}) collective-permute-start(f32[2,56,128]{2,1,0:T(8,128)S(1)} %get-tuple-element.45), channel_id=1, source_target_pairs={{0,16},{16,0},{1,17},{17,1},{2,18},{18,2},{3,19},{19,3},{4,20},{20... | collective-permute-start | bytes 172040 | tf_op jit(solution)/shard_map/ppermute | solution.py:684
  98.7 2.7 %collective-permute-done.8 = f32[2,56,128]{2,1,0:T(8,128)S(1)} collective-permute-done((f32[2,56,128]{2,1,0:T(8,128)S(1)}, f32[2,56,128]{2,1,0:T(8,128)S(1)}, u32[]{:S(2)}, u32[]{:S(2)}) %collective-permute-start.8) | collective-permute-done | bytes 57376 | tf_op jit(solution)/shard_map/ppermute | solution.py:684
  101.3 0.8 solve_and_strain.1
  (12 shorter events, 0.1 us)
Async XLA Ops:
  2.8 26.0 %collective-permute-start = (bf16[4,16,2304]{2,1,0:T(8,128)(2,1)}, bf16[4,16,2304]{2,1,0:T(8,128)(2,1)S(1)}, u32[]{:S(2)}, u32[]{:S(2)}) collective-permute-start(bf16[4,16,2304]{2,1,0:T(8,128)(2,1)} %get-tuple-element.29), channel_id=1, source_target_pairs={{0,12},{1,13},{2,14},{3,15},{4,8},{5,9},{6,10},{7,11},{8,4},{9,5},... | collective-permute-start | bytes 884744 | tf_op jit(solution)/shard_map/ppermute | solution.py:646
  6.1 0.7 copy-start
  6.8 35.1 %collective-permute-start.1 = (bf16[4,16,2304]{2,1,0:T(8,128)(2,1)}, bf16[4,16,2304]{2,1,0:T(8,128)(2,1)}, u32[]{:S(2)}, u32[]{:S(2)}) collective-permute-start(bf16[4,16,2304]{2,1,0:T(8,128)(2,1)} %get-tuple-element.30), channel_id=1, source_target_pairs={{0,8},{1,9},{2,10},{3,11},{4,12},{5,13},{6,14},{7,15},{8,0},{9,1},... | collective-permute-start | bytes 884744 | tf_op jit(solution)/shard_map/ppermute | solution.py:646
  10.3 31.6 %collective-permute-start.2 = (bf16[4,16,2304]{2,1,0:T(8,128)(2,1)}, bf16[4,16,2304]{2,1,0:T(8,128)(2,1)}, u32[]{:S(2)}, u32[]{:S(2)}) collective-permute-start(bf16[4,16,2304]{2,1,0:T(8,128)(2,1)} %get-tuple-element.31), channel_id=1, source_target_pairs={{0,4},{1,5},{2,6},{3,7},{4,0},{5,1},{6,2},{7,3},{8,12},{9,13},{10,... | collective-permute-start | bytes 884744 | tf_op jit(solution)/shard_map/ppermute | solution.py:646
  14.3 7.2 %copy-start.7 = (s32[1,256,2]{1,2,0:T(2,128)S(1)}, s32[1,256,2]{1,2,0:T(2,128)}, u32[]{:S(2)}) copy-start(s32[1,256,2]{1,2,0:T(2,128)} %param.10) | copy-start | bytes 6148
  14.3 37.0 %copy-start.8 = (f32[8,1024]{1,0:T(8,128)S(1)}, f32[8,1024]{1,0:T(8,128)}, u32[]{:S(2)}) copy-start(f32[8,1024]{1,0:T(8,128)} %param.15) | copy-start | bytes 98308
  14.3 37.0 %copy-start.9 = (s32[1,8,8]{2,1,0:T(8,128)S(1)}, s32[1,8,8]{2,1,0:T(8,128)}, u32[]{:S(2)}) copy-start(s32[1,8,8]{2,1,0:T(8,128)} %param.13) | copy-start | bytes 772
  14.3 59.3 %copy-start.6 = (f32[2,3]{1,0:T(2,128)S(1)}, f32[2,3]{1,0:T(2,128)}, u32[]{:S(2)}) copy-start(f32[2,3]{1,0:T(2,128)} %los_ref.1) | copy-start | bytes 76
  14.3 81.6 %all-to-all-start = ((bf16[16,16,5888]{2,1,0:T(8,128)(2,1)}), bf16[16,16,5888]{2,1,0:T(8,128)(2,1)S(1)}, u32[]{:S(2)}, u32[]{:S(2)}) async-start(bf16[16,16,5888]{2,1,0:T(8,128)(2,1)} %pack_inner.1), calls=%async_computation | async-start | bytes 6029312 | tf_op jit(solution)/shard_map/all_to_all | solution.py:653
  28.1 0.7 copy-start.4
  41.9 1.0 copy-start.1
  44.9 0.7 copy-start.2
  45.6 7.7 %collective-permute-start.3 = (bf16[4,16,2304]{2,1,0:T(8,128)(2,1)}, bf16[4,16,2304]{2,1,0:T(8,128)(2,1)}, u32[]{:S(2)}, u32[]{:S(2)}) collective-permute-start(bf16[4,16,2304]{2,1,0:T(8,128)(2,1)} %get-tuple-element.33), channel_id=1, source_target_pairs={{0,1},{1,0},{2,3},{3,2},{4,5},{5,4},{6,7},{7,6},{8,9},{9,8},{10,11... | collective-permute-start | bytes 884744 | tf_op jit(solution)/shard_map/ppermute | solution.py:651
  45.6 17.8 %collective-permute-start.4 = (bf16[4,16,2304]{2,1,0:T(8,128)(2,1)}, bf16[4,16,2304]{2,1,0:T(8,128)(2,1)}, u32[]{:S(2)}, u32[]{:S(2)}) collective-permute-start(bf16[4,16,2304]{2,1,0:T(8,128)(2,1)} %get-tuple-element.34), channel_id=1, source_target_pairs={{0,2},{1,3},{2,0},{3,1},{4,6},{5,7},{6,4},{7,5},{8,10},{9,11},{10,... | collective-permute-start | bytes 884744 | tf_op jit(solution)/shard_map/ppermute | solution.py:651
  51.1 22.5 %collective-permute-start.5 = (bf16[4,16,2304]{2,1,0:T(8,128)(2,1)}, bf16[4,16,2304]{2,1,0:T(8,128)(2,1)}, u32[]{:S(2)}, u32[]{:S(2)}) collective-permute-start(bf16[4,16,2304]{2,1,0:T(8,128)(2,1)} %get-tuple-element.35), channel_id=1, source_target_pairs={{0,3},{1,2},{2,1},{3,0},{4,7},{5,6},{6,5},{7,4},{8,11},{9,10},{10,... | collective-permute-start | bytes 884744 | tf_op jit(solution)/shard_map/ppermute | solution.py:651
  73.6 1.0 copy-start.3
  74.6 0.9 copy-start.5
  77.3 18.4 %collective-permute-start.6 = (f32[48,128]{1,0:T(8,128)S(1)}, f32[48,128]{1,0:T(8,128)S(1)}, u32[]{:S(2)}, u32[]{:S(2)}) collective-permute-start(f32[48,128]{1,0:T(8,128)S(1)} %get-tuple-element.40), channel_id=1, source_target_pairs={{0,1},{1,2},{2,3},{3,4},{4,5},{5,6},{6,7},{7,8},{8,9},{9,10},{10,1... | collective-permute-start | bytes 73736 | tf_op jit(solution)/shard_map/ppermute | solution.py:677
  79.3 16.4 %collective-permute-start.7 = (f32[48,128]{1,0:T(8,128)S(1)}, f32[48,128]{1,0:T(8,128)S(1)}, u32[]{:S(2)}, u32[]{:S(2)}) collective-permute-start(f32[48,128]{1,0:T(8,128)S(1)} %get-tuple-element.41), channel_id=1, source_target_pairs={{1,0},{2,1},{3,2},{4,3},{5,4},{6,5},{7,6},{8,7},{9,8},{10,9},{11,1... | collective-permute-start | bytes 73736 | tf_op jit(solution)/shard_map/ppermute | solution.py:678
  97.1 4.2 %collective-permute-start.8 = (f32[2,56,128]{2,1,0:T(8,128)S(1)}, f32[2,56,128]{2,1,0:T(8,128)S(1)}, u32[]{:S(2)}, u32[]{:S(2)}) collective-permute-start(f32[2,56,128]{2,1,0:T(8,128)S(1)} %get-tuple-element.45), channel_id=1, source_target_pairs={{0,16},{16,0},{1,17},{17,1},{2,18},{18,2},{3,19},{19,3},{4,20},{20... | collective-permute-start | bytes 172040 | tf_op jit(solution)/shard_map/ppermute | solution.py:684

commit v12 on v11

--- a/solution.py
+++ b/solution.py
@@ -154,7 +154,7 @@
 
 def snake(n, group):
     plane, column = n // group, n % group
-    return n + plane % 2 * (group - 1 - 2 * column)
+    return n + (plane + 1) % 2 * (group - 1 - 2 * column)
 
 
 def pack_inner_kernel(reach, group, flags_hbm, phases_ref, out_ref, flags_ref, stacked_ref, held_ref, flag_sem, in_sem):
@@ -597,9 +597,8 @@
     first = here * own - start
     for field in range(5):
         target, at = (east_up_ref, field) if field < 2 else (strain_ref, field - 2)
-        for i in range(lines):
-            for j in range(own):
-                target[at, i : i + 1, j * LANES : (j + 1) * LANES] = work_ref[field, pl.ds(i * span + first + j, 1), :]
+        for j in range(own):
+            target[at, :, j * LANES : (j + 1) * LANES] = work_ref[field, pl.ds(first + j, lines, stride=span), :]
 
 
 def final(sight, vals, others, north, tiles, span, own, tracks):

time: 103 us -> 103 us (level)
  starting transfers between devices: 24.9 us -> 20.4 us
  waiting for transfers between devices: 47.6 us -> 52.1 us
    ppermute x3, waiting for transfers between devices: 13.1 us -> 17.4 us  [per_device(): arrived[s] = lax.ppermute(packed[s], 'pix', far)]
    ppermute x3, starting transfers between devices: 5.67 us -> 1.86 us  [per_device(): pieces.append(lax.ppermute(by_column[j], 'pix', near))]
where the time goes in v12:
time: 103 us; the launch traced here: 102 us
  waiting for transfers between devices  52.1 us (51%)
  starting transfers between devices  20.4 us (20%)
  Pallas kernels  20.3 us (20%)
  local copies, waits for them, and re-layouts  8.44 us (8%)
    ppermute x3, waiting for transfers between devices, per_device(): pieces.append(lax.ppermute(by_column[j], 'pix', near))  20 us
    ppermute x3, waiting for transfers between devices, per_device(): arrived[s] = lax.ppermute(packed[s], 'pix', far)  17.4 us
    ppermute x1, waiting for transfers between devices, per_device(): before = lax.ppermute(for_after, 'pix', onward)  12.1 us
    unnamed x22, local copies, waits for them, and re-layouts  6.77 us
    all_to_all x1, starting transfers between devices, per_device(): lax.all_to_all(pack_inner(phases[0], later_flags, parts, group, tiles), '...  6.5 us
    pallas_call x1, Pallas kernels, setup_track(): pl.pallas_call(operator_kernel, in_specs=[vmem] * 2, out_specs=[vmem] * 3...  5.42 us
    pallas_call x2, Pallas kernels, pack_edges(): pl.pallas_call(functools.partial(pack_edges_kernel, tiles, group, steps),...  4.94 us
    ppermute x1, starting transfers between devices, per_device(): after = lax.ppermute(for_before, 'pix', back)  4.41 us
  transfers between devices with their start and end apart: 10, of which 5 were waited for; matrix products, arithmetic and copies ran while one was open for 3% of the time, Pallas kernels for 16%

profile of v12, /device:TPU:16, one launch (start us, length us, event | category | flops | bytes accessed | tf_op | source)
XLA Modules:
  0.0 102.1 jit_solution(6742254702734260195)
XLA Ops:
  0.6 2.1 %pack_edges.3 = (bf16[4,16,2304]{2,1,0:T(8,128)(2,1)}, f32[8,128]{1,0:T(8,128)}) custom-call(s32[16,1024]{1,0:T(8,128)} %bitcast.43, bf16[16,131072]{1,0:T(8,128)(2,1)} %bitcast.40), custom_call_target="tpu_custom_call" | custom-call | tf_op jit(solution)/shard_map/pack_edges/pallas_call | solution.py:116
  2.8 0.5 collective-permute-start
  3.3 2.8 %pack_edges.2 = (bf16[4,16,2304]{2,1,0:T(8,128)(2,1)S(1)}, bf16[4,16,2304]{2,1,0:T(8,128)(2,1)}, bf16[4,16,2304]{2,1,0:T(8,128)(2,1)}, f32[8,128]{1,0:T(8,128)}) custom-call(s32[16,1024]{1,0:T(8,128)} %bitcast.44, bf16[16,131072]{1,0:T(8,128)(2,1)} %bitcast.41), custom_call_target="tpu_custom_call" | custom-call | tf_op jit(solution)/shard_map/pack_edges/pallas_call | solution.py:116
  6.1 0.0 copy-start
  6.1 0.7 copy-done
  6.8 3.5 %collective-permute-start.1 = (bf16[4,16,2304]{2,1,0:T(8,128)(2,1)}, bf16[4,16,2304]{2,1,0:T(8,128)(2,1)}, u32[]{:S(2)}, u32[]{:S(2)}) collective-permute-start(bf16[4,16,2304]{2,1,0:T(8,128)(2,1)} %get-tuple-element.30), channel_id=1, source_target_pairs={{0,8},{1,9},{2,10},{3,11},{4,12},{5,13},{6,14},{7,15},{8,0},{9,1},... | collective-permute-start | bytes 884744 | tf_op jit(solution)/shard_map/ppermute | solution.py:645
  10.3 0.0 collective-permute-start.2
  10.3 4.0 %pack_inner.1 = bf16[16,16,5888]{2,1,0:T(8,128)(2,1)} custom-call(s32[16,1024]{1,0:T(8,128)} %bitcast.45, bf16[16,131072]{1,0:T(8,128)(2,1)} %bitcast.42), custom_call_target="tpu_custom_call" | custom-call | tf_op jit(solution)/shard_map/pack_inner/pallas_call | solution.py:193
  14.3 0.0 copy-start.7
  14.3 0.0 copy-start.8
  14.3 0.0 copy-start.9
  14.3 0.0 copy-start.6
  14.3 6.5 %all-to-all-start = ((bf16[16,16,5888]{2,1,0:T(8,128)(2,1)}), bf16[16,16,5888]{2,1,0:T(8,128)(2,1)S(1)}, u32[]{:S(2)}, u32[]{:S(2)}) async-start(bf16[16,16,5888]{2,1,0:T(8,128)(2,1)} %pack_inner.1), calls=%async_computation | async-start | bytes 6029312 | tf_op jit(solution)/shard_map/all_to_all | solution.py:652
  20.8 0.1 broadcast_in_dim.40
  20.9 0.1 broadcast_in_dim.34
  21.0 0.1 broadcast_in_dim.35
  21.1 0.1 broadcast_in_dim.41
  21.2 0.1 broadcast_in_dim.36
  21.2 0.0 copy-done.7
  21.2 0.1 fusion.9
  21.3 0.1 fusion.10
  21.4 0.1 reshape.158
  21.5 0.1 broadcast_in_dim.37
  21.6 0.1 broadcast_in_dim.38
  21.7 0.6 gather_fusion
  22.3 0.1 gather.7
  22.4 0.1 concatenate.4
  22.5 5.4 %misfit_operator.1 = (bf16[272,256]{1,0:T(8,128)(2,1)S(1)}, bf16[272,256]{1,0:T(8,128)(2,1)S(1)}, f32[8,128]{1,0:T(8,128)S(1)}) custom-call(s32[2,256]{1,0:T(2,128)S(1)} %bitcast.38, s32[2,256]{1,0:T(2,128)S(1)} %select_bitcast_fusion.other_ref), custom_call_target="tpu_custom_call" | custom-call | tf_op jit(solution)/shard_map/misfit_operator/pallas_call | solution.py:282
  27.9 0.0 copy-start.4
  27.9 0.7 copy-done.4
  28.6 0.0 collective-permute-done.refs_1_
  28.6 17.3 %collective-permute-done.1.refs_2_ = bf16[4,16,2304]{2,1,0:T(8,128)(2,1)} collective-permute-done((bf16[4,16,2304]{2,1,0:T(8,128)(2,1)}, bf16[4,16,2304]{2,1,0:T(8,128)(2,1)}, u32[]{:S(2)}, u32[]{:S(2)}) %collective-permute-start.1) | collective-permute-done | bytes 294944 | tf_op jit(solution)/shard_map/ppermute | solution.py:645
  45.9 0.0 collective-permute-done.2.refs_3_
  45.9 0.0 copy-start.1
  46.0 1.0 copy-done.1
  46.9 2.0 %regroup.1 = (bf16[4,16,2304]{2,1,0:T(8,128)(2,1)S(1)}, bf16[4,16,2304]{2,1,0:T(8,128)(2,1)}, bf16[4,16,2304]{2,1,0:T(8,128)(2,1)}, bf16[4,16,2304]{2,1,0:T(8,128)(2,1)}) custom-call(f32[8,128]{1,0:T(8,128)S(1)} %get-tuple-element.27.after_ref, bf16[4,16,2304]{2,1,0:T(8,128)(2,1)S(1)} %copy-done.1, bf16[4,16,2304]{2,1,0:T(8,128)(2,1)S(1)} %collective-permute-done.refs_1_, ...), custom_call_target="tpu_custom_call" | custom-call | tf_op jit(solution)/shard_map/regroup/pallas_call | solution.py:145
  48.9 0.0 copy-start.2
  48.9 0.7 copy-done.2
  49.6 0.0 collective-permute-start.3
  49.6 0.0 collective-permute-start.4
  49.6 1.9 %collective-permute-start.5 = (bf16[4,16,2304]{2,1,0:T(8,128)(2,1)}, bf16[4,16,2304]{2,1,0:T(8,128)(2,1)}, u32[]{:S(2)}, u32[]{:S(2)}) collective-permute-start(bf16[4,16,2304]{2,1,0:T(8,128)(2,1)} %get-tuple-element.35), channel_id=1, source_target_pairs={{0,3},{1,2},{2,1},{3,0},{4,7},{5,6},{6,5},{7,4},{8,11},{9,10},{10,... | collective-permute-start | bytes 884744 | tf_op jit(solution)/shard_map/ppermute | solution.py:650
  51.5 0.0 copy-done.8
  51.5 0.0 copy-done.9
  51.5 0.1 reshape.175.cover_ref
  51.6 0.9 copy.23
  52.5 0.9 copy.22
  53.4 0.1 edge_inputs.1
  53.5 0.0 collective-permute-done.3
  53.5 8.0 %collective-permute-done.4 = bf16[4,16,2304]{2,1,0:T(8,128)(2,1)} collective-permute-done((bf16[4,16,2304]{2,1,0:T(8,128)(2,1)}, bf16[4,16,2304]{2,1,0:T(8,128)(2,1)}, u32[]{:S(2)}, u32[]{:S(2)}) %collective-permute-start.4) | collective-permute-done | bytes 294944 | tf_op jit(solution)/shard_map/ppermute | solution.py:650
  61.5 12.0 %collective-permute-done.5 = bf16[4,16,2304]{2,1,0:T(8,128)(2,1)} collective-permute-done((bf16[4,16,2304]{2,1,0:T(8,128)(2,1)}, bf16[4,16,2304]{2,1,0:T(8,128)(2,1)}, u32[]{:S(2)}, u32[]{:S(2)}) %collective-permute-start.5) | collective-permute-done | bytes 294944 | tf_op jit(solution)/shard_map/ppermute | solution.py:650
  73.5 0.0 copy-done.6
  73.5 1.0 copy-done.3
  74.5 0.9 copy-done.5
  75.4 1.8 %edge_rows.1 = (f32[2,32,128]{2,1,0:T(8,128)S(1)}, f32[48,128]{1,0:T(8,128)S(1)}, f32[48,128]{1,0:T(8,128)S(1)}) custom-call(f32[2,3]{1,0:T(2,128)S(1)} %copy-done.6, bf16[64,2304]{1,0:T(8,128)(2,1)S(1)} %bitcast.39, bf16[64,2304]{1,0:T(8,128)(2,1)} %bitcast.8.refs_1_, bf16[64,2304]{1,0:T(8,128)(2,1)} %bitcast.9.refs_2_, bf16[64,2304]{1,0:T(8,128)(2,1)} %bitcast.10.refs_3_, ...), custom_call_target="tpu_custom_call" | custom-call | flops 54000001024 | tf_op jit(solution)/shard_map/edge_rows/pallas_call | solution.py:420
  77.2 2.0 %collective-permute-start.6 = (f32[48,128]{1,0:T(8,128)S(1)}, f32[48,128]{1,0:T(8,128)S(1)}, u32[]{:S(2)}, u32[]{:S(2)}) collective-permute-start(f32[48,128]{1,0:T(8,128)S(1)} %get-tuple-element.40), channel_id=1, source_target_pairs={{0,1},{1,2},{2,3},{3,4},{4,5},{5,6},{6,7},{7,8},{8,9},{9,10},{10,1... | collective-permute-start | bytes 73736 | tf_op jit(solution)/shard_map/ppermute | solution.py:676
  79.2 4.4 %collective-permute-start.7 = (f32[48,128]{1,0:T(8,128)S(1)}, f32[48,128]{1,0:T(8,128)S(1)}, u32[]{:S(2)}, u32[]{:S(2)}) collective-permute-start(f32[48,128]{1,0:T(8,128)S(1)} %get-tuple-element.41), channel_id=1, source_target_pairs={{1,0},{2,1},{3,2},{4,3},{5,4},{6,5},{7,6},{8,7},{9,8},{10,9},{11,1... | collective-permute-start | bytes 73736 | tf_op jit(solution)/shard_map/ppermute | solution.py:677
  83.7 12.1 %collective-permute-done.6.before_ref = f32[48,128]{1,0:T(8,128)S(1)} collective-permute-done((f32[48,128]{1,0:T(8,128)S(1)}, f32[48,128]{1,0:T(8,128)S(1)}, u32[]{:S(2)}, u32[]{:S(2)}) %collective-permute-start.6) | collective-permute-done | bytes 24608 | tf_op jit(solution)/shard_map/ppermute | solution.py:676
  95.7 0.0 collective-permute-done.7.after_ref
  95.7 0.2 edge_cells.1.edge_ref
  95.9 0.0 all-to-all-done
  95.9 1.2 %inner_rows.1 = (f32[2,56,128]{2,1,0:T(8,128)S(1)}, f32[2,56,128]{2,1,0:T(8,128)S(1)}, f32[24,128]{1,0:T(8,128)S(1)}) custom-call(bf16[256,5888]{1,0:T(8,128)(2,1)S(1)} %bitcast.28, f32[2,64,128]{2,1,0:T(8,128)S(1)} %edge_cells.1.edge_ref, bf16[272,256]{1,0:T(8,128)(2,1)S(1)} %get-tuple-element.42.operator_ref, s32[4,64,128]{2,1,0:T(8,128)S(1)} %bitcast.32, ...), custom_call_target="tpu_custom_call" | custom-call | tf_op jit(solution)/shard_map/inner_rows/pallas_call | solution.py:531
  97.1 1.6 %collective-permute-start.8 = (f32[2,56,128]{2,1,0:T(8,128)S(1)}, f32[2,56,128]{2,1,0:T(8,128)S(1)}, u32[]{:S(2)}, u32[]{:S(2)}) collective-permute-start(f32[2,56,128]{2,1,0:T(8,128)S(1)} %get-tuple-element.45), channel_id=1, source_target_pairs={{0,16},{16,0},{1,17},{17,1},{2,18},{18,2},{3,19},{19,3},{4,20},{20... | collective-permute-start | bytes 172040 | tf_op jit(solution)/shard_map/ppermute | solution.py:683
  98.7 2.7 %collective-permute-done.8 = f32[2,56,128]{2,1,0:T(8,128)S(1)} collective-permute-done((f32[2,56,128]{2,1,0:T(8,128)S(1)}, f32[2,56,128]{2,1,0:T(8,128)S(1)}, u32[]{:S(2)}, u32[]{:S(2)}) %collective-permute-start.8) | collective-permute-done | bytes 57376 | tf_op jit(solution)/shard_map/ppermute | solution.py:683
  101.3 0.8 solve_and_strain.1
  (12 shorter events, 0.1 us)
Async XLA Ops:
  2.8 25.8 %collective-permute-start = (bf16[4,16,2304]{2,1,0:T(8,128)(2,1)}, bf16[4,16,2304]{2,1,0:T(8,128)(2,1)S(1)}, u32[]{:S(2)}, u32[]{:S(2)}) collective-permute-start(bf16[4,16,2304]{2,1,0:T(8,128)(2,1)} %get-tuple-element.29), channel_id=1, source_target_pairs={{0,12},{1,13},{2,14},{3,15},{4,8},{5,9},{6,10},{7,11},{8,4},{9,5},... | collective-permute-start | bytes 884744 | tf_op jit(solution)/shard_map/ppermute | solution.py:645
  6.1 0.7 copy-start
  6.8 39.1 %collective-permute-start.1 = (bf16[4,16,2304]{2,1,0:T(8,128)(2,1)}, bf16[4,16,2304]{2,1,0:T(8,128)(2,1)}, u32[]{:S(2)}, u32[]{:S(2)}) collective-permute-start(bf16[4,16,2304]{2,1,0:T(8,128)(2,1)} %get-tuple-element.30), channel_id=1, source_target_pairs={{0,8},{1,9},{2,10},{3,11},{4,12},{5,13},{6,14},{7,15},{8,0},{9,1},... | collective-permute-start | bytes 884744 | tf_op jit(solution)/shard_map/ppermute | solution.py:645
  10.3 35.7 %collective-permute-start.2 = (bf16[4,16,2304]{2,1,0:T(8,128)(2,1)}, bf16[4,16,2304]{2,1,0:T(8,128)(2,1)}, u32[]{:S(2)}, u32[]{:S(2)}) collective-permute-start(bf16[4,16,2304]{2,1,0:T(8,128)(2,1)} %get-tuple-element.31), channel_id=1, source_target_pairs={{0,4},{1,5},{2,6},{3,7},{4,0},{5,1},{6,2},{7,3},{8,12},{9,13},{10,... | collective-permute-start | bytes 884744 | tf_op jit(solution)/shard_map/ppermute | solution.py:645
  14.3 7.0 %copy-start.7 = (s32[1,256,2]{1,2,0:T(2,128)S(1)}, s32[1,256,2]{1,2,0:T(2,128)}, u32[]{:S(2)}) copy-start(s32[1,256,2]{1,2,0:T(2,128)} %param.10) | copy-start | bytes 6148
  14.3 37.2 %copy-start.8 = (f32[8,1024]{1,0:T(8,128)S(1)}, f32[8,1024]{1,0:T(8,128)}, u32[]{:S(2)}) copy-start(f32[8,1024]{1,0:T(8,128)} %param.15) | copy-start | bytes 98308
  14.3 37.2 %copy-start.9 = (s32[1,8,8]{2,1,0:T(8,128)S(1)}, s32[1,8,8]{2,1,0:T(8,128)}, u32[]{:S(2)}) copy-start(s32[1,8,8]{2,1,0:T(8,128)} %param.13) | copy-start | bytes 772
  14.3 59.2 %copy-start.6 = (f32[2,3]{1,0:T(2,128)S(1)}, f32[2,3]{1,0:T(2,128)}, u32[]{:S(2)}) copy-start(f32[2,3]{1,0:T(2,128)} %los_ref.1) | copy-start | bytes 76
  14.3 81.6 %all-to-all-start = ((bf16[16,16,5888]{2,1,0:T(8,128)(2,1)}), bf16[16,16,5888]{2,1,0:T(8,128)(2,1)S(1)}, u32[]{:S(2)}, u32[]{:S(2)}) async-start(bf16[16,16,5888]{2,1,0:T(8,128)(2,1)} %pack_inner.1), calls=%async_computation | async-start | bytes 6029312 | tf_op jit(solution)/shard_map/all_to_all | solution.py:652
  27.9 0.7 copy-start.4
  45.9 1.0 copy-start.1
  48.9 0.7 copy-start.2
  49.6 3.9 %collective-permute-start.3 = (bf16[4,16,2304]{2,1,0:T(8,128)(2,1)}, bf16[4,16,2304]{2,1,0:T(8,128)(2,1)}, u32[]{:S(2)}, u32[]{:S(2)}) collective-permute-start(bf16[4,16,2304]{2,1,0:T(8,128)(2,1)} %get-tuple-element.33), channel_id=1, source_target_pairs={{0,1},{1,0},{2,3},{3,2},{4,5},{5,4},{6,7},{7,6},{8,9},{9,8},{10,11... | collective-permute-start | bytes 884744 | tf_op jit(solution)/shard_map/ppermute | solution.py:650
  49.6 11.9 %collective-permute-start.4 = (bf16[4,16,2304]{2,1,0:T(8,128)(2,1)}, bf16[4,16,2304]{2,1,0:T(8,128)(2,1)}, u32[]{:S(2)}, u32[]{:S(2)}) collective-permute-start(bf16[4,16,2304]{2,1,0:T(8,128)(2,1)} %get-tuple-element.34), channel_id=1, source_target_pairs={{0,2},{1,3},{2,0},{3,1},{4,6},{5,7},{6,4},{7,5},{8,10},{9,11},{10,... | collective-permute-start | bytes 884744 | tf_op jit(solution)/shard_map/ppermute | solution.py:650
  49.6 23.9 %collective-permute-start.5 = (bf16[4,16,2304]{2,1,0:T(8,128)(2,1)}, bf16[4,16,2304]{2,1,0:T(8,128)(2,1)}, u32[]{:S(2)}, u32[]{:S(2)}) collective-permute-start(bf16[4,16,2304]{2,1,0:T(8,128)(2,1)} %get-tuple-element.35), channel_id=1, source_target_pairs={{0,3},{1,2},{2,1},{3,0},{4,7},{5,6},{6,5},{7,4},{8,11},{9,10},{10,... | collective-permute-start | bytes 884744 | tf_op jit(solution)/shard_map/ppermute | solution.py:650
  73.5 1.0 copy-start.3
  74.5 0.9 copy-start.5
  77.2 18.6 %collective-permute-start.6 = (f32[48,128]{1,0:T(8,128)S(1)}, f32[48,128]{1,0:T(8,128)S(1)}, u32[]{:S(2)}, u32[]{:S(2)}) collective-permute-start(f32[48,128]{1,0:T(8,128)S(1)} %get-tuple-element.40), channel_id=1, source_target_pairs={{0,1},{1,2},{2,3},{3,4},{4,5},{5,6},{6,7},{7,8},{8,9},{9,10},{10,1... | collective-permute-start | bytes 73736 | tf_op jit(solution)/shard_map/ppermute | solution.py:676
  79.2 16.5 %collective-permute-start.7 = (f32[48,128]{1,0:T(8,128)S(1)}, f32[48,128]{1,0:T(8,128)S(1)}, u32[]{:S(2)}, u32[]{:S(2)}) collective-permute-start(f32[48,128]{1,0:T(8,128)S(1)} %get-tuple-element.41), channel_id=1, source_target_pairs={{1,0},{2,1},{3,2},{4,3},{5,4},{6,5},{7,6},{8,7},{9,8},{10,9},{11,1... | collective-permute-start | bytes 73736 | tf_op jit(solution)/shard_map/ppermute | solution.py:677
  97.1 4.2 %collective-permute-start.8 = (f32[2,56,128]{2,1,0:T(8,128)S(1)}, f32[2,56,128]{2,1,0:T(8,128)S(1)}, u32[]{:S(2)}, u32[]{:S(2)}) collective-permute-start(f32[2,56,128]{2,1,0:T(8,128)S(1)} %get-tuple-element.45), channel_id=1, source_target_pairs={{0,16},{16,0},{1,17},{17,1},{2,18},{18,2},{3,19},{19,3},{4,20},{20... | collective-permute-start | bytes 172040 | tf_op jit(solution)/shard_map/ppermute | solution.py:683

commit v13 on v12

--- a/solution.py
+++ b/solution.py
@@ -312,18 +312,16 @@
     lanes = lax.broadcasted_iota(jnp.int32, (8, LANES), 1)
     here = pl.ds(cell, 8)
     sums = [jnp.zeros((8, LANES), jnp.float32)] * 2
-    total = jnp.zeros((8, LANES), jnp.float32)
     for b in range(index_ref.shape[0]):
         weight = weight_ref[b, here, :]
         place = lanes + index_ref[b, here, :] + HALO
         lane = place & (LANES - 1)
         which = place >> 7
-        total = total + weight
         for f in range(2):
             low, mid, high = (pick(near[f][k], lane) for k in range(3))
             taken = jnp.where(which == 0, low, jnp.where(which == 1, mid, high))
             sums[f] = sums[f] + taken * weight
-    return sums[0] / total, sums[1] / total, total
+    return sums
 
 
 def boundary(row, offsets, weights, sources, wanted):
@@ -402,7 +400,7 @@
         for r in range(0, tiles, 8):
             base = half * (tiles + 2) + r
             near = [[fields_ref[f, base + k : base + k + 8, :] for k in range(3)] for f in range(2)]
-            velocity, variance, _ = resample(near, first + r, index_ref, weight_ref)
+            velocity, variance = resample(near, first + r, index_ref, weight_ref)
             for f, values in enumerate((velocity, variance)):
                 kept_ref[f, half * tiles + r : half * tiles + r + 8, :] = values
                 to_ref[f * tiles + r : f * tiles + r + 8, :] = values
@@ -508,7 +506,7 @@
     for r in range(0, rows - 2 * tiles, 8):
         near = [[fields_ref[f, r + k : r + k + 8, :] for k in range(3)] for f in range(2)]
         first = tiles + r
-        velocity, variance, _ = resample(near, first, index_ref, weight_ref)
+        velocity, variance = resample(near, first, index_ref, weight_ref)
         cover = cover_ref[first : first + 8, :].astype(jnp.float32)
         store_cells(out_ref, tiles + first, velocity, variance, cover, north_ref[first : first + 8, :], north_c)
 
@@ -658,9 +656,10 @@
         axis_index_groups=[order],
     )
     north_cells = north.reshape(rows, LANES)
+    weights = res_weight.reshape(-1, rows, LANES)
     cells = (
         res_index.reshape(-1, rows, LANES),
-        res_weight.reshape(-1, rows, LANES),
+        weights / jnp.sum(weights, axis=0, keepdims=True),
         coverage.reshape(rows, 1),
         north_cells,
     )

time: 103 us -> 103 us (level)
  other arithmetic: 0.05 us -> 1.96 us
    unnamed x22 -> x21, local copies, waits for them, and re-layouts: 6.77 us -> 5.87 us
  transfers between devices with their start and end apart: 10 -> 10, of which waited for: 5 -> 5; matrix products, arithmetic and copies ran while one was open for 3% -> 4% of each run, Pallas kernels for 16% -> 16%
where the time goes in v13:
time: 103 us; the launch traced here: 102 us
  waiting for transfers between devices  51.1 us (50%)
  starting transfers between devices  20.4 us (20%)
  Pallas kernels  20.3 us (20%)
  local copies, waits for them, and re-layouts  7.54 us (7%)
  other arithmetic  1.96 us (2%)
    ppermute x3, waiting for transfers between devices, per_device(): pieces.append(lax.ppermute(by_column[j], 'pix', near))  19 us
    ppermute x3, waiting for transfers between devices, per_device(): arrived[s] = lax.ppermute(packed[s], 'pix', far)  17.4 us
    ppermute x1, waiting for transfers between devices, per_device(): before = lax.ppermute(for_after, 'pix', onward)  12.1 us
    all_to_all x1, starting transfers between devices, per_device(): lax.all_to_all(pack_inner(phases[0], later_flags, parts, group, tiles), '...  6.51 us
    unnamed x21, local copies, waits for them, and re-layouts  5.87 us
    pallas_call x1, Pallas kernels, setup_track(): pl.pallas_call(operator_kernel, in_specs=[vmem] * 2, out_specs=[vmem] * 3...  5.42 us
    pallas_call x2, Pallas kernels, pack_edges(): pl.pallas_call(functools.partial(pack_edges_kernel, tiles, group, steps),...  4.95 us
    ppermute x1, starting transfers between devices, per_device(): after = lax.ppermute(for_before, 'pix', back)  4.4 us
  transfers between devices with their start and end apart: 10, of which 5 were waited for; matrix products, arithmetic and copies ran while one was open for 4% of the time, Pallas kernels for 16%

profile of v13, /device:TPU:16, one launch (start us, length us, event | category | flops | bytes accessed | tf_op | source)
XLA Modules:
  0.0 102.1 jit_solution(10189602553469091325)
XLA Ops:
  0.6 2.1 %pack_edges.3 = (bf16[4,16,2304]{2,1,0:T(8,128)(2,1)}, f32[8,128]{1,0:T(8,128)}) custom-call(s32[16,1024]{1,0:T(8,128)} %bitcast.39, bf16[16,131072]{1,0:T(8,128)(2,1)} %bitcast.36), custom_call_target="tpu_custom_call" | custom-call | tf_op jit(solution)/shard_map/pack_edges/pallas_call | solution.py:116
  2.8 0.5 collective-permute-start
  3.3 2.8 %pack_edges.2 = (bf16[4,16,2304]{2,1,0:T(8,128)(2,1)S(1)}, bf16[4,16,2304]{2,1,0:T(8,128)(2,1)}, bf16[4,16,2304]{2,1,0:T(8,128)(2,1)}, f32[8,128]{1,0:T(8,128)}) custom-call(s32[16,1024]{1,0:T(8,128)} %bitcast.40, bf16[16,131072]{1,0:T(8,128)(2,1)} %bitcast.37), custom_call_target="tpu_custom_call" | custom-call | tf_op jit(solution)/shard_map/pack_edges/pallas_call | solution.py:116
  6.1 0.0 copy-start
  6.1 0.7 copy-done
  6.8 3.5 %collective-permute-start.1 = (bf16[4,16,2304]{2,1,0:T(8,128)(2,1)}, bf16[4,16,2304]{2,1,0:T(8,128)(2,1)}, u32[]{:S(2)}, u32[]{:S(2)}) collective-permute-start(bf16[4,16,2304]{2,1,0:T(8,128)(2,1)} %get-tuple-element.30), channel_id=1, source_target_pairs={{0,8},{1,9},{2,10},{3,11},{4,12},{5,13},{6,14},{7,15},{8,0},{9,1},... | collective-permute-start | bytes 884744 | tf_op jit(solution)/shard_map/ppermute | solution.py:643
  10.3 0.0 collective-permute-start.2
  10.3 4.0 %pack_inner.1 = bf16[16,16,5888]{2,1,0:T(8,128)(2,1)} custom-call(s32[16,1024]{1,0:T(8,128)} %bitcast.41, bf16[16,131072]{1,0:T(8,128)(2,1)} %bitcast.38), custom_call_target="tpu_custom_call" | custom-call | tf_op jit(solution)/shard_map/pack_inner/pallas_call | solution.py:193
  14.2 0.0 copy-start.7
  14.3 0.0 copy-start.8
  14.3 0.0 copy-start.9
  14.3 0.0 copy-start.6
  14.3 6.5 %all-to-all-start = ((bf16[16,16,5888]{2,1,0:T(8,128)(2,1)}), bf16[16,16,5888]{2,1,0:T(8,128)(2,1)S(1)}, u32[]{:S(2)}, u32[]{:S(2)}) async-start(bf16[16,16,5888]{2,1,0:T(8,128)(2,1)} %pack_inner.1), calls=%async_computation | async-start | bytes 6029312 | tf_op jit(solution)/shard_map/all_to_all | solution.py:650
  20.8 0.1 broadcast_in_dim.41
  20.9 0.1 broadcast_in_dim.35
  21.0 0.1 broadcast_in_dim.36
  21.1 0.1 broadcast_in_dim.42
  21.1 0.1 broadcast_in_dim.37
  21.2 0.0 copy-done.7
  21.2 0.1 fusion.9
  21.3 0.1 fusion.10
  21.4 0.1 reshape.161
  21.5 0.1 broadcast_in_dim.38
  21.6 0.1 broadcast_in_dim.39
  21.7 0.6 gather_fusion
  22.3 0.1 gather.7
  22.4 0.1 concatenate.4
  22.5 5.4 %misfit_operator.1 = (bf16[272,256]{1,0:T(8,128)(2,1)S(1)}, bf16[272,256]{1,0:T(8,128)(2,1)S(1)}, f32[8,128]{1,0:T(8,128)S(1)}) custom-call(s32[2,256]{1,0:T(2,128)S(1)} %bitcast.34, s32[2,256]{1,0:T(2,128)S(1)} %select_bitcast_fusion.other_ref), custom_call_target="tpu_custom_call" | custom-call | tf_op jit(solution)/shard_map/misfit_operator/pallas_call | solution.py:282
  27.9 0.0 copy-start.4
  27.9 0.7 copy-done.4
  28.6 0.0 collective-permute-done.refs_1_
  28.6 17.4 %collective-permute-done.1.refs_2_ = bf16[4,16,2304]{2,1,0:T(8,128)(2,1)} collective-permute-done((bf16[4,16,2304]{2,1,0:T(8,128)(2,1)}, bf16[4,16,2304]{2,1,0:T(8,128)(2,1)}, u32[]{:S(2)}, u32[]{:S(2)}) %collective-permute-start.1) | collective-permute-done | bytes 294944 | tf_op jit(solution)/shard_map/ppermute | solution.py:643
  46.0 0.0 collective-permute-done.2.refs_3_
  46.0 0.0 copy-start.1
  46.0 1.0 copy-done.1
  46.9 2.0 %regroup.1 = (bf16[4,16,2304]{2,1,0:T(8,128)(2,1)S(1)}, bf16[4,16,2304]{2,1,0:T(8,128)(2,1)}, bf16[4,16,2304]{2,1,0:T(8,128)(2,1)}, bf16[4,16,2304]{2,1,0:T(8,128)(2,1)}) custom-call(f32[8,128]{1,0:T(8,128)S(1)} %get-tuple-element.27.after_ref, bf16[4,16,2304]{2,1,0:T(8,128)(2,1)S(1)} %copy-done.1, bf16[4,16,2304]{2,1,0:T(8,128)(2,1)S(1)} %collective-permute-done.refs_1_, ...), custom_call_target="tpu_custom_call" | custom-call | tf_op jit(solution)/shard_map/regroup/pallas_call | solution.py:145
  49.0 0.7 copy-done.2
  49.7 0.0 collective-permute-start.3
  49.7 0.0 collective-permute-start.4
  49.7 1.9 %collective-permute-start.5 = (bf16[4,16,2304]{2,1,0:T(8,128)(2,1)}, bf16[4,16,2304]{2,1,0:T(8,128)(2,1)}, u32[]{:S(2)}, u32[]{:S(2)}) collective-permute-start(bf16[4,16,2304]{2,1,0:T(8,128)(2,1)} %get-tuple-element.35), channel_id=1, source_target_pairs={{0,3},{1,2},{2,1},{3,0},{4,7},{5,6},{6,5},{7,4},{8,11},{9,10},{10,... | collective-permute-start | bytes 884744 | tf_op jit(solution)/shard_map/ppermute | solution.py:648
  51.5 0.0 copy-done.8
  51.6 0.0 copy-done.9
  51.6 0.1 reshape.178.cover_ref
  51.6 0.9 copy.22
  52.6 1.0 reduce_sum.9
  53.5 0.9 bitcast_divide_fusion.weight_ref.refs_6_
  54.5 0.1 edge_inputs.1
  54.5 0.0 collective-permute-done.3
  54.6 7.0 %collective-permute-done.4 = bf16[4,16,2304]{2,1,0:T(8,128)(2,1)} collective-permute-done((bf16[4,16,2304]{2,1,0:T(8,128)(2,1)}, bf16[4,16,2304]{2,1,0:T(8,128)(2,1)}, u32[]{:S(2)}, u32[]{:S(2)}) %collective-permute-start.4) | collective-permute-done | bytes 294944 | tf_op jit(solution)/shard_map/ppermute | solution.py:648
  61.5 12.0 %collective-permute-done.5 = bf16[4,16,2304]{2,1,0:T(8,128)(2,1)} collective-permute-done((bf16[4,16,2304]{2,1,0:T(8,128)(2,1)}, bf16[4,16,2304]{2,1,0:T(8,128)(2,1)}, u32[]{:S(2)}, u32[]{:S(2)}) %collective-permute-start.5) | collective-permute-done | bytes 294944 | tf_op jit(solution)/shard_map/ppermute | solution.py:648
  73.5 0.0 copy-done.6
  73.5 1.0 copy-done.3
  74.5 0.9 copy-done.5
  75.4 1.8 %edge_rows.1 = (f32[2,32,128]{2,1,0:T(8,128)S(1)}, f32[48,128]{1,0:T(8,128)S(1)}, f32[48,128]{1,0:T(8,128)S(1)}) custom-call(f32[2,3]{1,0:T(2,128)S(1)} %copy-done.6, bf16[64,2304]{1,0:T(8,128)(2,1)S(1)} %bitcast.35, bf16[64,2304]{1,0:T(8,128)(2,1)} %bitcast.8.refs_1_, bf16[64,2304]{1,0:T(8,128)(2,1)} %bitcast.9.refs_2_, bf16[64,2304]{1,0:T(8,128)(2,1)} %bitcast.10.refs_3_, ...), custom_call_target="tpu_custom_call" | custom-call | flops 54000001024 | tf_op jit(solution)/shard_map/edge_rows/pallas_call | solution.py:418
  77.2 2.1 %collective-permute-start.6 = (f32[48,128]{1,0:T(8,128)S(1)}, f32[48,128]{1,0:T(8,128)S(1)}, u32[]{:S(2)}, u32[]{:S(2)}) collective-permute-start(f32[48,128]{1,0:T(8,128)S(1)} %get-tuple-element.40), channel_id=1, source_target_pairs={{0,1},{1,2},{2,3},{3,4},{4,5},{5,6},{6,7},{7,8},{8,9},{9,10},{10,1... | collective-permute-start | bytes 73736 | tf_op jit(solution)/shard_map/ppermute | solution.py:675
  79.3 4.4 %collective-permute-start.7 = (f32[48,128]{1,0:T(8,128)S(1)}, f32[48,128]{1,0:T(8,128)S(1)}, u32[]{:S(2)}, u32[]{:S(2)}) collective-permute-start(f32[48,128]{1,0:T(8,128)S(1)} %get-tuple-element.41), channel_id=1, source_target_pairs={{1,0},{2,1},{3,2},{4,3},{5,4},{6,5},{7,6},{8,7},{9,8},{10,9},{11,1... | collective-permute-start | bytes 73736 | tf_op jit(solution)/shard_map/ppermute | solution.py:676
  83.7 12.1 %collective-permute-done.6.before_ref = f32[48,128]{1,0:T(8,128)S(1)} collective-permute-done((f32[48,128]{1,0:T(8,128)S(1)}, f32[48,128]{1,0:T(8,128)S(1)}, u32[]{:S(2)}, u32[]{:S(2)}) %collective-permute-start.6) | collective-permute-done | bytes 24608 | tf_op jit(solution)/shard_map/ppermute | solution.py:675
  95.7 0.0 collective-permute-done.7.after_ref
  95.7 0.2 edge_cells.1.edge_ref
  95.9 0.0 all-to-all-done
  95.9 1.2 %inner_rows.1 = (f32[2,56,128]{2,1,0:T(8,128)S(1)}, f32[2,56,128]{2,1,0:T(8,128)S(1)}, f32[24,128]{1,0:T(8,128)S(1)}) custom-call(bf16[256,5888]{1,0:T(8,128)(2,1)S(1)} %bitcast.28, f32[2,64,128]{2,1,0:T(8,128)S(1)} %edge_cells.1.edge_ref, bf16[272,256]{1,0:T(8,128)(2,1)S(1)} %get-tuple-element.42.operator_ref, s32[4,64,128]{2,1,0:T(8,128)S(1)} %bitcast.32, ...), custom_call_target="tpu_custom_call" | custom-call | tf_op jit(solution)/shard_map/inner_rows/pallas_call | solution.py:529
  97.1 1.6 %collective-permute-start.8 = (f32[2,56,128]{2,1,0:T(8,128)S(1)}, f32[2,56,128]{2,1,0:T(8,128)S(1)}, u32[]{:S(2)}, u32[]{:S(2)}) collective-permute-start(f32[2,56,128]{2,1,0:T(8,128)S(1)} %get-tuple-element.45), channel_id=1, source_target_pairs={{0,16},{16,0},{1,17},{17,1},{2,18},{18,2},{3,19},{19,3},{4,20},{20... | collective-permute-start | bytes 172040 | tf_op jit(solution)/shard_map/ppermute | solution.py:682
  98.7 2.7 %collective-permute-done.8 = f32[2,56,128]{2,1,0:T(8,128)S(1)} collective-permute-done((f32[2,56,128]{2,1,0:T(8,128)S(1)}, f32[2,56,128]{2,1,0:T(8,128)S(1)}, u32[]{:S(2)}, u32[]{:S(2)}) %collective-permute-start.8) | collective-permute-done | bytes 57376 | tf_op jit(solution)/shard_map/ppermute | solution.py:682
  101.3 0.8 solve_and_strain.1
  (13 shorter events, 0.1 us)
Async XLA Ops:
  2.8 25.8 %collective-permute-start = (bf16[4,16,2304]{2,1,0:T(8,128)(2,1)}, bf16[4,16,2304]{2,1,0:T(8,128)(2,1)S(1)}, u32[]{:S(2)}, u32[]{:S(2)}) collective-permute-start(bf16[4,16,2304]{2,1,0:T(8,128)(2,1)} %get-tuple-element.29), channel_id=1, source_target_pairs={{0,12},{1,13},{2,14},{3,15},{4,8},{5,9},{6,10},{7,11},{8,4},{9,5},... | collective-permute-start | bytes 884744 | tf_op jit(solution)/shard_map/ppermute | solution.py:643
  6.1 0.7 copy-start
  6.8 39.1 %collective-permute-start.1 = (bf16[4,16,2304]{2,1,0:T(8,128)(2,1)}, bf16[4,16,2304]{2,1,0:T(8,128)(2,1)}, u32[]{:S(2)}, u32[]{:S(2)}) collective-permute-start(bf16[4,16,2304]{2,1,0:T(8,128)(2,1)} %get-tuple-element.30), channel_id=1, source_target_pairs={{0,8},{1,9},{2,10},{3,11},{4,12},{5,13},{6,14},{7,15},{8,0},{9,1},... | collective-permute-start | bytes 884744 | tf_op jit(solution)/shard_map/ppermute | solution.py:643
  10.3 35.7 %collective-permute-start.2 = (bf16[4,16,2304]{2,1,0:T(8,128)(2,1)}, bf16[4,16,2304]{2,1,0:T(8,128)(2,1)}, u32[]{:S(2)}, u32[]{:S(2)}) collective-permute-start(bf16[4,16,2304]{2,1,0:T(8,128)(2,1)} %get-tuple-element.31), channel_id=1, source_target_pairs={{0,4},{1,5},{2,6},{3,7},{4,0},{5,1},{6,2},{7,3},{8,12},{9,13},{10,... | collective-permute-start | bytes 884744 | tf_op jit(solution)/shard_map/ppermute | solution.py:643
  14.2 7.0 %copy-start.7 = (s32[1,256,2]{1,2,0:T(2,128)S(1)}, s32[1,256,2]{1,2,0:T(2,128)}, u32[]{:S(2)}) copy-start(s32[1,256,2]{1,2,0:T(2,128)} %param.10) | copy-start | bytes 6148
  14.3 37.3 %copy-start.8 = (f32[8,1024]{1,0:T(8,128)S(1)}, f32[8,1024]{1,0:T(8,128)}, u32[]{:S(2)}) copy-start(f32[8,1024]{1,0:T(8,128)} %param.15) | copy-start | bytes 98308
  14.3 37.3 %copy-start.9 = (s32[1,8,8]{2,1,0:T(8,128)S(1)}, s32[1,8,8]{2,1,0:T(8,128)}, u32[]{:S(2)}) copy-start(s32[1,8,8]{2,1,0:T(8,128)} %param.13) | copy-start | bytes 772
  14.3 59.3 %copy-start.6 = (f32[2,3]{1,0:T(2,128)S(1)}, f32[2,3]{1,0:T(2,128)}, u32[]{:S(2)}) copy-start(f32[2,3]{1,0:T(2,128)} %los_ref.1) | copy-start | bytes 76
  14.3 81.6 %all-to-all-start = ((bf16[16,16,5888]{2,1,0:T(8,128)(2,1)}), bf16[16,16,5888]{2,1,0:T(8,128)(2,1)S(1)}, u32[]{:S(2)}, u32[]{:S(2)}) async-start(bf16[16,16,5888]{2,1,0:T(8,128)(2,1)} %pack_inner.1), calls=%async_computation | async-start | bytes 6029312 | tf_op jit(solution)/shard_map/all_to_all | solution.py:650
  27.9 0.7 copy-start.4
  46.0 1.0 copy-start.1
  48.9 0.7 copy-start.2
  49.7 4.9 %collective-permute-start.3 = (bf16[4,16,2304]{2,1,0:T(8,128)(2,1)}, bf16[4,16,2304]{2,1,0:T(8,128)(2,1)}, u32[]{:S(2)}, u32[]{:S(2)}) collective-permute-start(bf16[4,16,2304]{2,1,0:T(8,128)(2,1)} %get-tuple-element.33), channel_id=1, source_target_pairs={{0,1},{1,0},{2,3},{3,2},{4,5},{5,4},{6,7},{7,6},{8,9},{9,8},{10,11... | collective-permute-start | bytes 884744 | tf_op jit(solution)/shard_map/ppermute | solution.py:648
  49.7 11.8 %collective-permute-start.4 = (bf16[4,16,2304]{2,1,0:T(8,128)(2,1)}, bf16[4,16,2304]{2,1,0:T(8,128)(2,1)}, u32[]{:S(2)}, u32[]{:S(2)}) collective-permute-start(bf16[4,16,2304]{2,1,0:T(8,128)(2,1)} %get-tuple-element.34), channel_id=1, source_target_pairs={{0,2},{1,3},{2,0},{3,1},{4,6},{5,7},{6,4},{7,5},{8,10},{9,11},{10,... | collective-permute-start | bytes 884744 | tf_op jit(solution)/shard_map/ppermute | solution.py:648
  49.7 23.9 %collective-permute-start.5 = (bf16[4,16,2304]{2,1,0:T(8,128)(2,1)}, bf16[4,16,2304]{2,1,0:T(8,128)(2,1)}, u32[]{:S(2)}, u32[]{:S(2)}) collective-permute-start(bf16[4,16,2304]{2,1,0:T(8,128)(2,1)} %get-tuple-element.35), channel_id=1, source_target_pairs={{0,3},{1,2},{2,1},{3,0},{4,7},{5,6},{6,5},{7,4},{8,11},{9,10},{10,... | collective-permute-start | bytes 884744 | tf_op jit(solution)/shard_map/ppermute | solution.py:648
  73.5 1.0 copy-start.3
  74.5 0.9 copy-start.5
  77.2 18.6 %collective-permute-start.6 = (f32[48,128]{1,0:T(8,128)S(1)}, f32[48,128]{1,0:T(8,128)S(1)}, u32[]{:S(2)}, u32[]{:S(2)}) collective-permute-start(f32[48,128]{1,0:T(8,128)S(1)} %get-tuple-element.40), channel_id=1, source_target_pairs={{0,1},{1,2},{2,3},{3,4},{4,5},{5,6},{6,7},{7,8},{8,9},{9,10},{10,1... | collective-permute-start | bytes 73736 | tf_op jit(solution)/shard_map/ppermute | solution.py:675
  79.3 16.5 %collective-permute-start.7 = (f32[48,128]{1,0:T(8,128)S(1)}, f32[48,128]{1,0:T(8,128)S(1)}, u32[]{:S(2)}, u32[]{:S(2)}) collective-permute-start(f32[48,128]{1,0:T(8,128)S(1)} %get-tuple-element.41), channel_id=1, source_target_pairs={{1,0},{2,1},{3,2},{4,3},{5,4},{6,5},{7,6},{8,7},{9,8},{10,9},{11,1... | collective-permute-start | bytes 73736 | tf_op jit(solution)/shard_map/ppermute | solution.py:676
  97.1 4.2 %collective-permute-start.8 = (f32[2,56,128]{2,1,0:T(8,128)S(1)}, f32[2,56,128]{2,1,0:T(8,128)S(1)}, u32[]{:S(2)}, u32[]{:S(2)}) collective-permute-start(f32[2,56,128]{2,1,0:T(8,128)S(1)} %get-tuple-element.45), channel_id=1, source_target_pairs={{0,16},{16,0},{1,17},{17,1},{2,18},{18,2},{3,19},{19,3},{4,20},{20... | collective-permute-start | bytes 172040 | tf_op jit(solution)/shard_map/ppermute | solution.py:682

commit v14 on v12

--- a/solution.py
+++ b/solution.py
@@ -517,8 +517,9 @@
     lines = rows // tiles + 2
     for half, to_ref in zip((here, 1 - here), to_refs):
         start = half * (tiles - span)
-        for i in range(lines):
-            to_ref[:, i * span : (i + 1) * span, :] = out_ref[:, pl.ds(i * tiles + start, span), :]
+        for field in range(2):
+            for j in range(span):
+                to_ref[field, pl.ds(j, lines, stride=span), :] = out_ref[field, pl.ds(start + j, lines, stride=tiles), :]
         left = to_ref.shape[1] - lines * span
         if left:
             to_ref[:, lines * span :, :] = jnp.zeros((2, left, LANES), jnp.float32)

time: 103 us -> 103 us (level)
  no operation moved by 1% of the time
where the time goes in v14:
time: 103 us; the launch traced here: 102 us
  waiting for transfers between devices  52.1 us (51%)
  starting transfers between devices  20.4 us (20%)
  Pallas kernels  20.3 us (20%)
  local copies, waits for them, and re-layouts  8.44 us (8%)
    ppermute x3, waiting for transfers between devices, per_device(): pieces.append(lax.ppermute(by_column[j], 'pix', near))  20 us
    ppermute x3, waiting for transfers between devices, per_device(): arrived[s] = lax.ppermute(packed[s], 'pix', far)  17.4 us
    ppermute x1, waiting for transfers between devices, per_device(): before = lax.ppermute(for_after, 'pix', onward)  12.1 us
    unnamed x22, local copies, waits for them, and re-layouts  6.77 us
    all_to_all x1, starting transfers between devices, per_device(): lax.all_to_all(pack_inner(phases[0], later_flags, parts, group, tiles), '...  6.5 us
    pallas_call x1, Pallas kernels, setup_track(): pl.pallas_call(operator_kernel, in_specs=[vmem] * 2, out_specs=[vmem] * 3...  5.42 us
    pallas_call x2, Pallas kernels, pack_edges(): pl.pallas_call(functools.partial(pack_edges_kernel, tiles, group, steps),...  4.94 us
    ppermute x1, starting transfers between devices, per_device(): after = lax.ppermute(for_before, 'pix', back)  4.41 us
  transfers between devices with their start and end apart: 10, of which 5 were waited for; matrix products, arithmetic and copies ran while one was open for 3% of the time, Pallas kernels for 16%

profile of v14, /device:TPU:16, one launch (start us, length us, event | category | flops | bytes accessed | tf_op | source)
XLA Modules:
  0.0 102.1 jit_solution(4536467291020242637)
XLA Ops:
  0.6 2.1 %pack_edges.3 = (bf16[4,16,2304]{2,1,0:T(8,128)(2,1)}, f32[8,128]{1,0:T(8,128)}) custom-call(s32[16,1024]{1,0:T(8,128)} %bitcast.43, bf16[16,131072]{1,0:T(8,128)(2,1)} %bitcast.40), custom_call_target="tpu_custom_call" | custom-call | tf_op jit(solution)/shard_map/pack_edges/pallas_call | solution.py:116
  2.8 0.5 collective-permute-start
  3.3 2.8 %pack_edges.2 = (bf16[4,16,2304]{2,1,0:T(8,128)(2,1)S(1)}, bf16[4,16,2304]{2,1,0:T(8,128)(2,1)}, bf16[4,16,2304]{2,1,0:T(8,128)(2,1)}, f32[8,128]{1,0:T(8,128)}) custom-call(s32[16,1024]{1,0:T(8,128)} %bitcast.44, bf16[16,131072]{1,0:T(8,128)(2,1)} %bitcast.41), custom_call_target="tpu_custom_call" | custom-call | tf_op jit(solution)/shard_map/pack_edges/pallas_call | solution.py:116
  6.1 0.0 copy-start
  6.1 0.7 copy-done
  6.8 3.5 %collective-permute-start.1 = (bf16[4,16,2304]{2,1,0:T(8,128)(2,1)}, bf16[4,16,2304]{2,1,0:T(8,128)(2,1)}, u32[]{:S(2)}, u32[]{:S(2)}) collective-permute-start(bf16[4,16,2304]{2,1,0:T(8,128)(2,1)} %get-tuple-element.30), channel_id=1, source_target_pairs={{0,8},{1,9},{2,10},{3,11},{4,12},{5,13},{6,14},{7,15},{8,0},{9,1},... | collective-permute-start | bytes 884744 | tf_op jit(solution)/shard_map/ppermute | solution.py:646
  10.3 0.0 collective-permute-start.2
  10.3 4.0 %pack_inner.1 = bf16[16,16,5888]{2,1,0:T(8,128)(2,1)} custom-call(s32[16,1024]{1,0:T(8,128)} %bitcast.45, bf16[16,131072]{1,0:T(8,128)(2,1)} %bitcast.42), custom_call_target="tpu_custom_call" | custom-call | tf_op jit(solution)/shard_map/pack_inner/pallas_call | solution.py:193
  14.3 0.0 copy-start.7
  14.3 0.0 copy-start.8
  14.3 0.0 copy-start.9
  14.3 0.0 copy-start.6
  14.3 6.5 %all-to-all-start = ((bf16[16,16,5888]{2,1,0:T(8,128)(2,1)}), bf16[16,16,5888]{2,1,0:T(8,128)(2,1)S(1)}, u32[]{:S(2)}, u32[]{:S(2)}) async-start(bf16[16,16,5888]{2,1,0:T(8,128)(2,1)} %pack_inner.1), calls=%async_computation | async-start | bytes 6029312 | tf_op jit(solution)/shard_map/all_to_all | solution.py:653
  20.8 0.1 broadcast_in_dim.40
  20.9 0.1 broadcast_in_dim.34
  21.0 0.1 broadcast_in_dim.35
  21.1 0.1 broadcast_in_dim.41
  21.2 0.1 broadcast_in_dim.36
  21.2 0.0 copy-done.7
  21.2 0.1 fusion.9
  21.3 0.1 fusion.10
  21.4 0.1 reshape.158
  21.5 0.1 broadcast_in_dim.37
  21.6 0.1 broadcast_in_dim.38
  21.7 0.6 gather_fusion
  22.3 0.1 gather.7
  22.4 0.1 concatenate.4
  22.5 5.4 %misfit_operator.1 = (bf16[272,256]{1,0:T(8,128)(2,1)S(1)}, bf16[272,256]{1,0:T(8,128)(2,1)S(1)}, f32[8,128]{1,0:T(8,128)S(1)}) custom-call(s32[2,256]{1,0:T(2,128)S(1)} %bitcast.38, s32[2,256]{1,0:T(2,128)S(1)} %select_bitcast_fusion.other_ref), custom_call_target="tpu_custom_call" | custom-call | tf_op jit(solution)/shard_map/misfit_operator/pallas_call | solution.py:282
  27.9 0.0 copy-start.4
  27.9 0.7 copy-done.4
  28.6 0.0 collective-permute-done.refs_1_
  28.6 17.3 %collective-permute-done.1.refs_2_ = bf16[4,16,2304]{2,1,0:T(8,128)(2,1)} collective-permute-done((bf16[4,16,2304]{2,1,0:T(8,128)(2,1)}, bf16[4,16,2304]{2,1,0:T(8,128)(2,1)}, u32[]{:S(2)}, u32[]{:S(2)}) %collective-permute-start.1) | collective-permute-done | bytes 294944 | tf_op jit(solution)/shard_map/ppermute | solution.py:646
  45.9 0.0 collective-permute-done.2.refs_3_
  45.9 0.0 copy-start.1
  46.0 1.0 copy-done.1
  46.9 2.0 %regroup.1 = (bf16[4,16,2304]{2,1,0:T(8,128)(2,1)S(1)}, bf16[4,16,2304]{2,1,0:T(8,128)(2,1)}, bf16[4,16,2304]{2,1,0:T(8,128)(2,1)}, bf16[4,16,2304]{2,1,0:T(8,128)(2,1)}) custom-call(f32[8,128]{1,0:T(8,128)S(1)} %get-tuple-element.27.after_ref, bf16[4,16,2304]{2,1,0:T(8,128)(2,1)S(1)} %copy-done.1, bf16[4,16,2304]{2,1,0:T(8,128)(2,1)S(1)} %collective-permute-done.refs_1_, ...), custom_call_target="tpu_custom_call" | custom-call | tf_op jit(solution)/shard_map/regroup/pallas_call | solution.py:145
  48.9 0.0 copy-start.2
  48.9 0.7 copy-done.2
  49.6 0.0 collective-permute-start.3
  49.6 0.0 collective-permute-start.4
  49.6 1.9 %collective-permute-start.5 = (bf16[4,16,2304]{2,1,0:T(8,128)(2,1)}, bf16[4,16,2304]{2,1,0:T(8,128)(2,1)}, u32[]{:S(2)}, u32[]{:S(2)}) collective-permute-start(bf16[4,16,2304]{2,1,0:T(8,128)(2,1)} %get-tuple-element.35), channel_id=1, source_target_pairs={{0,3},{1,2},{2,1},{3,0},{4,7},{5,6},{6,5},{7,4},{8,11},{9,10},{10,... | collective-permute-start | bytes 884744 | tf_op jit(solution)/shard_map/ppermute | solution.py:651
  51.5 0.0 copy-done.8
  51.5 0.0 copy-done.9
  51.5 0.1 reshape.175.cover_ref
  51.6 0.9 copy.23
  52.5 0.9 copy.22
  53.4 0.1 edge_inputs.1
  53.5 0.0 collective-permute-done.3
  53.5 8.0 %collective-permute-done.4 = bf16[4,16,2304]{2,1,0:T(8,128)(2,1)} collective-permute-done((bf16[4,16,2304]{2,1,0:T(8,128)(2,1)}, bf16[4,16,2304]{2,1,0:T(8,128)(2,1)}, u32[]{:S(2)}, u32[]{:S(2)}) %collective-permute-start.4) | collective-permute-done | bytes 294944 | tf_op jit(solution)/shard_map/ppermute | solution.py:651
  61.5 12.0 %collective-permute-done.5 = bf16[4,16,2304]{2,1,0:T(8,128)(2,1)} collective-permute-done((bf16[4,16,2304]{2,1,0:T(8,128)(2,1)}, bf16[4,16,2304]{2,1,0:T(8,128)(2,1)}, u32[]{:S(2)}, u32[]{:S(2)}) %collective-permute-start.5) | collective-permute-done | bytes 294944 | tf_op jit(solution)/shard_map/ppermute | solution.py:651
  73.5 0.0 copy-done.6
  73.5 1.0 copy-done.3
  74.5 0.9 copy-done.5
  75.4 1.8 %edge_rows.1 = (f32[2,32,128]{2,1,0:T(8,128)S(1)}, f32[48,128]{1,0:T(8,128)S(1)}, f32[48,128]{1,0:T(8,128)S(1)}) custom-call(f32[2,3]{1,0:T(2,128)S(1)} %copy-done.6, bf16[64,2304]{1,0:T(8,128)(2,1)S(1)} %bitcast.39, bf16[64,2304]{1,0:T(8,128)(2,1)} %bitcast.8.refs_1_, bf16[64,2304]{1,0:T(8,128)(2,1)} %bitcast.9.refs_2_, bf16[64,2304]{1,0:T(8,128)(2,1)} %bitcast.10.refs_3_, ...), custom_call_target="tpu_custom_call" | custom-call | flops 54000001024 | tf_op jit(solution)/shard_map/edge_rows/pallas_call | solution.py:420
  77.2 2.0 %collective-permute-start.6 = (f32[48,128]{1,0:T(8,128)S(1)}, f32[48,128]{1,0:T(8,128)S(1)}, u32[]{:S(2)}, u32[]{:S(2)}) collective-permute-start(f32[48,128]{1,0:T(8,128)S(1)} %get-tuple-element.40), channel_id=1, source_target_pairs={{0,1},{1,2},{2,3},{3,4},{4,5},{5,6},{6,7},{7,8},{8,9},{9,10},{10,1... | collective-permute-start | bytes 73736 | tf_op jit(solution)/shard_map/ppermute | solution.py:677
  79.2 4.4 %collective-permute-start.7 = (f32[48,128]{1,0:T(8,128)S(1)}, f32[48,128]{1,0:T(8,128)S(1)}, u32[]{:S(2)}, u32[]{:S(2)}) collective-permute-start(f32[48,128]{1,0:T(8,128)S(1)} %get-tuple-element.41), channel_id=1, source_target_pairs={{1,0},{2,1},{3,2},{4,3},{5,4},{6,5},{7,6},{8,7},{9,8},{10,9},{11,1... | collective-permute-start | bytes 73736 | tf_op jit(solution)/shard_map/ppermute | solution.py:678
  83.7 12.1 %collective-permute-done.6.before_ref = f32[48,128]{1,0:T(8,128)S(1)} collective-permute-done((f32[48,128]{1,0:T(8,128)S(1)}, f32[48,128]{1,0:T(8,128)S(1)}, u32[]{:S(2)}, u32[]{:S(2)}) %collective-permute-start.6) | collective-permute-done | bytes 24608 | tf_op jit(solution)/shard_map/ppermute | solution.py:677
  95.7 0.0 collective-permute-done.7.after_ref
  95.7 0.2 edge_cells.1.edge_ref
  95.9 0.0 all-to-all-done
  95.9 1.2 %inner_rows.1 = (f32[2,56,128]{2,1,0:T(8,128)S(1)}, f32[2,56,128]{2,1,0:T(8,128)S(1)}, f32[24,128]{1,0:T(8,128)S(1)}) custom-call(bf16[256,5888]{1,0:T(8,128)(2,1)S(1)} %bitcast.28, f32[2,64,128]{2,1,0:T(8,128)S(1)} %edge_cells.1.edge_ref, bf16[272,256]{1,0:T(8,128)(2,1)S(1)} %get-tuple-element.42.operator_ref, s32[4,64,128]{2,1,0:T(8,128)S(1)} %bitcast.32, ...), custom_call_target="tpu_custom_call" | custom-call | tf_op jit(solution)/shard_map/inner_rows/pallas_call | solution.py:532
  97.1 1.6 %collective-permute-start.8 = (f32[2,56,128]{2,1,0:T(8,128)S(1)}, f32[2,56,128]{2,1,0:T(8,128)S(1)}, u32[]{:S(2)}, u32[]{:S(2)}) collective-permute-start(f32[2,56,128]{2,1,0:T(8,128)S(1)} %get-tuple-element.45), channel_id=1, source_target_pairs={{0,16},{16,0},{1,17},{17,1},{2,18},{18,2},{3,19},{19,3},{4,20},{20... | collective-permute-start | bytes 172040 | tf_op jit(solution)/shard_map/ppermute | solution.py:684
  98.7 2.7 %collective-permute-done.8 = f32[2,56,128]{2,1,0:T(8,128)S(1)} collective-permute-done((f32[2,56,128]{2,1,0:T(8,128)S(1)}, f32[2,56,128]{2,1,0:T(8,128)S(1)}, u32[]{:S(2)}, u32[]{:S(2)}) %collective-permute-start.8) | collective-permute-done | bytes 57376 | tf_op jit(solution)/shard_map/ppermute | solution.py:684
  101.3 0.8 solve_and_strain.1
  (12 shorter events, 0.1 us)
Async XLA Ops:
  2.8 25.8 %collective-permute-start = (bf16[4,16,2304]{2,1,0:T(8,128)(2,1)}, bf16[4,16,2304]{2,1,0:T(8,128)(2,1)S(1)}, u32[]{:S(2)}, u32[]{:S(2)}) collective-permute-start(bf16[4,16,2304]{2,1,0:T(8,128)(2,1)} %get-tuple-element.29), channel_id=1, source_target_pairs={{0,12},{1,13},{2,14},{3,15},{4,8},{5,9},{6,10},{7,11},{8,4},{9,5},... | collective-permute-start | bytes 884744 | tf_op jit(solution)/shard_map/ppermute | solution.py:646
  6.1 0.7 copy-start
  6.8 39.1 %collective-permute-start.1 = (bf16[4,16,2304]{2,1,0:T(8,128)(2,1)}, bf16[4,16,2304]{2,1,0:T(8,128)(2,1)}, u32[]{:S(2)}, u32[]{:S(2)}) collective-permute-start(bf16[4,16,2304]{2,1,0:T(8,128)(2,1)} %get-tuple-element.30), channel_id=1, source_target_pairs={{0,8},{1,9},{2,10},{3,11},{4,12},{5,13},{6,14},{7,15},{8,0},{9,1},... | collective-permute-start | bytes 884744 | tf_op jit(solution)/shard_map/ppermute | solution.py:646
  10.3 35.7 %collective-permute-start.2 = (bf16[4,16,2304]{2,1,0:T(8,128)(2,1)}, bf16[4,16,2304]{2,1,0:T(8,128)(2,1)}, u32[]{:S(2)}, u32[]{:S(2)}) collective-permute-start(bf16[4,16,2304]{2,1,0:T(8,128)(2,1)} %get-tuple-element.31), channel_id=1, source_target_pairs={{0,4},{1,5},{2,6},{3,7},{4,0},{5,1},{6,2},{7,3},{8,12},{9,13},{10,... | collective-permute-start | bytes 884744 | tf_op jit(solution)/shard_map/ppermute | solution.py:646
  14.3 7.0 %copy-start.7 = (s32[1,256,2]{1,2,0:T(2,128)S(1)}, s32[1,256,2]{1,2,0:T(2,128)}, u32[]{:S(2)}) copy-start(s32[1,256,2]{1,2,0:T(2,128)} %param.10) | copy-start | bytes 6148
  14.3 37.2 %copy-start.8 = (f32[8,1024]{1,0:T(8,128)S(1)}, f32[8,1024]{1,0:T(8,128)}, u32[]{:S(2)}) copy-start(f32[8,1024]{1,0:T(8,128)} %param.15) | copy-start | bytes 98308
  14.3 37.2 %copy-start.9 = (s32[1,8,8]{2,1,0:T(8,128)S(1)}, s32[1,8,8]{2,1,0:T(8,128)}, u32[]{:S(2)}) copy-start(s32[1,8,8]{2,1,0:T(8,128)} %param.13) | copy-start | bytes 772
  14.3 59.2 %copy-start.6 = (f32[2,3]{1,0:T(2,128)S(1)}, f32[2,3]{1,0:T(2,128)}, u32[]{:S(2)}) copy-start(f32[2,3]{1,0:T(2,128)} %los_ref.1) | copy-start | bytes 76
  14.3 81.6 %all-to-all-start = ((bf16[16,16,5888]{2,1,0:T(8,128)(2,1)}), bf16[16,16,5888]{2,1,0:T(8,128)(2,1)S(1)}, u32[]{:S(2)}, u32[]{:S(2)}) async-start(bf16[16,16,5888]{2,1,0:T(8,128)(2,1)} %pack_inner.1), calls=%async_computation | async-start | bytes 6029312 | tf_op jit(solution)/shard_map/all_to_all | solution.py:653
  27.9 0.7 copy-start.4
  45.9 1.0 copy-start.1
  48.9 0.7 copy-start.2
  49.6 3.9 %collective-permute-start.3 = (bf16[4,16,2304]{2,1,0:T(8,128)(2,1)}, bf16[4,16,2304]{2,1,0:T(8,128)(2,1)}, u32[]{:S(2)}, u32[]{:S(2)}) collective-permute-start(bf16[4,16,2304]{2,1,0:T(8,128)(2,1)} %get-tuple-element.33), channel_id=1, source_target_pairs={{0,1},{1,0},{2,3},{3,2},{4,5},{5,4},{6,7},{7,6},{8,9},{9,8},{10,11... | collective-permute-start | bytes 884744 | tf_op jit(solution)/shard_map/ppermute | solution.py:651
  49.6 11.9 %collective-permute-start.4 = (bf16[4,16,2304]{2,1,0:T(8,128)(2,1)}, bf16[4,16,2304]{2,1,0:T(8,128)(2,1)}, u32[]{:S(2)}, u32[]{:S(2)}) collective-permute-start(bf16[4,16,2304]{2,1,0:T(8,128)(2,1)} %get-tuple-element.34), channel_id=1, source_target_pairs={{0,2},{1,3},{2,0},{3,1},{4,6},{5,7},{6,4},{7,5},{8,10},{9,11},{10,... | collective-permute-start | bytes 884744 | tf_op jit(solution)/shard_map/ppermute | solution.py:651
  49.6 23.9 %collective-permute-start.5 = (bf16[4,16,2304]{2,1,0:T(8,128)(2,1)}, bf16[4,16,2304]{2,1,0:T(8,128)(2,1)}, u32[]{:S(2)}, u32[]{:S(2)}) collective-permute-start(bf16[4,16,2304]{2,1,0:T(8,128)(2,1)} %get-tuple-element.35), channel_id=1, source_target_pairs={{0,3},{1,2},{2,1},{3,0},{4,7},{5,6},{6,5},{7,4},{8,11},{9,10},{10,... | collective-permute-start | bytes 884744 | tf_op jit(solution)/shard_map/ppermute | solution.py:651
  73.5 1.0 copy-start.3
  74.5 0.9 copy-start.5
  77.2 18.6 %collective-permute-start.6 = (f32[48,128]{1,0:T(8,128)S(1)}, f32[48,128]{1,0:T(8,128)S(1)}, u32[]{:S(2)}, u32[]{:S(2)}) collective-permute-start(f32[48,128]{1,0:T(8,128)S(1)} %get-tuple-element.40), channel_id=1, source_target_pairs={{0,1},{1,2},{2,3},{3,4},{4,5},{5,6},{6,7},{7,8},{8,9},{9,10},{10,1... | collective-permute-start | bytes 73736 | tf_op jit(solution)/shard_map/ppermute | solution.py:677
  79.2 16.5 %collective-permute-start.7 = (f32[48,128]{1,0:T(8,128)S(1)}, f32[48,128]{1,0:T(8,128)S(1)}, u32[]{:S(2)}, u32[]{:S(2)}) collective-permute-start(f32[48,128]{1,0:T(8,128)S(1)} %get-tuple-element.41), channel_id=1, source_target_pairs={{1,0},{2,1},{3,2},{4,3},{5,4},{6,5},{7,6},{8,7},{9,8},{10,9},{11,1... | collective-permute-start | bytes 73736 | tf_op jit(solution)/shard_map/ppermute | solution.py:678
  97.1 4.2 %collective-permute-start.8 = (f32[2,56,128]{2,1,0:T(8,128)S(1)}, f32[2,56,128]{2,1,0:T(8,128)S(1)}, u32[]{:S(2)}, u32[]{:S(2)}) collective-permute-start(f32[2,56,128]{2,1,0:T(8,128)S(1)} %get-tuple-element.45), channel_id=1, source_target_pairs={{0,16},{16,0},{1,17},{17,1},{2,18},{18,2},{3,19},{19,3},{4,20},{20... | collective-permute-start | bytes 172040 | tf_op jit(solution)/shard_map/ppermute | solution.py:684
